TPU v7x, 256 devices: a whole 4x4x8 slice. The times are simulated.
256 devices in a mesh: row: 32 (over z, y), col: 8 (over x, core).
Axes of the slice: x: 4, y: 4, z: 8, core: 2. Of those that a mesh axis runs over, the one named last changes fastest.
Arguments:
- features: bfloat16 [256, 128, 640], P('row', 'col'), may hold values from -6 to 6
- cotangent: bfloat16 [256, 128, 640], P('row', 'col'), may hold values from -8 to 8
- conv_weight: bfloat16 [3, 3, 640, 640], replicated, may hold values from -0.078125 to 0.078125
- gain: float32 [640], replicated, may hold values from 0.25 to 1.75
- shift: float32 [640], replicated, may hold values from -3 to 3
Outputs:
- block_input_gradient: bfloat16 [256, 128, 640], P('row', 'col')
- weight_grad: float32 [3, 3, 640, 640], P(None, None, 'row', 'col')
- norm_gain_gradient: float32 [640], replicated
- norm_shift_gradient: float32 [640], replicated
- time_bias_grad: float32 [640], replicated
All inputs are finite; a program needn't handle non-finite values.
Results may differ from a plain program's by a relative error of at most 0.0095.
Values may be sent and summed in bfloat16 or wider, within the bound.
No kernel may reach another device: no remote copies, remote signals or barrier semaphores. Data moves between devices by JAX's collectives and lax.ppermute only.
A program may use at most 128 MiB of HBM per device.

v0:
```python
import jax
import jax.numpy as jnp
from jax import lax
from jax.sharding import PartitionSpec as P

GW = 40
GROUPS = 16


def with_halo(value, sides, width):
    for axis, dim in sides:
        count, length = (lax.axis_size(axis), value.shape[dim])
        up = [(i, (i + 1) % count) for i in range(count - 1)]
        down = [(j, i) for i, j in up]
        last = lax.slice_in_dim(value, length - width, length, axis=dim)
        leading = lax.slice_in_dim(value, 0, width, axis=dim)
        before = lax.ppermute(last, axis, up)
        after = lax.ppermute(leading, axis, down)
        value = jnp.concatenate([before, value, after], axis=dim)
    return value


def group_total(values):
    return values.reshape(GROUPS, GW).sum(1)


def per_channel(values):
    return jnp.repeat(values, GW)


def body(features, cotangent, conv_weight, gain, shift):
    height, width, chans = features.shape
    pixels = height * width
    element_count = float(height * width * lax.axis_size("row") * lax.axis_size("col") * GW)
    feat = features.astype(jnp.float32)
    local_sum = group_total(feat.sum((0, 1)))
    bias_part = cotangent.astype(jnp.float32).sum((0, 1))
    total, time_bias_grad = lax.psum((local_sum, bias_part), ("row", "col"))
    mean = total / element_count
    centered_input = feat - per_channel(mean)
    squares = group_total((centered_input * centered_input).sum((0, 1)))
    var = lax.psum(squares, ("row", "col")) / element_count
    inverse_deviation = per_channel(lax.rsqrt(var + 1e-05))
    normalized_input = centered_input * inverse_deviation
    preactivation = normalized_input * gain + shift
    sig = jax.nn.sigmoid(preactivation)
    hidden = (preactivation * sig).astype(jnp.bfloat16)
    hid_pad = with_halo(hidden, (("row", 0), ("col", 1)), 1)
    grad_pad = with_halo(cotangent, (("row", 0), ("col", 1)), 1)
    grad_flat = cotangent.reshape(pixels, chans)
    taps = []
    back = jnp.zeros((pixels, chans), jnp.float32)
    for i in range(3):
        row_taps = []
        for j in range(3):
            window = hid_pad[i : i + height, j : j + width].reshape(pixels, chans)
            row_taps.append(
                lax.dot_general(
                    window, grad_flat, (((0,), (0,)), ((), ())), preferred_element_type=jnp.float32
                )
            )
            moved = grad_pad[2 - i : 2 - i + height, 2 - j : 2 - j + width].reshape(pixels, chans)
            back = back + lax.dot_general(
                moved,
                conv_weight[i, j],
                (((1,), (1,)), ((), ())),
                preferred_element_type=jnp.float32,
            )
        taps.append(jnp.stack(row_taps))
    partial_weight = jnp.stack(taps)[None]
    pieces = lax.all_to_all(
        partial_weight.astype(jnp.bfloat16), "row", split_axis=3, concat_axis=0, tiled=True
    ).astype(partial_weight.dtype)
    reduced = jnp.sum(pieces, axis=0)
    weight_grad = lax.psum_scatter(
        reduced.astype(jnp.bfloat16), "col", scatter_dimension=3, tiled=True
    ).astype(jnp.float32)
    dh = back.reshape(height, width, chans)
    preactivation_grad = dh * sig * (1.0 + preactivation * (1.0 - sig))
    norm_shift_gradient, norm_gain_gradient = lax.psum(
        (preactivation_grad.sum((0, 1)), (preactivation_grad * normalized_input).sum((0, 1))),
        ("row", "col"),
    )
    first_moment = per_channel(group_total(gain * norm_shift_gradient))
    second_moment = per_channel(group_total(gain * norm_gain_gradient))
    block_input_gradient = inverse_deviation * (
        preactivation_grad * gain
        - first_moment / element_count
        - normalized_input * second_moment / element_count
    )
    return (
        block_input_gradient.astype(jnp.bfloat16),
        weight_grad,
        norm_gain_gradient,
        norm_shift_gradient,
        time_bias_grad,
    )


def solution(mesh):
    placed = (P("row", "col", None), P("row", "col", None), P(), P(), P())
    return jax.shard_map(
        body,
        mesh=mesh,
        in_specs=placed,
        out_specs=(P("row", "col", None), P(None, None, "row", "col"), P(), P(), P()),
        check_vma=False,
    )
```

profile of v0, /device:TPU:1, one launch (start us, length us, event | category | flops | bytes accessed | tf_op | source)
XLA Modules:
  0.0 574.1 jit_solution(90173149761694057)
XLA Ops:
  7.2 1.0 convert_reduce_fusion
  8.1 0.1 reshape.125
  8.2 0.8 fusion.75
  9.0 0.1 reduce_sum.94
  9.1 1.3 collective-permute-start.1
  10.4 83.3 %psum.35 = f32[16]{0:T(128)S(1)} all-reduce(f32[16]{0:T(128)S(1)} %reduce_sum.94), channel_id=1, replica_groups=mesh['row'=32,'col'=8] {'row','col'}, use_global_device_ids=true, to_apply=%region_2.0 | all-reduce | flops 16 | bytes 128 | tf_op jit(solution)/shard_map/psum | solution.py:38
  93.7 0.1 broadcast_in_dim.8
  93.8 0.1 sub.24
  93.9 1.0 fusion.52
  94.8 0.1 reshape.126
  94.9 0.1 reduce_sum.96
  95.0 2.5 collective-permute-start
  97.5 75.1 %psum.36 = f32[16]{0:T(128)S(1)} all-reduce(f32[16]{0:T(128)S(1)} %reduce_sum.96), channel_id=1, replica_groups=mesh['row'=32,'col'=8] {'row','col'}, use_global_device_ids=true, to_apply=%region_5.0 | all-reduce | flops 16 | bytes 128 | tf_op jit(solution)/shard_map/psum | solution.py:42
  172.6 0.1 mul.65
  172.8 1.3 pad_maximum_fusion.5
  174.1 3.1 collective-permute-start.2
  177.3 2.7 collective-permute-start.3
  179.9 1.5 fusion.13
  181.5 1.5 fusion.20
  183.0 0.3 pad_maximum_fusion.4
  183.3 1.5 fusion.11
  184.8 1.5 convolution_add_fusion.5
  186.4 0.4 convolution_add_fusion.4
  186.8 0.4 convolution_add_fusion.3
  187.2 0.4 convolution_add_fusion.2
  187.6 0.4 convolution_add_fusion.1
  187.9 0.4 fusion.10
  188.3 0.2 fusion.71
  188.6 1.5 collective-permute-start.4
  190.1 1.3 collective-permute-start.5
  191.4 0.4 fusion.4
  191.8 3.1 collective-permute-done.5
  195.0 3.2 collective-permute-start.6
  198.2 2.1 collective-permute-start.7
  200.3 0.4 fusion.1
  200.7 0.4 fusion.7
  201.1 2.2 collective-permute-done.7
  203.3 0.1 maximum_maximum_fusion
  203.5 0.4 fusion.6
  203.9 0.4 fusion.3
  204.3 0.4 fusion
  204.7 0.4 fusion.8
  205.1 0.4 fusion.5
  205.6 0.4 fusion.2
  206.0 0.3 maximum_bitcast_fusion.2
  206.3 0.7 maximum_bitcast_fusion
  207.0 1.0 pad_maximum_fusion
  208.1 30.6 %copy.12 = bf16[1,3,3,640,640]{4,2,1,0,3:T(4,128)(2,1)} copy(bf16[1,3,3,640,640]{4,3,2,1,0:T(8,128)(2,1)S(1)} %pad_maximum_fusion) | data formatting | bytes 14745600 | tf_op jit(solution)/shard_map/stack | solution.py:70
  238.6 11.0 %all-to-all-start = ((bf16[1,3,3,640,640]{4,2,1,0,3:T(4,128)(2,1)}), bf16[1,3,3,640,640]{4,2,1,0,3:T(4,128)(2,1)}, u32[]{:S(2)}, u32[]{:S(2)}) async-start(bf16[1,3,3,640,640]{4,2,1,0,3:T(4,128)(2,1)} %copy.12), calls=%async_computation | async-start | bytes 19660800 | tf_op jit(solution)/shard_map/all_to_all | solution.py:71
  249.8 277.7 %all-reduce = (f32[640]{0:T(1024)S(1)}, f32[640]{0:T(1024)S(1)}, f32[640]{0:T(1024)}) all-reduce(f32[640]{0:T(1024)S(1)} %get-tuple-element.6, f32[640]{0:T(1024)S(1)} %get-tuple-element.5, f32[640]{0:T(1024)S(1)} %convert_reduce_fusion.1), channel_id=1, replica_groups=mesh['row'=32,'col'=8] {'row','col'}, use_global_device_ids=true, to_apply=%region_10.0 | all-reduce | flops 1920 | bytes 15360 | tf_op jit(solution)/shard_map/psum | solution.py:80
  527.4 0.1 reshape.137
  527.5 0.1 reduce_sum.98
  527.6 7.8 %reduce_sum.101 = bf16[3,3,20,640]{3,1,0,2:T(4,128)(2,1)S(1)} reduce(bf16[3,3,32,20,640]{4,1,0,3,2:T(4,128)(2,1)} %bitcast.40, bf16[]{:T(256)} %constant.15.clone.1), dimensions={2}, to_apply=%region_12.0 | reduce | flops 3571200 | bytes 7603202 | tf_op jit(solution)/shard_map/reduce_sum | solution.py:74
  535.5 1.7 copy.15
  537.3 2.0 reshape.148
  539.4 0.1 div.25
  539.5 0.1 reshape.138
  539.6 0.1 reduce_sum.100
  539.8 0.1 mul.77
  539.9 0.8 fusion.51
  540.6 24.8 %reduce-scatter.4.cloned.1.call-done = bf16[80,180]{1,0:T(8,128)(2,1)} async-done(((bf16[640,180]{1,0:T(8,128)(2,1)}), bf16[80,180]{1,0:T(8,128)(2,1)}) %reduce-scatter.4.cloned.1.call-update) | async-done | bytes 28816
  565.4 1.0 reshape.149
  566.4 0.2 copy.16
  566.6 0.7 convert_element_type.29
  (36 shorter events, 0.5 us)
Async XLA Ops:
  9.1 163.7 %collective-permute-start.1 = (bf16[1,16,640]{2,1,0:T(8,128)(2,1)S(1)}, bf16[1,16,640]{2,1,0:T(8,128)(2,1)S(1)}, u32[]{:S(2)}, u32[]{:S(2)}) collective-permute-start(bf16[1,16,640]{2,1,0:T(8,128)(2,1)S(1)} %get-tuple-element.32), channel_id=1, source_target_pairs={{8,0},{16,8},{24,16},{32,24},{40,32},{48,40},{56,48},{64,56},{72,6... | collective-permute-start | bytes 61448 | tf_op jit(solution)/shard_map/ppermute | solution.py:18
  95.0 77.7 %collective-permute-start = (bf16[1,16,640]{2,1,0:T(8,128)(2,1)S(1)}, bf16[1,16,640]{2,1,0:T(8,128)(2,1)S(1)}, u32[]{:S(2)}, u32[]{:S(2)}) collective-permute-start(bf16[1,16,640]{2,1,0:T(8,128)(2,1)S(1)} %get-tuple-element.33), channel_id=1, source_target_pairs={{0,8},{8,16},{16,24},{24,32},{32,40},{40,48},{48,56},{56,64},{64,7... | collective-permute-start | bytes 61448 | tf_op jit(solution)/shard_map/ppermute | solution.py:17
  172.8 13.6 %copy-start = (bf16[3,3,640,640]{3,2,1,0:T(8,128)(2,1)S(1)}, bf16[3,3,640,640]{3,2,1,0:T(8,128)(2,1)}, u32[]{:S(2)}) copy-start(bf16[3,3,640,640]{3,2,1,0:T(8,128)(2,1)} %param.7) | copy-start | bytes 22118404
  174.1 8.9 %collective-permute-start.2 = (bf16[10,1,640]{2,1,0:T(2,128)(2,1)S(1)}, bf16[10,1,640]{2,1,0:T(2,128)(2,1)S(1)}, u32[]{:S(2)}, u32[]{:S(2)}) collective-permute-start(bf16[10,1,640]{2,1,0:T(2,128)(2,1)S(1)} %get-tuple-element.24), channel_id=1, source_target_pairs={{1,0},{2,1},{3,2},{4,3},{5,4},{6,5},{7,6},{9,8},{10,9},{11,10},{12... | collective-permute-start | bytes 38408 | tf_op jit(solution)/shard_map/ppermute | solution.py:18
  177.3 5.7 %collective-permute-start.3 = (bf16[10,1,640]{2,1,0:T(2,128)(2,1)S(1)}, bf16[10,1,640]{2,1,0:T(2,128)(2,1)S(1)}, u32[]{:S(2)}, u32[]{:S(2)}) collective-permute-start(bf16[10,1,640]{2,1,0:T(2,128)(2,1)S(1)} %get-tuple-element.25), channel_id=1, source_target_pairs={{0,1},{1,2},{2,3},{3,4},{4,5},{5,6},{6,7},{8,9},{9,10},{10,11},{11... | collective-permute-start | bytes 38408 | tf_op jit(solution)/shard_map/ppermute | solution.py:17
  184.8 2.3 copy-start.2
  187.1 1.2 copy-start.1
  187.2 1.2 copy-start.3
  187.2 1.2 copy-start.4
  188.6 3.2 collective-permute-start.4
  190.1 4.9 collective-permute-start.5
  195.0 6.1 %collective-permute-start.6 = (bf16[10,1,640]{2,1,0:T(2,128)(2,1)S(1)}, bf16[10,1,640]{2,1,0:T(2,128)(2,1)S(1)}, u32[]{:S(2)}, u32[]{:S(2)}) collective-permute-start(bf16[10,1,640]{2,1,0:T(2,128)(2,1)S(1)} %get-tuple-element.19), channel_id=1, source_target_pairs={{0,1},{1,2},{2,3},{3,4},{4,5},{5,6},{6,7},{8,9},{9,10},{10,11},{11... | collective-permute-start | bytes 38408 | tf_op jit(solution)/shard_map/ppermute | solution.py:17
  198.2 5.2 collective-permute-start.7
  238.6 289.0 %all-to-all-start = ((bf16[1,3,3,640,640]{4,2,1,0,3:T(4,128)(2,1)}), bf16[1,3,3,640,640]{4,2,1,0,3:T(4,128)(2,1)}, u32[]{:S(2)}, u32[]{:S(2)}) async-start(bf16[1,3,3,640,640]{4,2,1,0,3:T(4,128)(2,1)} %copy.12), calls=%async_computation | async-start | bytes 19660800 | tf_op jit(solution)/shard_map/all_to_all | solution.py:71
  249.7 315.8 %reduce-scatter.4.cloned.1.call-start = ((), (), s32[]{:S(2)}) async-start(), calls=%async_computation.2 | async-start | bytes 368640
  527.4 8.1 %copy-start.5 = (f32[640]{0:T(1024)}, f32[640]{0:T(1024)S(1)}, u32[]{:S(2)}) copy-start(f32[640]{0:T(1024)S(1)} %get-tuple-element.7) | copy-start | bytes 7684
  527.4 8.1 %copy-start.6 = (f32[640]{0:T(1024)}, f32[640]{0:T(1024)S(1)}, u32[]{:S(2)}) copy-start(f32[640]{0:T(1024)S(1)} %get-tuple-element.8) | copy-start | bytes 7684
Sparse Core Ops, SparseCore 0:
  539.4 25.9 reduce-scatter.3
where the time goes:
time: 576 us; the launch traced here: 574 us
  blocking collectives  436 us (76%)
  local copies, waits for them, and re-layouts  37.3 us (6%)
  waiting for transfers between devices  30.2 us (5%)
  starting transfers between devices  28.7 us (5%)
  other arithmetic  15.7 us (3%)
  between operations  14.5 us (3%)
  matrix products  11.6 us (2%)
    psum x1, blocking collectives, body(): lax.psum((preactivation_grad.sum((0, 1)), (preactivation_grad * normalize...  278 us
    psum x1, blocking collectives, body(): total, time_bias_grad = lax.psum((local_sum, bias_part), ('row', 'col'))  83.3 us
    psum x1, blocking collectives, body(): var = lax.psum(squares, ('row', 'col')) / element_count  75.1 us
    another operation x1, local copies, waits for them, and re-layouts, body(): partial_weight = jnp.stack(taps)[None]  30.6 us
    unnamed x2, waiting for transfers between devices  24.8 us
  transfers between devices with their start and end apart: 10, of which 3 were waited for; matrix products, arithmetic and copies ran while one was open for 1% of the time, Pallas kernels for 0%

commit v1 on v0

v1 whole, which is shorter than its diff:
```python
import numpy as np

import jax
import jax.numpy as jnp
from jax import lax
from jax.experimental import pallas as pl
from jax.experimental.pallas import tpu as pltpu
from jax.sharding import Mesh
from jax.sharding import PartitionSpec as P

C = 640
GW = 40
GROUPS = 16
TR, TC = 8, 16
PIX = TR * TC
NZ, NY, NX = 8, 4, 4
PEERS = NY * NX
ROWS = NY * TR
PL, QL = NZ * 32, 128
NQ = 80
TOTAL = float(NZ * PEERS * 2 * PIX * GW)
VMEM_LIMIT = 48 * 1024 * 1024


def feature_columns():
    out = np.full((1, NY * PL), -1, np.int32)
    for y in range(NY):
        for z in range(NZ):
            for k in range(20):
                out[0, y * PL + z * 32 + k] = z * 80 + y * 20 + k
    return out


def cotangent_columns():
    out = np.full((1, NX * QL), -10000, np.int32)
    for x in range(NX):
        out[0, x * QL : x * QL + NQ] = x * 160 + np.arange(NQ)
    return out


def vmem():
    return pl.BlockSpec(memory_space=pltpu.VMEM)


def group_matrix():
    chan = lax.broadcasted_iota(jnp.int32, (C, 128), 0)
    group = lax.broadcasted_iota(jnp.int32, (C, 128), 1)
    low = group * GW
    return jnp.where((chan >= low) & (chan < low + GW), 1.0, 0.0).astype(jnp.float32)


def exact_dot(a, b, dims):
    return lax.dot_general(
        a, b, (dims, ((), ())), precision=lax.Precision.HIGHEST, preferred_element_type=jnp.float32
    )


def pack_kernel(feat_ref, cot_ref, first_ref, second_ref, fcol_ref, ccol_ref, out_ref, stat_ref, bias_ref):
    feat = feat_ref[...]
    x = feat.astype(jnp.float32)
    groups = group_matrix()
    total = jnp.broadcast_to(x.sum(0, keepdims=True), (8, C))
    mean = exact_dot(total, groups, ((1,), (0,))) / float(PIX * GW)
    centre = x - exact_dot(mean, groups, ((1,), (1,)))[:1]
    squares = jnp.broadcast_to((centre * centre).sum(0, keepdims=True), (8, C))
    stat_ref[0] = mean
    stat_ref[1] = exact_dot(squares, groups, ((1,), (0,)))
    bias_ref[...] = jnp.broadcast_to(cot_ref[...].astype(jnp.float32).sum(0, keepdims=True), (8, C))
    rows = lax.broadcasted_iota(jnp.int32, (C, NY * PL), 0)
    pick = (rows == fcol_ref[...]).astype(jnp.float32).astype(jnp.bfloat16)
    moved = jnp.dot(feat, pick, preferred_element_type=jnp.float32).astype(jnp.bfloat16)
    rows = lax.broadcasted_iota(jnp.int32, (C, NX * QL), 0)
    pick = (rows == ccol_ref[...]).astype(jnp.float32).astype(jnp.bfloat16)
    first = jnp.dot(first_ref[...], pick, preferred_element_type=jnp.float32).astype(jnp.bfloat16)
    second = jnp.dot(second_ref[...], pick, preferred_element_type=jnp.float32).astype(jnp.bfloat16)
    for y in range(NY):
        for xx in range(NX):
            p = y * NX + xx
            out_ref[p, :, :PL] = moved[:, y * PL : (y + 1) * PL]
            out_ref[p, :, PL : PL + QL] = first[:, xx * QL : (xx + 1) * QL]
            out_ref[p, :, PL + QL :] = second[:, xx * QL : (xx + 1) * QL]


def back_kernel(top_ref, cot_ref, bottom_ref, left_ref, right_ref, w_ref, out_ref, shifted, acc):
    step = pl.program_id(0)
    rows = (TR + 2) * TC

    @pl.when(step == 0)
    def _():
        full = jnp.concatenate([top_ref[...], cot_ref[...], bottom_ref[...]], axis=0)
        shifted[1] = full
        wide = full.astype(jnp.float32)
        col = lax.broadcasted_iota(jnp.int32, (rows, C), 0) % TC
        left = left_ref[...].astype(jnp.float32)
        right = right_ref[...].astype(jnp.float32)
        left = jnp.broadcast_to(left[:, None, :], (TR + 2, TC, C)).reshape(rows, C)
        right = jnp.broadcast_to(right[:, None, :], (TR + 2, TC, C)).reshape(rows, C)
        shifted[0] = jnp.where(col == 0, left, pltpu.roll(wide, 1, 0)).astype(jnp.bfloat16)
        shifted[2] = jnp.where(col == TC - 1, right, pltpu.roll(wide, rows - 1, 0)).astype(jnp.bfloat16)
        acc[...] = jnp.zeros_like(acc)

    i, j = step // 3, step % 3
    lhs = shifted[2 - j, pl.ds(pl.multiple_of((2 - i) * TC, TC), PIX), :]
    acc[...] += lax.dot_general(
        lhs, w_ref[0, 0], (((1,), (1,)), ((), ())), preferred_element_type=jnp.float32
    )

    @pl.when(step == 8)
    def _():
        out_ref[...] = acc[...]


def terms_kernel(core_ref, own_ref, other_ref, above_ref, below_ref, par_ref, out_ref, hid, strips, cot3):
    core = core_ref[0]
    mean, scale, shift = par_ref[0:1], par_ref[1:2], par_ref[2:3]

    def put(block, peer, side):
        a = (block.astype(jnp.float32) - mean) * scale + shift
        value = (a * jax.nn.sigmoid(a)).astype(jnp.bfloat16)
        y, xx = peer // NX, peer % NX
        for r in range(TR):
            at = (y * TR + r) * 128 + xx * 32 + side * TC
            hid[pl.ds(pl.multiple_of(at, TC), TC), :] = value[r * TC : (r + 1) * TC]

    for peer in range(PEERS):
        put(own_ref[peer, :, :PL], peer, core)
        put(other_ref[peer], peer, 1 - core)
        y, xx = peer // NX, peer % NX
        for side in range(2):
            lanes = slice(PL + side * QL, PL + (side + 1) * QL)
            for r in range(TR):
                at = (y * TR + r + 1) * 128 + xx * 32 + side * TC
                strips[at : at + TC, :] = own_ref[peer, r * TC : (r + 1) * TC, lanes]
    strips[0:128, :] = above_ref[...]
    strips[(ROWS + 1) * 128 :, :] = below_ref[...]
    lane = lax.broadcasted_iota(jnp.int32, (NQ, 128), 1)
    for row in range(ROWS + 2):
        at = slice(row * 128, (row + 1) * 128)
        turned = strips[at, :].astype(jnp.float32).T[:NQ]
        before = jnp.where(lane == 0, 0.0, pltpu.roll(turned, 1, 1))
        after = jnp.where(lane == 127, 0.0, pltpu.roll(turned, 127, 1))
        cot3[0:NQ, at] = after.astype(jnp.bfloat16)
        cot3[NQ : 2 * NQ, at] = turned.astype(jnp.bfloat16)
        cot3[2 * NQ :, at] = before.astype(jnp.bfloat16)
    for i in range(3):
        lhs = cot3[:, (2 - i) * 128 : (2 - i) * 128 + ROWS * 128]
        turned = jnp.dot(lhs, hid[...], preferred_element_type=jnp.float32)
        out_ref[:, i] = turned.T.astype(jnp.bfloat16).reshape(NZ, 32, 3 * NQ)


def merge(stats, count):
    means, squares = stats[:, 0], stats[:, 1]
    mean = means.mean(0)
    return jnp.stack([mean, squares.sum(0) + count * ((means - mean) ** 2).sum(0)])


def flip(value):
    return lax.ppermute(value, "core", [(0, 1), (1, 0)])


def share(value, axes, count):
    return lax.all_to_all(jnp.broadcast_to(value, (count,) + value.shape), axes, 0, 0)


def per_channel(values):
    return jnp.repeat(values, GW)


def group_total(values):
    return values.reshape(GROUPS, GW).sum(1)


def body(features, cotangent, conv_weight, gain, shift):
    f32, bf16 = jnp.float32, jnp.bfloat16
    core, y = lax.axis_index("core"), lax.axis_index("y")
    feat = features.reshape(PIX, C)
    cot = cotangent.reshape(PIX, C)
    cot_other = flip(cot)
    up = [(k, k + 1) for k in range(NZ * NY - 1)]
    top = lax.ppermute(cotangent[TR - 1], ("z", "y"), up)
    bottom = lax.ppermute(cotangent[0], ("z", "y"), [(b, a) for a, b in up])
    edges = jnp.concatenate([top[None], cotangent, bottom[None]], axis=0)
    side = [(k, k + 1) for k in range(2 * NX - 1)]
    left = lax.ppermute(edges[:, TC - 1], ("x", "core"), side)
    right = lax.ppermute(edges[:, 0], ("x", "core"), [(b, a) for a, b in side])

    first = jnp.where(core == 0, cot, cot_other)
    second = jnp.where(core == 0, cot_other, cot)
    fcol = jnp.asarray(feature_columns())
    ccol = jnp.asarray(cotangent_columns()) + core * NQ
    packed, stats, bias = pl.pallas_call(
        pack_kernel,
        out_shape=(
            jax.ShapeDtypeStruct((PEERS, PIX, PL + 2 * QL), bf16),
            jax.ShapeDtypeStruct((2, 8, 128), f32),
            jax.ShapeDtypeStruct((8, C), f32),
        ),
        in_specs=[vmem()] * 6,
        out_specs=(vmem(), vmem(), vmem()),
        compiler_params=pltpu.CompilerParams(vmem_limit_bytes=VMEM_LIMIT),
        name="pack",
    )(feat, cot, first, second, fcol, ccol)

    stats = merge(share(stats[:, 0], ("y", "x"), PEERS), float(PIX * GW))
    slab = lax.all_to_all(packed, ("y", "x"), 0, 0)
    slab_other = flip(slab[:, :, :PL])
    stats = merge(share(stats, "z", NZ), float(PEERS * PIX * GW))
    stats = merge(jnp.stack([stats, flip(stats)]), float(NZ * PEERS * PIX * GW))
    mean = per_channel(stats[0, :GROUPS])
    rstd = per_channel(lax.rsqrt(stats[1, :GROUPS] / TOTAL + 1e-05))

    slab_cot = slab[:, :, PL:].reshape(NY, NX, TR, TC, 2, QL)
    last_row = slab_cot[NY - 1, :, TR - 1].transpose(0, 2, 1, 3).reshape(128, QL)
    first_row = slab_cot[0, :, 0].transpose(0, 2, 1, 3).reshape(128, QL)
    slabs = [(k, k + 1) for k in range(NZ - 1)]
    above = lax.ppermute(last_row, "z", slabs)
    below = lax.ppermute(first_row, "z", [(b, a) for a, b in slabs])

    back = pl.pallas_call(
        back_kernel,
        grid=(9,),
        out_shape=jax.ShapeDtypeStruct((PIX, C), f32),
        in_specs=[vmem()] * 5 + [pl.BlockSpec((1, 1, C, C), lambda t: (t // 3, t % 3, 0, 0))],
        out_specs=vmem(),
        scratch_shapes=[
            pltpu.VMEM((3, (TR + 2) * TC, C), bf16),
            pltpu.VMEM((PIX, C), f32),
        ],
        compiler_params=pltpu.CompilerParams(vmem_limit_bytes=VMEM_LIMIT),
        cost_estimate=pl.CostEstimate(flops=2 * PIX * 9 * C * C, bytes_accessed=18 * C * C, transcendentals=0),
        name="back",
    )(top, cot, bottom, left, right, conv_weight)

    xhat = (feat.astype(f32) - mean) * rstd
    act = xhat * gain + shift
    sig = jax.nn.sigmoid(act)
    da = back * sig * (1.0 + act * (1.0 - sig))
    sums = jnp.stack([da.sum(0), (da * xhat).sum(0), bias[0]])
    sums = sums + flip(sums)
    sums = share(sums, ("y", "x"), PEERS).sum(0)

    params = jnp.stack([mean, rstd * gain, shift]).reshape(3, NZ, NY, 20)
    params = lax.dynamic_index_in_dim(params, y, 2, keepdims=False)
    params = jnp.pad(params, ((0, 5), (0, 0), (0, 12))).reshape(8, PL)
    terms = pl.pallas_call(
        terms_kernel,
        out_shape=jax.ShapeDtypeStruct((NZ, 3, 32, 3 * NQ), bf16),
        in_specs=[pl.BlockSpec(memory_space=pltpu.SMEM)] + [vmem()] * 5,
        out_specs=vmem(),
        scratch_shapes=[
            pltpu.VMEM((ROWS * 128, PL), bf16),
            pltpu.VMEM(((ROWS + 2) * 128, QL), bf16),
            pltpu.VMEM((3 * NQ, (ROWS + 2) * 128), bf16),
        ],
        compiler_params=pltpu.CompilerParams(vmem_limit_bytes=VMEM_LIMIT),
        cost_estimate=pl.CostEstimate(
            flops=2 * PIX * 9 * C * C, bytes_accessed=4 << 20, transcendentals=ROWS * 128 * PL
        ),
        name="terms",
    )(core.reshape(1), slab, slab_other, above, below, params)
    pieces = lax.all_to_all(terms, "z", 0, 0)
    weight_grad = pieces.astype(f32).sum(0)[:, :20].reshape(3, 20, 3, NQ).transpose(0, 2, 1, 3)

    sums = share(sums, "z", NZ).sum(0)
    shift_grad, gain_grad, bias_grad = sums[0], sums[1], sums[2]
    moment1 = per_channel(group_total(gain * shift_grad))
    moment2 = per_channel(group_total(gain * gain_grad))
    grad = rstd * (da * gain - moment1 / TOTAL - xhat * moment2 / TOTAL)
    return grad.astype(bf16).reshape(features.shape), weight_grad, gain_grad, shift_grad, bias_grad


def solution(mesh):
    grid = Mesh(mesh.devices.reshape(NZ, NY, NX, 2), ("z", "y", "x", "core"))
    rows, cols = ("z", "y"), ("x", "core")
    tiled = P(rows, cols, None)
    return jax.shard_map(
        body,
        mesh=grid,
        in_specs=(tiled, tiled, P(), P(), P()),
        out_specs=(tiled, P(None, None, rows, cols), P(), P(), P()),
        check_vma=False,
    )
```

time: 576 us -> 147 us (0.26)
  the two profiles are of different devices: /device:TPU:1 before, /device:TPU:2 now
where the time goes in v1:
time: 147 us; the launch traced here: 146 us
  starting transfers between devices  52.5 us (36%)
  waiting for transfers between devices  46.3 us (31%)
  local copies, waits for them, and re-layouts  15 us (10%)
  Pallas kernels  13.7 us (9%)
  blocking collectives  12 us (8%)
  other arithmetic  5.01 us (3%)
    all_to_all x3, starting transfers between devices, share(): lax.all_to_all(jnp.broadcast_to(value, (count,) + value.shape), axes, 0, 0)  29.3 us
    all_to_all x3, waiting for transfers between devices, share(): lax.all_to_all(jnp.broadcast_to(value, (count,) + value.shape), axes, 0, 0)  16.7 us
    all_to_all x1, waiting for transfers between devices, body(): slab = lax.all_to_all(packed, ('y', 'x'), 0, 0)  15 us
    all_to_all x1, blocking collectives, share(): lax.all_to_all(jnp.broadcast_to(value, (count,) + value.shape), axes, 0, 0)  12 us
    all_to_all x1, waiting for transfers between devices, body(): pieces = lax.all_to_all(terms, 'z', 0, 0)  9.3 us
    pallas_call x1, Pallas kernels, body(): pl.pallas_call(back_kernel, grid=(9,), out_shape=jax.ShapeDtypeStruct((PI...  7.99 us
    unnamed x24, local copies, waits for them, and re-layouts  5.5 us
    all_to_all x1, starting transfers between devices, body(): slab = lax.all_to_all(packed, ('y', 'x'), 0, 0)  5.1 us
  transfers between devices with their start and end apart: 15, of which 8 were waited for; matrix products, arithmetic and copies ran while one was open for 10% of the time, Pallas kernels for 7%

profile of v1, /device:TPU:2, one launch (start us, length us, event | category | flops | bytes accessed | tf_op | source)
XLA Modules:
  0.0 145.6 jit_solution(14972193591115484676)
XLA Ops:
  0.6 0.8 slice_bitcast_fusion
  1.4 1.3 collective-permute-start.3
  2.7 4.5 %collective-permute-start.2 = (bf16[16,640]{1,0:T(8,128)(2,1)S(1)}, bf16[16,640]{1,0:T(8,128)(2,1)S(1)}, u32[]{:S(2)}, u32[]{:S(2)}) collective-permute-start(bf16[16,640]{1,0:T(8,128)(2,1)S(1)} %get-tuple-element.43), channel_id=1, source_target_pairs={{0,8},{8,16},{16,24},{24,32},{32,40},{40,48},{48,56},{56,64},{64,7... | collective-permute-start | bytes 61448 | tf_op jit(solution)/shard_map/ppermute | solution.py:180
  7.2 0.1 collective-permute-start
  7.3 0.7 broadcast_add_fusion.ccol_ref
  8.0 0.9 collective-permute-done
  8.9 1.0 broadcast_select_fusion
  9.9 0.9 copy-done
  10.8 0.9 copy-done.3
  11.7 0.7 copy-done.5
  12.4 1.7 %pack.1 = (bf16[16,128,512]{2,1,0:T(8,128)(2,1)S(1)}, f32[2,8,128]{2,1,0:T(8,128)S(1)}, f32[8,640]{1,0:T(8,128)S(1)}) custom-call(bf16[128,640]{1,0:T(8,128)(2,1)S(1)} %bitcast.63, bf16[128,640]{1,0:T(8,128)(2,1)S(1)} %bitcast.61, bf16[128,640]{1,0:T(8,128)(2,1)S(1)} %get-tuple-element.39.first_ref, bf16[128,640]{1,0:T(8,128)(2,1)S(1)} %get-tuple-element.38.second_ref, ...), custom_call_target="tpu_custom_call" | custom-call | tf_op jit(solution)/shard_map/pack/pallas_call | solution.py:191
  14.1 1.3 copy-done.2
  15.5 0.6 broadcast_in_dim.45
  16.1 9.4 %all-to-all-start = ((f32[16,2,128]{2,1,0:T(2,128)}), f32[16,2,128]{2,1,0:T(2,128)S(1)}, u32[]{:S(2)}, u32[]{:S(2)}) async-start(f32[16,2,128]{2,1,0:T(2,128)} %broadcast_in_dim.45), calls=%async_computation | async-start | bytes 32768 | tf_op jit(solution)/shard_map/all_to_all | solution.py:162
  25.5 0.9 copy.37
  26.6 5.2 %all-to-all-done = f32[16,2,128]{2,1,0:T(2,128)S(1)} async-done(((f32[16,2,128]{2,1,0:T(2,128)}), f32[16,2,128]{2,1,0:T(2,128)S(1)}, u32[]{:S(2)}, u32[]{:S(2)}) %all-to-all-start) | async-done | bytes 16416 | tf_op jit(solution)/shard_map/all_to_all | solution.py:162
  31.8 0.6 broadcast_in_dim.46
  32.4 8.5 %all-to-all-start.1 = ((f32[8,2,128]{2,1,0:T(2,128)}), f32[8,2,128]{2,1,0:T(2,128)S(1)}, u32[]{:S(2)}, u32[]{:S(2)}) async-start(f32[8,2,128]{2,1,0:T(2,128)} %broadcast_in_dim.46), calls=%async_computation.1 | async-start | bytes 16384 | tf_op jit(solution)/shard_map/all_to_all | solution.py:162
  40.9 1.9 %collective-permute-start.5 = (bf16[10,640]{1,0:T(8,128)(2,1)S(1)}, bf16[10,640]{1,0:T(8,128)(2,1)S(1)}, u32[]{:S(2)}, u32[]{:S(2)}) collective-permute-start(bf16[10,640]{1,0:T(8,128)(2,1)S(1)} %get-tuple-element.40), channel_id=1, source_target_pairs={{1,0},{2,1},{3,2},{4,3},{5,4},{6,5},{7,6},{9,8},{10,9},{11,10},{12... | collective-permute-start | bytes 38408 | tf_op jit(solution)/shard_map/ppermute | solution.py:185
  42.9 2.4 %collective-permute-start.4 = (bf16[10,640]{1,0:T(8,128)(2,1)S(1)}, bf16[10,640]{1,0:T(8,128)(2,1)S(1)}, u32[]{:S(2)}, u32[]{:S(2)}) collective-permute-start(bf16[10,640]{1,0:T(8,128)(2,1)S(1)} %get-tuple-element.41), channel_id=1, source_target_pairs={{0,1},{1,2},{2,3},{3,4},{4,5},{5,6},{6,7},{8,9},{9,10},{10,11},{11... | collective-permute-start | bytes 38408 | tf_op jit(solution)/shard_map/ppermute | solution.py:184
  45.3 3.4 %all-to-all-done.1 = f32[8,2,128]{2,1,0:T(2,128)S(1)} async-done(((f32[8,2,128]{2,1,0:T(2,128)}), f32[8,2,128]{2,1,0:T(2,128)S(1)}, u32[]{:S(2)}, u32[]{:S(2)}) %all-to-all-start.1) | async-done | bytes 8224 | tf_op jit(solution)/shard_map/all_to_all | solution.py:162
  48.6 5.1 %all-to-all-start.4 = ((bf16[16,128,512]{2,1,0:T(8,128)(2,1)}), bf16[16,128,512]{2,1,0:T(8,128)(2,1)S(1)}, u32[]{:S(2)}, u32[]{:S(2)}) async-start(bf16[16,128,512]{2,1,0:T(8,128)(2,1)} %copy-done.2), calls=%async_computation.4 | async-start | bytes 4194304 | tf_op jit(solution)/shard_map/all_to_all | solution.py:205
  53.9 0.1 collective-permute-start.1
  54.0 8.0 %back.1 = f32[128,640]{1,0:T(8,128)S(1)} custom-call(bf16[16,640]{1,0:T(8,128)(2,1)S(1)} %collective-permute-done.2.top_ref, bf16[128,640]{1,0:T(8,128)(2,1)S(1)} %bitcast.62, bf16[16,640]{1,0:T(8,128)(2,1)S(1)} %collective-permute-done.3.bottom_ref, bf16[10,640]{1,0:T(8,128)(2,1)S(1)} %collective-permute-done.4.left_ref, ...), custom_call_target="tpu_custom_call" | custom-call | flops 943718400 | bytes 7372800 | tf_op jit(solution)/shard_map/back/pallas_call | solution.py:219
  62.1 0.1 broadcast_in_dim.47
  62.2 0.1 mul.113
  62.4 0.1 sub.54
  62.5 0.9 fusion.10
  63.4 0.6 collective-permute-start.6
  64.0 15.0 %all-to-all-done.4.own_ref = bf16[16,128,512]{2,1,0:T(8,128)(2,1)S(1)} async-done(((bf16[16,128,512]{2,1,0:T(8,128)(2,1)}), bf16[16,128,512]{2,1,0:T(8,128)(2,1)S(1)}, u32[]{:S(2)}, u32[]{:S(2)}) %all-to-all-start.4) | async-done | bytes 2097184 | tf_op jit(solution)/shard_map/all_to_all | solution.py:205
  79.0 1.6 %fusion.12 = (bf16[16,128,256]{2,1,0:T(8,128)(2,1)}, bf16[16,128,256]{2,1,0:T(8,128)(2,1)}) fusion(bf16[16,128,512]{2,1,0:T(8,128)(2,1)S(1)} %all-to-all-done.4.own_ref), kind=kLoop, calls=%fused_computation.50 | loop fusion | bytes 4194304 | tf_op jit(solution)/shard_map/slice | solution.py:212
  80.7 12.0 %all_to_all.30 = f32[16,3,640]{2,1,0:T(4,128)S(1)} all-to-all(f32[16,3,640]{2,1,0:T(4,128)S(1)} %broadcast_in_dim.51), channel_id=1, replica_groups=mesh['z'=8,'y'=4,'x'=4,'core'=2] {'y','x'}, dimensions={0} | all-to-all | bytes 245760 | tf_op jit(solution)/shard_map/all_to_all | solution.py:162
  92.8 0.6 broadcast_in_dim.52
  93.4 11.4 %all-to-all-start.3 = ((f32[8,3,640]{2,1,0:T(4,128)}), f32[8,3,640]{2,1,0:T(4,128)S(1)}, u32[]{:S(2)}, u32[]{:S(2)}) async-start(f32[8,3,640]{2,1,0:T(4,128)} %broadcast_in_dim.52), calls=%async_computation.3 | async-start | bytes 163840 | tf_op jit(solution)/shard_map/all_to_all | solution.py:162
  104.8 0.1 stack.48
  104.9 0.1 broadcast_in_dim.55
  105.0 0.1 copy.43
  105.1 0.1 copy.44
  105.2 8.2 %all-to-all-done.3 = f32[8,3,640]{2,1,0:T(4,128)S(1)} async-done(((f32[8,3,640]{2,1,0:T(4,128)}), f32[8,3,640]{2,1,0:T(4,128)S(1)}, u32[]{:S(2)}, u32[]{:S(2)}) %all-to-all-start.3) | async-done | bytes 61472 | tf_op jit(solution)/shard_map/all_to_all | solution.py:162
  113.4 0.6 slice_reduce_fusion
  114.0 0.1 stack.47
  114.1 2.2 %reshape.161 = bf16[4,4,8,16,2,128]{5,4,3,2,1,0:T(2,128)(2,1)} reshape(bf16[16,128,256]{2,1,0:T(8,128)(2,1)} %get-tuple-element.34) | data formatting | bytes 2097152 | tf_op jit(solution)/shard_map/reshape | solution.py:212
  116.3 0.8 fusion.13
  117.1 2.5 %collective-permute-start.8 = (bf16[128,128]{1,0:T(8,128)(2,1)S(1)}, bf16[128,128]{1,0:T(8,128)(2,1)S(1)}, u32[]{:S(2)}, u32[]{:S(2)}) collective-permute-start(bf16[128,128]{1,0:T(8,128)(2,1)S(1)} %bitcast.74), channel_id=1, source_target_pairs={{0,32},{32,64},{64,96},{96,128},{128,160},{160,192},{192,224},{1,3... | collective-permute-start | bytes 98312 | tf_op jit(solution)/shard_map/ppermute | solution.py:216
  119.6 1.3 collective-permute-start.9
  120.9 0.1 broadcast_in_dim.58
  121.0 0.1 reshape.164.par_ref
  121.1 0.1 collective-permute-done.8.above_ref
  121.2 4.2 %collective-permute-done.9.below_ref = bf16[128,128]{1,0:T(8,128)(2,1)S(1)} collective-permute-done((bf16[128,128]{1,0:T(8,128)(2,1)S(1)}, bf16[128,128]{1,0:T(8,128)(2,1)S(1)}, u32[]{:S(2)}, u32[]{:S(2)}) %collective-permute-start.9) | collective-permute-done | bytes 32800 | tf_op jit(solution)/shard_map/ppermute | solution.py:217
  125.4 4.0 %terms.1 = bf16[8,3,32,240]{3,2,1,0:T(8,128)(2,1)} custom-call(s32[1]{0:T(128)} %bitcast.27.core_ref, bf16[16,128,512]{2,1,0:T(8,128)(2,1)S(1)} %all-to-all-done.4.own_ref, bf16[16,128,256]{2,1,0:T(8,128)(2,1)S(1)} %collective-permute-done.7.other_ref, bf16[128,128]{1,0:T(8,128)(2,1)S(1)} %collective-permute-done.8.above_ref, ...), custom_call_target="tpu_custom_call" | custom-call | flops 943718400 | bytes 4194304 | tf_op jit(solution)/shard_map/terms/pallas_call | solution.py:245
  129.5 3.5 %all-to-all-start.5 = ((bf16[8,3,32,240]{3,2,1,0:T(8,128)(2,1)}), bf16[8,3,32,240]{3,2,1,0:T(8,128)(2,1)S(1)}, u32[]{:S(2)}, u32[]{:S(2)}) async-start(bf16[8,3,32,240]{3,2,1,0:T(8,128)(2,1)} %terms.1), calls=%async_computation.5 | async-start | bytes 786432 | tf_op jit(solution)/shard_map/all_to_all | solution.py:261
  132.9 0.1 reshape.157
  133.0 0.1 reduce_sum.157
  133.1 0.1 broadcast_in_dim.53
  133.2 0.1 div.57
  133.3 0.1 reshape.158
  133.4 0.1 reduce_sum.158
  133.5 0.1 broadcast_in_dim.54
  133.6 0.1 mul.125
  133.7 1.8 %multiply_convert_fusion = bf16[128,640]{1,0:T(8,128)(2,1)} fusion(f32[128,640]{1,0:T(8,128)} %get-tuple-element.31, f32[640]{0:T(1024)S(1)} %mul.125, f32[640]{0:T(1024)S(1)} %div.57, f32[640]{0:T(1024)S(1)} %copy-done.6, f32[640]{0:T(1024)S(1)} %sub.54, f32[640]{0:T(1024)S(1)} %mul.113, bf16[8,16,640]{2,1,0:T(8,128)(2,1)S(1)} %copy-done.4), kind=kLoop, calls=%fused_computation.1 | loop fusion | flops 819200 | bytes 668160 | tf_op jit(solution)/shard_map/convert_element_type | solution.py:269
  135.4 9.3 %all-to-all-done.5 = bf16[8,3,32,240]{3,2,1,0:T(8,128)(2,1)S(1)} async-done(((bf16[8,3,32,240]{3,2,1,0:T(8,128)(2,1)}), bf16[8,3,32,240]{3,2,1,0:T(8,128)(2,1)S(1)}, u32[]{:S(2)}, u32[]{:S(2)}) %all-to-all-start.5) | async-done | bytes 368672 | tf_op jit(solution)/shard_map/all_to_all | solution.py:261
  144.7 0.1 convert_reduce_fusion
  144.8 0.1 reshape.165
  144.9 0.7 copy.45
  (65 shorter events, 0.7 us)
Async XLA Ops:
  1.4 25.1 %collective-permute-start.3 = (bf16[16,640]{1,0:T(8,128)(2,1)S(1)}, bf16[16,640]{1,0:T(8,128)(2,1)S(1)}, u32[]{:S(2)}, u32[]{:S(2)}) collective-permute-start(bf16[16,640]{1,0:T(8,128)(2,1)S(1)} %get-tuple-element.42), channel_id=1, source_target_pairs={{8,0},{16,8},{24,16},{32,24},{40,32},{48,40},{56,48},{64,56},{72,6... | collective-permute-start | bytes 61448 | tf_op jit(solution)/shard_map/ppermute | solution.py:181
  2.7 23.8 %collective-permute-start.2 = (bf16[16,640]{1,0:T(8,128)(2,1)S(1)}, bf16[16,640]{1,0:T(8,128)(2,1)S(1)}, u32[]{:S(2)}, u32[]{:S(2)}) collective-permute-start(bf16[16,640]{1,0:T(8,128)(2,1)S(1)} %get-tuple-element.43), channel_id=1, source_target_pairs={{0,8},{8,16},{16,24},{24,32},{32,40},{40,48},{48,56},{56,64},{64,7... | collective-permute-start | bytes 61448 | tf_op jit(solution)/shard_map/ppermute | solution.py:180
  7.2 1.7 %collective-permute-start = (bf16[128,640]{1,0:T(8,128)(2,1)}, bf16[128,640]{1,0:T(8,128)(2,1)S(1)}, u32[]{:S(2)}, u32[]{:S(2)}) collective-permute-start(bf16[128,640]{1,0:T(8,128)(2,1)} %bitcast.60), channel_id=1, source_target_pairs={{0,1},{1,0},{2,3},{3,2},{4,5},{5,4},{6,7},{7,6},{8,9},{9,8},{10,11... | collective-permute-start | bytes 491528 | tf_op jit(solution)/shard_map/ppermute | solution.py:158
  9.9 0.9 copy-start
  10.8 0.9 copy-start.3
  11.7 0.7 copy-start.5
  14.1 1.4 copy-start.2
  16.1 15.6 %all-to-all-start = ((f32[16,2,128]{2,1,0:T(2,128)}), f32[16,2,128]{2,1,0:T(2,128)S(1)}, u32[]{:S(2)}, u32[]{:S(2)}) async-start(f32[16,2,128]{2,1,0:T(2,128)} %broadcast_in_dim.45), calls=%async_computation | async-start | bytes 32768 | tf_op jit(solution)/shard_map/all_to_all | solution.py:162
  32.4 16.2 %all-to-all-start.1 = ((f32[8,2,128]{2,1,0:T(2,128)}), f32[8,2,128]{2,1,0:T(2,128)S(1)}, u32[]{:S(2)}, u32[]{:S(2)}) async-start(f32[8,2,128]{2,1,0:T(2,128)} %broadcast_in_dim.46), calls=%async_computation.1 | async-start | bytes 16384 | tf_op jit(solution)/shard_map/all_to_all | solution.py:162
  40.9 13.0 %collective-permute-start.5 = (bf16[10,640]{1,0:T(8,128)(2,1)S(1)}, bf16[10,640]{1,0:T(8,128)(2,1)S(1)}, u32[]{:S(2)}, u32[]{:S(2)}) collective-permute-start(bf16[10,640]{1,0:T(8,128)(2,1)S(1)} %get-tuple-element.40), channel_id=1, source_target_pairs={{1,0},{2,1},{3,2},{4,3},{5,4},{6,5},{7,6},{9,8},{10,9},{11,10},{12... | collective-permute-start | bytes 38408 | tf_op jit(solution)/shard_map/ppermute | solution.py:185
  42.9 11.1 %collective-permute-start.4 = (bf16[10,640]{1,0:T(8,128)(2,1)S(1)}, bf16[10,640]{1,0:T(8,128)(2,1)S(1)}, u32[]{:S(2)}, u32[]{:S(2)}) collective-permute-start(bf16[10,640]{1,0:T(8,128)(2,1)S(1)} %get-tuple-element.41), channel_id=1, source_target_pairs={{0,1},{1,2},{2,3},{3,4},{4,5},{5,6},{6,7},{8,9},{9,10},{10,11},{11... | collective-permute-start | bytes 38408 | tf_op jit(solution)/shard_map/ppermute | solution.py:184
  48.6 5.4 %copy-start.1 = (bf16[8,16,640]{2,1,0:T(8,128)(2,1)S(1)}, bf16[8,16,640]{2,1,0:T(8,128)(2,1)}, u32[]{:S(2)}) copy-start(bf16[8,16,640]{2,1,0:T(8,128)(2,1)} %param.8) | copy-start | bytes 491524
  48.6 30.4 %all-to-all-start.4 = ((bf16[16,128,512]{2,1,0:T(8,128)(2,1)}), bf16[16,128,512]{2,1,0:T(8,128)(2,1)S(1)}, u32[]{:S(2)}, u32[]{:S(2)}) async-start(bf16[16,128,512]{2,1,0:T(8,128)(2,1)} %copy-done.2), calls=%async_computation.4 | async-start | bytes 4194304 | tf_op jit(solution)/shard_map/all_to_all | solution.py:205
  53.8 8.6 %copy-start.4 = (bf16[8,16,640]{2,1,0:T(8,128)(2,1)S(1)}, bf16[8,16,640]{2,1,0:T(8,128)(2,1)}, u32[]{:S(2)}) copy-start(bf16[8,16,640]{2,1,0:T(8,128)(2,1)} %param.7) | copy-start | bytes 491524
  53.8 8.6 %copy-start.6 = (f32[640]{0:T(1024)S(1)}, f32[640]{0:T(1024)}, u32[]{:S(2)}) copy-start(f32[640]{0:T(1024)} %param.10) | copy-start | bytes 7684
  53.9 8.6 %copy-start.7 = (f32[640]{0:T(1024)S(1)}, f32[640]{0:T(1024)}, u32[]{:S(2)}) copy-start(f32[640]{0:T(1024)} %param.11) | copy-start | bytes 7684
  53.9 8.1 %collective-permute-start.1 = (f32[2,128]{1,0:T(2,128)S(1)}, f32[2,128]{1,0:T(2,128)S(1)}, u32[]{:S(2)}, u32[]{:S(2)}) collective-permute-start(f32[2,128]{1,0:T(2,128)S(1)} %get-tuple-element.53), channel_id=1, source_target_pairs={{0,1},{1,0},{2,3},{3,2},{4,5},{5,4},{6,7},{7,6},{8,9},{9,8},{10,11... | collective-permute-start | bytes 3080 | tf_op jit(solution)/shard_map/ppermute | solution.py:158
  63.4 17.2 %collective-permute-start.6 = (f32[3,640]{1,0:T(4,128)S(1)}, f32[3,640]{1,0:T(4,128)S(1)}, u32[]{:S(2)}, u32[]{:S(2)}) collective-permute-start(f32[3,640]{1,0:T(4,128)S(1)} %pad_maximum_fusion.2), channel_id=1, source_target_pairs={{0,1},{1,0},{2,3},{3,2},{4,5},{5,4},{6,7},{7,6},{8,9},{9,8},{10,11... | collective-permute-start | bytes 23048 | tf_op jit(solution)/shard_map/ppermute | solution.py:158
  80.7 44.8 %collective-permute-start.7 = (bf16[16,128,256]{2,1,0:T(8,128)(2,1)}, bf16[16,128,256]{2,1,0:T(8,128)(2,1)S(1)}, u32[]{:S(2)}, u32[]{:S(2)}) collective-permute-start(bf16[16,128,256]{2,1,0:T(8,128)(2,1)} %get-tuple-element.35), channel_id=1, source_target_pairs={{0,1},{1,0},{2,3},{3,2},{4,5},{5,4},{6,7},{7,6},{8,9},{9,8},{10,11... | collective-permute-start | bytes 3145736 | tf_op jit(solution)/shard_map/ppermute | solution.py:158
  93.4 19.9 %all-to-all-start.3 = ((f32[8,3,640]{2,1,0:T(4,128)}), f32[8,3,640]{2,1,0:T(4,128)S(1)}, u32[]{:S(2)}, u32[]{:S(2)}) async-start(f32[8,3,640]{2,1,0:T(4,128)} %broadcast_in_dim.52), calls=%async_computation.3 | async-start | bytes 163840 | tf_op jit(solution)/shard_map/all_to_all | solution.py:162
  114.0 15.5 %copy-start.8 = (f32[640]{0:T(1024)}, f32[640]{0:T(1024)S(1)}, u32[]{:S(2)}) copy-start(f32[640]{0:T(1024)S(1)} %get-tuple-element.29) | copy-start | bytes 7684
  114.0 15.5 %copy-start.9 = (f32[640]{0:T(1024)}, f32[640]{0:T(1024)S(1)}, u32[]{:S(2)}) copy-start(f32[640]{0:T(1024)S(1)} %get-tuple-element.30) | copy-start | bytes 7684
  117.1 4.1 %collective-permute-start.8 = (bf16[128,128]{1,0:T(8,128)(2,1)S(1)}, bf16[128,128]{1,0:T(8,128)(2,1)S(1)}, u32[]{:S(2)}, u32[]{:S(2)}) collective-permute-start(bf16[128,128]{1,0:T(8,128)(2,1)S(1)} %bitcast.74), channel_id=1, source_target_pairs={{0,32},{32,64},{64,96},{96,128},{128,160},{160,192},{192,224},{1,3... | collective-permute-start | bytes 98312 | tf_op jit(solution)/shard_map/ppermute | solution.py:216
  119.6 5.8 %collective-permute-start.9 = (bf16[128,128]{1,0:T(8,128)(2,1)S(1)}, bf16[128,128]{1,0:T(8,128)(2,1)S(1)}, u32[]{:S(2)}, u32[]{:S(2)}) collective-permute-start(bf16[128,128]{1,0:T(8,128)(2,1)S(1)} %bitcast.73), channel_id=1, source_target_pairs={{32,0},{64,32},{96,64},{128,96},{160,128},{192,160},{224,192},{33,... | collective-permute-start | bytes 98312 | tf_op jit(solution)/shard_map/ppermute | solution.py:217
  129.5 15.3 %all-to-all-start.5 = ((bf16[8,3,32,240]{3,2,1,0:T(8,128)(2,1)}), bf16[8,3,32,240]{3,2,1,0:T(8,128)(2,1)S(1)}, u32[]{:S(2)}, u32[]{:S(2)}) async-start(bf16[8,3,32,240]{3,2,1,0:T(8,128)(2,1)} %terms.1), calls=%async_computation.5 | async-start | bytes 786432 | tf_op jit(solution)/shard_map/all_to_all | solution.py:261

commit v2 on v0

v2 whole, which is shorter than its diff:
```python
import numpy as np

import jax
import jax.numpy as jnp
from jax import lax
from jax.experimental import pallas as pl
from jax.experimental.pallas import tpu as pltpu
from jax.sharding import Mesh
from jax.sharding import PartitionSpec as P

C = 640
GW = 40
TR, TC = 8, 16
PIX = TR * TC
NZ, NY, NX = 8, 4, 4
PEERS = NY * NX
ROWS = NY * TR
NQ = 80
CHIP = float(2 * PIX * GW)
TOTAL = float(NZ * PEERS) * CHIP
VMEM_LIMIT = 48 * 1024 * 1024
F_ROWS, C_ROWS, S_ROWS = 160, 160, 16
G_ROWS = F_ROWS + C_ROWS + S_ROWS
W_ROWS, V_ROWS = 64, 32
f32, bf16 = jnp.float32, jnp.bfloat16


def slab_channels(y):
    z, k = np.arange(NZ)[:, None], np.arange(20)[None]
    chans = z * 80 + y * 20 + k
    return chans[:, :16].reshape(-1), chans[:, 16:].reshape(-1)


def feature_columns():
    parts = [slab_channels(y) for y in range(NY)]
    return np.concatenate([p[0] for p in parts] + [p[1] for p in parts])[None].astype(np.int32)


def cotangent_columns(side):
    out = np.full((1, C), -10000, np.int32)
    for x in range(NX):
        out[0, x * 128 + side * 64 : x * 128 + side * 64 + 64] = x * 160 + np.arange(64)
        at = 512 + x * 32 + side * 16
        out[0, at : at + 16] = x * 160 + 64 + np.arange(16)
    return out


def term_columns():
    main, rest = slab_channels(0)
    return np.concatenate([main] + [rest] * 4)[None].astype(np.int32)


def vmem():
    return pl.BlockSpec(memory_space=pltpu.VMEM)


def smem():
    return pl.BlockSpec(memory_space=pltpu.SMEM)


def params(**kw):
    return pltpu.CompilerParams(vmem_limit_bytes=VMEM_LIMIT, **kw)


def group_matrix():
    chan = lax.broadcasted_iota(jnp.int32, (C, 128), 0)
    low = lax.broadcasted_iota(jnp.int32, (C, 128), 1) * GW
    return jnp.where((chan >= low) & (chan < low + GW), 1.0, 0.0).astype(f32)


def exact_dot(a, b, over):
    return lax.dot_general(
        a, b, (((1,), (over,)), ((), ())), precision=lax.Precision.HIGHEST, preferred_element_type=f32
    )


def rows8(row):
    return jnp.broadcast_to(row, (8, row.shape[1]))


def pick(columns):
    rows = lax.broadcasted_iota(jnp.int32, (C, columns.shape[1]), 0)
    return (rows == columns).astype(f32)


def three(value):
    high = value.astype(bf16).astype(f32)
    rest = value - high
    middle = rest.astype(bf16).astype(f32)
    return high, middle, rest - middle


def lanes32(value):
    group = lax.broadcasted_iota(jnp.int32, (32, 128), 1) // 32
    out = []
    for a in range(4):
        acc = jnp.zeros((32, 128), f32)
        for g in range(4):
            moved = pltpu.roll(value[32 * g : 32 * g + 32], (32 * (g - a)) % 128, 1)
            acc = jnp.where(group == g, moved, acc)
        out.append(acc)
    return out


def pack_kernel(core_ref, feat_ref, cot_ref, feat2_ref, cot2_ref, fcol_ref, c0_ref, c1_ref, out_ref, bias_ref):
    core = core_ref[0]
    feat, cot = feat_ref[...], cot_ref[...]
    x, x2 = feat.astype(f32), feat2_ref[...].astype(f32)
    groups = group_matrix()
    total = x.sum(0, keepdims=True) + x2.sum(0, keepdims=True)
    mean = exact_dot(rows8(total), groups, 0) / CHIP
    wide = exact_dot(mean, groups, 1)[:1]
    squares = ((x - wide) ** 2).sum(0, keepdims=True) + ((x2 - wide) ** 2).sum(0, keepdims=True)
    squares = exact_dot(rows8(squares), groups, 0)
    pieces = three(mean[:1]) + three(squares[:1])
    row = lax.broadcasted_iota(jnp.int32, (S_ROWS, 128), 0)
    stats = jnp.zeros((S_ROWS, 128), f32)
    for k in range(6):
        stats = jnp.where(row == k, pieces[k], stats)
    stats = stats.astype(bf16)
    bias_ref[...] = rows8(cot.astype(f32).sum(0, keepdims=True))

    moved = jnp.dot(feat, pick(fcol_ref[...]).astype(bf16), preferred_element_type=f32)
    own = jnp.where(core == 0, c0_ref[...], c1_ref[...]) + core * NQ
    other = jnp.where(core == 0, c1_ref[...], c0_ref[...]) + core * NQ
    terms = jnp.dot(cot, pick(own).astype(bf16), preferred_element_type=f32)
    terms = terms + jnp.dot(cot2_ref[...], pick(other).astype(bf16), preferred_element_type=f32)
    moved_rest = lanes32(moved[:, 512:])
    terms_rest = lanes32(terms[:, 512:])
    for y in range(NY):
        for xx in range(NX):
            p = y * NX + xx
            out_ref[p, 0:128] = moved[:, y * 128 : (y + 1) * 128].astype(bf16)
            out_ref[p, 128:160] = moved_rest[y].astype(bf16)
            out_ref[p, 160:288] = terms[:, xx * 128 : (xx + 1) * 128].astype(bf16)
            out_ref[p, 288:320] = terms_rest[xx].astype(bf16)
            out_ref[p, 320:336] = stats


def merge(means, squares, count):
    n = means.shape[0]
    mean = means.sum(0, keepdims=True) / n
    return mean, squares.sum(0, keepdims=True) + count * ((means - mean) ** 2).sum(0, keepdims=True)


def stats_kernel(slab_ref, out_ref):
    got = slab_ref[...].astype(f32)
    mean, squares = merge(
        got[:, 0] + got[:, 1] + got[:, 2], got[:, 3] + got[:, 4] + got[:, 5], CHIP
    )
    row = lax.broadcasted_iota(jnp.int32, (8, 128), 0)
    block = jnp.where(row == 0, mean, jnp.where(row == 1, squares, 0.0))
    for z in range(NZ):
        out_ref[z] = block


def cot_rows(main, rest, g, side):
    lane = lax.broadcasted_iota(jnp.int32, main.shape, 1)
    main = pltpu.roll(main, 64, 1) if side else main
    return jnp.where(lane < 64, main, pltpu.roll(rest, (64 - 32 * g - 16 * side) % 128, 1))


def split_kernel(slab_ref, feat_ref, first_ref, last_ref):
    feat_ref[...] = slab_ref[:, :F_ROWS]
    for xx in range(NX):
        for side in range(2):
            at = slice(xx * 32 + side * TC, xx * 32 + (side + 1) * TC)
            peer = xx
            block = cot_rows(slab_ref[peer, 160:176].astype(f32), slab_ref[peer, 288:304].astype(f32), 0, side)
            first_ref[at] = block.astype(bf16)
            peer = (NY - 1) * NX + xx
            block = cot_rows(slab_ref[peer, 272:288].astype(f32), slab_ref[peer, 304:320].astype(f32), 3, side)
            last_ref[at] = block.astype(bf16)


def back_kernel(core_ref, cot_ref, cot2_ref, mine_ref, theirs_ref, outer_ref, w_ref, out_ref, shifted, acc):
    step = pl.program_id(0)
    rows = (TR + 2) * TC

    @pl.when(step == 0)
    def _():
        lower = core_ref[0] == 0
        mine, theirs = mine_ref[...].astype(f32), theirs_ref[...].astype(f32)
        top, bottom = jnp.where(lower, mine, theirs), jnp.where(lower, theirs, mine)
        own_top, other_top = jnp.where(lower, top[:TC], top[TC:]), jnp.where(lower, top[TC:], top[:TC])
        own_bot, other_bot = jnp.where(lower, bottom[:TC], bottom[TC:]), jnp.where(lower, bottom[TC:], bottom[:TC])
        wide = jnp.concatenate([own_top, cot_ref[...].astype(f32), own_bot], axis=0)
        near = jnp.concatenate([other_top, cot2_ref[...].astype(f32), other_bot], axis=0)
        near = near.reshape(TR + 2, TC, C)
        inner = jnp.where(lower, near[:, :1], near[:, TC - 1 :])
        outer = outer_ref[...].astype(f32)[:, None, :]
        left, right = jnp.where(lower, outer, inner), jnp.where(lower, inner, outer)
        left = jnp.broadcast_to(left, (TR + 2, TC, C)).reshape(rows, C)
        right = jnp.broadcast_to(right, (TR + 2, TC, C)).reshape(rows, C)
        col = lax.broadcasted_iota(jnp.int32, (rows, C), 0) % TC
        shifted[0] = jnp.where(col == 0, left, pltpu.roll(wide, 1, 0)).astype(bf16)
        shifted[1] = wide.astype(bf16)
        shifted[2] = jnp.where(col == TC - 1, right, pltpu.roll(wide, rows - 1, 0)).astype(bf16)
        acc[...] = jnp.zeros_like(acc)

    i, j = step // 3, step % 3
    lhs = shifted[2 - j, pl.ds(pl.multiple_of((2 - i) * TC, TC), PIX), :]
    acc[...] += lax.dot_general(lhs, w_ref[0, 0], (((1,), (1,)), ((), ())), preferred_element_type=f32)

    @pl.when(step == 8)
    def _():
        out_ref[...] = acc[...]


def sums_kernel(y_ref, stat_ref, feat_ref, back_ref, gain_ref, shift_ref, bias_ref, col_ref,
                row_ref, da_ref, par_ref, out_ref, block):
    got = stat_ref[...]
    mean, squares = merge(got[:, 0], got[:, 1], PEERS * CHIP)
    groups = group_matrix()
    rstd = exact_dot(rows8(lax.rsqrt(squares / TOTAL + 1e-05)), groups, 1)[:1]
    mean = exact_dot(rows8(mean), groups, 1)[:1]
    gain, shift = gain_ref[...], shift_ref[...]
    row = lax.broadcasted_iota(jnp.int32, (8, C), 0)
    row_ref[...] = jnp.where(row == 0, mean, rstd)
    table = jnp.where(row == 0, mean, jnp.where(row == 1, rstd * gain, jnp.where(row == 2, shift, 0.0)))
    par_ref[...] = exact_dot(table, pick(col_ref[...] + y_ref[0] * 20), 0)
    xhat = (feat_ref[...].astype(f32) - mean) * rstd
    act = xhat * gain + shift
    sig = jax.nn.sigmoid(act)
    da = back_ref[...] * sig * (1.0 + act * (1.0 - sig))
    da_ref[...] = da
    sums = (da.sum(0, keepdims=True), (da * xhat).sum(0, keepdims=True), bias_ref[:1])
    block[...] = jnp.zeros_like(block)
    for s in range(3):
        for t in range(5):
            block[5 * s + t : 5 * s + t + 1] = sums[s][:, 128 * t : 128 * t + 128]
    value = block[...]
    for p in range(2 * PEERS):
        out_ref[p] = value


def terms_kernel(core_ref, own_ref, other_ref, above_ref, below_ref, par_ref, out_ref, hid, strips, cot3, rest):
    core = core_ref[0]

    def put(block, peer, side):
        y, xx = peer // NX, peer % NX

        def silu(x, lanes):
            a = (x.astype(f32) - par_ref[0:1, lanes]) * par_ref[1:2, lanes] + par_ref[2:3, lanes]
            return a * jax.nn.sigmoid(a)

        main = silu(block[:128], slice(0, 128)).astype(bf16)
        tail = silu(block[128:], slice(128, 256))
        for g in range(4):
            low = pltpu.roll(tail, (128 - 32 * g) % 128, 1).astype(bf16)
            for h in range(2):
                r = 2 * g + h
                at = pl.ds(pl.multiple_of((y * TR + r) * 128 + xx * 32 + side * TC, TC), TC)
                hid[at, 0:128] = main[r * TC : (r + 1) * TC]
                hid[at, 128:256] = low[h * TC : (h + 1) * TC]

    for peer in range(PEERS):
        put(own_ref[peer, :F_ROWS], peer, core)
        put(other_ref[peer], peer, 1 - core)
        y, xx = peer // NX, peer % NX
        tail = own_ref[peer, 288:320].astype(f32)
        for g in range(4):
            main = own_ref[peer, 160 + 32 * g : 192 + 32 * g].astype(f32)
            for side in range(2):
                value = cot_rows(main, tail, g, side).astype(bf16)
                for h in range(2):
                    at = (y * TR + 2 * g + h + 1) * 128 + xx * 32 + side * TC
                    strips[at : at + TC] = value[h * TC : (h + 1) * TC]
    strips[0:128] = above_ref[...]
    strips[(ROWS + 1) * 128 :] = below_ref[...]
    lane = lax.broadcasted_iota(jnp.int32, (NQ, 128), 1)
    for row in range(ROWS + 2):
        at = slice(row * 128, (row + 1) * 128)
        turned = strips[at].astype(f32).T[:NQ]
        before = jnp.where(lane == 0, 0.0, pltpu.roll(turned, 1, 1))
        after = jnp.where(lane == 127, 0.0, pltpu.roll(turned, 127, 1))
        cot3[0:NQ, at] = after.astype(bf16)
        cot3[NQ : 2 * NQ, at] = turned.astype(bf16)
        cot3[2 * NQ : 3 * NQ, at] = before.astype(bf16)
    cot3[3 * NQ :] = jnp.zeros((16, (ROWS + 2) * 128), bf16)
    rest[...] = jnp.zeros_like(rest)
    for i in range(3):
        lhs = cot3[:, (2 - i) * 128 : (2 - i) * 128 + ROWS * 128]
        turned = jnp.dot(lhs, hid[...], preferred_element_type=f32).T
        for z in range(NZ):
            out_ref[z, 16 * i : 16 * i + 16] = turned[16 * z : 16 * z + 16].astype(bf16)
            rest[z, 4 * i : 4 * i + 4] = turned[128 + 4 * z : 132 + 4 * z]
    for z in range(NZ):
        out_ref[z, 48:64] = rest[z].astype(bf16)


def join_kernel(sums_ref, terms_ref, out_ref):
    value = sums_ref[0]
    for p in range(1, 2 * PEERS):
        value = value + sums_ref[p]
    high, middle, low = three(value)
    zero = jnp.zeros_like(value)
    block = jnp.concatenate(
        [jnp.concatenate([high, middle], axis=1), jnp.concatenate([low, zero], axis=1)], axis=0
    ).astype(bf16)
    for z in range(NZ):
        out_ref[z, :W_ROWS] = terms_ref[z]
        out_ref[z, W_ROWS:] = block


def final_kernel(got_ref, feat_ref, da_ref, row_ref, gain_ref,
                 grad_ref, weight_ref, gain_grad_ref, shift_grad_ref, bias_ref):
    total = jnp.zeros((16, 128), f32)
    for z in range(NZ):
        upper, lower = got_ref[z, 64:80].astype(f32), got_ref[z, 80:96].astype(f32)
        total = total + (upper[:, :128] + upper[:, 128:] + lower[:, :128])
    sums = [jnp.concatenate([total[5 * s + t : 5 * s + t + 1] for t in range(5)], axis=1) for s in range(3)]
    shift_grad_ref[...], gain_grad_ref[...], bias_ref[...] = sums
    groups = group_matrix()
    gain, mean, rstd = gain_ref[...], row_ref[0:1], row_ref[1:2]

    def moment(value):
        return exact_dot(exact_dot(rows8(gain * value), groups, 0), groups, 1)[:1] / TOTAL

    first, second = moment(sums[0]), moment(sums[1])
    xhat = (feat_ref[...].astype(f32) - mean) * rstd
    grad_ref[...] = (rstd * (da_ref[...] * gain - first - xhat * second)).astype(bf16)
    weight = got_ref[0, :W_ROWS].astype(f32)
    for z in range(1, NZ):
        weight = weight + got_ref[z, :W_ROWS].astype(f32)
    for i in range(3):
        for j in range(3):
            lanes = slice(j * NQ, (j + 1) * NQ)
            weight_ref[i, j, 0:16] = weight[16 * i : 16 * i + 16, lanes]
            weight_ref[i, j, 16:20] = weight[48 + 4 * i : 52 + 4 * i, lanes]


def flip(value):
    return lax.ppermute(value, "core", [(0, 1), (1, 0)])


def shape(dims, dtype):
    return jax.ShapeDtypeStruct(dims, dtype)


def body(features, cotangent, conv_weight, gain, shift):
    core, y = lax.axis_index("core"), lax.axis_index("y")
    at_core, at_y = core.reshape(1), y.reshape(1)
    feat, cot = features.reshape(PIX, C), cotangent.reshape(PIX, C)
    gain, shift = gain.reshape(1, C), shift.reshape(1, C)
    cot2, feat2 = flip(cot), flip(feat)

    edge = jnp.where(
        core == 0,
        jnp.concatenate([cot[PIX - TC :], cot2[PIX - TC :]]),
        jnp.concatenate([cot2[:TC], cot[:TC]]),
    )
    count = NZ * NY
    ways = [(2 * k, 2 * k + 2) for k in range(count - 1)] + [(2 * k + 3, 2 * k + 1) for k in range(count - 1)]
    mine = lax.ppermute(edge, ("z", "y", "core"), ways)
    theirs = flip(mine)

    packed, bias = pl.pallas_call(
        pack_kernel,
        out_shape=(shape((PEERS, G_ROWS, 128), bf16), shape((8, C), f32)),
        in_specs=[smem()] + [vmem()] * 7,
        out_specs=(vmem(), vmem()),
        compiler_params=params(),
        name="pack",
    )(
        at_core, feat, cot, feat2, cot2, jnp.asarray(feature_columns()),
        jnp.asarray(cotangent_columns(0)), jnp.asarray(cotangent_columns(1)),
    )
    slab = lax.all_to_all(packed, ("y", "x"), 0, 0)

    top = jnp.where(core == 0, mine[0], theirs[2 * TC - 1])
    bottom = jnp.where(core == 0, theirs[0], mine[2 * TC - 1])
    column = jnp.where(core == 0, cotangent[:, 0], cotangent[:, TC - 1])
    column = jnp.concatenate([top[None], column, bottom[None]])
    pairs = [(2 * k + 1, 2 * k + 2) for k in range(NX - 1)]
    outer = lax.ppermute(column, ("x", "core"), pairs + [(b, a) for a, b in pairs])
    back = pl.pallas_call(
        back_kernel,
        grid=(9,),
        out_shape=shape((PIX, C), f32),
        in_specs=[smem()] + [vmem()] * 5 + [pl.BlockSpec((1, 1, C, C), lambda t: (t // 3, t % 3, 0, 0))],
        out_specs=vmem(),
        scratch_shapes=[pltpu.VMEM((3, (TR + 2) * TC, C), bf16), pltpu.VMEM((PIX, C), f32)],
        compiler_params=params(),
        cost_estimate=pl.CostEstimate(flops=2 * PIX * 9 * C * C, bytes_accessed=18 * C * C, transcendentals=0),
        name="back",
    )(at_core, cot, cot2, mine, theirs, outer, conv_weight)

    stats = pl.pallas_call(
        stats_kernel,
        grid=(1,),
        out_shape=shape((NZ, 8, 128), f32),
        in_specs=[pl.BlockSpec((PEERS, S_ROWS, 128), lambda t: (0, (F_ROWS + C_ROWS) // S_ROWS, 0))],
        out_specs=vmem(),
        compiler_params=params(),
        name="stats",
    )(slab)
    stats = lax.all_to_all(stats, "z", 0, 0)
    slab_feat, first_row, last_row = pl.pallas_call(
        split_kernel,
        out_shape=(shape((PEERS, F_ROWS, 128), bf16), shape((128, 128), bf16), shape((128, 128), bf16)),
        in_specs=[vmem()],
        out_specs=(vmem(), vmem(), vmem()),
        compiler_params=params(),
        name="split",
    )(slab)
    slab_other = flip(slab_feat)
    slabs = [(k, k + 1) for k in range(NZ - 1)]
    above = lax.ppermute(last_row, "z", slabs)
    below = lax.ppermute(first_row, "z", [(b, a) for a, b in slabs])

    row, da, table, sums = pl.pallas_call(
        sums_kernel,
        out_shape=(shape((8, C), f32), shape((PIX, C), f32), shape((8, 256), f32), shape((2 * PEERS, 16, 128), f32)),
        in_specs=[smem()] + [vmem()] * 7,
        out_specs=(vmem(), vmem(), vmem(), vmem()),
        scratch_shapes=[pltpu.VMEM((16, 128), f32)],
        compiler_params=params(),
        name="sums",
    )(at_y, stats, feat, back, gain, shift, bias, jnp.asarray(term_columns()))
    sums = lax.all_to_all(sums, ("y", "x", "core"), 0, 0)

    terms = pl.pallas_call(
        terms_kernel,
        out_shape=shape((NZ, W_ROWS, 256), bf16),
        in_specs=[smem()] + [vmem()] * 5,
        out_specs=vmem(),
        scratch_shapes=[
            pltpu.VMEM((ROWS * 128, 256), bf16),
            pltpu.VMEM(((ROWS + 2) * 128, 128), bf16),
            pltpu.VMEM((256, (ROWS + 2) * 128), bf16),
            pltpu.VMEM((NZ, 16, 256), f32),
        ],
        compiler_params=params(),
        cost_estimate=pl.CostEstimate(
            flops=2 * PIX * 9 * C * C, bytes_accessed=4 << 20, transcendentals=ROWS * 128 * 256
        ),
        name="terms",
    )(at_core, slab, slab_other, above, below, table)

    joined = pl.pallas_call(
        join_kernel,
        out_shape=shape((NZ, W_ROWS + V_ROWS, 256), bf16),
        in_specs=[vmem()] * 2,
        out_specs=vmem(),
        compiler_params=params(),
        name="join",
    )(sums, terms)
    joined = lax.all_to_all(joined, "z", 0, 0)
    grad, weight_grad, gain_grad, shift_grad, bias_grad = pl.pallas_call(
        final_kernel,
        out_shape=(
            shape((PIX, C), bf16),
            shape((3, 3, 20, NQ), f32),
            shape((1, C), f32),
            shape((1, C), f32),
            shape((1, C), f32),
        ),
        in_specs=[vmem()] * 5,
        out_specs=(vmem(),) * 5,
        compiler_params=params(),
        name="final",
    )(joined, feat, da, row, gain)
    return (
        grad.reshape(features.shape),
        weight_grad,
        gain_grad.reshape(C),
        shift_grad.reshape(C),
        bias_grad.reshape(C),
    )


def solution(mesh):
    grid = Mesh(mesh.devices.reshape(NZ, NY, NX, 2), ("z", "y", "x", "core"))
    rows, cols = ("z", "y"), ("x", "core")
    tiled = P(rows, cols, None)
    return jax.shard_map(
        body,
        mesh=grid,
        in_specs=(tiled, tiled, P(), P(), P()),
        out_specs=(tiled, P(None, None, rows, cols), P(), P(), P()),
        check_vma=False,
    )
```

time: 576 us -> 104 us (0.18)
  the two profiles are of different devices: /device:TPU:1 before, /device:TPU:2 now
where the time goes in v2:
time: 104 us; the launch traced here: 103 us
  starting transfers between devices  34.3 us (33%)
  waiting for transfers between devices  22.2 us (21%)
  blocking collectives  20.3 us (20%)
  Pallas kernels  19.7 us (19%)
  local copies, waits for them, and re-layouts  3.96 us (4%)
  other arithmetic  1.87 us (2%)
    all_to_all x1, blocking collectives, body(): joined = lax.all_to_all(joined, 'z', 0, 0)  20.3 us
    ppermute x1, waiting for transfers between devices, body(): mine = lax.ppermute(edge, ('z', 'y', 'core'), ways)  10.2 us
    all_to_all x1, starting transfers between devices, body(): stats = lax.all_to_all(stats, 'z', 0, 0)  8.46 us
    pallas_call x1, Pallas kernels, body(): pl.pallas_call(back_kernel, grid=(9,), out_shape=shape((PIX, C), f32), in...  8.07 us
    all_to_all x1, starting transfers between devices, body(): slab = lax.all_to_all(packed, ('y', 'x'), 0, 0)  7.61 us
    all_to_all x1, waiting for transfers between devices, body(): slab = lax.all_to_all(packed, ('y', 'x'), 0, 0)  6.16 us
    ppermute x1, starting transfers between devices, body(): lax.ppermute(column, ('x', 'core'), pairs + [(b, a) for a, b in pairs])  4.94 us
    ppermute x1, waiting for transfers between devices, body(): below = lax.ppermute(first_row, 'z', [(b, a) for a, b in slabs])  4.23 us
  transfers between devices with their start and end apart: 11, of which 6 were waited for; matrix products, arithmetic and copies ran while one was open for 0% of the time, Pallas kernels for 14%

profile of v2, /device:TPU:2, one launch (start us, length us, event | category | flops | bytes accessed | tf_op | source)
XLA Modules:
  0.0 103.3 jit_solution(9139432944256430255)
XLA Ops:
  0.6 0.1 collective-permute-start
  0.7 0.5 collective-permute-start.1
  1.2 1.1 %collective-permute-done.feat2_ref = bf16[128,640]{1,0:T(8,128)(2,1)S(1)} collective-permute-done((bf16[128,640]{1,0:T(8,128)(2,1)}, bf16[128,640]{1,0:T(8,128)(2,1)S(1)}, u32[]{:S(2)}, u32[]{:S(2)}) %collective-permute-start) | collective-permute-done | bytes 163872 | tf_op jit(solution)/shard_map/ppermute | solution.py:334
  2.3 0.2 collective-permute-done.1.cot2_ref
  2.6 0.0 copy-start
  2.6 0.9 copy-done
  3.5 0.0 copy-start.2
  3.5 0.9 copy-done.2
  4.4 0.0 copy-start.4
  4.4 0.7 copy-done.4
  5.1 0.0 copy-start.5
  5.1 0.7 copy-done.5
  5.8 0.0 copy-start.6
  5.8 0.7 copy-done.6
  6.4 2.9 %pack.1 = (bf16[16,336,128]{2,1,0:T(8,128)(2,1)}, f32[8,640]{1,0:T(8,128)S(1)}) custom-call(s32[1]{0:T(128)} %bitcast.1.core_ref, bf16[128,640]{1,0:T(8,128)(2,1)S(1)} %bitcast.12, bf16[128,640]{1,0:T(8,128)(2,1)S(1)} %bitcast.16, bf16[128,640]{1,0:T(8,128)(2,1)S(1)} %collective-permute-done.feat2_ref, bf16[128,640]{1,0:T(8,128)(2,1)S(1)} %collective-permute-done.1.cot2_ref, ...), custom_call_target="tpu_custom_call" | custom-call | tf_op jit(solution)/shard_map/pack/pallas_call | solution.py:358
  9.3 0.0 copy-start.3
  9.3 7.6 %all-to-all-start = ((bf16[16,336,128]{2,1,0:T(8,128)(2,1)}), bf16[16,336,128]{2,1,0:T(8,128)(2,1)S(1)}, u32[]{:S(2)}, u32[]{:S(2)}) async-start(bf16[16,336,128]{2,1,0:T(8,128)(2,1)} %get-tuple-element.19), calls=%async_computation | async-start | bytes 2752512 | tf_op jit(solution)/shard_map/all_to_all | solution.py:369
  16.9 0.0 copy-start.8
  16.9 0.0 copy-start.9
  16.9 0.0 copy-done.3
  17.0 3.4 %collective-permute-start.2 = (bf16[32,640]{1,0:T(8,128)(2,1)S(1)}, bf16[32,640]{1,0:T(8,128)(2,1)S(1)}, u32[]{:S(2)}, u32[]{:S(2)}) collective-permute-start(bf16[32,640]{1,0:T(8,128)(2,1)S(1)} %maximum_select_fusion), channel_id=1, source_target_pairs={{0,8},{8,16},{16,24},{24,32},{32,40},{40,48},{48,56},{56,64},{64,7... | collective-permute-start | bytes 122888 | tf_op jit(solution)/shard_map/ppermute | solution.py:355
  20.4 10.2 %collective-permute-done.2.mine_ref = bf16[32,640]{1,0:T(8,128)(2,1)S(1)} collective-permute-done((bf16[32,640]{1,0:T(8,128)(2,1)S(1)}, bf16[32,640]{1,0:T(8,128)(2,1)S(1)}, u32[]{:S(2)}, u32[]{:S(2)}) %collective-permute-start.2) | collective-permute-done | bytes 40992 | tf_op jit(solution)/shard_map/ppermute | solution.py:355
  30.6 0.0 collective-permute-start.3
  30.6 6.2 %all-to-all-done.slab_ref.own_ref = bf16[16,336,128]{2,1,0:T(8,128)(2,1)S(1)} async-done(((bf16[16,336,128]{2,1,0:T(8,128)(2,1)}), bf16[16,336,128]{2,1,0:T(8,128)(2,1)S(1)}, u32[]{:S(2)}, u32[]{:S(2)}) %all-to-all-start) | async-done | bytes 1376288 | tf_op jit(solution)/shard_map/all_to_all | solution.py:369
  36.8 0.9 split.1
  37.7 0.0 collective-permute-start.5
  37.7 0.0 collective-permute-done.3.theirs_ref
  37.8 4.9 %collective-permute-start.4 = (bf16[10,640]{1,0:T(8,128)(2,1)S(1)}, bf16[10,640]{1,0:T(8,128)(2,1)S(1)}, u32[]{:S(2)}, u32[]{:S(2)}) collective-permute-start(bf16[10,640]{1,0:T(8,128)(2,1)S(1)} %pad_maximum_fusion), channel_id=1, source_target_pairs={{1,2},{3,4},{5,6},{2,1},{4,3},{6,5},{9,10},{11,12},{13,14},{10,9},... | collective-permute-start | bytes 38408 | tf_op jit(solution)/shard_map/ppermute | solution.py:376
  42.7 0.0 copy-done.8
  42.7 0.0 copy-done.9
  42.8 0.7 stats.1
  43.4 8.5 %all-to-all-start.1 = ((f32[8,8,128]{2,1,0:T(8,128)}), f32[8,8,128]{2,1,0:T(8,128)S(1)}, u32[]{:S(2)}, u32[]{:S(2)}) async-start(f32[8,8,128]{2,1,0:T(8,128)} %stats.1), calls=%async_computation.1 | async-start | bytes 65536 | tf_op jit(solution)/shard_map/all_to_all | solution.py:398
  51.9 0.0 copy-start.1
  51.9 0.0 copy-start.7
  51.9 0.0 collective-permute-done.4.outer_ref
  51.9 8.1 %back.1.back_ref = f32[128,640]{1,0:T(8,128)S(1)} custom-call(s32[1]{0:T(128)} %bitcast.1.core_ref, bf16[128,640]{1,0:T(8,128)(2,1)S(1)} %bitcast.17, bf16[128,640]{1,0:T(8,128)(2,1)S(1)} %collective-permute-done.1.cot2_ref, bf16[32,640]{1,0:T(8,128)(2,1)S(1)} %collective-permute-done.2.mine_ref, bf16[32,640]{1,0:T(8,128)(2,1)S(1)} %collective-permute-done.3.theirs_ref, ...), custom_call_target="tpu_custom_call" | custom-call | flops 943718400 | bytes 7372800 | tf_op jit(solution)/shard_map/back/pallas_call | solution.py:377
  60.0 0.0 all-to-all-done.1.stat_ref
  60.0 0.0 copy-done.1
  60.0 0.0 copy-done.7
  60.0 1.8 %sums.1 = (f32[8,640]{1,0:T(8,128)S(1)}, f32[128,640]{1,0:T(8,128)S(1)}, f32[8,256]{1,0:T(8,128)S(1)}, f32[32,16,128]{2,1,0:T(8,128)}) custom-call(s32[1]{0:T(128)} %bitcast.y_ref, f32[8,8,128]{2,1,0:T(8,128)S(1)} %all-to-all-done.1.stat_ref, bf16[128,640]{1,0:T(8,128)(2,1)S(1)} %bitcast.13, f32[128,640]{1,0:T(8,128)S(1)} %back.1.back_ref, ...), custom_call_target="tpu_custom_call" | custom-call | tf_op jit(solution)/shard_map/sums/pallas_call | solution.py:412
  61.9 4.1 %all-to-all-start.2 = ((f32[32,16,128]{2,1,0:T(8,128)}), f32[32,16,128]{2,1,0:T(8,128)S(1)}, u32[]{:S(2)}, u32[]{:S(2)}) async-start(f32[32,16,128]{2,1,0:T(8,128)} %get-tuple-element.21), calls=%async_computation.2 | async-start | bytes 524288 | tf_op jit(solution)/shard_map/all_to_all | solution.py:421
  65.9 3.9 %collective-permute-start.6 = (bf16[128,128]{1,0:T(8,128)(2,1)S(1)}, bf16[128,128]{1,0:T(8,128)(2,1)S(1)}, u32[]{:S(2)}, u32[]{:S(2)}) collective-permute-start(bf16[128,128]{1,0:T(8,128)(2,1)S(1)} %get-tuple-element.23), channel_id=1, source_target_pairs={{0,32},{32,64},{64,96},{96,128},{128,160},{160,192},{192,224},{1,3... | collective-permute-start | bytes 98312 | tf_op jit(solution)/shard_map/ppermute | solution.py:409
  69.9 1.3 %collective-permute-start.7 = (bf16[128,128]{1,0:T(8,128)(2,1)S(1)}, bf16[128,128]{1,0:T(8,128)(2,1)S(1)}, u32[]{:S(2)}, u32[]{:S(2)}) collective-permute-start(bf16[128,128]{1,0:T(8,128)(2,1)S(1)} %get-tuple-element.24), channel_id=1, source_target_pairs={{32,0},{64,32},{96,64},{128,96},{160,128},{192,160},{224,192},{33,... | collective-permute-start | bytes 98312 | tf_op jit(solution)/shard_map/ppermute | solution.py:410
  71.2 0.3 collective-permute-done.6.above_ref
  71.5 4.2 %collective-permute-done.7.below_ref = bf16[128,128]{1,0:T(8,128)(2,1)S(1)} collective-permute-done((bf16[128,128]{1,0:T(8,128)(2,1)S(1)}, bf16[128,128]{1,0:T(8,128)(2,1)S(1)}, u32[]{:S(2)}, u32[]{:S(2)}) %collective-permute-start.7) | collective-permute-done | bytes 32800 | tf_op jit(solution)/shard_map/ppermute | solution.py:410
  75.7 0.0 collective-permute-done.5.other_ref
  75.7 3.2 %terms.1.terms_ref = bf16[8,64,256]{2,1,0:T(8,128)(2,1)S(1)} custom-call(s32[1]{0:T(128)} %bitcast.1.core_ref, bf16[16,336,128]{2,1,0:T(8,128)(2,1)S(1)} %all-to-all-done.slab_ref.own_ref, bf16[16,160,128]{2,1,0:T(8,128)(2,1)S(1)} %collective-permute-done.5.other_ref, bf16[128,128]{1,0:T(8,128)(2,1)S(1)} %collective-permute-done.6.above_ref, ...), custom_call_target="tpu_custom_call" | custom-call | flops 943718400 | bytes 4194304 | tf_op jit(solution)/shard_map/terms/pallas_call | solution.py:423
  78.9 0.0 all-to-all-done.2.sums_ref
  78.9 0.1 join.1
  78.9 20.3 %all_to_all.20.got_ref = bf16[8,96,256]{2,1,0:T(8,128)(2,1)S(1)} all-to-all(bf16[8,96,256]{2,1,0:T(8,128)(2,1)S(1)} %join.1), channel_id=1, replica_groups=mesh['z'=8,'y'=4,'x'=4,'core'=2] {'z'}, dimensions={0} | all-to-all | bytes 786432 | tf_op jit(solution)/shard_map/all_to_all | solution.py:449
  99.3 2.2 %final.1 = (bf16[128,640]{1,0:T(8,128)(2,1)}, f32[3,3,20,80]{3,2,1,0:T(8,128)}, f32[1,640]{1,0:T(1,128)S(1)}, f32[1,640]{1,0:T(1,128)S(1)}, f32[1,640]{1,0:T(1,128)S(1)}) custom-call(bf16[8,96,256]{2,1,0:T(8,128)(2,1)S(1)} %all_to_all.20.got_ref, bf16[128,640]{1,0:T(8,128)(2,1)S(1)} %bitcast.14, f32[128,640]{1,0:T(8,128)S(1)} %get-tuple-element.26.da_ref, ...), custom_call_target="tpu_custom_call" | custom-call | tf_op jit(solution)/shard_map/final/pallas_call | solution.py:450
  101.4 0.6 reduce
  102.0 0.6 reduce.1
  102.6 0.6 reduce.2
  (9 shorter events, 0.1 us)
Async XLA Ops:
  0.6 1.7 %collective-permute-start = (bf16[128,640]{1,0:T(8,128)(2,1)}, bf16[128,640]{1,0:T(8,128)(2,1)S(1)}, u32[]{:S(2)}, u32[]{:S(2)}) collective-permute-start(bf16[128,640]{1,0:T(8,128)(2,1)} %bitcast.11), channel_id=1, source_target_pairs={{0,1},{1,0},{2,3},{3,2},{4,5},{5,4},{6,7},{7,6},{8,9},{9,8},{10,11... | collective-permute-start | bytes 491528 | tf_op jit(solution)/shard_map/ppermute | solution.py:334
  0.7 1.8 %collective-permute-start.1 = (bf16[128,640]{1,0:T(8,128)(2,1)}, bf16[128,640]{1,0:T(8,128)(2,1)S(1)}, u32[]{:S(2)}, u32[]{:S(2)}) collective-permute-start(bf16[128,640]{1,0:T(8,128)(2,1)} %bitcast.15), channel_id=1, source_target_pairs={{0,1},{1,0},{2,3},{3,2},{4,5},{5,4},{6,7},{7,6},{8,9},{9,8},{10,11... | collective-permute-start | bytes 491528 | tf_op jit(solution)/shard_map/ppermute | solution.py:334
  2.6 0.9 copy-start
  3.5 0.9 copy-start.2
  4.4 0.7 copy-start.4
  5.1 0.7 copy-start.5
  5.8 0.7 copy-start.6
  9.3 7.6 %copy-start.3 = (bf16[8,16,640]{2,1,0:T(8,128)(2,1)S(1)}, bf16[8,16,640]{2,1,0:T(8,128)(2,1)}, u32[]{:S(2)}) copy-start(bf16[8,16,640]{2,1,0:T(8,128)(2,1)} %param.10) | copy-start | bytes 491524
  9.3 27.5 %all-to-all-start = ((bf16[16,336,128]{2,1,0:T(8,128)(2,1)}), bf16[16,336,128]{2,1,0:T(8,128)(2,1)S(1)}, u32[]{:S(2)}, u32[]{:S(2)}) async-start(bf16[16,336,128]{2,1,0:T(8,128)(2,1)} %get-tuple-element.19), calls=%async_computation | async-start | bytes 2752512 | tf_op jit(solution)/shard_map/all_to_all | solution.py:369
  16.9 25.8 %copy-start.8 = (f32[640]{0:T(1024)S(1)}, f32[640]{0:T(1024)}, u32[]{:S(2)}) copy-start(f32[640]{0:T(1024)} %param.12) | copy-start | bytes 7684
  16.9 25.8 %copy-start.9 = (f32[640]{0:T(1024)S(1)}, f32[640]{0:T(1024)}, u32[]{:S(2)}) copy-start(f32[640]{0:T(1024)} %param.13) | copy-start | bytes 7684
  17.0 13.6 %collective-permute-start.2 = (bf16[32,640]{1,0:T(8,128)(2,1)S(1)}, bf16[32,640]{1,0:T(8,128)(2,1)S(1)}, u32[]{:S(2)}, u32[]{:S(2)}) collective-permute-start(bf16[32,640]{1,0:T(8,128)(2,1)S(1)} %maximum_select_fusion), channel_id=1, source_target_pairs={{0,8},{8,16},{16,24},{24,32},{32,40},{40,48},{48,56},{56,64},{64,7... | collective-permute-start | bytes 122888 | tf_op jit(solution)/shard_map/ppermute | solution.py:355
  30.6 7.1 %collective-permute-start.3 = (bf16[32,640]{1,0:T(8,128)(2,1)S(1)}, bf16[32,640]{1,0:T(8,128)(2,1)S(1)}, u32[]{:S(2)}, u32[]{:S(2)}) collective-permute-start(bf16[32,640]{1,0:T(8,128)(2,1)S(1)} %collective-permute-done.2.mine_ref), channel_id=1, source_target_pairs={{0,1},{1,0},{2,3},{3,2},{4,5},{5,4},{6,7},{7,6},{8,9},{9,8},{10,11... | collective-permute-start | bytes 122888 | tf_op jit(solution)/shard_map/ppermute | solution.py:334
  37.7 38.0 %collective-permute-start.5 = (bf16[16,160,128]{2,1,0:T(8,128)(2,1)}, bf16[16,160,128]{2,1,0:T(8,128)(2,1)S(1)}, u32[]{:S(2)}, u32[]{:S(2)}) collective-permute-start(bf16[16,160,128]{2,1,0:T(8,128)(2,1)} %get-tuple-element.22), channel_id=1, source_target_pairs={{0,1},{1,0},{2,3},{3,2},{4,5},{5,4},{6,7},{7,6},{8,9},{9,8},{10,11... | collective-permute-start | bytes 1966088 | tf_op jit(solution)/shard_map/ppermute | solution.py:334
  37.8 14.1 %collective-permute-start.4 = (bf16[10,640]{1,0:T(8,128)(2,1)S(1)}, bf16[10,640]{1,0:T(8,128)(2,1)S(1)}, u32[]{:S(2)}, u32[]{:S(2)}) collective-permute-start(bf16[10,640]{1,0:T(8,128)(2,1)S(1)} %pad_maximum_fusion), channel_id=1, source_target_pairs={{1,2},{3,4},{5,6},{2,1},{4,3},{6,5},{9,10},{11,12},{13,14},{10,9},... | collective-permute-start | bytes 38408 | tf_op jit(solution)/shard_map/ppermute | solution.py:376
  43.4 16.6 %all-to-all-start.1 = ((f32[8,8,128]{2,1,0:T(8,128)}), f32[8,8,128]{2,1,0:T(8,128)S(1)}, u32[]{:S(2)}, u32[]{:S(2)}) async-start(f32[8,8,128]{2,1,0:T(8,128)} %stats.1), calls=%async_computation.1 | async-start | bytes 65536 | tf_op jit(solution)/shard_map/all_to_all | solution.py:398
  51.9 8.1 %copy-start.1 = (bf16[8,16,640]{2,1,0:T(8,128)(2,1)S(1)}, bf16[8,16,640]{2,1,0:T(8,128)(2,1)}, u32[]{:S(2)}) copy-start(bf16[8,16,640]{2,1,0:T(8,128)(2,1)} %param.9) | copy-start | bytes 491524
  51.9 8.1 %copy-start.7 = (s32[1,256]{1,0:T(1,128)S(1)}, s32[1,256]{1,0:T(1,128)}, u32[]{:S(2)}) copy-start(s32[1,256]{1,0:T(1,128)} %constant.22.clone.col_ref) | copy-start | bytes 3076
  61.9 17.0 %all-to-all-start.2 = ((f32[32,16,128]{2,1,0:T(8,128)}), f32[32,16,128]{2,1,0:T(8,128)S(1)}, u32[]{:S(2)}, u32[]{:S(2)}) async-start(f32[32,16,128]{2,1,0:T(8,128)} %get-tuple-element.21), calls=%async_computation.2 | async-start | bytes 524288 | tf_op jit(solution)/shard_map/all_to_all | solution.py:421
  65.9 5.5 %collective-permute-start.6 = (bf16[128,128]{1,0:T(8,128)(2,1)S(1)}, bf16[128,128]{1,0:T(8,128)(2,1)S(1)}, u32[]{:S(2)}, u32[]{:S(2)}) collective-permute-start(bf16[128,128]{1,0:T(8,128)(2,1)S(1)} %get-tuple-element.23), channel_id=1, source_target_pairs={{0,32},{32,64},{64,96},{96,128},{128,160},{160,192},{192,224},{1,3... | collective-permute-start | bytes 98312 | tf_op jit(solution)/shard_map/ppermute | solution.py:409
  69.9 5.8 %collective-permute-start.7 = (bf16[128,128]{1,0:T(8,128)(2,1)S(1)}, bf16[128,128]{1,0:T(8,128)(2,1)S(1)}, u32[]{:S(2)}, u32[]{:S(2)}) collective-permute-start(bf16[128,128]{1,0:T(8,128)(2,1)S(1)} %get-tuple-element.24), channel_id=1, source_target_pairs={{32,0},{64,32},{96,64},{128,96},{160,128},{192,160},{224,192},{33,... | collective-permute-start | bytes 98312 | tf_op jit(solution)/shard_map/ppermute | solution.py:410

commit v3 on v2

v3 whole, which is shorter than its diff:
```python
import jax
import jax.numpy as jnp
from jax import lax
from jax.experimental import pallas as pl
from jax.experimental.pallas import tpu as pltpu
from jax.sharding import Mesh
from jax.sharding import PartitionSpec as P

C = 640
GW = 40
TR, TC = 8, 16
PIX = TR * TC
NZ, NY, NX = 8, 4, 4
PEERS = NY * NX
ROWS = NY * TR
NQ = 80
CHIP = float(2 * PIX * GW)
TOTAL = float(NZ * PEERS) * CHIP
VMEM_LIMIT = 48 * 1024 * 1024
F_ROWS, C_ROWS, S_ROWS = 160, 160, 16
G_ROWS = F_ROWS + C_ROWS + S_ROWS
W_ROWS = 64
f32, bf16 = jnp.float32, jnp.bfloat16


def lanes(count):
    return lax.broadcasted_iota(jnp.int32, (1, count), 1)


def slab_channel(main, at):
    z = jnp.where(main, at >> 4, at >> 2)
    return z * 80 + jnp.where(main, at & 15, 16 + (at & 3))


def feature_columns():
    lane = lanes(C)
    main = lane < 512
    y = jnp.where(main, lane >> 7, (lane - 512) >> 5)
    return slab_channel(main, jnp.where(main, lane & 127, lane & 31)) + y * 20


def cotangent_columns(core, side):
    lane = lanes(C)
    main = lane < 512
    x = jnp.where(main, lane >> 7, (lane - 512) >> 5)
    at = jnp.where(main, lane & 127, lane & 31)
    q = jnp.where(main, at & 63, 64 + (at & 15))
    mine = jnp.where(main, at >> 6, at >> 4) == side
    return jnp.where(mine, x * 160 + core * NQ + q, -1)


def term_columns(y):
    lane = lanes(256)
    main = lane < 128
    return slab_channel(main, jnp.where(main, lane, lane & 31)) + y * 20


def vmem():
    return pl.BlockSpec(memory_space=pltpu.VMEM)


def smem():
    return pl.BlockSpec(memory_space=pltpu.SMEM)


def params(**kw):
    return pltpu.CompilerParams(vmem_limit_bytes=VMEM_LIMIT, **kw)


def whole(*dims):
    return pl.BlockSpec(dims, lambda t: (0,) * len(dims))


def group_matrix():
    chan = lax.broadcasted_iota(jnp.int32, (C, 128), 0)
    low = lax.broadcasted_iota(jnp.int32, (C, 128), 1) * GW
    return jnp.where((chan >= low) & (chan < low + GW), 1.0, 0.0).astype(bf16)


def exact_dot(value, matrix, over):
    high, middle, low = three(value)
    stacked = jnp.concatenate([high, middle, low, jnp.zeros_like(low)], axis=0).astype(bf16)
    out = lax.dot_general(stacked, matrix, (((1,), (over,)), ((), ())), preferred_element_type=f32)
    return out[0:8] + out[8:16] + out[16:24]


def rows8(row):
    return jnp.broadcast_to(row, (8, row.shape[1]))


def pick(columns):
    rows = lax.broadcasted_iota(jnp.int32, (C, columns.shape[1]), 0)
    return (rows == columns).astype(f32).astype(bf16)


def three(value):
    high = value.astype(bf16).astype(f32)
    rest = value - high
    middle = rest.astype(bf16).astype(f32)
    return high, middle, rest - middle


def lanes32(value):
    group = lax.broadcasted_iota(jnp.int32, (32, 128), 1) // 32
    out = []
    for a in range(4):
        acc = jnp.zeros((32, 128), f32)
        for g in range(4):
            moved = pltpu.roll(value[32 * g : 32 * g + 32], (32 * (g - a)) % 128, 1)
            acc = jnp.where(group == g, moved, acc)
        out.append(acc)
    return out


def pack_kernel(core_ref, feat_ref, cot_ref, feat2_ref, cot2_ref, out_ref, bias_ref):
    core = core_ref[0]
    feat, cot = feat_ref[...], cot_ref[...]
    x, x2 = feat.astype(f32), feat2_ref[...].astype(f32)
    groups = group_matrix()
    total = x.sum(0, keepdims=True) + x2.sum(0, keepdims=True)
    mean = exact_dot(rows8(total), groups, 0) / CHIP
    wide = exact_dot(mean, groups, 1)[:1]
    squares = ((x - wide) ** 2).sum(0, keepdims=True) + ((x2 - wide) ** 2).sum(0, keepdims=True)
    squares = exact_dot(rows8(squares), groups, 0)
    pieces = three(mean[:1]) + three(squares[:1])
    row = lax.broadcasted_iota(jnp.int32, (S_ROWS, 128), 0)
    stats = jnp.zeros((S_ROWS, 128), f32)
    for k in range(6):
        stats = jnp.where(row == k, pieces[k], stats)
    stats = stats.astype(bf16)
    bias_ref[...] = rows8(cot.astype(f32).sum(0, keepdims=True))

    moved = jnp.dot(feat, pick(feature_columns()), preferred_element_type=f32)
    terms = jnp.dot(cot, pick(cotangent_columns(core, core)), preferred_element_type=f32)
    terms = terms + jnp.dot(cot2_ref[...], pick(cotangent_columns(core, 1 - core)), preferred_element_type=f32)
    moved_rest = lanes32(moved[:, 512:])
    terms_rest = lanes32(terms[:, 512:])
    for y in range(NY):
        for xx in range(NX):
            p = y * NX + xx
            out_ref[p, 0:128] = moved[:, y * 128 : (y + 1) * 128].astype(bf16)
            out_ref[p, 128:160] = moved_rest[y].astype(bf16)
            out_ref[p, 160:288] = terms[:, xx * 128 : (xx + 1) * 128].astype(bf16)
            out_ref[p, 288:320] = terms_rest[xx].astype(bf16)
            out_ref[p, 320:336] = stats


def merge(means, squares, count):
    n = means.shape[0]
    mean = means.sum(0, keepdims=True) / n
    return mean, squares.sum(0, keepdims=True) + count * ((means - mean) ** 2).sum(0, keepdims=True)


def stats_kernel(slab_ref, out_ref):
    got = slab_ref[...].astype(f32)
    mean, squares = merge(
        got[:, 0] + got[:, 1] + got[:, 2], got[:, 3] + got[:, 4] + got[:, 5], CHIP
    )
    row = lax.broadcasted_iota(jnp.int32, (8, 128), 0)
    block = jnp.where(row == 0, mean, jnp.where(row == 1, squares, 0.0))
    for z in range(NZ):
        out_ref[z] = block


def cot_rows(main, rest, g, side):
    lane = lax.broadcasted_iota(jnp.int32, main.shape, 1)
    main = pltpu.roll(main, 64, 1) if side else main
    return jnp.where(lane < 64, main, pltpu.roll(rest, (64 - 32 * g - 16 * side) % 128, 1))


def split_kernel(core_ref, slab_ref, feat_ref, keep_ref, give_ref):
    lower = core_ref[0] == 0
    feat_ref[...] = slab_ref[:, :F_ROWS]
    for xx in range(NX):
        for side in range(2):
            at = slice(xx * 32 + side * TC, xx * 32 + (side + 1) * TC)
            peer = (NY - 1) * NX + xx
            first = cot_rows(slab_ref[xx, 160:176].astype(f32), slab_ref[xx, 288:304].astype(f32), 0, side)
            last = cot_rows(slab_ref[peer, 272:288].astype(f32), slab_ref[peer, 304:320].astype(f32), 3, side)
            keep_ref[at] = jnp.where(lower, last, first).astype(bf16)
            give_ref[at] = jnp.where(lower, first, last).astype(bf16)


def back_kernel(core_ref, cot_ref, cot2_ref, mine_ref, theirs_ref, outer_ref, w_hbm, out_ref, shifted, w_ref, sem):
    copies = [pltpu.make_async_copy(w_hbm.at[t // 3, t % 3], w_ref.at[t], sem.at[t]) for t in range(9)]
    for copy in copies:
        copy.start()
    rows = (TR + 2) * TC
    lower = core_ref[0] == 0
    mine, theirs = mine_ref[...].astype(f32), theirs_ref[...].astype(f32)
    top, bottom = jnp.where(lower, mine, theirs), jnp.where(lower, theirs, mine)
    own_top, other_top = jnp.where(lower, top[:TC], top[TC:]), jnp.where(lower, top[TC:], top[:TC])
    own_bot, other_bot = jnp.where(lower, bottom[:TC], bottom[TC:]), jnp.where(lower, bottom[TC:], bottom[:TC])
    wide = jnp.concatenate([own_top, cot_ref[...].astype(f32), own_bot], axis=0)
    near = jnp.concatenate([other_top, cot2_ref[...].astype(f32), other_bot], axis=0)
    near = near.reshape(TR + 2, TC, C)
    inner = jnp.where(lower, near[:, :1], near[:, TC - 1 :])
    outer = outer_ref[...].astype(f32)[:, None, :]
    left, right = jnp.where(lower, outer, inner), jnp.where(lower, inner, outer)
    left = jnp.broadcast_to(left, (TR + 2, TC, C)).reshape(rows, C)
    right = jnp.broadcast_to(right, (TR + 2, TC, C)).reshape(rows, C)
    col = lax.broadcasted_iota(jnp.int32, (rows, C), 0) % TC
    shifted[0] = jnp.where(col == 0, left, pltpu.roll(wide, 1, 0)).astype(bf16)
    shifted[1] = wide.astype(bf16)
    shifted[2] = jnp.where(col == TC - 1, right, pltpu.roll(wide, rows - 1, 0)).astype(bf16)
    total = jnp.zeros((C, PIX), f32)
    for t in range(9):
        i, j = t // 3, t % 3
        copies[t].wait()
        pixels = shifted[2 - j, (2 - i) * TC : (2 - i) * TC + PIX]
        total = total + lax.dot_general(
            w_ref[t], pixels, (((1,), (1,)), ((), ())), preferred_element_type=f32
        )
    out_ref[...] = total.T


def sums_kernel(y_ref, stat_ref, feat_ref, back_ref, gain_ref, shift_ref, bias_ref,
                row_ref, da_ref, par_ref, out_ref, block):
    got = stat_ref[...]
    mean, squares = merge(got[:, 0], got[:, 1], PEERS * CHIP)
    groups = group_matrix()
    both = jnp.concatenate([mean, lax.rsqrt(squares / TOTAL + 1e-05), jnp.zeros((6, 128), f32)], axis=0)
    both = exact_dot(both, groups, 1)
    mean, rstd = both[0:1], both[1:2]
    gain, shift = gain_ref[...], shift_ref[...]
    row = lax.broadcasted_iota(jnp.int32, (8, C), 0)
    row_ref[...] = jnp.where(row == 0, mean, rstd)
    table = jnp.where(row == 0, mean, jnp.where(row == 1, rstd * gain, jnp.where(row == 2, shift, 0.0)))
    par_ref[...] = exact_dot(table, pick(term_columns(y_ref[0])), 0)
    xhat = (feat_ref[...].astype(f32) - mean) * rstd
    act = xhat * gain + shift
    sig = jax.nn.sigmoid(act)
    da = back_ref[...] * sig * (1.0 + act * (1.0 - sig))
    da_ref[...] = da
    sums = (da.sum(0, keepdims=True), (da * xhat).sum(0, keepdims=True), bias_ref[:1])
    block[...] = jnp.zeros_like(block)
    for s in range(3):
        for t in range(5):
            block[5 * s + t : 5 * s + t + 1] = sums[s][:, 128 * t : 128 * t + 128]
    value = block[...]
    for p in range(2 * PEERS):
        out_ref[p] = value


def terms_kernel(core_ref, own_ref, other_ref, edge_ref, swap_ref, par_ref, out_ref, hid, strips, cot3, rest):
    core = core_ref[0]

    def put(block, peer, side):
        y, xx = peer // NX, peer % NX

        def silu(x, lanes):
            a = (x.astype(f32) - par_ref[0:1, lanes]) * par_ref[1:2, lanes] + par_ref[2:3, lanes]
            return a * jax.nn.sigmoid(a)

        main = silu(block[:128], slice(0, 128)).astype(bf16)
        tail = silu(block[128:], slice(128, 256))
        for g in range(4):
            low = pltpu.roll(tail, (128 - 32 * g) % 128, 1).astype(bf16)
            for h in range(2):
                r = 2 * g + h
                at = pl.ds(pl.multiple_of((y * TR + r) * 128 + xx * 32 + side * TC, TC), TC)
                hid[at, 0:128] = main[r * TC : (r + 1) * TC]
                hid[at, 128:256] = low[h * TC : (h + 1) * TC]

    for peer in range(PEERS):
        put(own_ref[peer, :F_ROWS], peer, core)
        put(other_ref[peer], peer, 1 - core)
        y, xx = peer // NX, peer % NX
        tail = own_ref[peer, 288:320].astype(f32)
        for g in range(4):
            main = own_ref[peer, 160 + 32 * g : 192 + 32 * g].astype(f32)
            for side in range(2):
                value = cot_rows(main, tail, g, side).astype(bf16)
                for h in range(2):
                    at = (y * TR + 2 * g + h + 1) * 128 + xx * 32 + side * TC
                    strips[at : at + TC] = value[h * TC : (h + 1) * TC]
    edge, swap = edge_ref[...].astype(f32), swap_ref[...].astype(f32)
    strips[0:128] = jnp.where(core == 0, edge, swap).astype(bf16)
    strips[(ROWS + 1) * 128 :] = jnp.where(core == 0, swap, edge).astype(bf16)
    lane = lax.broadcasted_iota(jnp.int32, (NQ, 128), 1)
    for row in range(ROWS + 2):
        at = slice(row * 128, (row + 1) * 128)
        turned = strips[at].astype(f32).T[:NQ]
        before = jnp.where(lane == 0, 0.0, pltpu.roll(turned, 1, 1))
        after = jnp.where(lane == 127, 0.0, pltpu.roll(turned, 127, 1))
        cot3[0:NQ, at] = after.astype(bf16)
        cot3[NQ : 2 * NQ, at] = turned.astype(bf16)
        cot3[2 * NQ : 3 * NQ, at] = before.astype(bf16)
    cot3[3 * NQ :] = jnp.zeros((16, (ROWS + 2) * 128), bf16)
    rest[...] = jnp.zeros_like(rest)
    for i in range(3):
        lhs = cot3[:, (2 - i) * 128 : (2 - i) * 128 + ROWS * 128]
        turned = jnp.dot(lhs, hid[...], preferred_element_type=f32).T
        for z in range(NZ):
            out_ref[z, 16 * i : 16 * i + 16] = turned[16 * z : 16 * z + 16].astype(bf16)
            rest[z, 4 * i : 4 * i + 4] = turned[128 + 4 * z : 132 + 4 * z]
    for z in range(NZ):
        out_ref[z, 48:64] = rest[z].astype(bf16)


def join_kernel(sums_ref, out_ref):
    value = sums_ref[0]
    for p in range(1, 2 * PEERS):
        value = value + sums_ref[p]
    for z in range(NZ):
        out_ref[z] = value


def final_kernel(sums_ref, got_ref, feat_ref, da_ref, row_ref, gain_ref,
                 grad_ref, weight_ref, gain_grad_ref, shift_grad_ref, bias_ref):
    total = sums_ref[0]
    for z in range(1, NZ):
        total = total + sums_ref[z]
    sums = [jnp.concatenate([total[5 * s + t : 5 * s + t + 1] for t in range(5)], axis=1) for s in range(3)]
    shift_grad_ref[...], gain_grad_ref[...], bias_ref[...] = [value.reshape(C) for value in sums]
    groups = group_matrix()
    gain, mean, rstd = gain_ref[...], row_ref[0:1], row_ref[1:2]

    both = jnp.concatenate([gain * sums[0], gain * sums[1], jnp.zeros((6, C), f32)], axis=0)
    both = exact_dot(exact_dot(both, groups, 0), groups, 1) / TOTAL
    first, second = both[0:1], both[1:2]
    xhat = (feat_ref[...].astype(f32) - mean) * rstd
    grad_ref[...] = (rstd * (da_ref[...] * gain - first - xhat * second)).astype(bf16)
    weight = got_ref[0].astype(f32)
    for z in range(1, NZ):
        weight = weight + got_ref[z].astype(f32)
    for i in range(3):
        for j in range(3):
            at = slice(j * NQ, (j + 1) * NQ)
            weight_ref[i, j, 0:16] = weight[16 * i : 16 * i + 16, at]
            weight_ref[i, j, 16:20] = weight[48 + 4 * i : 52 + 4 * i, at]


def flip(value):
    return lax.ppermute(value, "core", [(0, 1), (1, 0)])


def shape(dims, dtype):
    return jax.ShapeDtypeStruct(dims, dtype)


def body(features, cotangent, conv_weight, gain, shift):
    core, y = lax.axis_index("core"), lax.axis_index("y")
    at_core, at_y = core.reshape(1), y.reshape(1)
    feat, cot = features.reshape(PIX, C), cotangent.reshape(PIX, C)
    gain, shift = gain.reshape(1, C), shift.reshape(1, C)
    cot2, feat2 = flip(cot), flip(feat)

    edge = jnp.where(
        core == 0,
        jnp.concatenate([cot[PIX - TC :], cot2[PIX - TC :]]),
        jnp.concatenate([cot2[:TC], cot[:TC]]),
    )
    count = NZ * NY
    ways = [(2 * k, 2 * k + 2) for k in range(count - 1)] + [(2 * k + 3, 2 * k + 1) for k in range(count - 1)]
    mine = lax.ppermute(edge, ("z", "y", "core"), ways)
    theirs = flip(mine)

    packed, bias = pl.pallas_call(
        pack_kernel,
        grid=(1,),
        out_shape=(shape((PEERS, G_ROWS, 128), bf16), shape((8, C), f32)),
        in_specs=[smem()] + [whole(PIX, C)] * 4,
        out_specs=(vmem(), vmem()),
        compiler_params=params(),
        name="pack",
    )(at_core, feat, cot, feat2, cot2)
    packed, mine = lax.optimization_barrier((packed, mine))
    slab = lax.all_to_all(packed, ("y", "x"), 0, 0)

    top = jnp.where(core == 0, mine[0], theirs[2 * TC - 1])
    bottom = jnp.where(core == 0, theirs[0], mine[2 * TC - 1])
    column = jnp.where(core == 0, cotangent[:, 0], cotangent[:, TC - 1])
    column = jnp.concatenate([top[None], column, bottom[None]])
    pairs = [(2 * k + 1, 2 * k + 2) for k in range(NX - 1)]
    outer = lax.ppermute(column, ("x", "core"), pairs + [(b, a) for a, b in pairs])
    back = pl.pallas_call(
        back_kernel,
        out_shape=shape((PIX, C), f32),
        in_specs=[smem()] + [vmem()] * 5 + [pl.BlockSpec(memory_space=pl.ANY)],
        out_specs=vmem(),
        scratch_shapes=[
            pltpu.VMEM((3, (TR + 2) * TC, C), bf16),
            pltpu.VMEM((9, C, C), bf16),
            pltpu.SemaphoreType.DMA((9,)),
        ],
        compiler_params=params(),
        cost_estimate=pl.CostEstimate(flops=2 * PIX * 9 * C * C, bytes_accessed=18 * C * C, transcendentals=0),
        name="back",
    )(at_core, cot, cot2, mine, theirs, outer, conv_weight)
    slab, back = lax.optimization_barrier((slab, back))

    stats = pl.pallas_call(
        stats_kernel,
        grid=(1,),
        out_shape=shape((NZ, 8, 128), f32),
        in_specs=[pl.BlockSpec((PEERS, S_ROWS, 128), lambda t: (0, (F_ROWS + C_ROWS) // S_ROWS, 0))],
        out_specs=vmem(),
        compiler_params=params(),
        name="stats",
    )(slab)
    stats = lax.all_to_all(stats, "z", 0, 0)
    slab_feat, keep, give = pl.pallas_call(
        split_kernel,
        out_shape=(shape((PEERS, F_ROWS, 128), bf16), shape((128, 128), bf16), shape((128, 128), bf16)),
        in_specs=[smem(), vmem()],
        out_specs=(vmem(), vmem(), vmem()),
        compiler_params=params(),
        name="split",
    )(at_core, slab)
    slab_other = flip(slab_feat)
    ways = [(2 * k, 2 * k + 2) for k in range(NZ - 1)] + [(2 * k + 3, 2 * k + 1) for k in range(NZ - 1)]
    strip = lax.ppermute(jnp.stack([keep, flip(give)]), ("z", "core"), ways)
    edge, swap = strip[0], flip(strip[1])

    row, da, table, sums = pl.pallas_call(
        sums_kernel,
        out_shape=(shape((8, C), f32), shape((PIX, C), f32), shape((8, 256), f32), shape((2 * PEERS, 16, 128), f32)),
        in_specs=[smem()] + [vmem()] * 6,
        out_specs=(vmem(), vmem(), vmem(), vmem()),
        scratch_shapes=[pltpu.VMEM((16, 128), f32)],
        compiler_params=params(),
        name="sums",
    )(at_y, stats, feat, back, gain, shift, bias)
    sums = lax.all_to_all(sums, ("y", "x", "core"), 0, 0)

    terms = pl.pallas_call(
        terms_kernel,
        out_shape=shape((NZ, W_ROWS, 256), bf16),
        in_specs=[smem()] + [vmem()] * 5,
        out_specs=vmem(),
        scratch_shapes=[
            pltpu.VMEM((ROWS * 128, 256), bf16),
            pltpu.VMEM(((ROWS + 2) * 128, 128), bf16),
            pltpu.VMEM((256, (ROWS + 2) * 128), bf16),
            pltpu.VMEM((NZ, 16, 256), f32),
        ],
        compiler_params=params(),
        cost_estimate=pl.CostEstimate(
            flops=2 * PIX * 9 * C * C, bytes_accessed=4 << 20, transcendentals=ROWS * 128 * 256
        ),
        name="terms",
    )(at_core, slab, slab_other, edge, swap, table)

    terms = lax.all_to_all(terms, "z", 0, 0)
    sums = pl.pallas_call(
        join_kernel,
        out_shape=shape((NZ, 16, 128), f32),
        in_specs=[vmem()],
        out_specs=vmem(),
        compiler_params=params(),
        name="join",
    )(sums)
    sums = lax.all_to_all(sums, "z", 0, 0)
    grad, weight_grad, gain_grad, shift_grad, bias_grad = pl.pallas_call(
        final_kernel,
        out_shape=(shape((PIX, C), bf16), shape((3, 3, 20, NQ), f32)) + (shape((C,), f32),) * 3,
        in_specs=[vmem()] * 6,
        out_specs=(vmem(),) * 5,
        compiler_params=params(),
        name="final",
    )(sums, terms, feat, da, row, gain)
    return grad.reshape(features.shape), weight_grad, gain_grad, shift_grad, bias_grad


def solution(mesh):
    grid = Mesh(mesh.devices.reshape(NZ, NY, NX, 2), ("z", "y", "x", "core"))
    rows, cols = ("z", "y"), ("x", "core")
    tiled = P(rows, cols, None)
    return jax.shard_map(
        body,
        mesh=grid,
        in_specs=(tiled, tiled, P(), P(), P()),
        out_specs=(tiled, P(None, None, rows, cols), P(), P(), P()),
        check_vma=False,
    )
```

time: 104 us -> 103 us (level)
  the two profiles are of different devices: /device:TPU:2 before, /device:TPU:1 now
where the time goes in v3:
time: 103 us; the launch traced here: 101 us
  starting transfers between devices  39.1 us (38%)
  waiting for transfers between devices  30.4 us (30%)
  Pallas kernels  15.7 us (15%)
  blocking collectives  12.7 us (12%)
  local copies, waits for them, and re-layouts  2.65 us (3%)
    all_to_all x1, blocking collectives, body(): terms = lax.all_to_all(terms, 'z', 0, 0)  12.7 us
    ppermute x1, waiting for transfers between devices, body(): lax.ppermute(column, ('x', 'core'), pairs + [(b, a) for a, b in pairs])  11.4 us
    all_to_all x1, starting transfers between devices, body(): sums = lax.all_to_all(sums, ('y', 'x', 'core'), 0, 0)  8.83 us
    all_to_all x1, waiting for transfers between devices, body(): sums = lax.all_to_all(sums, ('y', 'x', 'core'), 0, 0)  8.55 us
    all_to_all x1, starting transfers between devices, body(): stats = lax.all_to_all(stats, 'z', 0, 0)  8.19 us
    all_to_all x1, starting transfers between devices, body(): slab = lax.all_to_all(packed, ('y', 'x'), 0, 0)  6.27 us
    ppermute x6, starting transfers between devices, flip(): return lax.ppermute(value, 'core', [(0, 1), (1, 0)])  5.89 us
    pallas_call x1, Pallas kernels, body(): pl.pallas_call(back_kernel, out_shape=shape((PIX, C), f32), in_specs=[sme...  5.68 us
  transfers between devices with their start and end apart: 13, of which 6 were waited for; matrix products, arithmetic and copies ran while one was open for 1% of the time, Pallas kernels for 14%

profile of v3, /device:TPU:1, one launch (start us, length us, event | category | flops | bytes accessed | tf_op | source)
XLA Modules:
  0.0 101.4 jit_solution(7473357824893851452)
XLA Ops:
  0.6 3.3 %collective-permute-start.1 = (bf16[128,640]{1,0:T(8,128)(2,1)}, bf16[128,640]{1,0:T(8,128)(2,1)S(1)}, u32[]{:S(2)}, u32[]{:S(2)}) collective-permute-start(bf16[128,640]{1,0:T(8,128)(2,1)} %bitcast.21), channel_id=1, source_target_pairs={{0,1},{1,0},{2,3},{3,2},{4,5},{5,4},{6,7},{7,6},{8,9},{9,8},{10,11... | collective-permute-start | bytes 491528 | tf_op jit(solution)/shard_map/ppermute | solution.py:335
  4.0 0.1 collective-permute-start
  4.1 0.7 slice_bitcast_fusion.2
  4.8 0.4 collective-permute-done.1.cot2_ref
  5.2 1.3 %collective-permute-start.2 = (bf16[32,640]{1,0:T(8,128)(2,1)S(1)}, bf16[32,640]{1,0:T(8,128)(2,1)S(1)}, u32[]{:S(2)}, u32[]{:S(2)}) collective-permute-start(bf16[32,640]{1,0:T(8,128)(2,1)S(1)} %maximum_select_fusion), channel_id=1, source_target_pairs={{0,8},{8,16},{16,24},{24,32},{32,40},{40,48},{48,56},{56,64},{64,7... | collective-permute-start | bytes 122888 | tf_op jit(solution)/shard_map/ppermute | solution.py:356
  6.5 0.0 collective-permute-done.feat2_ref
  6.5 0.0 copy-start
  6.5 0.9 copy-done
  7.4 0.0 copy-start.2
  7.5 0.9 copy-done.2
  8.4 2.4 %pack.1 = (bf16[16,336,128]{2,1,0:T(8,128)(2,1)}, f32[8,640]{1,0:T(8,128)S(1)}) custom-call(s32[1]{0:T(128)} %bitcast.1.core_ref, bf16[128,640]{1,0:T(8,128)(2,1)S(1)} %bitcast.18, bf16[128,640]{1,0:T(8,128)(2,1)S(1)} %bitcast.22, bf16[128,640]{1,0:T(8,128)(2,1)S(1)} %collective-permute-done.feat2_ref, bf16[128,640]{1,0:T(8,128)(2,1)S(1)} %collective-permute-done.1.cot2_ref), custom_call_target="tpu_custom_call" | custom-call | tf_op jit(solution)/shard_map/pack/pallas_call | solution.py:359
  10.8 0.0 collective-permute-done.2.mine_ref
  10.8 0.0 copy-start.3
  10.8 6.3 %all-to-all-start = ((bf16[16,336,128]{2,1,0:T(8,128)(2,1)}), bf16[16,336,128]{2,1,0:T(8,128)(2,1)S(1)}, u32[]{:S(2)}, u32[]{:S(2)}) async-start(bf16[16,336,128]{2,1,0:T(8,128)(2,1)} %get-tuple-element.24), calls=%async_computation | async-start | bytes 2752512 | tf_op jit(solution)/shard_map/all_to_all | solution.py:369
  17.1 0.0 copy-done.3
  17.1 1.6 %collective-permute-start.3 = (bf16[32,640]{1,0:T(8,128)(2,1)S(1)}, bf16[32,640]{1,0:T(8,128)(2,1)S(1)}, u32[]{:S(2)}, u32[]{:S(2)}) collective-permute-start(bf16[32,640]{1,0:T(8,128)(2,1)S(1)} %collective-permute-done.2.mine_ref), channel_id=1, source_target_pairs={{0,1},{1,0},{2,3},{3,2},{4,5},{5,4},{6,7},{7,6},{8,9},{9,8},{10,11... | collective-permute-start | bytes 122888 | tf_op jit(solution)/shard_map/ppermute | solution.py:335
  18.7 0.9 collective-permute-done.3.theirs_ref
  19.6 3.8 %collective-permute-start.4 = (bf16[10,640]{1,0:T(8,128)(2,1)S(1)}, bf16[10,640]{1,0:T(8,128)(2,1)S(1)}, u32[]{:S(2)}, u32[]{:S(2)}) collective-permute-start(bf16[10,640]{1,0:T(8,128)(2,1)S(1)} %pad_maximum_fusion.1), channel_id=1, source_target_pairs={{1,2},{3,4},{5,6},{2,1},{4,3},{6,5},{9,10},{11,12},{13,14},{10,9},... | collective-permute-start | bytes 38408 | tf_op jit(solution)/shard_map/ppermute | solution.py:376
  23.4 11.4 %collective-permute-done.4.outer_ref = bf16[10,640]{1,0:T(8,128)(2,1)S(1)} collective-permute-done((bf16[10,640]{1,0:T(8,128)(2,1)S(1)}, bf16[10,640]{1,0:T(8,128)(2,1)S(1)}, u32[]{:S(2)}, u32[]{:S(2)}) %collective-permute-start.4) | collective-permute-done | bytes 12832 | tf_op jit(solution)/shard_map/ppermute | solution.py:376
  34.9 5.7 %back.1.back_ref = f32[128,640]{1,0:T(8,128)S(1)} custom-call(s32[1]{0:T(128)} %bitcast.1.core_ref, bf16[128,640]{1,0:T(8,128)(2,1)S(1)} %bitcast.23, bf16[128,640]{1,0:T(8,128)(2,1)S(1)} %collective-permute-done.1.cot2_ref, bf16[32,640]{1,0:T(8,128)(2,1)S(1)} %collective-permute-done.2.mine_ref, bf16[32,640]{1,0:T(8,128)(2,1)S(1)} %collective-permute-done.3.theirs_ref, ...), custom_call_target="tpu_custom_call" | custom-call | flops 943718400 | bytes 7372800 | tf_op jit(solution)/shard_map/back/pallas_call | solution.py:377
  40.6 0.0 copy-start.4
  40.6 0.0 copy-start.5
  40.6 0.0 copy-start.1
  40.6 0.0 all-to-all-done.slab_ref.own_ref
  40.6 0.9 split.1
  41.5 0.0 collective-permute-start.5
  41.5 0.5 collective-permute-start.6
  42.0 0.7 stats.1
  42.7 8.2 %all-to-all-start.1 = ((f32[8,8,128]{2,1,0:T(8,128)}), f32[8,8,128]{2,1,0:T(8,128)S(1)}, u32[]{:S(2)}, u32[]{:S(2)}) async-start(f32[8,8,128]{2,1,0:T(8,128)} %stats.1), calls=%async_computation.1 | async-start | bytes 65536 | tf_op jit(solution)/shard_map/all_to_all | solution.py:402
  50.9 0.0 collective-permute-done.6
  50.9 1.3 %collective-permute-start.7 = (bf16[2,128,128]{2,1,0:T(8,128)(2,1)S(1)}, bf16[2,128,128]{2,1,0:T(8,128)(2,1)S(1)}, u32[]{:S(2)}, u32[]{:S(2)}) collective-permute-start(bf16[2,128,128]{2,1,0:T(8,128)(2,1)S(1)} %pad_maximum_fusion), channel_id=1, source_target_pairs={{0,32},{32,64},{64,96},{96,128},{128,160},{160,192},{192,224},{33,... | collective-permute-start | bytes 196616 | tf_op jit(solution)/shard_map/ppermute | solution.py:413
  52.2 0.0 copy-done.4
  52.2 0.0 copy-done.5
  52.2 5.5 %all-to-all-done.1.stat_ref = f32[8,8,128]{2,1,0:T(8,128)S(1)} async-done(((f32[8,8,128]{2,1,0:T(8,128)}), f32[8,8,128]{2,1,0:T(8,128)S(1)}, u32[]{:S(2)}, u32[]{:S(2)}) %all-to-all-start.1) | async-done | bytes 32800 | tf_op jit(solution)/shard_map/all_to_all | solution.py:402
  57.7 0.0 copy-done.1
  57.7 1.1 %sums.1 = (f32[8,640]{1,0:T(8,128)S(1)}, f32[128,640]{1,0:T(8,128)S(1)}, f32[8,256]{1,0:T(8,128)S(1)}, f32[32,16,128]{2,1,0:T(8,128)}) custom-call(s32[1]{0:T(128)} %bitcast.y_ref, f32[8,8,128]{2,1,0:T(8,128)S(1)} %all-to-all-done.1.stat_ref, bf16[128,640]{1,0:T(8,128)(2,1)S(1)} %bitcast.19, f32[128,640]{1,0:T(8,128)S(1)} %back.1.back_ref, ...), custom_call_target="tpu_custom_call" | custom-call | tf_op jit(solution)/shard_map/sums/pallas_call | solution.py:416
  58.9 8.8 %all-to-all-start.2 = ((f32[32,16,128]{2,1,0:T(8,128)}), f32[32,16,128]{2,1,0:T(8,128)S(1)}, u32[]{:S(2)}, u32[]{:S(2)}) async-start(f32[32,16,128]{2,1,0:T(8,128)} %get-tuple-element.29), calls=%async_computation.2 | async-start | bytes 524288 | tf_op jit(solution)/shard_map/all_to_all | solution.py:425
  67.7 0.0 collective-permute-done.7
  67.7 0.3 collective-permute-start.8
  68.0 8.6 %all-to-all-done.2.sums_ref = f32[32,16,128]{2,1,0:T(8,128)S(1)} async-done(((f32[32,16,128]{2,1,0:T(8,128)}), f32[32,16,128]{2,1,0:T(8,128)S(1)}, u32[]{:S(2)}, u32[]{:S(2)}) %all-to-all-start.2) | async-done | bytes 262176 | tf_op jit(solution)/shard_map/all_to_all | solution.py:425
  76.6 0.7 join.1
  77.3 3.5 %all-to-all-start.3 = ((f32[8,16,128]{2,1,0:T(8,128)}), f32[8,16,128]{2,1,0:T(8,128)S(1)}, u32[]{:S(2)}, u32[]{:S(2)}) async-start(f32[8,16,128]{2,1,0:T(8,128)} %join.1), calls=%async_computation.3 | async-start | bytes 131072 | tf_op jit(solution)/shard_map/all_to_all | solution.py:454
  80.8 0.0 collective-permute-done.8.swap_ref
  80.8 0.0 collective-permute-done.5.other_ref
  80.8 3.2 %terms.1 = bf16[8,64,256]{2,1,0:T(8,128)(2,1)S(1)} custom-call(s32[1]{0:T(128)} %bitcast.1.core_ref, bf16[16,336,128]{2,1,0:T(8,128)(2,1)S(1)} %all-to-all-done.slab_ref.own_ref, bf16[16,160,128]{2,1,0:T(8,128)(2,1)S(1)} %collective-permute-done.5.other_ref, bf16[128,128]{1,0:T(8,128)(2,1)S(1)} %get-tuple-element.50.edge_ref, ...), custom_call_target="tpu_custom_call" | custom-call | flops 943718400 | bytes 4194304 | tf_op jit(solution)/shard_map/terms/pallas_call | solution.py:427
  84.1 3.6 %all-to-all-done.3.sums_ref = f32[8,16,128]{2,1,0:T(8,128)S(1)} async-done(((f32[8,16,128]{2,1,0:T(8,128)}), f32[8,16,128]{2,1,0:T(8,128)S(1)}, u32[]{:S(2)}, u32[]{:S(2)}) %all-to-all-start.3) | async-done | bytes 65568 | tf_op jit(solution)/shard_map/all_to_all | solution.py:454
  87.7 12.7 %all_to_all.25.got_ref = bf16[8,64,256]{2,1,0:T(8,128)(2,1)S(1)} all-to-all(bf16[8,64,256]{2,1,0:T(8,128)(2,1)S(1)} %terms.1), channel_id=1, replica_groups=mesh['z'=8,'y'=4,'x'=4,'core'=2] {'z'}, dimensions={0} | all-to-all | bytes 524288 | tf_op jit(solution)/shard_map/all_to_all | solution.py:445
  100.3 1.1 %final.1 = (bf16[128,640]{1,0:T(8,128)(2,1)}, f32[3,3,20,80]{3,2,1,0:T(8,128)}, f32[640]{0:T(1024)}, f32[640]{0:T(1024)}, f32[640]{0:T(1024)}) custom-call(f32[8,16,128]{2,1,0:T(8,128)S(1)} %all-to-all-done.3.sums_ref, bf16[8,64,256]{2,1,0:T(8,128)(2,1)S(1)} %all_to_all.25.got_ref, bf16[128,640]{1,0:T(8,128)(2,1)S(1)} %bitcast.20, ...), custom_call_target="tpu_custom_call" | custom-call | tf_op jit(solution)/shard_map/final/pallas_call | solution.py:455
  (10 shorter events, 0.1 us)
Async XLA Ops:
  0.6 4.6 %collective-permute-start.1 = (bf16[128,640]{1,0:T(8,128)(2,1)}, bf16[128,640]{1,0:T(8,128)(2,1)S(1)}, u32[]{:S(2)}, u32[]{:S(2)}) collective-permute-start(bf16[128,640]{1,0:T(8,128)(2,1)} %bitcast.21), channel_id=1, source_target_pairs={{0,1},{1,0},{2,3},{3,2},{4,5},{5,4},{6,7},{7,6},{8,9},{9,8},{10,11... | collective-permute-start | bytes 491528 | tf_op jit(solution)/shard_map/ppermute | solution.py:335
  4.0 2.6 %collective-permute-start = (bf16[128,640]{1,0:T(8,128)(2,1)}, bf16[128,640]{1,0:T(8,128)(2,1)S(1)}, u32[]{:S(2)}, u32[]{:S(2)}) collective-permute-start(bf16[128,640]{1,0:T(8,128)(2,1)} %bitcast.17), channel_id=1, source_target_pairs={{0,1},{1,0},{2,3},{3,2},{4,5},{5,4},{6,7},{7,6},{8,9},{9,8},{10,11... | collective-permute-start | bytes 491528 | tf_op jit(solution)/shard_map/ppermute | solution.py:335
  5.2 5.6 %collective-permute-start.2 = (bf16[32,640]{1,0:T(8,128)(2,1)S(1)}, bf16[32,640]{1,0:T(8,128)(2,1)S(1)}, u32[]{:S(2)}, u32[]{:S(2)}) collective-permute-start(bf16[32,640]{1,0:T(8,128)(2,1)S(1)} %maximum_select_fusion), channel_id=1, source_target_pairs={{0,8},{8,16},{16,24},{24,32},{32,40},{40,48},{48,56},{56,64},{64,7... | collective-permute-start | bytes 122888 | tf_op jit(solution)/shard_map/ppermute | solution.py:356
  6.5 0.9 copy-start
  7.4 0.9 copy-start.2
  10.8 6.3 %copy-start.3 = (bf16[8,16,640]{2,1,0:T(8,128)(2,1)S(1)}, bf16[8,16,640]{2,1,0:T(8,128)(2,1)}, u32[]{:S(2)}) copy-start(bf16[8,16,640]{2,1,0:T(8,128)(2,1)} %param.6) | copy-start | bytes 491524
  10.8 29.8 %all-to-all-start = ((bf16[16,336,128]{2,1,0:T(8,128)(2,1)}), bf16[16,336,128]{2,1,0:T(8,128)(2,1)S(1)}, u32[]{:S(2)}, u32[]{:S(2)}) async-start(bf16[16,336,128]{2,1,0:T(8,128)(2,1)} %get-tuple-element.24), calls=%async_computation | async-start | bytes 2752512 | tf_op jit(solution)/shard_map/all_to_all | solution.py:369
  17.1 2.5 %collective-permute-start.3 = (bf16[32,640]{1,0:T(8,128)(2,1)S(1)}, bf16[32,640]{1,0:T(8,128)(2,1)S(1)}, u32[]{:S(2)}, u32[]{:S(2)}) collective-permute-start(bf16[32,640]{1,0:T(8,128)(2,1)S(1)} %collective-permute-done.2.mine_ref), channel_id=1, source_target_pairs={{0,1},{1,0},{2,3},{3,2},{4,5},{5,4},{6,7},{7,6},{8,9},{9,8},{10,11... | collective-permute-start | bytes 122888 | tf_op jit(solution)/shard_map/ppermute | solution.py:335
  19.6 15.2 %collective-permute-start.4 = (bf16[10,640]{1,0:T(8,128)(2,1)S(1)}, bf16[10,640]{1,0:T(8,128)(2,1)S(1)}, u32[]{:S(2)}, u32[]{:S(2)}) collective-permute-start(bf16[10,640]{1,0:T(8,128)(2,1)S(1)} %pad_maximum_fusion.1), channel_id=1, source_target_pairs={{1,2},{3,4},{5,6},{2,1},{4,3},{6,5},{9,10},{11,12},{13,14},{10,9},... | collective-permute-start | bytes 38408 | tf_op jit(solution)/shard_map/ppermute | solution.py:376
  40.6 11.6 %copy-start.4 = (f32[640]{0:T(1024)S(1)}, f32[640]{0:T(1024)}, u32[]{:S(2)}) copy-start(f32[640]{0:T(1024)} %param.8) | copy-start | bytes 7684
  40.6 11.6 %copy-start.5 = (f32[640]{0:T(1024)S(1)}, f32[640]{0:T(1024)}, u32[]{:S(2)}) copy-start(f32[640]{0:T(1024)} %param.9) | copy-start | bytes 7684
  40.6 17.1 %copy-start.1 = (bf16[8,16,640]{2,1,0:T(8,128)(2,1)S(1)}, bf16[8,16,640]{2,1,0:T(8,128)(2,1)}, u32[]{:S(2)}) copy-start(bf16[8,16,640]{2,1,0:T(8,128)(2,1)} %param.5) | copy-start | bytes 491524
  41.5 39.3 %collective-permute-start.5 = (bf16[16,160,128]{2,1,0:T(8,128)(2,1)}, bf16[16,160,128]{2,1,0:T(8,128)(2,1)S(1)}, u32[]{:S(2)}, u32[]{:S(2)}) collective-permute-start(bf16[16,160,128]{2,1,0:T(8,128)(2,1)} %get-tuple-element.30), channel_id=1, source_target_pairs={{0,1},{1,0},{2,3},{3,2},{4,5},{5,4},{6,7},{7,6},{8,9},{9,8},{10,11... | collective-permute-start | bytes 1966088 | tf_op jit(solution)/shard_map/ppermute | solution.py:335
  41.5 9.4 %collective-permute-start.6 = (bf16[128,128]{1,0:T(8,128)(2,1)S(1)}, bf16[128,128]{1,0:T(8,128)(2,1)S(1)}, u32[]{:S(2)}, u32[]{:S(2)}) collective-permute-start(bf16[128,128]{1,0:T(8,128)(2,1)S(1)} %get-tuple-element.32), channel_id=1, source_target_pairs={{0,1},{1,0},{2,3},{3,2},{4,5},{5,4},{6,7},{7,6},{8,9},{9,8},{10,11... | collective-permute-start | bytes 98312 | tf_op jit(solution)/shard_map/ppermute | solution.py:335
  42.7 15.1 %all-to-all-start.1 = ((f32[8,8,128]{2,1,0:T(8,128)}), f32[8,8,128]{2,1,0:T(8,128)S(1)}, u32[]{:S(2)}, u32[]{:S(2)}) async-start(f32[8,8,128]{2,1,0:T(8,128)} %stats.1), calls=%async_computation.1 | async-start | bytes 65536 | tf_op jit(solution)/shard_map/all_to_all | solution.py:402
  50.9 16.8 %collective-permute-start.7 = (bf16[2,128,128]{2,1,0:T(8,128)(2,1)S(1)}, bf16[2,128,128]{2,1,0:T(8,128)(2,1)S(1)}, u32[]{:S(2)}, u32[]{:S(2)}) collective-permute-start(bf16[2,128,128]{2,1,0:T(8,128)(2,1)S(1)} %pad_maximum_fusion), channel_id=1, source_target_pairs={{0,32},{32,64},{64,96},{96,128},{128,160},{160,192},{192,224},{33,... | collective-permute-start | bytes 196616 | tf_op jit(solution)/shard_map/ppermute | solution.py:413
  58.9 17.7 %all-to-all-start.2 = ((f32[32,16,128]{2,1,0:T(8,128)}), f32[32,16,128]{2,1,0:T(8,128)S(1)}, u32[]{:S(2)}, u32[]{:S(2)}) async-start(f32[32,16,128]{2,1,0:T(8,128)} %get-tuple-element.29), calls=%async_computation.2 | async-start | bytes 524288 | tf_op jit(solution)/shard_map/all_to_all | solution.py:425
  67.7 13.1 %collective-permute-start.8 = (bf16[128,128]{1,0:T(8,128)(2,1)S(1)}, bf16[128,128]{1,0:T(8,128)(2,1)S(1)}, u32[]{:S(2)}, u32[]{:S(2)}) collective-permute-start(bf16[128,128]{1,0:T(8,128)(2,1)S(1)} %get-tuple-element.49), channel_id=1, source_target_pairs={{0,1},{1,0},{2,3},{3,2},{4,5},{5,4},{6,7},{7,6},{8,9},{9,8},{10,11... | collective-permute-start | bytes 98312 | tf_op jit(solution)/shard_map/ppermute | solution.py:335
  77.3 10.4 %all-to-all-start.3 = ((f32[8,16,128]{2,1,0:T(8,128)}), f32[8,16,128]{2,1,0:T(8,128)S(1)}, u32[]{:S(2)}, u32[]{:S(2)}) async-start(f32[8,16,128]{2,1,0:T(8,128)} %join.1), calls=%async_computation.3 | async-start | bytes 131072 | tf_op jit(solution)/shard_map/all_to_all | solution.py:454

commit v4 on v3

--- a/solution.py
+++ b/solution.py
@@ -17,9 +17,11 @@
 CHIP = float(2 * PIX * GW)
 TOTAL = float(NZ * PEERS) * CHIP
 VMEM_LIMIT = 48 * 1024 * 1024
-F_ROWS, C_ROWS, S_ROWS = 160, 160, 16
-G_ROWS = F_ROWS + C_ROWS + S_ROWS
-W_ROWS = 64
+F_ROWS, C_ROWS, H_ROWS, S_ROWS = 160, 160, 32, 16
+H_AT = F_ROWS + C_ROWS
+S_AT = H_AT + H_ROWS
+G_ROWS = S_AT + S_ROWS
+W_ROWS, V_ROWS = 64, 16
 f32, bf16 = jnp.float32, jnp.bfloat16
 
 
@@ -100,49 +102,70 @@
     return high, middle, rest - middle
 
 
-def lanes32(value):
-    group = lax.broadcasted_iota(jnp.int32, (32, 128), 1) // 32
+def lanes32(value, height):
+    group = lax.broadcasted_iota(jnp.int32, (height, 128), 1) // 32
     out = []
     for a in range(4):
-        acc = jnp.zeros((32, 128), f32)
+        acc = jnp.zeros((height, 128), f32)
         for g in range(4):
-            moved = pltpu.roll(value[32 * g : 32 * g + 32], (32 * (g - a)) % 128, 1)
+            moved = pltpu.roll(value[height * g : height * (g + 1)], (32 * (g - a)) % 128, 1)
             acc = jnp.where(group == g, moved, acc)
         out.append(acc)
     return out
 
 
-def pack_kernel(core_ref, feat_ref, cot_ref, feat2_ref, cot2_ref, out_ref, bias_ref):
-    core = core_ref[0]
-    feat, cot = feat_ref[...], cot_ref[...]
-    x, x2 = feat.astype(f32), feat2_ref[...].astype(f32)
+def stats_kernel(feat_hbm, cot_hbm, feat2_ref, out_ref, bias_ref, feat_ref, cot_ref, sem):
+    copies = [
+        pltpu.make_async_copy(feat_hbm, feat_ref, sem.at[0]),
+        pltpu.make_async_copy(cot_hbm, cot_ref, sem.at[1]),
+    ]
+    for copy in copies:
+        copy.start()
     groups = group_matrix()
+    for copy in copies:
+        copy.wait()
+    x, x2 = feat_ref[...].astype(f32), feat2_ref[...].astype(f32)
     total = x.sum(0, keepdims=True) + x2.sum(0, keepdims=True)
     mean = exact_dot(rows8(total), groups, 0) / CHIP
     wide = exact_dot(mean, groups, 1)[:1]
     squares = ((x - wide) ** 2).sum(0, keepdims=True) + ((x2 - wide) ** 2).sum(0, keepdims=True)
     squares = exact_dot(rows8(squares), groups, 0)
-    pieces = three(mean[:1]) + three(squares[:1])
-    row = lax.broadcasted_iota(jnp.int32, (S_ROWS, 128), 0)
-    stats = jnp.zeros((S_ROWS, 128), f32)
-    for k in range(6):
-        stats = jnp.where(row == k, pieces[k], stats)
-    stats = stats.astype(bf16)
-    bias_ref[...] = rows8(cot.astype(f32).sum(0, keepdims=True))
-
-    moved = jnp.dot(feat, pick(feature_columns()), preferred_element_type=f32)
-    terms = jnp.dot(cot, pick(cotangent_columns(core, core)), preferred_element_type=f32)
-    terms = terms + jnp.dot(cot2_ref[...], pick(cotangent_columns(core, 1 - core)), preferred_element_type=f32)
-    moved_rest = lanes32(moved[:, 512:])
-    terms_rest = lanes32(terms[:, 512:])
+    row = lax.broadcasted_iota(jnp.int32, (8, 128), 0)
+    block = jnp.where(row == 0, mean, jnp.where(row == 1, squares, 0.0))
+    for z in range(NZ):
+        out_ref[z] = block
+    bias_ref[...] = rows8(cot_ref[...].astype(f32).sum(0, keepdims=True))
+
+
+def pack_kernel(core_ref, feat_ref, cot_ref, cot2_ref, mine_ref, theirs_ref, out_ref, rest_ref):
+    core = core_ref[0]
+    lower = core == 0
+
+    def pair(own, other):
+        a, b = own[...].astype(f32), other[...].astype(f32)
+        return jnp.where(lower, a, b).astype(bf16), jnp.where(lower, b, a).astype(bf16)
+
+    first, second = pair(cot_ref, cot2_ref)
+    top, bottom = pair(mine_ref, theirs_ref)
+    moved = jnp.dot(feat_ref[...], pick(feature_columns()), preferred_element_type=f32)
+    terms = jnp.dot(
+        jnp.concatenate([first, top], axis=0), pick(cotangent_columns(core, 0)), preferred_element_type=f32
+    ) + jnp.dot(
+        jnp.concatenate([second, bottom], axis=0), pick(cotangent_columns(core, 1)), preferred_element_type=f32
+    )
+    moved_rest = lanes32(moved[:, 512:], 32)
+    terms_rest = lanes32(terms[:PIX, 512:], 32)
+    halo_rest = lanes32(terms[PIX:, 512:], 8)
+    for xx in range(NX):
+        rest_ref[xx] = halo_rest[xx]
     for y in range(NY):
         for xx in range(NX):
             p = y * NX + xx
             out_ref[p, 0:128] = moved[:, y * 128 : (y + 1) * 128].astype(bf16)
             out_ref[p, 128:160] = moved_rest[y].astype(bf16)
-            out_ref[p, 160:288] = terms[:, xx * 128 : (xx + 1) * 128].astype(bf16)
+            out_ref[p, 160:288] = terms[:PIX, xx * 128 : (xx + 1) * 128].astype(bf16)
             out_ref[p, 288:320] = terms_rest[xx].astype(bf16)
-            out_ref[p, 320:336] = stats
+            out_ref[p, H_AT:S_AT] = terms[PIX:, xx * 128 : (xx + 1) * 128].astype(bf16)
 
 
 def merge(means, squares, count):
@@ -151,34 +174,25 @@
     return mean, squares.sum(0, keepdims=True) + count * ((means - mean) ** 2).sum(0, keepdims=True)
 
 
-def stats_kernel(slab_ref, out_ref):
-    got = slab_ref[...].astype(f32)
-    mean, squares = merge(
-        got[:, 0] + got[:, 1] + got[:, 2], got[:, 3] + got[:, 4] + got[:, 5], CHIP
-    )
+def patch_kernel(stat_ref, rest_ref, packed_ref, out_ref, block, sem):
+    got = stat_ref[...]
+    mean, squares = merge(got[:, 0], got[:, 1], CHIP)
+    pieces = three(mean) + three(squares)
     row = lax.broadcasted_iota(jnp.int32, (8, 128), 0)
-    block = jnp.where(row == 0, mean, jnp.where(row == 1, squares, 0.0))
-    for z in range(NZ):
-        out_ref[z] = block
+    stats = jnp.zeros((8, 128), f32)
+    for k in range(6):
+        stats = jnp.where(row == k, pieces[k], stats)
+    for p in range(PEERS):
+        block[p] = jnp.concatenate([stats, rest_ref[p % NX]], axis=0).astype(bf16)
+    copy = pltpu.make_async_copy(block, out_ref.at[:, S_AT:, :], sem)
+    copy.start()
+    copy.wait()
 
 
 def cot_rows(main, rest, g, side):
     lane = lax.broadcasted_iota(jnp.int32, main.shape, 1)
     main = pltpu.roll(main, 64, 1) if side else main
     return jnp.where(lane < 64, main, pltpu.roll(rest, (64 - 32 * g - 16 * side) % 128, 1))
-
-
-def split_kernel(core_ref, slab_ref, feat_ref, keep_ref, give_ref):
-    lower = core_ref[0] == 0
-    feat_ref[...] = slab_ref[:, :F_ROWS]
-    for xx in range(NX):
-        for side in range(2):
-            at = slice(xx * 32 + side * TC, xx * 32 + (side + 1) * TC)
-            peer = (NY - 1) * NX + xx
-            first = cot_rows(slab_ref[xx, 160:176].astype(f32), slab_ref[xx, 288:304].astype(f32), 0, side)
-            last = cot_rows(slab_ref[peer, 272:288].astype(f32), slab_ref[peer, 304:320].astype(f32), 3, side)
-            keep_ref[at] = jnp.where(lower, last, first).astype(bf16)
-            give_ref[at] = jnp.where(lower, first, last).astype(bf16)
 
 
 def back_kernel(core_ref, cot_ref, cot2_ref, mine_ref, theirs_ref, outer_ref, w_hbm, out_ref, shifted, w_ref, sem):
@@ -214,10 +228,12 @@
     out_ref[...] = total.T
 
 
-def sums_kernel(y_ref, stat_ref, feat_ref, back_ref, gain_ref, shift_ref, bias_ref,
+def sums_kernel(y_ref, slab_ref, feat_ref, back_ref, gain_ref, shift_ref, bias_ref,
                 row_ref, da_ref, par_ref, out_ref, block):
-    got = stat_ref[...]
-    mean, squares = merge(got[:, 0], got[:, 1], PEERS * CHIP)
+    got = slab_ref[:, S_AT:].astype(f32)
+    mean, squares = merge(
+        got[:, 0] + got[:, 1] + got[:, 2], got[:, 3] + got[:, 4] + got[:, 5], NZ * CHIP
+    )
     groups = group_matrix()
     both = jnp.concatenate([mean, lax.rsqrt(squares / TOTAL + 1e-05), jnp.zeros((6, 128), f32)], axis=0)
     both = exact_dot(both, groups, 1)
@@ -237,12 +253,11 @@
     for s in range(3):
         for t in range(5):
             block[5 * s + t : 5 * s + t + 1] = sums[s][:, 128 * t : 128 * t + 128]
-    value = block[...]
     for p in range(2 * PEERS):
-        out_ref[p] = value
-
-
-def terms_kernel(core_ref, own_ref, other_ref, edge_ref, swap_ref, par_ref, out_ref, hid, strips, cot3, rest):
+        out_ref[p] = block[8 * (p % 2) : 8 * (p % 2) + 8]
+
+
+def terms_kernel(core_ref, own_ref, other_ref, par_ref, out_ref, hid, strips, cot3, rest):
     core = core_ref[0]
 
     def put(block, peer, side):
@@ -264,7 +279,7 @@
 
     for peer in range(PEERS):
         put(own_ref[peer, :F_ROWS], peer, core)
-        put(other_ref[peer], peer, 1 - core)
+        put(other_ref[peer, :F_ROWS], peer, 1 - core)
         y, xx = peer // NX, peer % NX
         tail = own_ref[peer, 288:320].astype(f32)
         for g in range(4):
@@ -274,9 +289,13 @@
                 for h in range(2):
                     at = (y * TR + 2 * g + h + 1) * 128 + xx * 32 + side * TC
                     strips[at : at + TC] = value[h * TC : (h + 1) * TC]
-    edge, swap = edge_ref[...].astype(f32), swap_ref[...].astype(f32)
-    strips[0:128] = jnp.where(core == 0, edge, swap).astype(bf16)
-    strips[(ROWS + 1) * 128 :] = jnp.where(core == 0, swap, edge).astype(bf16)
+    for xx in range(NX):
+        for side, peer, start in ((0, xx, 0), (1, (NY - 1) * NX + xx, (ROWS + 1) * 128)):
+            tail = own_ref[peer, S_AT:].astype(f32)[8:]
+            main = own_ref[peer, H_AT:S_AT].astype(f32)
+            value = [cot_rows(main[8 * g : 8 * g + 8], tail, g, side) for g in range(4)]
+            at = start + xx * 32
+            strips[at : at + 32] = jnp.concatenate(value, axis=0).astype(bf16)
     lane = lax.broadcasted_iota(jnp.int32, (NQ, 128), 1)
     for row in range(ROWS + 2):
         at = slice(row * 128, (row + 1) * 128)
@@ -298,19 +317,31 @@
         out_ref[z, 48:64] = rest[z].astype(bf16)
 
 
-def join_kernel(sums_ref, out_ref):
+def join_kernel(sums_ref, terms_ref, out_ref):
     value = sums_ref[0]
     for p in range(1, 2 * PEERS):
         value = value + sums_ref[p]
+    high, middle, low = three(value)
+    block = jnp.concatenate(
+        [jnp.concatenate([high, middle], axis=1), jnp.concatenate([low, jnp.zeros_like(low)], axis=1)], axis=0
+    ).astype(bf16)
     for z in range(NZ):
-        out_ref[z] = value
-
-
-def final_kernel(sums_ref, got_ref, feat_ref, da_ref, row_ref, gain_ref,
+        out_ref[z, :W_ROWS] = terms_ref[z]
+        out_ref[z, W_ROWS:] = block
+
+
+def final_kernel(core_ref, got_ref, other_ref, feat_ref, da_ref, row_ref, gain_ref,
                  grad_ref, weight_ref, gain_grad_ref, shift_grad_ref, bias_ref):
-    total = sums_ref[0]
-    for z in range(1, NZ):
-        total = total + sums_ref[z]
+    def half(ref):
+        total = jnp.zeros((8, 128), f32)
+        for z in range(NZ):
+            part = ref[z, W_ROWS:].astype(f32)
+            total = total + (part[:8, :128] + part[:8, 128:] + part[8:, :128])
+        return total
+
+    own, other = half(got_ref), half(other_ref)
+    lower = core_ref[0] == 0
+    total = jnp.concatenate([jnp.where(lower, own, other), jnp.where(lower, other, own)], axis=0)
     sums = [jnp.concatenate([total[5 * s + t : 5 * s + t + 1] for t in range(5)], axis=1) for s in range(3)]
     shift_grad_ref[...], gain_grad_ref[...], bias_ref[...] = [value.reshape(C) for value in sums]
     groups = group_matrix()
@@ -321,9 +352,9 @@
     first, second = both[0:1], both[1:2]
     xhat = (feat_ref[...].astype(f32) - mean) * rstd
     grad_ref[...] = (rstd * (da_ref[...] * gain - first - xhat * second)).astype(bf16)
-    weight = got_ref[0].astype(f32)
+    weight = got_ref[0, :W_ROWS].astype(f32)
     for z in range(1, NZ):
-        weight = weight + got_ref[z].astype(f32)
+        weight = weight + got_ref[z, :W_ROWS].astype(f32)
     for i in range(3):
         for j in range(3):
             at = slice(j * NQ, (j + 1) * NQ)
@@ -356,28 +387,51 @@
     mine = lax.ppermute(edge, ("z", "y", "core"), ways)
     theirs = flip(mine)
 
-    packed, bias = pl.pallas_call(
+    stats, bias = pl.pallas_call(
+        stats_kernel,
+        out_shape=(shape((NZ, 8, 128), f32), shape((8, C), f32)),
+        in_specs=[pl.BlockSpec(memory_space=pltpu.HBM)] * 2 + [vmem()],
+        out_specs=(vmem(), vmem()),
+        scratch_shapes=[pltpu.VMEM((PIX, C), bf16)] * 2 + [pltpu.SemaphoreType.DMA((2,))],
+        compiler_params=params(),
+        name="stats",
+    )(feat, cot, feat2)
+    stats, mine = lax.optimization_barrier((stats, mine))
+    stats = lax.all_to_all(stats, "z", 0, 0)
+    packed, rest = pl.pallas_call(
         pack_kernel,
         grid=(1,),
-        out_shape=(shape((PEERS, G_ROWS, 128), bf16), shape((8, C), f32)),
-        in_specs=[smem()] + [whole(PIX, C)] * 4,
+        out_shape=(shape((PEERS, G_ROWS, 128), bf16), shape((NX, 8, 128), f32)),
+        in_specs=[smem()] + [whole(PIX, C)] * 3 + [vmem()] * 2,
         out_specs=(vmem(), vmem()),
         compiler_params=params(),
         name="pack",
-    )(at_core, feat, cot, feat2, cot2)
-    packed, mine = lax.optimization_barrier((packed, mine))
-    slab = lax.all_to_all(packed, ("y", "x"), 0, 0)
-
+    )(at_core, feat, cot, cot2, mine, theirs)
     top = jnp.where(core == 0, mine[0], theirs[2 * TC - 1])
     bottom = jnp.where(core == 0, theirs[0], mine[2 * TC - 1])
     column = jnp.where(core == 0, cotangent[:, 0], cotangent[:, TC - 1])
     column = jnp.concatenate([top[None], column, bottom[None]])
     pairs = [(2 * k + 1, 2 * k + 2) for k in range(NX - 1)]
     outer = lax.ppermute(column, ("x", "core"), pairs + [(b, a) for a, b in pairs])
+    packed, outer = lax.optimization_barrier((packed, outer))
+    packed = pl.pallas_call(
+        patch_kernel,
+        out_shape=shape((PEERS, G_ROWS, 128), bf16),
+        in_specs=[vmem(), vmem(), pl.BlockSpec(memory_space=pl.ANY)],
+        out_specs=pl.BlockSpec(memory_space=pl.ANY),
+        scratch_shapes=[pltpu.VMEM((PEERS, S_ROWS, 128), bf16), pltpu.SemaphoreType.DMA],
+        input_output_aliases={2: 0},
+        compiler_params=params(),
+        name="patch",
+    )(stats, rest, packed)
+    slab = lax.all_to_all(packed, ("y", "x"), 0, 0)
+    slab_other = flip(slab)
+
     back = pl.pallas_call(
         back_kernel,
+        grid=(1,),
         out_shape=shape((PIX, C), f32),
-        in_specs=[smem()] + [vmem()] * 5 + [pl.BlockSpec(memory_space=pl.ANY)],
+        in_specs=[smem()] + [whole(PIX, C)] * 2 + [vmem()] * 3 + [pl.BlockSpec(memory_space=pl.ANY)],
         out_specs=vmem(),
         scratch_shapes=[
             pltpu.VMEM((3, (TR + 2) * TC, C), bf16),
@@ -390,44 +444,22 @@
     )(at_core, cot, cot2, mine, theirs, outer, conv_weight)
     slab, back = lax.optimization_barrier((slab, back))
 
-    stats = pl.pallas_call(
-        stats_kernel,
-        grid=(1,),
-        out_shape=shape((NZ, 8, 128), f32),
-        in_specs=[pl.BlockSpec((PEERS, S_ROWS, 128), lambda t: (0, (F_ROWS + C_ROWS) // S_ROWS, 0))],
-        out_specs=vmem(),
-        compiler_params=params(),
-        name="stats",
-    )(slab)
-    stats = lax.all_to_all(stats, "z", 0, 0)
-    slab_feat, keep, give = pl.pallas_call(
-        split_kernel,
-        out_shape=(shape((PEERS, F_ROWS, 128), bf16), shape((128, 128), bf16), shape((128, 128), bf16)),
-        in_specs=[smem(), vmem()],
-        out_specs=(vmem(), vmem(), vmem()),
-        compiler_params=params(),
-        name="split",
-    )(at_core, slab)
-    slab_other = flip(slab_feat)
-    ways = [(2 * k, 2 * k + 2) for k in range(NZ - 1)] + [(2 * k + 3, 2 * k + 1) for k in range(NZ - 1)]
-    strip = lax.ppermute(jnp.stack([keep, flip(give)]), ("z", "core"), ways)
-    edge, swap = strip[0], flip(strip[1])
-
     row, da, table, sums = pl.pallas_call(
         sums_kernel,
-        out_shape=(shape((8, C), f32), shape((PIX, C), f32), shape((8, 256), f32), shape((2 * PEERS, 16, 128), f32)),
-        in_specs=[smem()] + [vmem()] * 6,
+        grid=(1,),
+        out_shape=(shape((8, C), f32), shape((PIX, C), f32), shape((8, 256), f32), shape((2 * PEERS, 8, 128), f32)),
+        in_specs=[smem(), vmem(), whole(PIX, C), vmem(), whole(1, C), whole(1, C), vmem()],
         out_specs=(vmem(), vmem(), vmem(), vmem()),
         scratch_shapes=[pltpu.VMEM((16, 128), f32)],
         compiler_params=params(),
         name="sums",
-    )(at_y, stats, feat, back, gain, shift, bias)
+    )(at_y, slab, feat, back, gain, shift, bias)
     sums = lax.all_to_all(sums, ("y", "x", "core"), 0, 0)
 
     terms = pl.pallas_call(
         terms_kernel,
         out_shape=shape((NZ, W_ROWS, 256), bf16),
-        in_specs=[smem()] + [vmem()] * 5,
+        in_specs=[smem()] + [vmem()] * 3,
         out_specs=vmem(),
         scratch_shapes=[
             pltpu.VMEM((ROWS * 128, 256), bf16),
@@ -440,26 +472,26 @@
             flops=2 * PIX * 9 * C * C, bytes_accessed=4 << 20, transcendentals=ROWS * 128 * 256
         ),
         name="terms",
-    )(at_core, slab, slab_other, edge, swap, table)
-
-    terms = lax.all_to_all(terms, "z", 0, 0)
-    sums = pl.pallas_call(
+    )(at_core, slab, slab_other, table)
+
+    joined = pl.pallas_call(
         join_kernel,
-        out_shape=shape((NZ, 16, 128), f32),
-        in_specs=[vmem()],
+        out_shape=shape((NZ, W_ROWS + V_ROWS, 256), bf16),
+        in_specs=[vmem()] * 2,
         out_specs=vmem(),
         compiler_params=params(),
         name="join",
-    )(sums)
-    sums = lax.all_to_all(sums, "z", 0, 0)
+    )(sums, terms)
+    joined = lax.all_to_all(joined, "z", 0, 0)
     grad, weight_grad, gain_grad, shift_grad, bias_grad = pl.pallas_call(
         final_kernel,
+        grid=(1,),
         out_shape=(shape((PIX, C), bf16), shape((3, 3, 20, NQ), f32)) + (shape((C,), f32),) * 3,
-        in_specs=[vmem()] * 6,
+        in_specs=[smem(), vmem(), vmem(), whole(PIX, C), vmem(), vmem(), whole(1, C)],
         out_specs=(vmem(),) * 5,
         compiler_params=params(),
         name="final",
-    )(sums, terms, feat, da, row, gain)
+    )(at_core, joined, flip(joined), feat, da, row, gain)
     return grad.reshape(features.shape), weight_grad, gain_grad, shift_grad, bias_grad
 
 

time: 103 us -> 101 us (0.981)
  blocking collectives: 12.7 us -> 43.1 us
  waiting for transfers between devices: 30.4 us -> 8.15 us
  starting transfers between devices: 39.1 us -> 27.2 us
  local copies, waits for them, and re-layouts: 2.65 us -> 5.4 us
    all_to_all x1 -> x2, blocking collectives: 12.7 us -> 43.1 us  [the longest x1 24.7 us: body(): slab = lax.all_to_all(packed, ('y', 'x'), 0, 0)]
    ppermute x1, waiting for transfers between devices: 11.4 us -> 0.01 us  [body(): lax.ppermute(column, ('x', 'core'), pairs + [(b, a) for a, b in pairs])]
    all_to_all x2 -> x0, starting transfers between devices: 9.8 us -> none  [the longest x1 6.27 us: body(): slab = lax.all_to_all(packed, ('y', 'x'), 0, 0)]
    all_to_all x1, waiting for transfers between devices: 8.55 us -> 2.95 us  [body(): sums = lax.all_to_all(sums, ('y', 'x', 'core'), 0, 0)]
    all_to_all x1, starting transfers between devices: 8.83 us -> 3.65 us  [body(): sums = lax.all_to_all(sums, ('y', 'x', 'core'), 0, 0)]
    all_to_all x1, waiting for transfers between devices: 5.51 us -> 0.7 us  [body(): stats = lax.all_to_all(stats, 'z', 0, 0)]
    all_to_all x2 -> x0, waiting for transfers between devices: 3.63 us -> none  [the longest x1 3.62 us: body(): sums = lax.all_to_all(sums, 'z', 0, 0)]
    all_to_all x1, starting transfers between devices: 8.19 us -> 11.2 us  [body(): stats = lax.all_to_all(stats, 'z', 0, 0)]
  transfers between devices with their start and end apart: 13 -> 9, of which waited for: 6 -> 5; matrix products, arithmetic and copies ran while one was open for 1% -> 2% of each run, Pallas kernels for 14% -> 14%
where the time goes in v4:
time: 101 us; the launch traced here: 100 us
  blocking collectives  43.1 us (43%)
  starting transfers between devices  27.2 us (27%)
  Pallas kernels  15.4 us (15%)
  waiting for transfers between devices  8.15 us (8%)
  local copies, waits for them, and re-layouts  5.4 us (5%)
    all_to_all x1, blocking collectives, body(): slab = lax.all_to_all(packed, ('y', 'x'), 0, 0)  24.7 us
    all_to_all x1, blocking collectives, body(): joined = lax.all_to_all(joined, 'z', 0, 0)  18.4 us
    all_to_all x1, starting transfers between devices, body(): stats = lax.all_to_all(stats, 'z', 0, 0)  11.2 us
    ppermute x5, starting transfers between devices, flip(): return lax.ppermute(value, 'core', [(0, 1), (1, 0)])  7.84 us
    pallas_call x1, Pallas kernels, body(): pl.pallas_call(back_kernel, grid=(1,), out_shape=shape((PIX, C), f32), in...  5.71 us
    pallas_call x1, Pallas kernels, body(): pl.pallas_call(terms_kernel, out_shape=shape((NZ, W_ROWS, 256), bf16), in...  4.65 us
    unnamed x16, local copies, waits for them, and re-layouts  3.68 us
    all_to_all x1, starting transfers between devices, body(): sums = lax.all_to_all(sums, ('y', 'x', 'core'), 0, 0)  3.65 us
  transfers between devices with their start and end apart: 9, of which 5 were waited for; matrix products, arithmetic and copies ran while one was open for 2% of the time, Pallas kernels for 14%

profile of v4, /device:TPU:1, one launch (start us, length us, event | category | flops | bytes accessed | tf_op | source)
XLA Modules:
  0.0 100.2 jit_solution(1366459497841098411)
XLA Ops:
  0.6 3.3 %collective-permute-start = (bf16[128,640]{1,0:T(8,128)(2,1)}, bf16[128,640]{1,0:T(8,128)(2,1)S(1)}, u32[]{:S(2)}, u32[]{:S(2)}) collective-permute-start(bf16[128,640]{1,0:T(8,128)(2,1)} %bitcast.11), channel_id=1, source_target_pairs={{0,1},{1,0},{2,3},{3,2},{4,5},{5,4},{6,7},{7,6},{8,9},{9,8},{10,11... | collective-permute-start | bytes 491528 | tf_op jit(solution)/shard_map/ppermute | solution.py:366
  4.0 0.1 collective-permute-start.1
  4.1 0.7 slice_bitcast_fusion
  4.8 0.8 collective-permute-done.1.cot2_ref
  5.6 1.3 %collective-permute-start.2 = (bf16[32,640]{1,0:T(8,128)(2,1)S(1)}, bf16[32,640]{1,0:T(8,128)(2,1)S(1)}, u32[]{:S(2)}, u32[]{:S(2)}) collective-permute-start(bf16[32,640]{1,0:T(8,128)(2,1)S(1)} %maximum_select_fusion), channel_id=1, source_target_pairs={{0,8},{8,16},{16,24},{24,32},{32,40},{40,48},{48,56},{56,64},{64,7... | collective-permute-start | bytes 122888 | tf_op jit(solution)/shard_map/ppermute | solution.py:387
  6.9 1.0 fusion.1
  7.9 2.5 %collective-permute-done.2.mine_ref = bf16[32,640]{1,0:T(8,128)(2,1)S(1)} collective-permute-done((bf16[32,640]{1,0:T(8,128)(2,1)S(1)}, bf16[32,640]{1,0:T(8,128)(2,1)S(1)}, u32[]{:S(2)}, u32[]{:S(2)}) %collective-permute-start.2) | collective-permute-done | bytes 40992 | tf_op jit(solution)/shard_map/ppermute | solution.py:387
  10.3 0.0 collective-permute-start.3
  10.3 0.0 collective-permute-done.feat2_ref
  10.4 0.0 copy-start
  10.4 0.9 copy-done
  11.3 0.0 copy-start.3
  11.3 0.9 copy-done.3
  12.2 1.7 %stats.1 = (f32[8,8,128]{2,1,0:T(8,128)}, f32[8,640]{1,0:T(8,128)S(1)}) custom-call(bf16[128,640]{1,0:T(8,128)(2,1)S(1)} %bitcast.12, bf16[128,640]{1,0:T(8,128)(2,1)S(1)} %bitcast.17, bf16[128,640]{1,0:T(8,128)(2,1)S(1)} %collective-permute-done.feat2_ref), custom_call_target="tpu_custom_call" | custom-call | tf_op jit(solution)/shard_map/stats/pallas_call | solution.py:390
  13.9 11.2 %all-to-all-start = ((f32[8,8,128]{2,1,0:T(8,128)}), f32[8,8,128]{2,1,0:T(8,128)S(1)}, u32[]{:S(2)}, u32[]{:S(2)}) async-start(f32[8,8,128]{2,1,0:T(8,128)} %get-tuple-element.25), calls=%async_computation | async-start | bytes 65536 | tf_op jit(solution)/shard_map/all_to_all | solution.py:400
  25.1 0.0 collective-permute-done.3.theirs_ref
  25.2 3.3 %collective-permute-start.4 = (bf16[10,640]{1,0:T(8,128)(2,1)S(1)}, bf16[10,640]{1,0:T(8,128)(2,1)S(1)}, u32[]{:S(2)}, u32[]{:S(2)}) collective-permute-start(bf16[10,640]{1,0:T(8,128)(2,1)S(1)} %pad_maximum_fusion), channel_id=1, source_target_pairs={{1,2},{3,4},{5,6},{2,1},{4,3},{6,5},{9,10},{11,12},{13,14},{10,9},... | collective-permute-start | bytes 38408 | tf_op jit(solution)/shard_map/ppermute | solution.py:415
  28.5 0.0 copy-start.1
  28.5 0.9 copy-done.1
  29.4 0.0 copy-start.4
  29.4 0.9 copy-done.4
  30.3 1.0 pack.1
  31.3 0.0 collective-permute-done.4.outer_ref
  31.3 0.7 all-to-all-done.stat_ref
  32.0 0.1 patch.1
  32.0 0.0 copy-start.6
  32.1 0.0 copy-start.7
  32.1 0.0 copy-start.5
  32.1 24.7 %all_to_all.20.slab_ref.own_ref = bf16[16,368,128]{2,1,0:T(8,128)(2,1)S(1)} all-to-all(bf16[16,368,128]{2,1,0:T(8,128)(2,1)S(1)} %patch.1), channel_id=1, replica_groups=mesh['z'=8,'y'=4,'x'=4,'core'=2] {'y','x'}, dimensions={0} | all-to-all | bytes 3014656 | tf_op jit(solution)/shard_map/all_to_all | solution.py:427
  56.8 2.9 %collective-permute-start.5 = (bf16[16,368,128]{2,1,0:T(8,128)(2,1)S(1)}, bf16[16,368,128]{2,1,0:T(8,128)(2,1)}, u32[]{:S(2)}, u32[]{:S(2)}) collective-permute-start(bf16[16,368,128]{2,1,0:T(8,128)(2,1)S(1)} %all_to_all.20.slab_ref.own_ref), channel_id=1, source_target_pairs={{0,1},{1,0},{2,3},{3,2},{4,5},{5,4},{6,7},{7,6},{8,9},{9,8},{10,11... | collective-permute-start | bytes 4521992 | tf_op jit(solution)/shard_map/ppermute | solution.py:366
  59.7 0.0 copy-done.6
  59.7 0.0 copy-done.7
  59.7 0.0 copy-done.5
  59.7 0.0 copy-start.2
  59.7 5.7 %back.1.back_ref = f32[128,640]{1,0:T(8,128)S(1)} custom-call(s32[1]{0:T(128)} %bitcast.core_ref, bf16[128,640]{1,0:T(8,128)(2,1)S(1)} %bitcast.19, bf16[128,640]{1,0:T(8,128)(2,1)S(1)} %collective-permute-done.1.cot2_ref, bf16[32,640]{1,0:T(8,128)(2,1)S(1)} %collective-permute-done.2.mine_ref, bf16[32,640]{1,0:T(8,128)(2,1)S(1)} %collective-permute-done.3.theirs_ref, ...), custom_call_target="tpu_custom_call" | custom-call | flops 943718400 | bytes 7372800 | tf_op jit(solution)/shard_map/back/pallas_call | solution.py:430
  65.5 0.0 copy-done.2
  65.5 1.1 %sums.1 = (f32[8,640]{1,0:T(8,128)S(1)}, f32[128,640]{1,0:T(8,128)S(1)}, f32[8,256]{1,0:T(8,128)S(1)}, f32[32,8,128]{2,1,0:T(8,128)}) custom-call(s32[1]{0:T(128)} %bitcast.1.y_ref, bf16[16,368,128]{2,1,0:T(8,128)(2,1)S(1)} %all_to_all.20.slab_ref.own_ref, bf16[128,640]{1,0:T(8,128)(2,1)S(1)} %bitcast.14, f32[128,640]{1,0:T(8,128)S(1)} %back.1.back_ref, ...), custom_call_target="tpu_custom_call" | custom-call | tf_op jit(solution)/shard_map/sums/pallas_call | solution.py:447
  66.5 3.6 %all-to-all-start.2 = ((f32[32,8,128]{2,1,0:T(8,128)}), f32[32,8,128]{2,1,0:T(8,128)S(1)}, u32[]{:S(2)}, u32[]{:S(2)}) async-start(f32[32,8,128]{2,1,0:T(8,128)} %get-tuple-element.34), calls=%async_computation.2 | async-start | bytes 262144 | tf_op jit(solution)/shard_map/all_to_all | solution.py:457
  70.2 0.0 collective-permute-done.5.other_ref
  70.2 4.7 %terms.1.terms_ref = bf16[8,64,256]{2,1,0:T(8,128)(2,1)S(1)} custom-call(s32[1]{0:T(128)} %bitcast.core_ref, bf16[16,368,128]{2,1,0:T(8,128)(2,1)S(1)} %all_to_all.20.slab_ref.own_ref, bf16[16,368,128]{2,1,0:T(8,128)(2,1)} %collective-permute-done.5.other_ref, f32[8,256]{1,0:T(8,128)S(1)} %get-tuple-element.35.par_ref), custom_call_target="tpu_custom_call" | custom-call | flops 943718400 | bytes 4194304 | tf_op jit(solution)/shard_map/terms/pallas_call | solution.py:459
  74.9 3.0 %all-to-all-done.2.sums_ref = f32[32,8,128]{2,1,0:T(8,128)S(1)} async-done(((f32[32,8,128]{2,1,0:T(8,128)}), f32[32,8,128]{2,1,0:T(8,128)S(1)}, u32[]{:S(2)}, u32[]{:S(2)}) %all-to-all-start.2) | async-done | bytes 131104 | tf_op jit(solution)/shard_map/all_to_all | solution.py:457
  77.9 18.4 %all_to_all.21.got_ref = bf16[8,80,256]{2,1,0:T(8,128)(2,1)S(1)} all-to-all(bf16[8,80,256]{2,1,0:T(8,128)(2,1)S(1)} %join.1), channel_id=1, replica_groups=mesh['z'=8,'y'=4,'x'=4,'core'=2] {'z'}, dimensions={0} | all-to-all | bytes 655360 | tf_op jit(solution)/shard_map/all_to_all | solution.py:485
  96.3 1.5 %collective-permute-start.6 = (bf16[8,80,256]{2,1,0:T(8,128)(2,1)S(1)}, bf16[8,80,256]{2,1,0:T(8,128)(2,1)S(1)}, u32[]{:S(2)}, u32[]{:S(2)}) collective-permute-start(bf16[8,80,256]{2,1,0:T(8,128)(2,1)S(1)} %all_to_all.21.got_ref), channel_id=1, source_target_pairs={{0,1},{1,0},{2,3},{3,2},{4,5},{5,4},{6,7},{7,6},{8,9},{9,8},{10,11... | collective-permute-start | bytes 983048 | tf_op jit(solution)/shard_map/ppermute | solution.py:366
  97.8 1.3 %collective-permute-done.6.other_ref = bf16[8,80,256]{2,1,0:T(8,128)(2,1)S(1)} collective-permute-done((bf16[8,80,256]{2,1,0:T(8,128)(2,1)S(1)}, bf16[8,80,256]{2,1,0:T(8,128)(2,1)S(1)}, u32[]{:S(2)}, u32[]{:S(2)}) %collective-permute-start.6) | collective-permute-done | bytes 327712 | tf_op jit(solution)/shard_map/ppermute | solution.py:366
  99.1 1.1 %final.1 = (bf16[128,640]{1,0:T(8,128)(2,1)}, f32[3,3,20,80]{3,2,1,0:T(8,128)}, f32[640]{0:T(1024)}, f32[640]{0:T(1024)}, f32[640]{0:T(1024)}) custom-call(s32[1]{0:T(128)} %bitcast.core_ref, bf16[8,80,256]{2,1,0:T(8,128)(2,1)S(1)} %all_to_all.21.got_ref, bf16[8,80,256]{2,1,0:T(8,128)(2,1)S(1)} %collective-permute-done.6.other_ref, ...), custom_call_target="tpu_custom_call" | custom-call | tf_op jit(solution)/shard_map/final/pallas_call | solution.py:486
  (8 shorter events, 0.1 us)
Async XLA Ops:
  0.6 9.7 %collective-permute-start = (bf16[128,640]{1,0:T(8,128)(2,1)}, bf16[128,640]{1,0:T(8,128)(2,1)S(1)}, u32[]{:S(2)}, u32[]{:S(2)}) collective-permute-start(bf16[128,640]{1,0:T(8,128)(2,1)} %bitcast.11), channel_id=1, source_target_pairs={{0,1},{1,0},{2,3},{3,2},{4,5},{5,4},{6,7},{7,6},{8,9},{9,8},{10,11... | collective-permute-start | bytes 491528 | tf_op jit(solution)/shard_map/ppermute | solution.py:366
  4.0 1.6 %collective-permute-start.1 = (bf16[128,640]{1,0:T(8,128)(2,1)}, bf16[128,640]{1,0:T(8,128)(2,1)S(1)}, u32[]{:S(2)}, u32[]{:S(2)}) collective-permute-start(bf16[128,640]{1,0:T(8,128)(2,1)} %bitcast.16), channel_id=1, source_target_pairs={{0,1},{1,0},{2,3},{3,2},{4,5},{5,4},{6,7},{7,6},{8,9},{9,8},{10,11... | collective-permute-start | bytes 491528 | tf_op jit(solution)/shard_map/ppermute | solution.py:366
  5.6 4.7 %collective-permute-start.2 = (bf16[32,640]{1,0:T(8,128)(2,1)S(1)}, bf16[32,640]{1,0:T(8,128)(2,1)S(1)}, u32[]{:S(2)}, u32[]{:S(2)}) collective-permute-start(bf16[32,640]{1,0:T(8,128)(2,1)S(1)} %maximum_select_fusion), channel_id=1, source_target_pairs={{0,8},{8,16},{16,24},{24,32},{32,40},{40,48},{48,56},{56,64},{64,7... | collective-permute-start | bytes 122888 | tf_op jit(solution)/shard_map/ppermute | solution.py:387
  10.3 14.8 %collective-permute-start.3 = (bf16[32,640]{1,0:T(8,128)(2,1)S(1)}, bf16[32,640]{1,0:T(8,128)(2,1)S(1)}, u32[]{:S(2)}, u32[]{:S(2)}) collective-permute-start(bf16[32,640]{1,0:T(8,128)(2,1)S(1)} %collective-permute-done.2.mine_ref), channel_id=1, source_target_pairs={{0,1},{1,0},{2,3},{3,2},{4,5},{5,4},{6,7},{7,6},{8,9},{9,8},{10,11... | collective-permute-start | bytes 122888 | tf_op jit(solution)/shard_map/ppermute | solution.py:366
  10.4 0.9 copy-start
  11.3 0.9 copy-start.3
  13.9 18.0 %all-to-all-start = ((f32[8,8,128]{2,1,0:T(8,128)}), f32[8,8,128]{2,1,0:T(8,128)S(1)}, u32[]{:S(2)}, u32[]{:S(2)}) async-start(f32[8,8,128]{2,1,0:T(8,128)} %get-tuple-element.25), calls=%async_computation | async-start | bytes 65536 | tf_op jit(solution)/shard_map/all_to_all | solution.py:400
  25.2 6.1 %collective-permute-start.4 = (bf16[10,640]{1,0:T(8,128)(2,1)S(1)}, bf16[10,640]{1,0:T(8,128)(2,1)S(1)}, u32[]{:S(2)}, u32[]{:S(2)}) collective-permute-start(bf16[10,640]{1,0:T(8,128)(2,1)S(1)} %pad_maximum_fusion), channel_id=1, source_target_pairs={{1,2},{3,4},{5,6},{2,1},{4,3},{6,5},{9,10},{11,12},{13,14},{10,9},... | collective-permute-start | bytes 38408 | tf_op jit(solution)/shard_map/ppermute | solution.py:415
  28.5 0.9 copy-start.1
  29.4 0.9 copy-start.4
  32.0 27.7 %copy-start.6 = (f32[640]{0:T(1024)S(1)}, f32[640]{0:T(1024)}, u32[]{:S(2)}) copy-start(f32[640]{0:T(1024)} %param.8) | copy-start | bytes 7684
  32.1 27.6 %copy-start.7 = (f32[640]{0:T(1024)S(1)}, f32[640]{0:T(1024)}, u32[]{:S(2)}) copy-start(f32[640]{0:T(1024)} %param.9) | copy-start | bytes 7684
  32.1 27.6 %copy-start.5 = (bf16[8,16,640]{2,1,0:T(8,128)(2,1)S(1)}, bf16[8,16,640]{2,1,0:T(8,128)(2,1)}, u32[]{:S(2)}) copy-start(bf16[8,16,640]{2,1,0:T(8,128)(2,1)} %param.6) | copy-start | bytes 491524
  56.8 13.4 %collective-permute-start.5 = (bf16[16,368,128]{2,1,0:T(8,128)(2,1)S(1)}, bf16[16,368,128]{2,1,0:T(8,128)(2,1)}, u32[]{:S(2)}, u32[]{:S(2)}) collective-permute-start(bf16[16,368,128]{2,1,0:T(8,128)(2,1)S(1)} %all_to_all.20.slab_ref.own_ref), channel_id=1, source_target_pairs={{0,1},{1,0},{2,3},{3,2},{4,5},{5,4},{6,7},{7,6},{8,9},{9,8},{10,11... | collective-permute-start | bytes 4521992 | tf_op jit(solution)/shard_map/ppermute | solution.py:366
  59.7 5.7 %copy-start.2 = (bf16[8,16,640]{2,1,0:T(8,128)(2,1)S(1)}, bf16[8,16,640]{2,1,0:T(8,128)(2,1)}, u32[]{:S(2)}) copy-start(bf16[8,16,640]{2,1,0:T(8,128)(2,1)} %param.5) | copy-start | bytes 491524
  66.5 11.3 %all-to-all-start.2 = ((f32[32,8,128]{2,1,0:T(8,128)}), f32[32,8,128]{2,1,0:T(8,128)S(1)}, u32[]{:S(2)}, u32[]{:S(2)}) async-start(f32[32,8,128]{2,1,0:T(8,128)} %get-tuple-element.34), calls=%async_computation.2 | async-start | bytes 262144 | tf_op jit(solution)/shard_map/all_to_all | solution.py:457
  96.3 2.8 %collective-permute-start.6 = (bf16[8,80,256]{2,1,0:T(8,128)(2,1)S(1)}, bf16[8,80,256]{2,1,0:T(8,128)(2,1)S(1)}, u32[]{:S(2)}, u32[]{:S(2)}) collective-permute-start(bf16[8,80,256]{2,1,0:T(8,128)(2,1)S(1)} %all_to_all.21.got_ref), channel_id=1, source_target_pairs={{0,1},{1,0},{2,3},{3,2},{4,5},{5,4},{6,7},{7,6},{8,9},{9,8},{10,11... | collective-permute-start | bytes 983048 | tf_op jit(solution)/shard_map/ppermute | solution.py:366

commit v5 on v4

--- a/solution.py
+++ b/solution.py
@@ -17,10 +17,10 @@
 CHIP = float(2 * PIX * GW)
 TOTAL = float(NZ * PEERS) * CHIP
 VMEM_LIMIT = 48 * 1024 * 1024
-F_ROWS, C_ROWS, H_ROWS, S_ROWS = 160, 160, 32, 16
-H_AT = F_ROWS + C_ROWS
-S_AT = H_AT + H_ROWS
+F_ROWS, C_ROWS, S_ROWS = 160, 160, 16
+S_AT = F_ROWS + C_ROWS
 G_ROWS = S_AT + S_ROWS
+E_ROWS = 96
 W_ROWS, V_ROWS = 64, 16
 f32, bf16 = jnp.float32, jnp.bfloat16
 
@@ -65,12 +65,19 @@
     return pl.BlockSpec(memory_space=pltpu.SMEM)
 
 
+def hbm():
+    return pl.BlockSpec(memory_space=pltpu.HBM)
+
+
+def fetch(pairs, sem):
+    copies = [pltpu.make_async_copy(src, dst, sem.at[k]) for k, (src, dst) in enumerate(pairs)]
+    for copy in copies:
+        copy.start()
+    return copies
+
+
 def params(**kw):
     return pltpu.CompilerParams(vmem_limit_bytes=VMEM_LIMIT, **kw)
-
-
-def whole(*dims):
-    return pl.BlockSpec(dims, lambda t: (0,) * len(dims))
 
 
 def group_matrix():
@@ -114,58 +121,55 @@
     return out
 
 
-def stats_kernel(feat_hbm, cot_hbm, feat2_ref, out_ref, bias_ref, feat_ref, cot_ref, sem):
-    copies = [
-        pltpu.make_async_copy(feat_hbm, feat_ref, sem.at[0]),
-        pltpu.make_async_copy(cot_hbm, cot_ref, sem.at[1]),
-    ]
-    for copy in copies:
-        copy.start()
+def put_pieces(mean, squares):
+    pieces = three(mean) + three(squares)
+    row = lax.broadcasted_iota(jnp.int32, (S_ROWS, 128), 0)
+    out = jnp.zeros((S_ROWS, 128), f32)
+    for k in range(6):
+        out = jnp.where(row == k, pieces[k], out)
+    return out.astype(bf16)
+
+
+def merge_pieces(got, count):
+    got = got.astype(f32)
+    return merge(got[:, 0] + got[:, 1] + got[:, 2], got[:, 3] + got[:, 4] + got[:, 5], count)
+
+
+def in_order(core, own, other):
+    a, b = own[...].astype(f32), other[...].astype(f32)
+    return jnp.where(core == 0, a, b).astype(bf16), jnp.where(core == 0, b, a).astype(bf16)
+
+
+def blocks(core, first, second):
+    return jnp.dot(first, pick(cotangent_columns(core, 0)), preferred_element_type=f32) + jnp.dot(
+        second, pick(cotangent_columns(core, 1)), preferred_element_type=f32
+    )
+
+
+def pack_kernel(core_ref, both_ref, feat2_ref, cot2_ref, out_ref, bias_ref):
+    core = core_ref[0]
+    feat_ref, cot_ref = both_ref.at[:PIX], both_ref.at[PIX:]
+    x, x2 = feat_ref[...].astype(f32), feat2_ref[...].astype(f32)
     groups = group_matrix()
-    for copy in copies:
-        copy.wait()
-    x, x2 = feat_ref[...].astype(f32), feat2_ref[...].astype(f32)
     total = x.sum(0, keepdims=True) + x2.sum(0, keepdims=True)
     mean = exact_dot(rows8(total), groups, 0) / CHIP
     wide = exact_dot(mean, groups, 1)[:1]
     squares = ((x - wide) ** 2).sum(0, keepdims=True) + ((x2 - wide) ** 2).sum(0, keepdims=True)
-    squares = exact_dot(rows8(squares), groups, 0)
-    row = lax.broadcasted_iota(jnp.int32, (8, 128), 0)
-    block = jnp.where(row == 0, mean, jnp.where(row == 1, squares, 0.0))
-    for z in range(NZ):
-        out_ref[z] = block
+    stats = put_pieces(mean[:1], exact_dot(rows8(squares), groups, 0)[:1])
     bias_ref[...] = rows8(cot_ref[...].astype(f32).sum(0, keepdims=True))
-
-
-def pack_kernel(core_ref, feat_ref, cot_ref, cot2_ref, mine_ref, theirs_ref, out_ref, rest_ref):
-    core = core_ref[0]
-    lower = core == 0
-
-    def pair(own, other):
-        a, b = own[...].astype(f32), other[...].astype(f32)
-        return jnp.where(lower, a, b).astype(bf16), jnp.where(lower, b, a).astype(bf16)
-
-    first, second = pair(cot_ref, cot2_ref)
-    top, bottom = pair(mine_ref, theirs_ref)
+    first, second = in_order(core, cot_ref, cot2_ref)
     moved = jnp.dot(feat_ref[...], pick(feature_columns()), preferred_element_type=f32)
-    terms = jnp.dot(
-        jnp.concatenate([first, top], axis=0), pick(cotangent_columns(core, 0)), preferred_element_type=f32
-    ) + jnp.dot(
-        jnp.concatenate([second, bottom], axis=0), pick(cotangent_columns(core, 1)), preferred_element_type=f32
-    )
+    terms = blocks(core, first, second)
     moved_rest = lanes32(moved[:, 512:], 32)
-    terms_rest = lanes32(terms[:PIX, 512:], 32)
-    halo_rest = lanes32(terms[PIX:, 512:], 8)
-    for xx in range(NX):
-        rest_ref[xx] = halo_rest[xx]
+    terms_rest = lanes32(terms[:, 512:], 32)
     for y in range(NY):
         for xx in range(NX):
             p = y * NX + xx
             out_ref[p, 0:128] = moved[:, y * 128 : (y + 1) * 128].astype(bf16)
             out_ref[p, 128:160] = moved_rest[y].astype(bf16)
-            out_ref[p, 160:288] = terms[:PIX, xx * 128 : (xx + 1) * 128].astype(bf16)
+            out_ref[p, 160:288] = terms[:, xx * 128 : (xx + 1) * 128].astype(bf16)
             out_ref[p, 288:320] = terms_rest[xx].astype(bf16)
-            out_ref[p, H_AT:S_AT] = terms[PIX:, xx * 128 : (xx + 1) * 128].astype(bf16)
+            out_ref[p, S_AT:] = stats
 
 
 def merge(means, squares, count):
@@ -174,42 +178,57 @@
     return mean, squares.sum(0, keepdims=True) + count * ((means - mean) ** 2).sum(0, keepdims=True)
 
 
-def patch_kernel(stat_ref, rest_ref, packed_ref, out_ref, block, sem):
-    got = stat_ref[...]
-    mean, squares = merge(got[:, 0], got[:, 1], CHIP)
-    pieces = three(mean) + three(squares)
-    row = lax.broadcasted_iota(jnp.int32, (8, 128), 0)
-    stats = jnp.zeros((8, 128), f32)
-    for k in range(6):
-        stats = jnp.where(row == k, pieces[k], stats)
-    for p in range(PEERS):
-        block[p] = jnp.concatenate([stats, rest_ref[p % NX]], axis=0).astype(bf16)
-    copy = pltpu.make_async_copy(block, out_ref.at[:, S_AT:, :], sem)
-    copy.start()
-    copy.wait()
-
-
 def cot_rows(main, rest, g, side):
     lane = lax.broadcasted_iota(jnp.int32, main.shape, 1)
     main = pltpu.roll(main, 64, 1) if side else main
     return jnp.where(lane < 64, main, pltpu.roll(rest, (64 - 32 * g - 16 * side) % 128, 1))
 
 
-def back_kernel(core_ref, cot_ref, cot2_ref, mine_ref, theirs_ref, outer_ref, w_hbm, out_ref, shifted, w_ref, sem):
-    copies = [pltpu.make_async_copy(w_hbm.at[t // 3, t % 3], w_ref.at[t], sem.at[t]) for t in range(9)]
-    for copy in copies:
-        copy.start()
+def split_kernel(z_ref, slab_ref, out_ref):
+    mean, squares = merge_pieces(slab_ref[:, S_AT:], CHIP)
+    stats = put_pieces(mean, squares)
+    group = lax.broadcasted_iota(jnp.int32, (TC, 128), 1) // 32
+    first, last = jnp.zeros((TC, 128), f32), jnp.zeros((TC, 128), f32)
+    for xx in range(NX):
+        tail = slab_ref[xx, 288:304].astype(f32)
+        first = jnp.where(group == xx, pltpu.roll(tail, 32 * xx, 1) if xx else tail, first)
+        tail = slab_ref[(NY - 1) * NX + xx, 304:320].astype(f32)
+        last = jnp.where(group == xx, pltpu.roll(tail, (32 * xx + 32) % 128, 1) if xx < 3 else tail, last)
+    first, last = first.astype(bf16), last.astype(bf16)
+    for p in range(NZ):
+        out_ref[p, :S_ROWS] = stats
+
+        @pl.when(z_ref[0] < p)
+        def _():
+            for xx in range(NX):
+                out_ref[p, 16 + 16 * xx : 32 + 16 * xx] = slab_ref[(NY - 1) * NX + xx, 272:288]
+            out_ref[p, 80:] = last
+
+        @pl.when(z_ref[0] >= p)
+        def _():
+            for xx in range(NX):
+                out_ref[p, 16 + 16 * xx : 32 + 16 * xx] = slab_ref[xx, 160:176]
+            out_ref[p, 80:] = first
+
+
+def back_kernel(core_ref, both_ref, cot2_ref, mine_ref, theirs_ref, outer_ref, w_hbm, out_ref, shifted, w_ref, sem):
+    copies = fetch([(w_hbm.at[t // 3, t % 3], w_ref.at[t]) for t in range(9)], sem)
     rows = (TR + 2) * TC
     lower = core_ref[0] == 0
     mine, theirs = mine_ref[...].astype(f32), theirs_ref[...].astype(f32)
     top, bottom = jnp.where(lower, mine, theirs), jnp.where(lower, theirs, mine)
-    own_top, other_top = jnp.where(lower, top[:TC], top[TC:]), jnp.where(lower, top[TC:], top[:TC])
-    own_bot, other_bot = jnp.where(lower, bottom[:TC], bottom[TC:]), jnp.where(lower, bottom[TC:], bottom[:TC])
-    wide = jnp.concatenate([own_top, cot_ref[...].astype(f32), own_bot], axis=0)
+    corner = 2 * TC
+    own_top, other_top = jnp.where(lower, top[:TC], top[TC:corner]), jnp.where(lower, top[TC:corner], top[:TC])
+    own_bot, other_bot = jnp.where(lower, bottom[:TC], bottom[TC:corner]), jnp.where(lower, bottom[TC:corner], bottom[:TC])
+    wide = jnp.concatenate([own_top, both_ref[PIX:].astype(f32), own_bot], axis=0)
     near = jnp.concatenate([other_top, cot2_ref[...].astype(f32), other_bot], axis=0)
     near = near.reshape(TR + 2, TC, C)
     inner = jnp.where(lower, near[:, :1], near[:, TC - 1 :])
-    outer = outer_ref[...].astype(f32)[:, None, :]
+    top_corner = jnp.where(lower, top[corner : corner + 1], top[corner + 1 : corner + 2])
+    bot_corner = jnp.where(lower, bottom[corner : corner + 1], bottom[corner + 1 : corner + 2])
+    outer = jnp.concatenate(
+        [top_corner[None], outer_ref[...].astype(f32)[:, None, :], bot_corner[None]], axis=0
+    )
     left, right = jnp.where(lower, outer, inner), jnp.where(lower, inner, outer)
     left = jnp.broadcast_to(left, (TR + 2, TC, C)).reshape(rows, C)
     right = jnp.broadcast_to(right, (TR + 2, TC, C)).reshape(rows, C)
@@ -228,12 +247,10 @@
     out_ref[...] = total.T
 
 
-def sums_kernel(y_ref, slab_ref, feat_ref, back_ref, gain_ref, shift_ref, bias_ref,
-                row_ref, da_ref, par_ref, out_ref, block):
-    got = slab_ref[:, S_AT:].astype(f32)
-    mean, squares = merge(
-        got[:, 0] + got[:, 1] + got[:, 2], got[:, 3] + got[:, 4] + got[:, 5], NZ * CHIP
-    )
+def sums_kernel(y_ref, stat_ref, feat_hbm, back_ref, gain_ref, shift_ref, bias_ref,
+                row_ref, da_ref, par_ref, out_ref, block, feat_ref, sem):
+    copies = fetch(((feat_hbm, feat_ref),), sem)
+    mean, squares = merge_pieces(stat_ref[:, :S_ROWS], PEERS * CHIP)
     groups = group_matrix()
     both = jnp.concatenate([mean, lax.rsqrt(squares / TOTAL + 1e-05), jnp.zeros((6, 128), f32)], axis=0)
     both = exact_dot(both, groups, 1)
@@ -243,6 +260,7 @@
     row_ref[...] = jnp.where(row == 0, mean, rstd)
     table = jnp.where(row == 0, mean, jnp.where(row == 1, rstd * gain, jnp.where(row == 2, shift, 0.0)))
     par_ref[...] = exact_dot(table, pick(term_columns(y_ref[0])), 0)
+    copies[0].wait()
     xhat = (feat_ref[...].astype(f32) - mean) * rstd
     act = xhat * gain + shift
     sig = jax.nn.sigmoid(act)
@@ -257,7 +275,7 @@
         out_ref[p] = block[8 * (p % 2) : 8 * (p % 2) + 8]
 
 
-def terms_kernel(core_ref, own_ref, other_ref, par_ref, out_ref, hid, strips, cot3, rest):
+def terms_kernel(core_ref, z_ref, own_ref, other_ref, edge_ref, par_ref, out_ref, hid, strips, cot3, rest):
     core = core_ref[0]
 
     def put(block, peer, side):
@@ -289,13 +307,15 @@
                 for h in range(2):
                     at = (y * TR + 2 * g + h + 1) * 128 + xx * 32 + side * TC
                     strips[at : at + TC] = value[h * TC : (h + 1) * TC]
-    for xx in range(NX):
-        for side, peer, start in ((0, xx, 0), (1, (NY - 1) * NX + xx, (ROWS + 1) * 128)):
-            tail = own_ref[peer, S_AT:].astype(f32)[8:]
-            main = own_ref[peer, H_AT:S_AT].astype(f32)
-            value = [cot_rows(main[8 * g : 8 * g + 8], tail, g, side) for g in range(4)]
-            at = start + xx * 32
-            strips[at : at + 32] = jnp.concatenate(value, axis=0).astype(bf16)
+    z = z_ref[0]
+    for start, peer, there in ((0, jnp.maximum(z - 1, 0), z > 0),
+                               ((ROWS + 1) * 128, jnp.minimum(z + 1, NZ - 1), z < NZ - 1)):
+        got = jnp.where(there, edge_ref[peer].astype(f32), 0.0)
+        for xx in range(NX):
+            for side in range(2):
+                at = start + xx * 32 + side * TC
+                value = cot_rows(got[16 + 16 * xx : 32 + 16 * xx], got[80:], xx, side)
+                strips[at : at + TC] = value.astype(bf16)
     lane = lax.broadcasted_iota(jnp.int32, (NQ, 128), 1)
     for row in range(ROWS + 2):
         at = slice(row * 128, (row + 1) * 128)
@@ -330,8 +350,10 @@
         out_ref[z, W_ROWS:] = block
 
 
-def final_kernel(core_ref, got_ref, other_ref, feat_ref, da_ref, row_ref, gain_ref,
-                 grad_ref, weight_ref, gain_grad_ref, shift_grad_ref, bias_ref):
+def final_kernel(core_ref, got_ref, other_ref, feat_hbm, da_ref, row_ref, gain_ref,
+                 grad_ref, weight_ref, gain_grad_ref, shift_grad_ref, bias_ref, feat_ref, sem):
+    copies = fetch(((feat_hbm, feat_ref),), sem)
+
     def half(ref):
         total = jnp.zeros((8, 128), f32)
         for z in range(NZ):
@@ -350,6 +372,7 @@
     both = jnp.concatenate([gain * sums[0], gain * sums[1], jnp.zeros((6, C), f32)], axis=0)
     both = exact_dot(exact_dot(both, groups, 0), groups, 1) / TOTAL
     first, second = both[0:1], both[1:2]
+    copies[0].wait()
     xhat = (feat_ref[...].astype(f32) - mean) * rstd
     grad_ref[...] = (rstd * (da_ref[...] * gain - first - xhat * second)).astype(bf16)
     weight = got_ref[0, :W_ROWS].astype(f32)
@@ -371,67 +394,53 @@
 
 
 def body(features, cotangent, conv_weight, gain, shift):
-    core, y = lax.axis_index("core"), lax.axis_index("y")
-    at_core, at_y = core.reshape(1), y.reshape(1)
+    core, y, z = lax.axis_index("core"), lax.axis_index("y"), lax.axis_index("z")
+    at_core, at_y, at_z = core.reshape(1), y.reshape(1), z.reshape(1)
     feat, cot = features.reshape(PIX, C), cotangent.reshape(PIX, C)
     gain, shift = gain.reshape(1, C), shift.reshape(1, C)
     cot2, feat2 = flip(cot), flip(feat)
-
+    both = jnp.concatenate([feat, cot])
+    column = jnp.where(core == 0, cotangent[:, 0], cotangent[:, TC - 1])
+    pairs = [(2 * k + 1, 2 * k + 2) for k in range(NX - 1)]
+    outer = lax.ppermute(column, ("x", "core"), pairs + [(b, a) for a, b in pairs])
+    outer2 = flip(outer)
+    spare = jnp.zeros((6, C), bf16)
     edge = jnp.where(
         core == 0,
-        jnp.concatenate([cot[PIX - TC :], cot2[PIX - TC :]]),
-        jnp.concatenate([cot2[:TC], cot[:TC]]),
+        jnp.concatenate([cot[PIX - TC :], cot2[PIX - TC :], outer[TR - 1 :], outer2[TR - 1 :], spare]),
+        jnp.concatenate([cot2[:TC], cot[:TC], outer2[:1], outer[:1], spare]),
     )
     count = NZ * NY
     ways = [(2 * k, 2 * k + 2) for k in range(count - 1)] + [(2 * k + 3, 2 * k + 1) for k in range(count - 1)]
     mine = lax.ppermute(edge, ("z", "y", "core"), ways)
+
+    packed, bias = pl.pallas_call(
+        pack_kernel,
+        out_shape=(shape((PEERS, G_ROWS, 128), bf16), shape((8, C), f32)),
+        in_specs=[smem()] + [vmem()] * 3,
+        out_specs=(vmem(), vmem()),
+        compiler_params=params(),
+        cost_estimate=pl.CostEstimate(flops=1 << 28, bytes_accessed=2 << 20, transcendentals=0),
+        name="pack",
+    )(at_core, both, feat2, cot2)
+    packed, outer = lax.optimization_barrier((packed, outer))
+    slab = lax.all_to_all(packed, ("y", "x"), 0, 0)
+    slab, mine = lax.optimization_barrier((slab, mine))
+    edges = pl.pallas_call(
+        split_kernel,
+        out_shape=shape((NZ, E_ROWS, 128), bf16),
+        in_specs=[smem(), vmem()],
+        out_specs=vmem(),
+        compiler_params=params(),
+        name="split",
+    )(at_z, slab)
+    slab_other = flip(slab)
+    edges = lax.all_to_all(edges, "z", 0, 0)
     theirs = flip(mine)
-
-    stats, bias = pl.pallas_call(
-        stats_kernel,
-        out_shape=(shape((NZ, 8, 128), f32), shape((8, C), f32)),
-        in_specs=[pl.BlockSpec(memory_space=pltpu.HBM)] * 2 + [vmem()],
-        out_specs=(vmem(), vmem()),
-        scratch_shapes=[pltpu.VMEM((PIX, C), bf16)] * 2 + [pltpu.SemaphoreType.DMA((2,))],
-        compiler_params=params(),
-        name="stats",
-    )(feat, cot, feat2)
-    stats, mine = lax.optimization_barrier((stats, mine))
-    stats = lax.all_to_all(stats, "z", 0, 0)
-    packed, rest = pl.pallas_call(
-        pack_kernel,
-        grid=(1,),
-        out_shape=(shape((PEERS, G_ROWS, 128), bf16), shape((NX, 8, 128), f32)),
-        in_specs=[smem()] + [whole(PIX, C)] * 3 + [vmem()] * 2,
-        out_specs=(vmem(), vmem()),
-        compiler_params=params(),
-        name="pack",
-    )(at_core, feat, cot, cot2, mine, theirs)
-    top = jnp.where(core == 0, mine[0], theirs[2 * TC - 1])
-    bottom = jnp.where(core == 0, theirs[0], mine[2 * TC - 1])
-    column = jnp.where(core == 0, cotangent[:, 0], cotangent[:, TC - 1])
-    column = jnp.concatenate([top[None], column, bottom[None]])
-    pairs = [(2 * k + 1, 2 * k + 2) for k in range(NX - 1)]
-    outer = lax.ppermute(column, ("x", "core"), pairs + [(b, a) for a, b in pairs])
-    packed, outer = lax.optimization_barrier((packed, outer))
-    packed = pl.pallas_call(
-        patch_kernel,
-        out_shape=shape((PEERS, G_ROWS, 128), bf16),
-        in_specs=[vmem(), vmem(), pl.BlockSpec(memory_space=pl.ANY)],
-        out_specs=pl.BlockSpec(memory_space=pl.ANY),
-        scratch_shapes=[pltpu.VMEM((PEERS, S_ROWS, 128), bf16), pltpu.SemaphoreType.DMA],
-        input_output_aliases={2: 0},
-        compiler_params=params(),
-        name="patch",
-    )(stats, rest, packed)
-    slab = lax.all_to_all(packed, ("y", "x"), 0, 0)
-    slab_other = flip(slab)
-
     back = pl.pallas_call(
         back_kernel,
-        grid=(1,),
         out_shape=shape((PIX, C), f32),
-        in_specs=[smem()] + [whole(PIX, C)] * 2 + [vmem()] * 3 + [pl.BlockSpec(memory_space=pl.ANY)],
+        in_specs=[smem()] + [vmem()] * 5 + [hbm()],
         out_specs=vmem(),
         scratch_shapes=[
             pltpu.VMEM((3, (TR + 2) * TC, C), bf16),
@@ -441,25 +450,28 @@
         compiler_params=params(),
         cost_estimate=pl.CostEstimate(flops=2 * PIX * 9 * C * C, bytes_accessed=18 * C * C, transcendentals=0),
         name="back",
-    )(at_core, cot, cot2, mine, theirs, outer, conv_weight)
-    slab, back = lax.optimization_barrier((slab, back))
+    )(at_core, both, cot2, mine, theirs, outer, conv_weight)
+
 
     row, da, table, sums = pl.pallas_call(
         sums_kernel,
-        grid=(1,),
         out_shape=(shape((8, C), f32), shape((PIX, C), f32), shape((8, 256), f32), shape((2 * PEERS, 8, 128), f32)),
-        in_specs=[smem(), vmem(), whole(PIX, C), vmem(), whole(1, C), whole(1, C), vmem()],
+        in_specs=[smem(), vmem(), hbm(), vmem(), vmem(), vmem(), vmem()],
         out_specs=(vmem(), vmem(), vmem(), vmem()),
-        scratch_shapes=[pltpu.VMEM((16, 128), f32)],
+        scratch_shapes=[
+            pltpu.VMEM((16, 128), f32),
+            pltpu.VMEM((PIX, C), bf16),
+            pltpu.SemaphoreType.DMA((1,)),
+        ],
         compiler_params=params(),
         name="sums",
-    )(at_y, slab, feat, back, gain, shift, bias)
+    )(at_y, edges, feat, back, gain, shift, bias)
     sums = lax.all_to_all(sums, ("y", "x", "core"), 0, 0)
 
     terms = pl.pallas_call(
         terms_kernel,
         out_shape=shape((NZ, W_ROWS, 256), bf16),
-        in_specs=[smem()] + [vmem()] * 3,
+        in_specs=[smem()] * 2 + [vmem()] * 4,
         out_specs=vmem(),
         scratch_shapes=[
             pltpu.VMEM((ROWS * 128, 256), bf16),
@@ -472,7 +484,7 @@
             flops=2 * PIX * 9 * C * C, bytes_accessed=4 << 20, transcendentals=ROWS * 128 * 256
         ),
         name="terms",
-    )(at_core, slab, slab_other, table)
+    )(at_core, at_z, slab, slab_other, edges, table)
 
     joined = pl.pallas_call(
         join_kernel,
@@ -485,10 +497,10 @@
     joined = lax.all_to_all(joined, "z", 0, 0)
     grad, weight_grad, gain_grad, shift_grad, bias_grad = pl.pallas_call(
         final_kernel,
-        grid=(1,),
         out_shape=(shape((PIX, C), bf16), shape((3, 3, 20, NQ), f32)) + (shape((C,), f32),) * 3,
-        in_specs=[smem(), vmem(), vmem(), whole(PIX, C), vmem(), vmem(), whole(1, C)],
+        in_specs=[smem(), vmem(), vmem(), hbm(), vmem(), vmem(), vmem()],
         out_specs=(vmem(),) * 5,
+        scratch_shapes=[pltpu.VMEM((PIX, C), bf16), pltpu.SemaphoreType.DMA((1,))],
         compiler_params=params(),
         name="final",
     )(at_core, joined, flip(joined), feat, da, row, gain)

time: 101 us -> 95 us (0.941)
  blocking collectives: 43.1 us -> 15.3 us
  waiting for transfers between devices: 8.15 us -> 31.2 us
  local copies, waits for them, and re-layouts: 5.4 us -> 1.89 us
  Pallas kernels: 15.4 us -> 16.6 us
    all_to_all x1 -> x0, blocking collectives: 24.7 us -> none  [body(): slab = lax.all_to_all(packed, ('y', 'x'), 0, 0)]
    all_to_all x1 -> x2, waiting for transfers between devices: 0.7 us -> 17.4 us  [the longest x1 13.5 us: body(): slab = lax.all_to_all(packed, ('y', 'x'), 0, 0)]
    ppermute x1, waiting for transfers between devices: 2.48 us -> 7.36 us  [body(): mine = lax.ppermute(edge, ('z', 'y', 'core'), ways)]
    unnamed x16 -> x6, local copies, waits for them, and re-layouts: 3.68 us -> 0.02 us
    all_to_all x1 -> x2, starting transfers between devices: 11.2 us -> 14.4 us  [the longest x1 8.18 us: body(): edges = lax.all_to_all(edges, 'z', 0, 0)]
    all_to_all x1, blocking collectives: 18.4 us -> 15.3 us  [body(): joined = lax.all_to_all(joined, 'z', 0, 0)]
    ppermute x5 -> x6, starting transfers between devices: 7.84 us -> 5.83 us  [flip(): return lax.ppermute(value, 'core', [(0, 1), (1, 0)])]
    ppermute x1, starting transfers between devices: 3.3 us -> 1.92 us  [body(): lax.ppermute(column, ('x', 'core'), pairs + [(b, a) for a, b in pairs])]
  transfers between devices with their start and end apart: 9 -> 11, of which waited for: 5 -> 7; matrix products, arithmetic and copies ran while one was open for 2% -> 3% of each run, Pallas kernels for 14% -> 16%
where the time goes in v5:
time: 95 us; the launch traced here: 94.4 us
  waiting for transfers between devices  31.2 us (33%)
  starting transfers between devices  27.6 us (29%)
  Pallas kernels  16.6 us (17%)
  blocking collectives  15.3 us (16%)
  local copies, waits for them, and re-layouts  1.89 us (2%)
  other arithmetic  1.04 us (1%)
    all_to_all x1, blocking collectives, body(): joined = lax.all_to_all(joined, 'z', 0, 0)  15.3 us
    all_to_all x1, waiting for transfers between devices, body(): slab = lax.all_to_all(packed, ('y', 'x'), 0, 0)  13.5 us
    all_to_all x1, starting transfers between devices, body(): edges = lax.all_to_all(edges, 'z', 0, 0)  8.18 us
    ppermute x1, waiting for transfers between devices, body(): mine = lax.ppermute(edge, ('z', 'y', 'core'), ways)  7.36 us
    all_to_all x1, starting transfers between devices, body(): slab = lax.all_to_all(packed, ('y', 'x'), 0, 0)  6.22 us
    ppermute x6, starting transfers between devices, flip(): return lax.ppermute(value, 'core', [(0, 1), (1, 0)])  5.83 us
    pallas_call x1, Pallas kernels, body(): pl.pallas_call(back_kernel, out_shape=shape((PIX, C), f32), in_specs=[sme...  5.68 us
    pallas_call x1, Pallas kernels, body(): pl.pallas_call(terms_kernel, out_shape=shape((NZ, W_ROWS, 256), bf16), in...  4.61 us
  transfers between devices with their start and end apart: 11, of which 7 were waited for; matrix products, arithmetic and copies ran while one was open for 3% of the time, Pallas kernels for 16%

profile of v5, /device:TPU:1, one launch (start us, length us, event | category | flops | bytes accessed | tf_op | source)
XLA Modules:
  0.0 94.4 jit_solution(8354533907929818284)
XLA Ops:
  0.6 3.3 %collective-permute-start = (bf16[128,640]{1,0:T(8,128)(2,1)}, bf16[128,640]{1,0:T(8,128)(2,1)S(1)}, u32[]{:S(2)}, u32[]{:S(2)}) collective-permute-start(bf16[128,640]{1,0:T(8,128)(2,1)} %bitcast.12), channel_id=1, source_target_pairs={{0,1},{1,0},{2,3},{3,2},{4,5},{5,4},{6,7},{7,6},{8,9},{9,8},{10,11... | collective-permute-start | bytes 491528 | tf_op jit(solution)/shard_map/ppermute | solution.py:389
  4.0 0.1 collective-permute-start.1
  4.1 1.0 %fusion.2 = (bf16[8,1,640]{2,1,0:T(2,128)(2,1)S(1)}, bf16[8,1,640]{2,1,0:T(2,128)(2,1)S(1)}) fusion(bf16[8,16,640]{2,1,0:T(8,128)(2,1)} %param.6), kind=kLoop, calls=%fused_computation.7 | loop fusion | bytes 40960 | tf_op jit(solution)/shard_map/slice | solution.py:403
  5.0 1.9 %collective-permute-start.2 = (bf16[8,640]{1,0:T(8,128)(2,1)S(1)}, bf16[8,640]{1,0:T(8,128)(2,1)S(1)}, u32[]{:S(2)}, u32[]{:S(2)}) collective-permute-start(bf16[8,640]{1,0:T(8,128)(2,1)S(1)} %fusion), channel_id=1, source_target_pairs={{1,2},{3,4},{5,6},{2,1},{4,3},{6,5},{9,10},{11,12},{13,14},{10,9},... | collective-permute-start | bytes 30728 | tf_op jit(solution)/shard_map/ppermute | solution.py:405
  7.0 1.0 %pad_maximum_fusion.both_ref = bf16[256,640]{1,0:T(8,128)(2,1)S(1)} fusion(bf16[128,640]{1,0:T(8,128)(2,1)} %bitcast.17, bf16[128,640]{1,0:T(8,128)(2,1)} %bitcast.13), kind=kLoop, calls=%fused_computation | loop fusion | flops 655360 | bytes 655360 | tf_op jit(solution)/shard_map/concatenate | solution.py:402
  8.0 0.0 collective-permute-done.feat2_ref
  8.0 0.0 collective-permute-done.1.cot2_ref
  8.0 2.5 %pack.1 = (bf16[16,336,128]{2,1,0:T(8,128)(2,1)}, f32[8,640]{1,0:T(8,128)S(1)}) custom-call(s32[1]{0:T(128)} %bitcast.core_ref, bf16[256,640]{1,0:T(8,128)(2,1)S(1)} %pad_maximum_fusion.both_ref, bf16[128,640]{1,0:T(8,128)(2,1)S(1)} %collective-permute-done.feat2_ref, bf16[128,640]{1,0:T(8,128)(2,1)S(1)} %collective-permute-done.1.cot2_ref), custom_call_target="tpu_custom_call" | custom-call | flops 268435456 | bytes 2097152 | tf_op jit(solution)/shard_map/pack/pallas_call | solution.py:417
  10.5 0.0 collective-permute-done.2.outer_ref
  10.5 6.2 %all-to-all-start = ((bf16[16,336,128]{2,1,0:T(8,128)(2,1)}), bf16[16,336,128]{2,1,0:T(8,128)(2,1)S(1)}, u32[]{:S(2)}, u32[]{:S(2)}) async-start(bf16[16,336,128]{2,1,0:T(8,128)(2,1)} %get-tuple-element.21), calls=%async_computation | async-start | bytes 2752512 | tf_op jit(solution)/shard_map/all_to_all | solution.py:427
  16.8 0.0 copy-start.1
  16.8 0.0 copy-start.2
  16.8 0.8 slice_bitcast_fusion
  17.5 0.0 collective-permute-start.3
  17.6 1.2 %collective-permute-done.3 = bf16[8,640]{1,0:T(8,128)(2,1)S(1)} collective-permute-done((bf16[8,640]{1,0:T(8,128)(2,1)S(1)}, bf16[8,640]{1,0:T(8,128)(2,1)S(1)}, u32[]{:S(2)}, u32[]{:S(2)}) %collective-permute-start.3) | collective-permute-done | bytes 10272 | tf_op jit(solution)/shard_map/ppermute | solution.py:389
  18.8 0.1 concatenate.11
  18.8 0.1 concatenate.10
  18.9 1.3 %collective-permute-start.4 = (bf16[40,640]{1,0:T(8,128)(2,1)S(1)}, bf16[40,640]{1,0:T(8,128)(2,1)S(1)}, u32[]{:S(2)}, u32[]{:S(2)}) collective-permute-start(bf16[40,640]{1,0:T(8,128)(2,1)S(1)} %broadcast_select_fusion), channel_id=1, source_target_pairs={{0,8},{8,16},{16,24},{24,32},{32,40},{40,48},{48,56},{56,64},{64,7... | collective-permute-start | bytes 153608 | tf_op jit(solution)/shard_map/ppermute | solution.py:415
  20.2 7.4 %collective-permute-done.4.mine_ref = bf16[40,640]{1,0:T(8,128)(2,1)S(1)} collective-permute-done((bf16[40,640]{1,0:T(8,128)(2,1)S(1)}, bf16[40,640]{1,0:T(8,128)(2,1)S(1)}, u32[]{:S(2)}, u32[]{:S(2)}) %collective-permute-start.4) | collective-permute-done | bytes 51232 | tf_op jit(solution)/shard_map/ppermute | solution.py:415
  27.5 13.5 %all-to-all-done.slab_ref.own_ref = bf16[16,336,128]{2,1,0:T(8,128)(2,1)S(1)} async-done(((bf16[16,336,128]{2,1,0:T(8,128)(2,1)}), bf16[16,336,128]{2,1,0:T(8,128)(2,1)S(1)}, u32[]{:S(2)}, u32[]{:S(2)}) %all-to-all-start) | async-done | bytes 1376288 | tf_op jit(solution)/shard_map/all_to_all | solution.py:427
  41.1 0.6 collective-permute-start.6
  41.7 0.8 split.1
  42.5 8.2 %all-to-all-start.1 = ((bf16[8,96,128]{2,1,0:T(8,128)(2,1)}), bf16[8,96,128]{2,1,0:T(8,128)(2,1)S(1)}, u32[]{:S(2)}, u32[]{:S(2)}) async-start(bf16[8,96,128]{2,1,0:T(8,128)(2,1)} %split.1), calls=%async_computation.1 | async-start | bytes 393216 | tf_op jit(solution)/shard_map/all_to_all | solution.py:438
  50.7 0.3 collective-permute-start.5
  51.0 0.0 copy-done.1
  51.0 0.0 copy-done.2
  51.0 0.0 copy-start
  51.0 0.9 collective-permute-done.5.theirs_ref
  51.9 5.7 %back.1.back_ref = f32[128,640]{1,0:T(8,128)S(1)} custom-call(s32[1]{0:T(128)} %bitcast.core_ref, bf16[256,640]{1,0:T(8,128)(2,1)S(1)} %pad_maximum_fusion.both_ref, bf16[128,640]{1,0:T(8,128)(2,1)S(1)} %collective-permute-done.1.cot2_ref, bf16[40,640]{1,0:T(8,128)(2,1)S(1)} %collective-permute-done.4.mine_ref, ...), custom_call_target="tpu_custom_call" | custom-call | flops 943718400 | bytes 7372800 | tf_op jit(solution)/shard_map/back/pallas_call | solution.py:440
  57.6 3.9 %all-to-all-done.1.stat_ref.edge_ref = bf16[8,96,128]{2,1,0:T(8,128)(2,1)S(1)} async-done(((bf16[8,96,128]{2,1,0:T(8,128)(2,1)}), bf16[8,96,128]{2,1,0:T(8,128)(2,1)S(1)}, u32[]{:S(2)}, u32[]{:S(2)}) %all-to-all-start.1) | async-done | bytes 196640 | tf_op jit(solution)/shard_map/all_to_all | solution.py:438
  61.5 0.0 copy-done
  61.5 1.5 %sums.1 = (f32[8,640]{1,0:T(8,128)S(1)}, f32[128,640]{1,0:T(8,128)S(1)}, f32[8,256]{1,0:T(8,128)S(1)}, f32[32,8,128]{2,1,0:T(8,128)}) custom-call(s32[1]{0:T(128)} %bitcast.1.y_ref, bf16[8,96,128]{2,1,0:T(8,128)(2,1)S(1)} %all-to-all-done.1.stat_ref.edge_ref, bf16[128,640]{1,0:T(8,128)(2,1)S(1)} %bitcast.14, f32[128,640]{1,0:T(8,128)S(1)} %back.1.back_ref, ...), custom_call_target="tpu_custom_call" | custom-call | tf_op jit(solution)/shard_map/sums/pallas_call | solution.py:456
  63.0 4.1 %all-to-all-start.2 = ((f32[32,8,128]{2,1,0:T(8,128)}), f32[32,8,128]{2,1,0:T(8,128)S(1)}, u32[]{:S(2)}, u32[]{:S(2)}) async-start(f32[32,8,128]{2,1,0:T(8,128)} %get-tuple-element.26), calls=%async_computation.2 | async-start | bytes 262144 | tf_op jit(solution)/shard_map/all_to_all | solution.py:469
  67.1 0.0 collective-permute-done.6.other_ref
  67.2 4.6 %terms.1.terms_ref = bf16[8,64,256]{2,1,0:T(8,128)(2,1)S(1)} custom-call(s32[1]{0:T(128)} %bitcast.core_ref, s32[1]{0:T(128)} %bitcast.2.z_ref, bf16[16,336,128]{2,1,0:T(8,128)(2,1)S(1)} %all-to-all-done.slab_ref.own_ref, bf16[16,336,128]{2,1,0:T(8,128)(2,1)} %collective-permute-done.6.other_ref, bf16[8,96,128]{2,1,0:T(8,128)(2,1)S(1)} %all-to-all-done.1.stat_ref.edge_ref, ...), custom_call_target="tpu_custom_call" | custom-call | flops 943718400 | bytes 4194304 | tf_op jit(solution)/shard_map/terms/pallas_call | solution.py:471
  71.8 3.1 %all-to-all-done.2.sums_ref = f32[32,8,128]{2,1,0:T(8,128)S(1)} async-done(((f32[32,8,128]{2,1,0:T(8,128)}), f32[32,8,128]{2,1,0:T(8,128)S(1)}, u32[]{:S(2)}, u32[]{:S(2)}) %all-to-all-start.2) | async-done | bytes 131104 | tf_op jit(solution)/shard_map/all_to_all | solution.py:469
  74.9 15.3 %all_to_all.20.got_ref = bf16[8,80,256]{2,1,0:T(8,128)(2,1)S(1)} all-to-all(bf16[8,80,256]{2,1,0:T(8,128)(2,1)S(1)} %join.1), channel_id=1, replica_groups=mesh['z'=8,'y'=4,'x'=4,'core'=2] {'z'}, dimensions={0} | all-to-all | bytes 655360 | tf_op jit(solution)/shard_map/all_to_all | solution.py:497
  90.2 1.5 %collective-permute-start.7 = (bf16[8,80,256]{2,1,0:T(8,128)(2,1)S(1)}, bf16[8,80,256]{2,1,0:T(8,128)(2,1)S(1)}, u32[]{:S(2)}, u32[]{:S(2)}) collective-permute-start(bf16[8,80,256]{2,1,0:T(8,128)(2,1)S(1)} %all_to_all.20.got_ref), channel_id=1, source_target_pairs={{0,1},{1,0},{2,3},{3,2},{4,5},{5,4},{6,7},{7,6},{8,9},{9,8},{10,11... | collective-permute-start | bytes 983048 | tf_op jit(solution)/shard_map/ppermute | solution.py:389
  91.7 1.3 %collective-permute-done.7.other_ref = bf16[8,80,256]{2,1,0:T(8,128)(2,1)S(1)} collective-permute-done((bf16[8,80,256]{2,1,0:T(8,128)(2,1)S(1)}, bf16[8,80,256]{2,1,0:T(8,128)(2,1)S(1)}, u32[]{:S(2)}, u32[]{:S(2)}) %collective-permute-start.7) | collective-permute-done | bytes 327712 | tf_op jit(solution)/shard_map/ppermute | solution.py:389
  93.0 1.4 %final.1 = (bf16[128,640]{1,0:T(8,128)(2,1)}, f32[3,3,20,80]{3,2,1,0:T(8,128)}, f32[640]{0:T(1024)}, f32[640]{0:T(1024)}, f32[640]{0:T(1024)}) custom-call(s32[1]{0:T(128)} %bitcast.core_ref, bf16[8,80,256]{2,1,0:T(8,128)(2,1)S(1)} %all_to_all.20.got_ref, bf16[8,80,256]{2,1,0:T(8,128)(2,1)S(1)} %collective-permute-done.7.other_ref, ...), custom_call_target="tpu_custom_call" | custom-call | tf_op jit(solution)/shard_map/final/pallas_call | solution.py:498
  (9 shorter events, 0.1 us)
Async XLA Ops:
  0.6 7.4 %collective-permute-start = (bf16[128,640]{1,0:T(8,128)(2,1)}, bf16[128,640]{1,0:T(8,128)(2,1)S(1)}, u32[]{:S(2)}, u32[]{:S(2)}) collective-permute-start(bf16[128,640]{1,0:T(8,128)(2,1)} %bitcast.12), channel_id=1, source_target_pairs={{0,1},{1,0},{2,3},{3,2},{4,5},{5,4},{6,7},{7,6},{8,9},{9,8},{10,11... | collective-permute-start | bytes 491528 | tf_op jit(solution)/shard_map/ppermute | solution.py:389
  4.0 4.1 %collective-permute-start.1 = (bf16[128,640]{1,0:T(8,128)(2,1)}, bf16[128,640]{1,0:T(8,128)(2,1)S(1)}, u32[]{:S(2)}, u32[]{:S(2)}) collective-permute-start(bf16[128,640]{1,0:T(8,128)(2,1)} %bitcast.16), channel_id=1, source_target_pairs={{0,1},{1,0},{2,3},{3,2},{4,5},{5,4},{6,7},{7,6},{8,9},{9,8},{10,11... | collective-permute-start | bytes 491528 | tf_op jit(solution)/shard_map/ppermute | solution.py:389
  5.0 5.5 %collective-permute-start.2 = (bf16[8,640]{1,0:T(8,128)(2,1)S(1)}, bf16[8,640]{1,0:T(8,128)(2,1)S(1)}, u32[]{:S(2)}, u32[]{:S(2)}) collective-permute-start(bf16[8,640]{1,0:T(8,128)(2,1)S(1)} %fusion), channel_id=1, source_target_pairs={{1,2},{3,4},{5,6},{2,1},{4,3},{6,5},{9,10},{11,12},{13,14},{10,9},... | collective-permute-start | bytes 30728 | tf_op jit(solution)/shard_map/ppermute | solution.py:405
  10.5 30.5 %all-to-all-start = ((bf16[16,336,128]{2,1,0:T(8,128)(2,1)}), bf16[16,336,128]{2,1,0:T(8,128)(2,1)S(1)}, u32[]{:S(2)}, u32[]{:S(2)}) async-start(bf16[16,336,128]{2,1,0:T(8,128)(2,1)} %get-tuple-element.21), calls=%async_computation | async-start | bytes 2752512 | tf_op jit(solution)/shard_map/all_to_all | solution.py:427
  16.8 34.2 %copy-start.1 = (f32[640]{0:T(1024)S(1)}, f32[640]{0:T(1024)}, u32[]{:S(2)}) copy-start(f32[640]{0:T(1024)} %param.8) | copy-start | bytes 7684
  16.8 34.2 %copy-start.2 = (f32[640]{0:T(1024)S(1)}, f32[640]{0:T(1024)}, u32[]{:S(2)}) copy-start(f32[640]{0:T(1024)} %param.9) | copy-start | bytes 7684
  17.5 1.2 %collective-permute-start.3 = (bf16[8,640]{1,0:T(8,128)(2,1)S(1)}, bf16[8,640]{1,0:T(8,128)(2,1)S(1)}, u32[]{:S(2)}, u32[]{:S(2)}) collective-permute-start(bf16[8,640]{1,0:T(8,128)(2,1)S(1)} %collective-permute-done.2.outer_ref), channel_id=1, source_target_pairs={{0,1},{1,0},{2,3},{3,2},{4,5},{5,4},{6,7},{7,6},{8,9},{9,8},{10,11... | collective-permute-start | bytes 30728 | tf_op jit(solution)/shard_map/ppermute | solution.py:389
  18.9 8.7 %collective-permute-start.4 = (bf16[40,640]{1,0:T(8,128)(2,1)S(1)}, bf16[40,640]{1,0:T(8,128)(2,1)S(1)}, u32[]{:S(2)}, u32[]{:S(2)}) collective-permute-start(bf16[40,640]{1,0:T(8,128)(2,1)S(1)} %broadcast_select_fusion), channel_id=1, source_target_pairs={{0,8},{8,16},{16,24},{24,32},{32,40},{40,48},{48,56},{56,64},{64,7... | collective-permute-start | bytes 153608 | tf_op jit(solution)/shard_map/ppermute | solution.py:415
  41.1 26.1 %collective-permute-start.6 = (bf16[16,336,128]{2,1,0:T(8,128)(2,1)S(1)}, bf16[16,336,128]{2,1,0:T(8,128)(2,1)}, u32[]{:S(2)}, u32[]{:S(2)}) collective-permute-start(bf16[16,336,128]{2,1,0:T(8,128)(2,1)S(1)} %all-to-all-done.slab_ref.own_ref), channel_id=1, source_target_pairs={{0,1},{1,0},{2,3},{3,2},{4,5},{5,4},{6,7},{7,6},{8,9},{9,8},{10,11... | collective-permute-start | bytes 4128776 | tf_op jit(solution)/shard_map/ppermute | solution.py:389
  42.5 19.0 %all-to-all-start.1 = ((bf16[8,96,128]{2,1,0:T(8,128)(2,1)}), bf16[8,96,128]{2,1,0:T(8,128)(2,1)S(1)}, u32[]{:S(2)}, u32[]{:S(2)}) async-start(bf16[8,96,128]{2,1,0:T(8,128)(2,1)} %split.1), calls=%async_computation.1 | async-start | bytes 393216 | tf_op jit(solution)/shard_map/all_to_all | solution.py:438
  50.7 1.2 %collective-permute-start.5 = (bf16[40,640]{1,0:T(8,128)(2,1)S(1)}, bf16[40,640]{1,0:T(8,128)(2,1)S(1)}, u32[]{:S(2)}, u32[]{:S(2)}) collective-permute-start(bf16[40,640]{1,0:T(8,128)(2,1)S(1)} %collective-permute-done.4.mine_ref), channel_id=1, source_target_pairs={{0,1},{1,0},{2,3},{3,2},{4,5},{5,4},{6,7},{7,6},{8,9},{9,8},{10,11... | collective-permute-start | bytes 153608 | tf_op jit(solution)/shard_map/ppermute | solution.py:389
  51.0 10.5 %copy-start = (bf16[8,16,640]{2,1,0:T(8,128)(2,1)S(1)}, bf16[8,16,640]{2,1,0:T(8,128)(2,1)}, u32[]{:S(2)}) copy-start(bf16[8,16,640]{2,1,0:T(8,128)(2,1)} %param.5) | copy-start | bytes 491524
  63.0 11.9 %all-to-all-start.2 = ((f32[32,8,128]{2,1,0:T(8,128)}), f32[32,8,128]{2,1,0:T(8,128)S(1)}, u32[]{:S(2)}, u32[]{:S(2)}) async-start(f32[32,8,128]{2,1,0:T(8,128)} %get-tuple-element.26), calls=%async_computation.2 | async-start | bytes 262144 | tf_op jit(solution)/shard_map/all_to_all | solution.py:469
  90.2 2.8 %collective-permute-start.7 = (bf16[8,80,256]{2,1,0:T(8,128)(2,1)S(1)}, bf16[8,80,256]{2,1,0:T(8,128)(2,1)S(1)}, u32[]{:S(2)}, u32[]{:S(2)}) collective-permute-start(bf16[8,80,256]{2,1,0:T(8,128)(2,1)S(1)} %all_to_all.20.got_ref), channel_id=1, source_target_pairs={{0,1},{1,0},{2,3},{3,2},{4,5},{5,4},{6,7},{7,6},{8,9},{9,8},{10,11... | collective-permute-start | bytes 983048 | tf_op jit(solution)/shard_map/ppermute | solution.py:389

commit v6 on v5

--- a/solution.py
+++ b/solution.py
@@ -146,7 +146,7 @@
     )
 
 
-def pack_kernel(core_ref, both_ref, feat2_ref, cot2_ref, out_ref, bias_ref):
+def pack_kernel(core_ref, both_ref, feat2_ref, cot2_ref, out_hbm, bias_ref, out_ref, sem):
     core = core_ref[0]
     feat_ref, cot_ref = both_ref.at[:PIX], both_ref.at[PIX:]
     x, x2 = feat_ref[...].astype(f32), feat2_ref[...].astype(f32)
@@ -157,19 +157,24 @@
     squares = ((x - wide) ** 2).sum(0, keepdims=True) + ((x2 - wide) ** 2).sum(0, keepdims=True)
     stats = put_pieces(mean[:1], exact_dot(rows8(squares), groups, 0)[:1])
     bias_ref[...] = rows8(cot_ref[...].astype(f32).sum(0, keepdims=True))
+    moved = jnp.dot(feat_ref[...], pick(feature_columns()), preferred_element_type=f32)
+    moved_rest = lanes32(moved[:, 512:], 32)
+    for p in range(PEERS):
+        y = p // NX
+        out_ref[p, 0:128] = moved[:, y * 128 : (y + 1) * 128].astype(bf16)
+        out_ref[p, 128:160] = moved_rest[y].astype(bf16)
+    copies = fetch(((out_ref.at[:, :F_ROWS, :], out_hbm.at[:, :F_ROWS, :]),), sem.at[0:1])
     first, second = in_order(core, cot_ref, cot2_ref)
-    moved = jnp.dot(feat_ref[...], pick(feature_columns()), preferred_element_type=f32)
     terms = blocks(core, first, second)
-    moved_rest = lanes32(moved[:, 512:], 32)
     terms_rest = lanes32(terms[:, 512:], 32)
-    for y in range(NY):
-        for xx in range(NX):
-            p = y * NX + xx
-            out_ref[p, 0:128] = moved[:, y * 128 : (y + 1) * 128].astype(bf16)
-            out_ref[p, 128:160] = moved_rest[y].astype(bf16)
-            out_ref[p, 160:288] = terms[:, xx * 128 : (xx + 1) * 128].astype(bf16)
-            out_ref[p, 288:320] = terms_rest[xx].astype(bf16)
-            out_ref[p, S_AT:] = stats
+    for p in range(PEERS):
+        xx = p % NX
+        out_ref[p, 160:288] = terms[:, xx * 128 : (xx + 1) * 128].astype(bf16)
+        out_ref[p, 288:320] = terms_rest[xx].astype(bf16)
+        out_ref[p, S_AT:] = stats
+    copies += fetch(((out_ref.at[:, F_ROWS:, :], out_hbm.at[:, F_ROWS:, :]),), sem.at[1:2])
+    for copy in copies:
+        copy.wait()
 
 
 def merge(means, squares, count):
@@ -211,7 +216,7 @@
             out_ref[p, 80:] = first
 
 
-def back_kernel(core_ref, both_ref, cot2_ref, mine_ref, theirs_ref, outer_ref, w_hbm, out_ref, shifted, w_ref, sem):
+def back_kernel(core_ref, both_ref, cot2_ref, mine_ref, theirs_ref, beside_ref, w_hbm, out_ref, shifted, w_ref, sem):
     copies = fetch([(w_hbm.at[t // 3, t % 3], w_ref.at[t]) for t in range(9)], sem)
     rows = (TR + 2) * TC
     lower = core_ref[0] == 0
@@ -226,9 +231,9 @@
     inner = jnp.where(lower, near[:, :1], near[:, TC - 1 :])
     top_corner = jnp.where(lower, top[corner : corner + 1], top[corner + 1 : corner + 2])
     bot_corner = jnp.where(lower, bottom[corner : corner + 1], bottom[corner + 1 : corner + 2])
-    outer = jnp.concatenate(
-        [top_corner[None], outer_ref[...].astype(f32)[:, None, :], bot_corner[None]], axis=0
-    )
+    beside = beside_ref[...].astype(f32).reshape(TR, TC, C)
+    outer = jnp.where(lower, beside[:, TC - 1 :], beside[:, :1])
+    outer = jnp.concatenate([top_corner[None], outer, bot_corner[None]], axis=0)
     left, right = jnp.where(lower, outer, inner), jnp.where(lower, inner, outer)
     left = jnp.broadcast_to(left, (TR + 2, TC, C)).reshape(rows, C)
     right = jnp.broadcast_to(right, (TR + 2, TC, C)).reshape(rows, C)
@@ -247,9 +252,8 @@
     out_ref[...] = total.T
 
 
-def sums_kernel(y_ref, stat_ref, feat_hbm, back_ref, gain_ref, shift_ref, bias_ref,
-                row_ref, da_ref, par_ref, out_ref, block, feat_ref, sem):
-    copies = fetch(((feat_hbm, feat_ref),), sem)
+def sums_kernel(y_ref, stat_ref, both_ref, back_ref, gain_ref, shift_ref, bias_ref,
+                row_ref, da_ref, par_ref, out_ref, block):
     mean, squares = merge_pieces(stat_ref[:, :S_ROWS], PEERS * CHIP)
     groups = group_matrix()
     both = jnp.concatenate([mean, lax.rsqrt(squares / TOTAL + 1e-05), jnp.zeros((6, 128), f32)], axis=0)
@@ -260,8 +264,7 @@
     row_ref[...] = jnp.where(row == 0, mean, rstd)
     table = jnp.where(row == 0, mean, jnp.where(row == 1, rstd * gain, jnp.where(row == 2, shift, 0.0)))
     par_ref[...] = exact_dot(table, pick(term_columns(y_ref[0])), 0)
-    copies[0].wait()
-    xhat = (feat_ref[...].astype(f32) - mean) * rstd
+    xhat = (both_ref[:PIX].astype(f32) - mean) * rstd
     act = xhat * gain + shift
     sig = jax.nn.sigmoid(act)
     da = back_ref[...] * sig * (1.0 + act * (1.0 - sig))
@@ -275,7 +278,9 @@
         out_ref[p] = block[8 * (p % 2) : 8 * (p % 2) + 8]
 
 
-def terms_kernel(core_ref, z_ref, own_ref, other_ref, edge_ref, par_ref, out_ref, hid, strips, cot3, rest):
+def terms_kernel(core_ref, z_ref, own_ref, other_hbm, edge_ref, par_ref, out_ref,
+                 hid, strips, cot3, rest, other_ref, sem):
+    copies = fetch(((other_hbm.at[:, :F_ROWS, :], other_ref),), sem)
     core = core_ref[0]
 
     def put(block, peer, side):
@@ -297,7 +302,6 @@
 
     for peer in range(PEERS):
         put(own_ref[peer, :F_ROWS], peer, core)
-        put(other_ref[peer, :F_ROWS], peer, 1 - core)
         y, xx = peer // NX, peer % NX
         tail = own_ref[peer, 288:320].astype(f32)
         for g in range(4):
@@ -307,6 +311,9 @@
                 for h in range(2):
                     at = (y * TR + 2 * g + h + 1) * 128 + xx * 32 + side * TC
                     strips[at : at + TC] = value[h * TC : (h + 1) * TC]
+    copies[0].wait()
+    for peer in range(PEERS):
+        put(other_ref[peer], peer, 1 - core)
     z = z_ref[0]
     for start, peer, there in ((0, jnp.maximum(z - 1, 0), z > 0),
                                ((ROWS + 1) * 128, jnp.minimum(z + 1, NZ - 1), z < NZ - 1)):
@@ -350,9 +357,8 @@
         out_ref[z, W_ROWS:] = block
 
 
-def final_kernel(core_ref, got_ref, other_ref, feat_hbm, da_ref, row_ref, gain_ref,
-                 grad_ref, weight_ref, gain_grad_ref, shift_grad_ref, bias_ref, feat_ref, sem):
-    copies = fetch(((feat_hbm, feat_ref),), sem)
+def final_kernel(core_ref, got_ref, other_ref, both_ref, da_ref, row_ref, gain_ref,
+                 grad_ref, gain_grad_ref, shift_grad_ref, bias_ref):
 
     def half(ref):
         total = jnp.zeros((8, 128), f32)
@@ -372,9 +378,11 @@
     both = jnp.concatenate([gain * sums[0], gain * sums[1], jnp.zeros((6, C), f32)], axis=0)
     both = exact_dot(exact_dot(both, groups, 0), groups, 1) / TOTAL
     first, second = both[0:1], both[1:2]
-    copies[0].wait()
-    xhat = (feat_ref[...].astype(f32) - mean) * rstd
+    xhat = (both_ref[:PIX].astype(f32) - mean) * rstd
     grad_ref[...] = (rstd * (da_ref[...] * gain - first - xhat * second)).astype(bf16)
+
+
+def gather_kernel(got_ref, weight_ref):
     weight = got_ref[0, :W_ROWS].astype(f32)
     for z in range(1, NZ):
         weight = weight + got_ref[z, :W_ROWS].astype(f32)
@@ -400,15 +408,16 @@
     gain, shift = gain.reshape(1, C), shift.reshape(1, C)
     cot2, feat2 = flip(cot), flip(feat)
     both = jnp.concatenate([feat, cot])
-    column = jnp.where(core == 0, cotangent[:, 0], cotangent[:, TC - 1])
     pairs = [(2 * k + 1, 2 * k + 2) for k in range(NX - 1)]
-    outer = lax.ppermute(column, ("x", "core"), pairs + [(b, a) for a, b in pairs])
-    outer2 = flip(outer)
+    beside = lax.ppermute(cot, ("x", "core"), pairs + [(b, a) for a, b in pairs])
+    upper = jnp.where(core == 0, beside[TC - 1 : TC], beside[:1])
+    lower = jnp.where(core == 0, beside[PIX - 1 :], beside[PIX - TC : PIX - TC + 1])
+    corners = flip(jnp.concatenate([upper, lower]))
     spare = jnp.zeros((6, C), bf16)
     edge = jnp.where(
         core == 0,
-        jnp.concatenate([cot[PIX - TC :], cot2[PIX - TC :], outer[TR - 1 :], outer2[TR - 1 :], spare]),
-        jnp.concatenate([cot2[:TC], cot[:TC], outer2[:1], outer[:1], spare]),
+        jnp.concatenate([cot[PIX - TC :], cot2[PIX - TC :], lower, corners[1:], spare]),
+        jnp.concatenate([cot2[:TC], cot[:TC], corners[:1], upper, spare]),
     )
     count = NZ * NY
     ways = [(2 * k, 2 * k + 2) for k in range(count - 1)] + [(2 * k + 3, 2 * k + 1) for k in range(count - 1)]
@@ -418,12 +427,13 @@
         pack_kernel,
         out_shape=(shape((PEERS, G_ROWS, 128), bf16), shape((8, C), f32)),
         in_specs=[smem()] + [vmem()] * 3,
-        out_specs=(vmem(), vmem()),
+        out_specs=(hbm(), vmem()),
+        scratch_shapes=[pltpu.VMEM((PEERS, G_ROWS, 128), bf16), pltpu.SemaphoreType.DMA((2,))],
         compiler_params=params(),
         cost_estimate=pl.CostEstimate(flops=1 << 28, bytes_accessed=2 << 20, transcendentals=0),
         name="pack",
     )(at_core, both, feat2, cot2)
-    packed, outer = lax.optimization_barrier((packed, outer))
+    packed, beside = lax.optimization_barrier((packed, beside))
     slab = lax.all_to_all(packed, ("y", "x"), 0, 0)
     slab, mine = lax.optimization_barrier((slab, mine))
     edges = pl.pallas_call(
@@ -450,34 +460,32 @@
         compiler_params=params(),
         cost_estimate=pl.CostEstimate(flops=2 * PIX * 9 * C * C, bytes_accessed=18 * C * C, transcendentals=0),
         name="back",
-    )(at_core, both, cot2, mine, theirs, outer, conv_weight)
+    )(at_core, both, cot2, mine, theirs, beside, conv_weight)
 
 
     row, da, table, sums = pl.pallas_call(
         sums_kernel,
         out_shape=(shape((8, C), f32), shape((PIX, C), f32), shape((8, 256), f32), shape((2 * PEERS, 8, 128), f32)),
-        in_specs=[smem(), vmem(), hbm(), vmem(), vmem(), vmem(), vmem()],
+        in_specs=[smem()] + [vmem()] * 6,
         out_specs=(vmem(), vmem(), vmem(), vmem()),
-        scratch_shapes=[
-            pltpu.VMEM((16, 128), f32),
-            pltpu.VMEM((PIX, C), bf16),
-            pltpu.SemaphoreType.DMA((1,)),
-        ],
+        scratch_shapes=[pltpu.VMEM((16, 128), f32)],
         compiler_params=params(),
         name="sums",
-    )(at_y, edges, feat, back, gain, shift, bias)
+    )(at_y, edges, both, back, gain, shift, bias)
     sums = lax.all_to_all(sums, ("y", "x", "core"), 0, 0)
 
     terms = pl.pallas_call(
         terms_kernel,
         out_shape=shape((NZ, W_ROWS, 256), bf16),
-        in_specs=[smem()] * 2 + [vmem()] * 4,
+        in_specs=[smem()] * 2 + [vmem(), hbm(), vmem(), vmem()],
         out_specs=vmem(),
         scratch_shapes=[
             pltpu.VMEM((ROWS * 128, 256), bf16),
             pltpu.VMEM(((ROWS + 2) * 128, 128), bf16),
             pltpu.VMEM((256, (ROWS + 2) * 128), bf16),
             pltpu.VMEM((NZ, 16, 256), f32),
+            pltpu.VMEM((PEERS, F_ROWS, 128), bf16),
+            pltpu.SemaphoreType.DMA((1,)),
         ],
         compiler_params=params(),
         cost_estimate=pl.CostEstimate(
@@ -495,15 +503,23 @@
         name="join",
     )(sums, terms)
     joined = lax.all_to_all(joined, "z", 0, 0)
-    grad, weight_grad, gain_grad, shift_grad, bias_grad = pl.pallas_call(
+    weight_grad = pl.pallas_call(
+        gather_kernel,
+        out_shape=shape((3, 3, 20, NQ), f32),
+        in_specs=[vmem()],
+        out_specs=vmem(),
+        compiler_params=params(),
+        cost_estimate=pl.CostEstimate(flops=1 << 22, bytes_accessed=1 << 20, transcendentals=0),
+        name="gather",
+    )(joined)
+    grad, gain_grad, shift_grad, bias_grad = pl.pallas_call(
         final_kernel,
-        out_shape=(shape((PIX, C), bf16), shape((3, 3, 20, NQ), f32)) + (shape((C,), f32),) * 3,
-        in_specs=[smem(), vmem(), vmem(), hbm(), vmem(), vmem(), vmem()],
-        out_specs=(vmem(),) * 5,
-        scratch_shapes=[pltpu.VMEM((PIX, C), bf16), pltpu.SemaphoreType.DMA((1,))],
+        out_shape=(shape((PIX, C), bf16),) + (shape((C,), f32),) * 3,
+        in_specs=[smem()] + [vmem()] * 6,
+        out_specs=(vmem(),) * 4,
         compiler_params=params(),
         name="final",
-    )(at_core, joined, flip(joined), feat, da, row, gain)
+    )(at_core, joined, flip(joined), both, da, row, gain)
     return grad.reshape(features.shape), weight_grad, gain_grad, shift_grad, bias_grad
 
 

time: 95 us -> 91.5 us (0.963)
  waiting for transfers between devices: 31.2 us -> 28.2 us
  starting transfers between devices: 27.6 us -> 28.6 us
  local copies, waits for them, and re-layouts: 1.89 us -> 0.91 us
    all_to_all x1, waiting for transfers between devices: 13.5 us -> 10.8 us  [body(): slab = lax.all_to_all(packed, ('y', 'x'), 0, 0)]
    ppermute x6, starting transfers between devices: 5.83 us -> 8 us  [flip(): return lax.ppermute(value, 'core', [(0, 1), (1, 0)])]
    ppermute x1, waiting for transfers between devices: 0.01 us -> 1.55 us  [body(): lax.ppermute(cot, ('x', 'core'), pairs + [(b, a) for a, b in pairs])]
    all_to_all x1, starting transfers between devices: 6.22 us -> 5.04 us  [body(): slab = lax.all_to_all(packed, ('y', 'x'), 0, 0)]
    ppermute x6, waiting for transfers between devices: 3.34 us -> 2.25 us  [flip(): return lax.ppermute(value, 'core', [(0, 1), (1, 0)])]
    ppermute x1, waiting for transfers between devices: 7.36 us -> 6.38 us  [body(): mine = lax.ppermute(edge, ('z', 'y', 'core'), ways)]
    slice x3 -> x1, local copies, waits for them, and re-layouts: 0.97 us -> 0.01 us  [body(): corners[:1]]
  transfers between devices with their start and end apart: 11 -> 11, of which waited for: 7 -> 8; matrix products, arithmetic and copies ran while one was open for 3% -> 2% of each run, Pallas kernels for 16% -> 17%
where the time goes in v6:
time: 91.5 us; the launch traced here: 91 us
  starting transfers between devices  28.6 us (31%)
  waiting for transfers between devices  28.2 us (31%)
  Pallas kernels  16.2 us (18%)
  blocking collectives  15.2 us (17%)
  other arithmetic  1.06 us (1%)
    all_to_all x1, blocking collectives, body(): joined = lax.all_to_all(joined, 'z', 0, 0)  15.2 us
    all_to_all x1, waiting for transfers between devices, body(): slab = lax.all_to_all(packed, ('y', 'x'), 0, 0)  10.8 us
    all_to_all x1, starting transfers between devices, body(): edges = lax.all_to_all(edges, 'z', 0, 0)  8.18 us
    ppermute x6, starting transfers between devices, flip(): return lax.ppermute(value, 'core', [(0, 1), (1, 0)])  8 us
    ppermute x1, waiting for transfers between devices, body(): mine = lax.ppermute(edge, ('z', 'y', 'core'), ways)  6.38 us
    pallas_call x1, Pallas kernels, body(): pl.pallas_call(back_kernel, out_shape=shape((PIX, C), f32), in_specs=[sme...  5.68 us
    all_to_all x1, starting transfers between devices, body(): slab = lax.all_to_all(packed, ('y', 'x'), 0, 0)  5.04 us
    pallas_call x1, Pallas kernels, body(): pl.pallas_call(terms_kernel, out_shape=shape((NZ, W_ROWS, 256), bf16), in...  4.4 us
  transfers between devices with their start and end apart: 11, of which 8 were waited for; matrix products, arithmetic and copies ran while one was open for 2% of the time, Pallas kernels for 17%

profile of v6, /device:TPU:1, one launch (start us, length us, event | category | flops | bytes accessed | tf_op | source)
XLA Modules:
  0.0 91.0 jit_solution(2842683230393699217)
XLA Ops:
  0.6 3.3 %collective-permute-start = (bf16[128,640]{1,0:T(8,128)(2,1)}, bf16[128,640]{1,0:T(8,128)(2,1)S(1)}, u32[]{:S(2)}, u32[]{:S(2)}) collective-permute-start(bf16[128,640]{1,0:T(8,128)(2,1)} %bitcast.13), channel_id=1, source_target_pairs={{0,1},{1,0},{2,3},{3,2},{4,5},{5,4},{6,7},{7,6},{8,9},{9,8},{10,11... | collective-permute-start | bytes 491528 | tf_op jit(solution)/shard_map/ppermute | solution.py:397
  4.0 0.1 collective-permute-start.1
  4.1 1.9 %collective-permute-start.2 = (bf16[128,640]{1,0:T(8,128)(2,1)}, bf16[128,640]{1,0:T(8,128)(2,1)S(1)}, u32[]{:S(2)}, u32[]{:S(2)}) collective-permute-start(bf16[128,640]{1,0:T(8,128)(2,1)} %bitcast.11), channel_id=1, source_target_pairs={{1,2},{3,4},{5,6},{2,1},{4,3},{6,5},{9,10},{11,12},{13,14},{10,9},... | collective-permute-start | bytes 491528 | tf_op jit(solution)/shard_map/ppermute | solution.py:412
  6.0 1.0 %pad_maximum_fusion.both_ref = bf16[256,640]{1,0:T(8,128)(2,1)S(1)} fusion(bf16[128,640]{1,0:T(8,128)(2,1)} %bitcast.12, bf16[128,640]{1,0:T(8,128)(2,1)} %bitcast.14), kind=kLoop, calls=%fused_computation | loop fusion | flops 655360 | bytes 655360 | tf_op jit(solution)/shard_map/concatenate | solution.py:410
  7.0 0.0 collective-permute-done.feat2_ref
  7.0 0.0 collective-permute-done.1.cot2_ref
  7.0 2.3 %pack.1 = (bf16[16,336,128]{2,1,0:T(8,128)(2,1)}, f32[8,640]{1,0:T(8,128)S(1)}) custom-call(s32[1]{0:T(128)} %bitcast.core_ref, bf16[256,640]{1,0:T(8,128)(2,1)S(1)} %pad_maximum_fusion.both_ref, bf16[128,640]{1,0:T(8,128)(2,1)S(1)} %collective-permute-done.feat2_ref, bf16[128,640]{1,0:T(8,128)(2,1)S(1)} %collective-permute-done.1.cot2_ref), custom_call_target="tpu_custom_call" | custom-call | flops 268435456 | bytes 2097152 | tf_op jit(solution)/shard_map/pack/pallas_call | solution.py:426
  9.3 1.5 %collective-permute-done.2.beside_ref = bf16[128,640]{1,0:T(8,128)(2,1)S(1)} collective-permute-done((bf16[128,640]{1,0:T(8,128)(2,1)}, bf16[128,640]{1,0:T(8,128)(2,1)S(1)}, u32[]{:S(2)}, u32[]{:S(2)}) %collective-permute-start.2) | collective-permute-done | bytes 163872 | tf_op jit(solution)/shard_map/ppermute | solution.py:412
  10.9 5.0 %all-to-all-start = ((bf16[16,336,128]{2,1,0:T(8,128)(2,1)}), bf16[16,336,128]{2,1,0:T(8,128)(2,1)S(1)}, u32[]{:S(2)}, u32[]{:S(2)}) async-start(bf16[16,336,128]{2,1,0:T(8,128)(2,1)} %get-tuple-element.20), calls=%async_computation | async-start | bytes 2752512 | tf_op jit(solution)/shard_map/all_to_all | solution.py:437
  15.9 0.0 copy-start
  16.0 0.0 copy-start.1
  16.0 0.8 slice_bitcast_fusion
  16.8 0.8 collective-permute-start.3
  17.5 0.8 collective-permute-done.3
  18.4 0.1 concatenate.15
  18.4 0.1 concatenate.14
  18.5 1.3 %collective-permute-start.4 = (bf16[40,640]{1,0:T(8,128)(2,1)S(1)}, bf16[40,640]{1,0:T(8,128)(2,1)S(1)}, u32[]{:S(2)}, u32[]{:S(2)}) collective-permute-start(bf16[40,640]{1,0:T(8,128)(2,1)S(1)} %broadcast_select_fusion), channel_id=1, source_target_pairs={{0,8},{8,16},{16,24},{24,32},{32,40},{40,48},{48,56},{56,64},{64,7... | collective-permute-start | bytes 153608 | tf_op jit(solution)/shard_map/ppermute | solution.py:424
  19.8 6.4 %collective-permute-done.4.mine_ref = bf16[40,640]{1,0:T(8,128)(2,1)S(1)} collective-permute-done((bf16[40,640]{1,0:T(8,128)(2,1)S(1)}, bf16[40,640]{1,0:T(8,128)(2,1)S(1)}, u32[]{:S(2)}, u32[]{:S(2)}) %collective-permute-start.4) | collective-permute-done | bytes 51232 | tf_op jit(solution)/shard_map/ppermute | solution.py:424
  26.2 10.8 %all-to-all-done.slab_ref.own_ref = bf16[16,336,128]{2,1,0:T(8,128)(2,1)S(1)} async-done(((bf16[16,336,128]{2,1,0:T(8,128)(2,1)}), bf16[16,336,128]{2,1,0:T(8,128)(2,1)S(1)}, u32[]{:S(2)}, u32[]{:S(2)}) %all-to-all-start) | async-done | bytes 1376288 | tf_op jit(solution)/shard_map/all_to_all | solution.py:437
  37.0 2.0 %collective-permute-start.6 = (bf16[16,336,128]{2,1,0:T(8,128)(2,1)S(1)}, bf16[16,336,128]{2,1,0:T(8,128)(2,1)}, u32[]{:S(2)}, u32[]{:S(2)}) collective-permute-start(bf16[16,336,128]{2,1,0:T(8,128)(2,1)S(1)} %all-to-all-done.slab_ref.own_ref), channel_id=1, source_target_pairs={{0,1},{1,0},{2,3},{3,2},{4,5},{5,4},{6,7},{7,6},{8,9},{9,8},{10,11... | collective-permute-start | bytes 4128776 | tf_op jit(solution)/shard_map/ppermute | solution.py:397
  39.0 0.8 split.1
  39.9 8.2 %all-to-all-start.1 = ((bf16[8,96,128]{2,1,0:T(8,128)(2,1)}), bf16[8,96,128]{2,1,0:T(8,128)(2,1)S(1)}, u32[]{:S(2)}, u32[]{:S(2)}) async-start(bf16[8,96,128]{2,1,0:T(8,128)(2,1)} %split.1), calls=%async_computation.1 | async-start | bytes 393216 | tf_op jit(solution)/shard_map/all_to_all | solution.py:448
  48.0 0.3 collective-permute-start.5
  48.3 0.0 copy-done
  48.3 0.0 copy-done.1
  48.4 0.9 %collective-permute-done.5.theirs_ref = bf16[40,640]{1,0:T(8,128)(2,1)S(1)} collective-permute-done((bf16[40,640]{1,0:T(8,128)(2,1)S(1)}, bf16[40,640]{1,0:T(8,128)(2,1)S(1)}, u32[]{:S(2)}, u32[]{:S(2)}) %collective-permute-start.5) | collective-permute-done | bytes 51232 | tf_op jit(solution)/shard_map/ppermute | solution.py:397
  49.3 5.7 %back.1.back_ref = f32[128,640]{1,0:T(8,128)S(1)} custom-call(s32[1]{0:T(128)} %bitcast.core_ref, bf16[256,640]{1,0:T(8,128)(2,1)S(1)} %pad_maximum_fusion.both_ref, bf16[128,640]{1,0:T(8,128)(2,1)S(1)} %collective-permute-done.1.cot2_ref, bf16[40,640]{1,0:T(8,128)(2,1)S(1)} %collective-permute-done.4.mine_ref, ...), custom_call_target="tpu_custom_call" | custom-call | flops 943718400 | bytes 7372800 | tf_op jit(solution)/shard_map/back/pallas_call | solution.py:450
  55.0 3.9 %all-to-all-done.1.stat_ref.edge_ref = bf16[8,96,128]{2,1,0:T(8,128)(2,1)S(1)} async-done(((bf16[8,96,128]{2,1,0:T(8,128)(2,1)}), bf16[8,96,128]{2,1,0:T(8,128)(2,1)S(1)}, u32[]{:S(2)}, u32[]{:S(2)}) %all-to-all-start.1) | async-done | bytes 196640 | tf_op jit(solution)/shard_map/all_to_all | solution.py:448
  58.9 1.1 %sums.1 = (f32[8,640]{1,0:T(8,128)S(1)}, f32[128,640]{1,0:T(8,128)S(1)}, f32[8,256]{1,0:T(8,128)S(1)}, f32[32,8,128]{2,1,0:T(8,128)}) custom-call(s32[1]{0:T(128)} %bitcast.1.y_ref, bf16[8,96,128]{2,1,0:T(8,128)(2,1)S(1)} %all-to-all-done.1.stat_ref.edge_ref, bf16[256,640]{1,0:T(8,128)(2,1)S(1)} %pad_maximum_fusion.both_ref, f32[128,640]{1,0:T(8,128)S(1)} %back.1.back_ref, ...), custom_call_target="tpu_custom_call" | custom-call | tf_op jit(solution)/shard_map/sums/pallas_call | solution.py:466
  59.9 4.1 %all-to-all-start.2 = ((f32[32,8,128]{2,1,0:T(8,128)}), f32[32,8,128]{2,1,0:T(8,128)S(1)}, u32[]{:S(2)}, u32[]{:S(2)}) async-start(f32[32,8,128]{2,1,0:T(8,128)} %get-tuple-element.25), calls=%async_computation.2 | async-start | bytes 262144 | tf_op jit(solution)/shard_map/all_to_all | solution.py:475
  64.1 0.0 collective-permute-done.6.other_hbm
  64.1 4.4 %terms.1.terms_ref = bf16[8,64,256]{2,1,0:T(8,128)(2,1)S(1)} custom-call(s32[1]{0:T(128)} %bitcast.core_ref, s32[1]{0:T(128)} %bitcast.2.z_ref, bf16[16,336,128]{2,1,0:T(8,128)(2,1)S(1)} %all-to-all-done.slab_ref.own_ref, bf16[16,336,128]{2,1,0:T(8,128)(2,1)} %collective-permute-done.6.other_hbm, bf16[8,96,128]{2,1,0:T(8,128)(2,1)S(1)} %all-to-all-done.1.stat_ref.edge_ref, ...), custom_call_target="tpu_custom_call" | custom-call | flops 943718400 | bytes 4194304 | tf_op jit(solution)/shard_map/terms/pallas_call | solution.py:477
  68.5 3.3 %all-to-all-done.2.sums_ref = f32[32,8,128]{2,1,0:T(8,128)S(1)} async-done(((f32[32,8,128]{2,1,0:T(8,128)}), f32[32,8,128]{2,1,0:T(8,128)S(1)}, u32[]{:S(2)}, u32[]{:S(2)}) %all-to-all-start.2) | async-done | bytes 131104 | tf_op jit(solution)/shard_map/all_to_all | solution.py:475
  71.9 15.2 %all_to_all.20.got_ref = bf16[8,80,256]{2,1,0:T(8,128)(2,1)S(1)} all-to-all(bf16[8,80,256]{2,1,0:T(8,128)(2,1)S(1)} %join.1), channel_id=1, replica_groups=mesh['z'=8,'y'=4,'x'=4,'core'=2] {'z'}, dimensions={0} | all-to-all | bytes 655360 | tf_op jit(solution)/shard_map/all_to_all | solution.py:505
  87.1 1.5 %collective-permute-start.7 = (bf16[8,80,256]{2,1,0:T(8,128)(2,1)S(1)}, bf16[8,80,256]{2,1,0:T(8,128)(2,1)S(1)}, u32[]{:S(2)}, u32[]{:S(2)}) collective-permute-start(bf16[8,80,256]{2,1,0:T(8,128)(2,1)S(1)} %all_to_all.20.got_ref), channel_id=1, source_target_pairs={{0,1},{1,0},{2,3},{3,2},{4,5},{5,4},{6,7},{7,6},{8,9},{9,8},{10,11... | collective-permute-start | bytes 983048 | tf_op jit(solution)/shard_map/ppermute | solution.py:397
  88.6 0.8 gather.1
  89.4 0.5 collective-permute-done.7.other_ref
  89.9 1.1 %final.1 = (bf16[128,640]{1,0:T(8,128)(2,1)}, f32[640]{0:T(1024)}, f32[640]{0:T(1024)}, f32[640]{0:T(1024)}) custom-call(s32[1]{0:T(128)} %bitcast.core_ref, bf16[8,80,256]{2,1,0:T(8,128)(2,1)S(1)} %all_to_all.20.got_ref, bf16[8,80,256]{2,1,0:T(8,128)(2,1)S(1)} %collective-permute-done.7.other_ref, bf16[256,640]{1,0:T(8,128)(2,1)S(1)} %pad_maximum_fusion.both_ref, ...), custom_call_target="tpu_custom_call" | custom-call | tf_op jit(solution)/shard_map/final/pallas_call | solution.py:515
  (9 shorter events, 0.1 us)
Async XLA Ops:
  0.6 6.4 %collective-permute-start = (bf16[128,640]{1,0:T(8,128)(2,1)}, bf16[128,640]{1,0:T(8,128)(2,1)S(1)}, u32[]{:S(2)}, u32[]{:S(2)}) collective-permute-start(bf16[128,640]{1,0:T(8,128)(2,1)} %bitcast.13), channel_id=1, source_target_pairs={{0,1},{1,0},{2,3},{3,2},{4,5},{5,4},{6,7},{7,6},{8,9},{9,8},{10,11... | collective-permute-start | bytes 491528 | tf_op jit(solution)/shard_map/ppermute | solution.py:397
  4.0 3.1 %collective-permute-start.1 = (bf16[128,640]{1,0:T(8,128)(2,1)}, bf16[128,640]{1,0:T(8,128)(2,1)S(1)}, u32[]{:S(2)}, u32[]{:S(2)}) collective-permute-start(bf16[128,640]{1,0:T(8,128)(2,1)} %bitcast.10), channel_id=1, source_target_pairs={{0,1},{1,0},{2,3},{3,2},{4,5},{5,4},{6,7},{7,6},{8,9},{9,8},{10,11... | collective-permute-start | bytes 491528 | tf_op jit(solution)/shard_map/ppermute | solution.py:397
  4.1 6.8 %collective-permute-start.2 = (bf16[128,640]{1,0:T(8,128)(2,1)}, bf16[128,640]{1,0:T(8,128)(2,1)S(1)}, u32[]{:S(2)}, u32[]{:S(2)}) collective-permute-start(bf16[128,640]{1,0:T(8,128)(2,1)} %bitcast.11), channel_id=1, source_target_pairs={{1,2},{3,4},{5,6},{2,1},{4,3},{6,5},{9,10},{11,12},{13,14},{10,9},... | collective-permute-start | bytes 491528 | tf_op jit(solution)/shard_map/ppermute | solution.py:412
  10.9 26.1 %all-to-all-start = ((bf16[16,336,128]{2,1,0:T(8,128)(2,1)}), bf16[16,336,128]{2,1,0:T(8,128)(2,1)S(1)}, u32[]{:S(2)}, u32[]{:S(2)}) async-start(bf16[16,336,128]{2,1,0:T(8,128)(2,1)} %get-tuple-element.20), calls=%async_computation | async-start | bytes 2752512 | tf_op jit(solution)/shard_map/all_to_all | solution.py:437
  15.9 32.4 %copy-start = (f32[640]{0:T(1024)S(1)}, f32[640]{0:T(1024)}, u32[]{:S(2)}) copy-start(f32[640]{0:T(1024)} %param.8) | copy-start | bytes 7684
  16.0 32.4 %copy-start.1 = (f32[640]{0:T(1024)S(1)}, f32[640]{0:T(1024)}, u32[]{:S(2)}) copy-start(f32[640]{0:T(1024)} %param.9) | copy-start | bytes 7684
  16.8 1.6 %collective-permute-start.3 = (bf16[2,640]{1,0:T(2,128)(2,1)S(1)}, bf16[2,640]{1,0:T(2,128)(2,1)S(1)}, u32[]{:S(2)}, u32[]{:S(2)}) collective-permute-start(bf16[2,640]{1,0:T(2,128)(2,1)S(1)} %pad_maximum_fusion.1), channel_id=1, source_target_pairs={{0,1},{1,0},{2,3},{3,2},{4,5},{5,4},{6,7},{7,6},{8,9},{9,8},{10,11... | collective-permute-start | bytes 7688 | tf_op jit(solution)/shard_map/ppermute | solution.py:397
  18.5 7.7 %collective-permute-start.4 = (bf16[40,640]{1,0:T(8,128)(2,1)S(1)}, bf16[40,640]{1,0:T(8,128)(2,1)S(1)}, u32[]{:S(2)}, u32[]{:S(2)}) collective-permute-start(bf16[40,640]{1,0:T(8,128)(2,1)S(1)} %broadcast_select_fusion), channel_id=1, source_target_pairs={{0,8},{8,16},{16,24},{24,32},{32,40},{40,48},{48,56},{56,64},{64,7... | collective-permute-start | bytes 153608 | tf_op jit(solution)/shard_map/ppermute | solution.py:424
  37.0 27.1 %collective-permute-start.6 = (bf16[16,336,128]{2,1,0:T(8,128)(2,1)S(1)}, bf16[16,336,128]{2,1,0:T(8,128)(2,1)}, u32[]{:S(2)}, u32[]{:S(2)}) collective-permute-start(bf16[16,336,128]{2,1,0:T(8,128)(2,1)S(1)} %all-to-all-done.slab_ref.own_ref), channel_id=1, source_target_pairs={{0,1},{1,0},{2,3},{3,2},{4,5},{5,4},{6,7},{7,6},{8,9},{9,8},{10,11... | collective-permute-start | bytes 4128776 | tf_op jit(solution)/shard_map/ppermute | solution.py:397
  39.9 19.0 %all-to-all-start.1 = ((bf16[8,96,128]{2,1,0:T(8,128)(2,1)}), bf16[8,96,128]{2,1,0:T(8,128)(2,1)S(1)}, u32[]{:S(2)}, u32[]{:S(2)}) async-start(bf16[8,96,128]{2,1,0:T(8,128)(2,1)} %split.1), calls=%async_computation.1 | async-start | bytes 393216 | tf_op jit(solution)/shard_map/all_to_all | solution.py:448
  48.0 1.2 %collective-permute-start.5 = (bf16[40,640]{1,0:T(8,128)(2,1)S(1)}, bf16[40,640]{1,0:T(8,128)(2,1)S(1)}, u32[]{:S(2)}, u32[]{:S(2)}) collective-permute-start(bf16[40,640]{1,0:T(8,128)(2,1)S(1)} %collective-permute-done.4.mine_ref), channel_id=1, source_target_pairs={{0,1},{1,0},{2,3},{3,2},{4,5},{5,4},{6,7},{7,6},{8,9},{9,8},{10,11... | collective-permute-start | bytes 153608 | tf_op jit(solution)/shard_map/ppermute | solution.py:397
  59.9 11.9 %all-to-all-start.2 = ((f32[32,8,128]{2,1,0:T(8,128)}), f32[32,8,128]{2,1,0:T(8,128)S(1)}, u32[]{:S(2)}, u32[]{:S(2)}) async-start(f32[32,8,128]{2,1,0:T(8,128)} %get-tuple-element.25), calls=%async_computation.2 | async-start | bytes 262144 | tf_op jit(solution)/shard_map/all_to_all | solution.py:475
  87.1 2.8 %collective-permute-start.7 = (bf16[8,80,256]{2,1,0:T(8,128)(2,1)S(1)}, bf16[8,80,256]{2,1,0:T(8,128)(2,1)S(1)}, u32[]{:S(2)}, u32[]{:S(2)}) collective-permute-start(bf16[8,80,256]{2,1,0:T(8,128)(2,1)S(1)} %all_to_all.20.got_ref), channel_id=1, source_target_pairs={{0,1},{1,0},{2,3},{3,2},{4,5},{5,4},{6,7},{7,6},{8,9},{9,8},{10,11... | collective-permute-start | bytes 983048 | tf_op jit(solution)/shard_map/ppermute | solution.py:397

commit v7 on v6

--- a/solution.py
+++ b/solution.py
@@ -216,25 +216,19 @@
             out_ref[p, 80:] = first
 
 
-def back_kernel(core_ref, both_ref, cot2_ref, mine_ref, theirs_ref, beside_ref, w_hbm, out_ref, shifted, w_ref, sem):
+def back_kernel(core_ref, both_ref, cot2_ref, mine_ref, theirs_ref, w_hbm, out_ref, shifted, w_ref, sem):
     copies = fetch([(w_hbm.at[t // 3, t % 3], w_ref.at[t]) for t in range(9)], sem)
     rows = (TR + 2) * TC
     lower = core_ref[0] == 0
     mine, theirs = mine_ref[...].astype(f32), theirs_ref[...].astype(f32)
     top, bottom = jnp.where(lower, mine, theirs), jnp.where(lower, theirs, mine)
-    corner = 2 * TC
-    own_top, other_top = jnp.where(lower, top[:TC], top[TC:corner]), jnp.where(lower, top[TC:corner], top[:TC])
-    own_bot, other_bot = jnp.where(lower, bottom[:TC], bottom[TC:corner]), jnp.where(lower, bottom[TC:corner], bottom[:TC])
+    own_top, other_top = jnp.where(lower, top[:TC], top[TC:]), jnp.where(lower, top[TC:], top[:TC])
+    own_bot, other_bot = jnp.where(lower, bottom[:TC], bottom[TC:]), jnp.where(lower, bottom[TC:], bottom[:TC])
     wide = jnp.concatenate([own_top, both_ref[PIX:].astype(f32), own_bot], axis=0)
     near = jnp.concatenate([other_top, cot2_ref[...].astype(f32), other_bot], axis=0)
     near = near.reshape(TR + 2, TC, C)
     inner = jnp.where(lower, near[:, :1], near[:, TC - 1 :])
-    top_corner = jnp.where(lower, top[corner : corner + 1], top[corner + 1 : corner + 2])
-    bot_corner = jnp.where(lower, bottom[corner : corner + 1], bottom[corner + 1 : corner + 2])
-    beside = beside_ref[...].astype(f32).reshape(TR, TC, C)
-    outer = jnp.where(lower, beside[:, TC - 1 :], beside[:, :1])
-    outer = jnp.concatenate([top_corner[None], outer, bot_corner[None]], axis=0)
-    left, right = jnp.where(lower, outer, inner), jnp.where(lower, inner, outer)
+    left, right = jnp.where(lower, 0.0, inner), jnp.where(lower, inner, 0.0)
     left = jnp.broadcast_to(left, (TR + 2, TC, C)).reshape(rows, C)
     right = jnp.broadcast_to(right, (TR + 2, TC, C)).reshape(rows, C)
     col = lax.broadcasted_iota(jnp.int32, (rows, C), 0) % TC
@@ -252,7 +246,28 @@
     out_ref[...] = total.T
 
 
-def sums_kernel(y_ref, stat_ref, both_ref, back_ref, gain_ref, shift_ref, bias_ref,
+def side_kernel(core_ref, both_ref, mine_ref, theirs_ref, w_hbm, out_ref, w_ref, sem):
+    j = 2 * core_ref[0]
+    copies = fetch([(w_hbm.at[i, j], w_ref.at[i]) for i in range(3)], sem)
+    lower = core_ref[0] == 0
+    tile = both_ref[PIX:].astype(f32).reshape(TR, TC, C)
+    tile = jnp.where(lower, tile[:, :1], tile[:, TC - 1 :])
+    mine, theirs = mine_ref[...].astype(f32), theirs_ref[...].astype(f32)
+    mine = jnp.where(lower, mine[:1], mine[2 * TC - 1 :])
+    theirs = jnp.where(lower, theirs[:1], theirs[2 * TC - 1 :])
+    top, bottom = jnp.where(lower, mine, theirs), jnp.where(lower, theirs, mine)
+    column = jnp.concatenate([top[None], tile, bottom[None]], axis=0)
+    total = jnp.zeros((TR, C), f32)
+    for i in range(3):
+        copies[i].wait()
+        pixels = column[2 - i : 2 - i + TR].reshape(TR, C).astype(bf16)
+        total = total + lax.dot_general(
+            pixels, w_ref[i], (((1,), (1,)), ((), ())), preferred_element_type=f32
+        )
+    out_ref[...] = total
+
+
+def sums_kernel(core_ref, y_ref, stat_ref, both_ref, back_ref, side_ref, gain_ref, shift_ref, bias_ref,
                 row_ref, da_ref, par_ref, out_ref, block):
     mean, squares = merge_pieces(stat_ref[:, :S_ROWS], PEERS * CHIP)
     groups = group_matrix()
@@ -267,7 +282,10 @@
     xhat = (both_ref[:PIX].astype(f32) - mean) * rstd
     act = xhat * gain + shift
     sig = jax.nn.sigmoid(act)
-    da = back_ref[...] * sig * (1.0 + act * (1.0 - sig))
+    column = lax.broadcasted_iota(jnp.int32, (TR, TC, C), 1)
+    side = jnp.broadcast_to(side_ref[...][:, None, :], (TR, TC, C))
+    side = jnp.where(column == core_ref[0] * (TC - 1), side, 0.0).reshape(PIX, C)
+    da = (back_ref[...] + side) * sig * (1.0 + act * (1.0 - sig))
     da_ref[...] = da
     sums = (da.sum(0, keepdims=True), (da * xhat).sum(0, keepdims=True), bias_ref[:1])
     block[...] = jnp.zeros_like(block)
@@ -408,16 +426,10 @@
     gain, shift = gain.reshape(1, C), shift.reshape(1, C)
     cot2, feat2 = flip(cot), flip(feat)
     both = jnp.concatenate([feat, cot])
-    pairs = [(2 * k + 1, 2 * k + 2) for k in range(NX - 1)]
-    beside = lax.ppermute(cot, ("x", "core"), pairs + [(b, a) for a, b in pairs])
-    upper = jnp.where(core == 0, beside[TC - 1 : TC], beside[:1])
-    lower = jnp.where(core == 0, beside[PIX - 1 :], beside[PIX - TC : PIX - TC + 1])
-    corners = flip(jnp.concatenate([upper, lower]))
-    spare = jnp.zeros((6, C), bf16)
     edge = jnp.where(
         core == 0,
-        jnp.concatenate([cot[PIX - TC :], cot2[PIX - TC :], lower, corners[1:], spare]),
-        jnp.concatenate([cot2[:TC], cot[:TC], corners[:1], upper, spare]),
+        jnp.concatenate([cot[PIX - TC :], cot2[PIX - TC :]]),
+        jnp.concatenate([cot2[:TC], cot[:TC]]),
     )
     count = NZ * NY
     ways = [(2 * k, 2 * k + 2) for k in range(count - 1)] + [(2 * k + 3, 2 * k + 1) for k in range(count - 1)]
@@ -433,9 +445,20 @@
         cost_estimate=pl.CostEstimate(flops=1 << 28, bytes_accessed=2 << 20, transcendentals=0),
         name="pack",
     )(at_core, both, feat2, cot2)
-    packed, beside = lax.optimization_barrier((packed, beside))
     slab = lax.all_to_all(packed, ("y", "x"), 0, 0)
-    slab, mine = lax.optimization_barrier((slab, mine))
+    theirs = flip(mine)
+    side = pl.pallas_call(
+        side_kernel,
+        out_shape=shape((TR, C), f32),
+        in_specs=[smem()] + [vmem()] * 3 + [hbm()],
+        out_specs=vmem(),
+        scratch_shapes=[pltpu.VMEM((3, C, C), bf16), pltpu.SemaphoreType.DMA((3,))],
+        compiler_params=params(),
+        name="side",
+    )(at_core, both, mine, theirs, conv_weight)
+    slab, side = lax.optimization_barrier((slab, side))
+    pairs = [(2 * k + 1, 2 * k + 2) for k in range(NX - 1)]
+    side = lax.ppermute(side, ("x", "core"), pairs + [(b, a) for a, b in pairs])
     edges = pl.pallas_call(
         split_kernel,
         out_shape=shape((NZ, E_ROWS, 128), bf16),
@@ -446,11 +469,10 @@
     )(at_z, slab)
     slab_other = flip(slab)
     edges = lax.all_to_all(edges, "z", 0, 0)
-    theirs = flip(mine)
     back = pl.pallas_call(
         back_kernel,
         out_shape=shape((PIX, C), f32),
-        in_specs=[smem()] + [vmem()] * 5 + [hbm()],
+        in_specs=[smem()] + [vmem()] * 4 + [hbm()],
         out_specs=vmem(),
         scratch_shapes=[
             pltpu.VMEM((3, (TR + 2) * TC, C), bf16),
@@ -460,18 +482,18 @@
         compiler_params=params(),
         cost_estimate=pl.CostEstimate(flops=2 * PIX * 9 * C * C, bytes_accessed=18 * C * C, transcendentals=0),
         name="back",
-    )(at_core, both, cot2, mine, theirs, beside, conv_weight)
+    )(at_core, both, cot2, mine, theirs, conv_weight)
 
 
     row, da, table, sums = pl.pallas_call(
         sums_kernel,
         out_shape=(shape((8, C), f32), shape((PIX, C), f32), shape((8, 256), f32), shape((2 * PEERS, 8, 128), f32)),
-        in_specs=[smem()] + [vmem()] * 6,
+        in_specs=[smem()] * 2 + [vmem()] * 7,
         out_specs=(vmem(), vmem(), vmem(), vmem()),
         scratch_shapes=[pltpu.VMEM((16, 128), f32)],
         compiler_params=params(),
         name="sums",
-    )(at_y, edges, both, back, gain, shift, bias)
+    )(at_core, at_y, edges, both, back, side, gain, shift, bias)
     sums = lax.all_to_all(sums, ("y", "x", "core"), 0, 0)
 
     terms = pl.pallas_call(

time: 91.5 us -> 91.5 us (level)
  waiting for transfers between devices: 28.2 us -> 24.4 us
  Pallas kernels: 16.2 us -> 18.5 us
  blocking collectives: 15.2 us -> 16.9 us
    all_to_all x1, waiting for transfers between devices: 10.8 us -> 7.88 us  [body(): slab = lax.all_to_all(packed, ('y', 'x'), 0, 0)]
    pallas_call x0 -> x1, Pallas kernels: none -> 2.28 us  [body(): pl.pallas_call(side_kernel, out_shape=shape((TR, C), f32), in_specs=[smem...]
    all_to_all x1, blocking collectives: 15.2 us -> 16.9 us  [body(): joined = lax.all_to_all(joined, 'z', 0, 0)]
    ppermute x1, waiting for transfers between devices: 6.38 us -> 8.01 us  [body(): mine = lax.ppermute(edge, ('z', 'y', 'core'), ways)]
    ppermute x1, waiting for transfers between devices: 1.55 us -> 0.01 us  [body(): side = lax.ppermute(side, ('x', 'core'), pairs + [(b, a) for a, b in pairs])]
    all_to_all x1, starting transfers between devices: 4.13 us -> 5.54 us  [body(): sums = lax.all_to_all(sums, ('y', 'x', 'core'), 0, 0)]
    ppermute x6 -> x5, starting transfers between devices: 8 us -> 6.62 us  [flip(): return lax.ppermute(value, 'core', [(0, 1), (1, 0)])]
    ppermute x6 -> x5, waiting for transfers between devices: 2.25 us -> 2.2 us  [flip(): return lax.ppermute(value, 'core', [(0, 1), (1, 0)])]
  transfers between devices with their start and end apart: 11 -> 10, of which waited for: 8 -> 8; matrix products, arithmetic and copies ran while one was open for 2% -> 2% of each run, Pallas kernels for 17% -> 17%
where the time goes in v7:
time: 91.5 us; the launch traced here: 91 us
  starting transfers between devices  28.6 us (31%)
  waiting for transfers between devices  24.4 us (27%)
  Pallas kernels  18.5 us (20%)
  blocking collectives  16.9 us (18%)
  other arithmetic  1.04 us (1%)
    all_to_all x1, blocking collectives, body(): joined = lax.all_to_all(joined, 'z', 0, 0)  16.9 us
    all_to_all x1, starting transfers between devices, body(): edges = lax.all_to_all(edges, 'z', 0, 0)  8.18 us
    ppermute x1, waiting for transfers between devices, body(): mine = lax.ppermute(edge, ('z', 'y', 'core'), ways)  8.01 us
    all_to_all x1, waiting for transfers between devices, body(): slab = lax.all_to_all(packed, ('y', 'x'), 0, 0)  7.88 us
    ppermute x5, starting transfers between devices, flip(): return lax.ppermute(value, 'core', [(0, 1), (1, 0)])  6.62 us
    pallas_call x1, Pallas kernels, body(): pl.pallas_call(back_kernel, out_shape=shape((PIX, C), f32), in_specs=[sme...  5.69 us
    all_to_all x1, starting transfers between devices, body(): sums = lax.all_to_all(sums, ('y', 'x', 'core'), 0, 0)  5.54 us
    all_to_all x1, starting transfers between devices, body(): slab = lax.all_to_all(packed, ('y', 'x'), 0, 0)  5.03 us
  transfers between devices with their start and end apart: 10, of which 8 were waited for; matrix products, arithmetic and copies ran while one was open for 2% of the time, Pallas kernels for 17%

profile of v7, /device:TPU:1, one launch (start us, length us, event | category | flops | bytes accessed | tf_op | source)
XLA Modules:
  0.0 91.0 jit_solution(12084979232159070937)
XLA Ops:
  0.6 3.3 %collective-permute-start = (bf16[128,640]{1,0:T(8,128)(2,1)}, bf16[128,640]{1,0:T(8,128)(2,1)S(1)}, u32[]{:S(2)}, u32[]{:S(2)}) collective-permute-start(bf16[128,640]{1,0:T(8,128)(2,1)} %bitcast.12), channel_id=1, source_target_pairs={{0,1},{1,0},{2,3},{3,2},{4,5},{5,4},{6,7},{7,6},{8,9},{9,8},{10,11... | collective-permute-start | bytes 491528 | tf_op jit(solution)/shard_map/ppermute | solution.py:415
  4.0 0.1 collective-permute-start.1
  4.1 1.0 %pad_maximum_fusion.both_ref = bf16[256,640]{1,0:T(8,128)(2,1)S(1)} fusion(bf16[128,640]{1,0:T(8,128)(2,1)} %bitcast.11, bf16[128,640]{1,0:T(8,128)(2,1)} %bitcast.13), kind=kLoop, calls=%fused_computation | loop fusion | flops 655360 | bytes 655360 | tf_op jit(solution)/shard_map/concatenate | solution.py:428
  5.1 0.1 collective-permute-done.feat2_ref
  5.2 0.4 collective-permute-done.1.cot2_ref
  5.6 2.3 %pack.1 = (bf16[16,336,128]{2,1,0:T(8,128)(2,1)}, f32[8,640]{1,0:T(8,128)S(1)}) custom-call(s32[1]{0:T(128)} %bitcast.core_ref, bf16[256,640]{1,0:T(8,128)(2,1)S(1)} %pad_maximum_fusion.both_ref, bf16[128,640]{1,0:T(8,128)(2,1)S(1)} %collective-permute-done.feat2_ref, bf16[128,640]{1,0:T(8,128)(2,1)S(1)} %collective-permute-done.1.cot2_ref), custom_call_target="tpu_custom_call" | custom-call | flops 268435456 | bytes 2097152 | tf_op jit(solution)/shard_map/pack/pallas_call | solution.py:438
  7.8 5.0 %all-to-all-start = ((bf16[16,336,128]{2,1,0:T(8,128)(2,1)}), bf16[16,336,128]{2,1,0:T(8,128)(2,1)S(1)}, u32[]{:S(2)}, u32[]{:S(2)}) async-start(bf16[16,336,128]{2,1,0:T(8,128)(2,1)} %get-tuple-element.17), calls=%async_computation | async-start | bytes 2752512 | tf_op jit(solution)/shard_map/all_to_all | solution.py:448
  12.9 0.8 slice_bitcast_fusion
  13.7 1.3 %collective-permute-start.2 = (bf16[32,640]{1,0:T(8,128)(2,1)S(1)}, bf16[32,640]{1,0:T(8,128)(2,1)S(1)}, u32[]{:S(2)}, u32[]{:S(2)}) collective-permute-start(bf16[32,640]{1,0:T(8,128)(2,1)S(1)} %maximum_select_fusion), channel_id=1, source_target_pairs={{0,8},{8,16},{16,24},{24,32},{32,40},{40,48},{48,56},{56,64},{64,7... | collective-permute-start | bytes 122888 | tf_op jit(solution)/shard_map/ppermute | solution.py:436
  15.0 8.0 %collective-permute-done.2.mine_ref = bf16[32,640]{1,0:T(8,128)(2,1)S(1)} collective-permute-done((bf16[32,640]{1,0:T(8,128)(2,1)S(1)}, bf16[32,640]{1,0:T(8,128)(2,1)S(1)}, u32[]{:S(2)}, u32[]{:S(2)}) %collective-permute-start.2) | collective-permute-done | bytes 40992 | tf_op jit(solution)/shard_map/ppermute | solution.py:436
  23.0 0.0 collective-permute-start.3
  23.0 1.2 %collective-permute-done.3.theirs_ref = bf16[32,640]{1,0:T(8,128)(2,1)S(1)} collective-permute-done((bf16[32,640]{1,0:T(8,128)(2,1)S(1)}, bf16[32,640]{1,0:T(8,128)(2,1)S(1)}, u32[]{:S(2)}, u32[]{:S(2)}) %collective-permute-start.3) | collective-permute-done | bytes 40992 | tf_op jit(solution)/shard_map/ppermute | solution.py:415
  24.2 2.3 %side.1 = f32[8,640]{1,0:T(8,128)S(1)} custom-call(s32[1]{0:T(128)} %bitcast.core_ref, bf16[256,640]{1,0:T(8,128)(2,1)S(1)} %pad_maximum_fusion.both_ref, bf16[32,640]{1,0:T(8,128)(2,1)S(1)} %collective-permute-done.2.mine_ref, bf16[32,640]{1,0:T(8,128)(2,1)S(1)} %collective-permute-done.3.theirs_ref, bf16[3,3,640,640]{3,2,1,0:T(8,128)(2,1)} %w_hbm.3), custom_call_target="tpu_custom_call" | custom-call | tf_op jit(solution)/shard_map/side/pallas_call | solution.py:450
  26.5 0.0 copy-start
  26.5 0.0 copy-start.1
  26.5 7.9 %all-to-all-done.slab_ref.own_ref = bf16[16,336,128]{2,1,0:T(8,128)(2,1)S(1)} async-done(((bf16[16,336,128]{2,1,0:T(8,128)(2,1)}), bf16[16,336,128]{2,1,0:T(8,128)(2,1)S(1)}, u32[]{:S(2)}, u32[]{:S(2)}) %all-to-all-start) | async-done | bytes 1376288 | tf_op jit(solution)/shard_map/all_to_all | solution.py:448
  34.4 1.7 %collective-permute-start.5 = (bf16[16,336,128]{2,1,0:T(8,128)(2,1)S(1)}, bf16[16,336,128]{2,1,0:T(8,128)(2,1)}, u32[]{:S(2)}, u32[]{:S(2)}) collective-permute-start(bf16[16,336,128]{2,1,0:T(8,128)(2,1)S(1)} %all-to-all-done.slab_ref.own_ref), channel_id=1, source_target_pairs={{0,1},{1,0},{2,3},{3,2},{4,5},{5,4},{6,7},{7,6},{8,9},{9,8},{10,11... | collective-permute-start | bytes 4128776 | tf_op jit(solution)/shard_map/ppermute | solution.py:415
  36.1 0.8 split.1
  36.9 8.2 %all-to-all-start.1 = ((bf16[8,96,128]{2,1,0:T(8,128)(2,1)}), bf16[8,96,128]{2,1,0:T(8,128)(2,1)S(1)}, u32[]{:S(2)}, u32[]{:S(2)}) async-start(bf16[8,96,128]{2,1,0:T(8,128)(2,1)} %split.1), calls=%async_computation.1 | async-start | bytes 393216 | tf_op jit(solution)/shard_map/all_to_all | solution.py:471
  45.1 0.0 copy-done
  45.1 0.0 copy-done.1
  45.1 1.9 %collective-permute-start.4 = (f32[8,640]{1,0:T(8,128)S(1)}, f32[8,640]{1,0:T(8,128)S(1)}, u32[]{:S(2)}, u32[]{:S(2)}) collective-permute-start(f32[8,640]{1,0:T(8,128)S(1)} %side.1), channel_id=1, source_target_pairs={{1,2},{3,4},{5,6},{2,1},{4,3},{6,5},{9,10},{11,12},{13,14},{10,9},... | collective-permute-start | bytes 61448 | tf_op jit(solution)/shard_map/ppermute | solution.py:461
  47.1 5.7 %back.1.back_ref = f32[128,640]{1,0:T(8,128)S(1)} custom-call(s32[1]{0:T(128)} %bitcast.core_ref, bf16[256,640]{1,0:T(8,128)(2,1)S(1)} %pad_maximum_fusion.both_ref, bf16[128,640]{1,0:T(8,128)(2,1)S(1)} %collective-permute-done.1.cot2_ref, bf16[32,640]{1,0:T(8,128)(2,1)S(1)} %collective-permute-done.2.mine_ref, ...), custom_call_target="tpu_custom_call" | custom-call | flops 943718400 | bytes 7372800 | tf_op jit(solution)/shard_map/back/pallas_call | solution.py:472
  52.8 0.0 collective-permute-done.4.side_ref
  52.8 3.1 %all-to-all-done.1.stat_ref.edge_ref = bf16[8,96,128]{2,1,0:T(8,128)(2,1)S(1)} async-done(((bf16[8,96,128]{2,1,0:T(8,128)(2,1)}), bf16[8,96,128]{2,1,0:T(8,128)(2,1)S(1)}, u32[]{:S(2)}, u32[]{:S(2)}) %all-to-all-start.1) | async-done | bytes 196640 | tf_op jit(solution)/shard_map/all_to_all | solution.py:471
  55.9 1.1 %sums.1 = (f32[8,640]{1,0:T(8,128)S(1)}, f32[128,640]{1,0:T(8,128)S(1)}, f32[8,256]{1,0:T(8,128)S(1)}, f32[32,8,128]{2,1,0:T(8,128)}) custom-call(s32[1]{0:T(128)} %bitcast.core_ref, s32[1]{0:T(128)} %bitcast.1.y_ref, bf16[8,96,128]{2,1,0:T(8,128)(2,1)S(1)} %all-to-all-done.1.stat_ref.edge_ref, bf16[256,640]{1,0:T(8,128)(2,1)S(1)} %pad_maximum_fusion.both_ref, ...), custom_call_target="tpu_custom_call" | custom-call | tf_op jit(solution)/shard_map/sums/pallas_call | solution.py:488
  57.0 5.5 %all-to-all-start.2 = ((f32[32,8,128]{2,1,0:T(8,128)}), f32[32,8,128]{2,1,0:T(8,128)S(1)}, u32[]{:S(2)}, u32[]{:S(2)}) async-start(f32[32,8,128]{2,1,0:T(8,128)} %get-tuple-element.21), calls=%async_computation.2 | async-start | bytes 262144 | tf_op jit(solution)/shard_map/all_to_all | solution.py:497
  62.6 0.0 collective-permute-done.5.other_hbm
  62.6 4.4 %terms.1.terms_ref = bf16[8,64,256]{2,1,0:T(8,128)(2,1)S(1)} custom-call(s32[1]{0:T(128)} %bitcast.core_ref, s32[1]{0:T(128)} %bitcast.2.z_ref, bf16[16,336,128]{2,1,0:T(8,128)(2,1)S(1)} %all-to-all-done.slab_ref.own_ref, bf16[16,336,128]{2,1,0:T(8,128)(2,1)} %collective-permute-done.5.other_hbm, bf16[8,96,128]{2,1,0:T(8,128)(2,1)S(1)} %all-to-all-done.1.stat_ref.edge_ref, ...), custom_call_target="tpu_custom_call" | custom-call | flops 943718400 | bytes 4194304 | tf_op jit(solution)/shard_map/terms/pallas_call | solution.py:499
  67.0 3.2 %all-to-all-done.2.sums_ref = f32[32,8,128]{2,1,0:T(8,128)S(1)} async-done(((f32[32,8,128]{2,1,0:T(8,128)}), f32[32,8,128]{2,1,0:T(8,128)S(1)}, u32[]{:S(2)}, u32[]{:S(2)}) %all-to-all-start.2) | async-done | bytes 131104 | tf_op jit(solution)/shard_map/all_to_all | solution.py:497
  70.2 16.9 %all_to_all.20.got_ref = bf16[8,80,256]{2,1,0:T(8,128)(2,1)S(1)} all-to-all(bf16[8,80,256]{2,1,0:T(8,128)(2,1)S(1)} %join.1), channel_id=1, replica_groups=mesh['z'=8,'y'=4,'x'=4,'core'=2] {'z'}, dimensions={0} | all-to-all | bytes 655360 | tf_op jit(solution)/shard_map/all_to_all | solution.py:527
  87.1 1.5 %collective-permute-start.6 = (bf16[8,80,256]{2,1,0:T(8,128)(2,1)S(1)}, bf16[8,80,256]{2,1,0:T(8,128)(2,1)S(1)}, u32[]{:S(2)}, u32[]{:S(2)}) collective-permute-start(bf16[8,80,256]{2,1,0:T(8,128)(2,1)S(1)} %all_to_all.20.got_ref), channel_id=1, source_target_pairs={{0,1},{1,0},{2,3},{3,2},{4,5},{5,4},{6,7},{7,6},{8,9},{9,8},{10,11... | collective-permute-start | bytes 983048 | tf_op jit(solution)/shard_map/ppermute | solution.py:415
  88.6 0.8 gather.1
  89.4 0.5 collective-permute-done.6.other_ref
  89.9 1.1 %final.1 = (bf16[128,640]{1,0:T(8,128)(2,1)}, f32[640]{0:T(1024)}, f32[640]{0:T(1024)}, f32[640]{0:T(1024)}) custom-call(s32[1]{0:T(128)} %bitcast.core_ref, bf16[8,80,256]{2,1,0:T(8,128)(2,1)S(1)} %all_to_all.20.got_ref, bf16[8,80,256]{2,1,0:T(8,128)(2,1)S(1)} %collective-permute-done.6.other_ref, bf16[256,640]{1,0:T(8,128)(2,1)S(1)} %pad_maximum_fusion.both_ref, ...), custom_call_target="tpu_custom_call" | custom-call | tf_op jit(solution)/shard_map/final/pallas_call | solution.py:537
  (5 shorter events, 0.1 us)
Async XLA Ops:
  0.6 4.6 %collective-permute-start = (bf16[128,640]{1,0:T(8,128)(2,1)}, bf16[128,640]{1,0:T(8,128)(2,1)S(1)}, u32[]{:S(2)}, u32[]{:S(2)}) collective-permute-start(bf16[128,640]{1,0:T(8,128)(2,1)} %bitcast.12), channel_id=1, source_target_pairs={{0,1},{1,0},{2,3},{3,2},{4,5},{5,4},{6,7},{7,6},{8,9},{9,8},{10,11... | collective-permute-start | bytes 491528 | tf_op jit(solution)/shard_map/ppermute | solution.py:415
  4.0 1.6 %collective-permute-start.1 = (bf16[128,640]{1,0:T(8,128)(2,1)}, bf16[128,640]{1,0:T(8,128)(2,1)S(1)}, u32[]{:S(2)}, u32[]{:S(2)}) collective-permute-start(bf16[128,640]{1,0:T(8,128)(2,1)} %bitcast.10), channel_id=1, source_target_pairs={{0,1},{1,0},{2,3},{3,2},{4,5},{5,4},{6,7},{7,6},{8,9},{9,8},{10,11... | collective-permute-start | bytes 491528 | tf_op jit(solution)/shard_map/ppermute | solution.py:415
  7.8 26.5 %all-to-all-start = ((bf16[16,336,128]{2,1,0:T(8,128)(2,1)}), bf16[16,336,128]{2,1,0:T(8,128)(2,1)S(1)}, u32[]{:S(2)}, u32[]{:S(2)}) async-start(bf16[16,336,128]{2,1,0:T(8,128)(2,1)} %get-tuple-element.17), calls=%async_computation | async-start | bytes 2752512 | tf_op jit(solution)/shard_map/all_to_all | solution.py:448
  13.7 9.3 %collective-permute-start.2 = (bf16[32,640]{1,0:T(8,128)(2,1)S(1)}, bf16[32,640]{1,0:T(8,128)(2,1)S(1)}, u32[]{:S(2)}, u32[]{:S(2)}) collective-permute-start(bf16[32,640]{1,0:T(8,128)(2,1)S(1)} %maximum_select_fusion), channel_id=1, source_target_pairs={{0,8},{8,16},{16,24},{24,32},{32,40},{40,48},{48,56},{56,64},{64,7... | collective-permute-start | bytes 122888 | tf_op jit(solution)/shard_map/ppermute | solution.py:436
  23.0 1.2 %collective-permute-start.3 = (bf16[32,640]{1,0:T(8,128)(2,1)S(1)}, bf16[32,640]{1,0:T(8,128)(2,1)S(1)}, u32[]{:S(2)}, u32[]{:S(2)}) collective-permute-start(bf16[32,640]{1,0:T(8,128)(2,1)S(1)} %collective-permute-done.2.mine_ref), channel_id=1, source_target_pairs={{0,1},{1,0},{2,3},{3,2},{4,5},{5,4},{6,7},{7,6},{8,9},{9,8},{10,11... | collective-permute-start | bytes 122888 | tf_op jit(solution)/shard_map/ppermute | solution.py:415
  26.5 18.6 %copy-start = (f32[640]{0:T(1024)S(1)}, f32[640]{0:T(1024)}, u32[]{:S(2)}) copy-start(f32[640]{0:T(1024)} %param.8) | copy-start | bytes 7684
  26.5 18.6 %copy-start.1 = (f32[640]{0:T(1024)S(1)}, f32[640]{0:T(1024)}, u32[]{:S(2)}) copy-start(f32[640]{0:T(1024)} %param.9) | copy-start | bytes 7684
  34.4 28.2 %collective-permute-start.5 = (bf16[16,336,128]{2,1,0:T(8,128)(2,1)S(1)}, bf16[16,336,128]{2,1,0:T(8,128)(2,1)}, u32[]{:S(2)}, u32[]{:S(2)}) collective-permute-start(bf16[16,336,128]{2,1,0:T(8,128)(2,1)S(1)} %all-to-all-done.slab_ref.own_ref), channel_id=1, source_target_pairs={{0,1},{1,0},{2,3},{3,2},{4,5},{5,4},{6,7},{7,6},{8,9},{9,8},{10,11... | collective-permute-start | bytes 4128776 | tf_op jit(solution)/shard_map/ppermute | solution.py:415
  36.9 19.0 %all-to-all-start.1 = ((bf16[8,96,128]{2,1,0:T(8,128)(2,1)}), bf16[8,96,128]{2,1,0:T(8,128)(2,1)S(1)}, u32[]{:S(2)}, u32[]{:S(2)}) async-start(bf16[8,96,128]{2,1,0:T(8,128)(2,1)} %split.1), calls=%async_computation.1 | async-start | bytes 393216 | tf_op jit(solution)/shard_map/all_to_all | solution.py:471
  45.1 7.6 %collective-permute-start.4 = (f32[8,640]{1,0:T(8,128)S(1)}, f32[8,640]{1,0:T(8,128)S(1)}, u32[]{:S(2)}, u32[]{:S(2)}) collective-permute-start(f32[8,640]{1,0:T(8,128)S(1)} %side.1), channel_id=1, source_target_pairs={{1,2},{3,4},{5,6},{2,1},{4,3},{6,5},{9,10},{11,12},{13,14},{10,9},... | collective-permute-start | bytes 61448 | tf_op jit(solution)/shard_map/ppermute | solution.py:461
  57.0 13.2 %all-to-all-start.2 = ((f32[32,8,128]{2,1,0:T(8,128)}), f32[32,8,128]{2,1,0:T(8,128)S(1)}, u32[]{:S(2)}, u32[]{:S(2)}) async-start(f32[32,8,128]{2,1,0:T(8,128)} %get-tuple-element.21), calls=%async_computation.2 | async-start | bytes 262144 | tf_op jit(solution)/shard_map/all_to_all | solution.py:497
  87.1 2.8 %collective-permute-start.6 = (bf16[8,80,256]{2,1,0:T(8,128)(2,1)S(1)}, bf16[8,80,256]{2,1,0:T(8,128)(2,1)S(1)}, u32[]{:S(2)}, u32[]{:S(2)}) collective-permute-start(bf16[8,80,256]{2,1,0:T(8,128)(2,1)S(1)} %all_to_all.20.got_ref), channel_id=1, source_target_pairs={{0,1},{1,0},{2,3},{3,2},{4,5},{5,4},{6,7},{7,6},{8,9},{9,8},{10,11... | collective-permute-start | bytes 983048 | tf_op jit(solution)/shard_map/ppermute | solution.py:415

commit v8 on v7

--- a/solution.py
+++ b/solution.py
@@ -21,7 +21,7 @@
 S_AT = F_ROWS + C_ROWS
 G_ROWS = S_AT + S_ROWS
 E_ROWS = 96
-W_ROWS, V_ROWS = 64, 16
+W_ROWS = 64
 f32, bf16 = jnp.float32, jnp.bfloat16
 
 
@@ -100,6 +100,18 @@
 def pick(columns):
     rows = lax.broadcasted_iota(jnp.int32, (C, columns.shape[1]), 0)
     return (rows == columns).astype(f32).astype(bf16)
+
+
+def sigmoid(value):
+    return 0.5 * jnp.tanh(0.5 * value) + 0.5
+
+
+def fold(row):
+    return jnp.concatenate([row[:, 128 * t : 128 * t + 128] for t in range(5)], axis=0)
+
+
+def unfold(rows):
+    return jnp.concatenate([rows[t : t + 1] for t in range(5)], axis=1)
 
 
 def three(value):
@@ -121,18 +133,19 @@
     return out
 
 
-def put_pieces(mean, squares):
-    pieces = three(mean) + three(squares)
-    row = lax.broadcasted_iota(jnp.int32, (S_ROWS, 128), 0)
-    out = jnp.zeros((S_ROWS, 128), f32)
-    for k in range(6):
-        out = jnp.where(row == k, pieces[k], out)
-    return out.astype(bf16)
+def put_pieces(mean, squares, bias):
+    high, middle, _ = three(bias)
+    rows = three(mean) + three(squares) + (high, middle)
+    return jnp.concatenate(list(rows), axis=0).astype(bf16)
 
 
 def merge_pieces(got, count):
     got = got.astype(f32)
-    return merge(got[:, 0] + got[:, 1] + got[:, 2], got[:, 3] + got[:, 4] + got[:, 5], count)
+    mean, squares = merge(got[:, 0] + got[:, 1] + got[:, 2], got[:, 3] + got[:, 4] + got[:, 5], count)
+    total = got[0]
+    for p in range(1, got.shape[0]):
+        total = total + got[p]
+    return mean, squares, total[6:11] + total[11:16]
 
 
 def in_order(core, own, other):
@@ -146,7 +159,7 @@
     )
 
 
-def pack_kernel(core_ref, both_ref, feat2_ref, cot2_ref, out_hbm, bias_ref, out_ref, sem):
+def pack_kernel(core_ref, both_ref, feat2_ref, cot2_ref, out_hbm, out_ref, sem):
     core = core_ref[0]
     feat_ref, cot_ref = both_ref.at[:PIX], both_ref.at[PIX:]
     x, x2 = feat_ref[...].astype(f32), feat2_ref[...].astype(f32)
@@ -155,8 +168,8 @@
     mean = exact_dot(rows8(total), groups, 0) / CHIP
     wide = exact_dot(mean, groups, 1)[:1]
     squares = ((x - wide) ** 2).sum(0, keepdims=True) + ((x2 - wide) ** 2).sum(0, keepdims=True)
-    stats = put_pieces(mean[:1], exact_dot(rows8(squares), groups, 0)[:1])
-    bias_ref[...] = rows8(cot_ref[...].astype(f32).sum(0, keepdims=True))
+    bias = cot_ref[...].astype(f32).sum(0, keepdims=True) + cot2_ref[...].astype(f32).sum(0, keepdims=True)
+    stats = put_pieces(mean[:1], exact_dot(rows8(squares), groups, 0)[:1], fold(bias))
     moved = jnp.dot(feat_ref[...], pick(feature_columns()), preferred_element_type=f32)
     moved_rest = lanes32(moved[:, 512:], 32)
     for p in range(PEERS):
@@ -190,8 +203,7 @@
 
 
 def split_kernel(z_ref, slab_ref, out_ref):
-    mean, squares = merge_pieces(slab_ref[:, S_AT:], CHIP)
-    stats = put_pieces(mean, squares)
+    stats = put_pieces(*merge_pieces(slab_ref[:, S_AT:], CHIP))
     group = lax.broadcasted_iota(jnp.int32, (TC, 128), 1) // 32
     first, last = jnp.zeros((TC, 128), f32), jnp.zeros((TC, 128), f32)
     for xx in range(NX):
@@ -267,9 +279,10 @@
     out_ref[...] = total
 
 
-def sums_kernel(core_ref, y_ref, stat_ref, both_ref, back_ref, side_ref, gain_ref, shift_ref, bias_ref,
-                row_ref, da_ref, par_ref, out_ref, block):
-    mean, squares = merge_pieces(stat_ref[:, :S_ROWS], PEERS * CHIP)
+def sums_kernel(core_ref, y_ref, stat_ref, both_ref, back_ref, side_ref, gain_ref, shift_ref,
+                row_ref, da_ref, par_ref, out_ref, bias_ref):
+    mean, squares, bias = merge_pieces(stat_ref[:, :S_ROWS], PEERS * CHIP)
+    bias_ref[...] = unfold(bias).reshape(C)
     groups = group_matrix()
     both = jnp.concatenate([mean, lax.rsqrt(squares / TOTAL + 1e-05), jnp.zeros((6, 128), f32)], axis=0)
     both = exact_dot(both, groups, 1)
@@ -281,19 +294,17 @@
     par_ref[...] = exact_dot(table, pick(term_columns(y_ref[0])), 0)
     xhat = (both_ref[:PIX].astype(f32) - mean) * rstd
     act = xhat * gain + shift
-    sig = jax.nn.sigmoid(act)
+    sig = sigmoid(act)
     column = lax.broadcasted_iota(jnp.int32, (TR, TC, C), 1)
     side = jnp.broadcast_to(side_ref[...][:, None, :], (TR, TC, C))
     side = jnp.where(column == core_ref[0] * (TC - 1), side, 0.0).reshape(PIX, C)
     da = (back_ref[...] + side) * sig * (1.0 + act * (1.0 - sig))
     da_ref[...] = da
-    sums = (da.sum(0, keepdims=True), (da * xhat).sum(0, keepdims=True), bias_ref[:1])
-    block[...] = jnp.zeros_like(block)
-    for s in range(3):
-        for t in range(5):
-            block[5 * s + t : 5 * s + t + 1] = sums[s][:, 128 * t : 128 * t + 128]
-    for p in range(2 * PEERS):
-        out_ref[p] = block[8 * (p % 2) : 8 * (p % 2) + 8]
+    empty = jnp.zeros((3, 128), f32)
+    for side, value in enumerate((da, da * xhat)):
+        block = jnp.concatenate([fold(value.sum(0, keepdims=True)), empty], axis=0)
+        for p in range(side, 2 * PEERS, 2):
+            out_ref[p] = block
 
 
 def terms_kernel(core_ref, z_ref, own_ref, other_hbm, edge_ref, par_ref, out_ref,
@@ -306,7 +317,7 @@
 
         def silu(x, lanes):
             a = (x.astype(f32) - par_ref[0:1, lanes]) * par_ref[1:2, lanes] + par_ref[2:3, lanes]
-            return a * jax.nn.sigmoid(a)
+            return a * sigmoid(a)
 
         main = silu(block[:128], slice(0, 128)).astype(bf16)
         tail = silu(block[128:], slice(128, 256))
@@ -366,30 +377,44 @@
     value = sums_ref[0]
     for p in range(1, 2 * PEERS):
         value = value + sums_ref[p]
-    high, middle, low = three(value)
-    block = jnp.concatenate(
-        [jnp.concatenate([high, middle], axis=1), jnp.concatenate([low, jnp.zeros_like(low)], axis=1)], axis=0
-    ).astype(bf16)
+    high, middle, _ = three(value)
+    lane = lax.broadcasted_iota(jnp.int32, (16, 128), 1)
+    row = lax.broadcasted_iota(jnp.int32, (16, 128), 0)
+    tails = [
+        jnp.concatenate([pltpu.roll(middle, (112 - 16 * c) % 128, 1) for c in (2 * k, 2 * k + 1)], axis=0)
+        for k in range(4)
+    ]
     for z in range(NZ):
-        out_ref[z, :W_ROWS] = terms_ref[z]
-        out_ref[z, W_ROWS:] = block
+        for k in range(4):
+            at = slice(16 * k, 16 * k + 16)
+            block = terms_ref[z, at].astype(f32)
+            left, right = block[:, :128], block[:, 128:]
+            right = jnp.where(lane >= 112, tails[k], right)
+            if k == 3:
+                left = jnp.concatenate([left[:12], high[:4]], axis=0)
+                right = jnp.where(row == 13, high[4:5], right)
+            out_ref[z, at] = jnp.concatenate([left, right], axis=1).astype(bf16)
 
 
 def final_kernel(core_ref, got_ref, other_ref, both_ref, da_ref, row_ref, gain_ref,
-                 grad_ref, gain_grad_ref, shift_grad_ref, bias_ref):
-
-    def half(ref):
-        total = jnp.zeros((8, 128), f32)
-        for z in range(NZ):
-            part = ref[z, W_ROWS:].astype(f32)
-            total = total + (part[:8, :128] + part[:8, 128:] + part[8:, :128])
-        return total
-
-    own, other = half(got_ref), half(other_ref)
+                 grad_ref, gain_grad_ref, shift_grad_ref):
+    lane = lax.broadcasted_iota(jnp.int32, (8, 128), 1)
+
+    def total(ref):
+        out = ref[0].astype(f32)
+        for z in range(1, NZ):
+            out = out + ref[z].astype(f32)
+        high = jnp.concatenate([out[60:64, :128], out[61:62, 128:]], axis=0)
+        middle = jnp.zeros((8, 128), f32)
+        for c in range(8):
+            part = pltpu.roll(out[8 * c : 8 * c + 8, 128:], (16 * c - 112) % 128, 1)
+            middle = jnp.where(lane // 16 == c, part, middle)
+        return unfold(high + middle[:5])
+
+    own, other = total(got_ref), total(other_ref)
     lower = core_ref[0] == 0
-    total = jnp.concatenate([jnp.where(lower, own, other), jnp.where(lower, other, own)], axis=0)
-    sums = [jnp.concatenate([total[5 * s + t : 5 * s + t + 1] for t in range(5)], axis=1) for s in range(3)]
-    shift_grad_ref[...], gain_grad_ref[...], bias_ref[...] = [value.reshape(C) for value in sums]
+    sums = (jnp.where(lower, own, other), jnp.where(lower, other, own))
+    shift_grad_ref[...], gain_grad_ref[...] = [value.reshape(C) for value in sums]
     groups = group_matrix()
     gain, mean, rstd = gain_ref[...], row_ref[0:1], row_ref[1:2]
 
@@ -401,9 +426,9 @@
 
 
 def gather_kernel(got_ref, weight_ref):
-    weight = got_ref[0, :W_ROWS].astype(f32)
+    weight = got_ref[0].astype(f32)
     for z in range(1, NZ):
-        weight = weight + got_ref[z, :W_ROWS].astype(f32)
+        weight = weight + got_ref[z].astype(f32)
     for i in range(3):
         for j in range(3):
             at = slice(j * NQ, (j + 1) * NQ)
@@ -435,11 +460,11 @@
     ways = [(2 * k, 2 * k + 2) for k in range(count - 1)] + [(2 * k + 3, 2 * k + 1) for k in range(count - 1)]
     mine = lax.ppermute(edge, ("z", "y", "core"), ways)
 
-    packed, bias = pl.pallas_call(
+    packed = pl.pallas_call(
         pack_kernel,
-        out_shape=(shape((PEERS, G_ROWS, 128), bf16), shape((8, C), f32)),
+        out_shape=shape((PEERS, G_ROWS, 128), bf16),
         in_specs=[smem()] + [vmem()] * 3,
-        out_specs=(hbm(), vmem()),
+        out_specs=hbm(),
         scratch_shapes=[pltpu.VMEM((PEERS, G_ROWS, 128), bf16), pltpu.SemaphoreType.DMA((2,))],
         compiler_params=params(),
         cost_estimate=pl.CostEstimate(flops=1 << 28, bytes_accessed=2 << 20, transcendentals=0),
@@ -485,15 +510,20 @@
     )(at_core, both, cot2, mine, theirs, conv_weight)
 
 
-    row, da, table, sums = pl.pallas_call(
+    row, da, table, sums, bias_grad = pl.pallas_call(
         sums_kernel,
-        out_shape=(shape((8, C), f32), shape((PIX, C), f32), shape((8, 256), f32), shape((2 * PEERS, 8, 128), f32)),
-        in_specs=[smem()] * 2 + [vmem()] * 7,
-        out_specs=(vmem(), vmem(), vmem(), vmem()),
-        scratch_shapes=[pltpu.VMEM((16, 128), f32)],
+        out_shape=(
+            shape((8, C), f32),
+            shape((PIX, C), f32),
+            shape((8, 256), f32),
+            shape((2 * PEERS, 8, 128), f32),
+            shape((C,), f32),
+        ),
+        in_specs=[smem()] * 2 + [vmem()] * 6,
+        out_specs=(vmem(),) * 5,
         compiler_params=params(),
         name="sums",
-    )(at_core, at_y, edges, both, back, side, gain, shift, bias)
+    )(at_core, at_y, edges, both, back, side, gain, shift)
     sums = lax.all_to_all(sums, ("y", "x", "core"), 0, 0)
 
     terms = pl.pallas_call(
@@ -518,7 +548,7 @@
 
     joined = pl.pallas_call(
         join_kernel,
-        out_shape=shape((NZ, W_ROWS + V_ROWS, 256), bf16),
+        out_shape=shape((NZ, W_ROWS, 256), bf16),
         in_specs=[vmem()] * 2,
         out_specs=vmem(),
         compiler_params=params(),
@@ -534,11 +564,11 @@
         cost_estimate=pl.CostEstimate(flops=1 << 22, bytes_accessed=1 << 20, transcendentals=0),
         name="gather",
     )(joined)
-    grad, gain_grad, shift_grad, bias_grad = pl.pallas_call(
+    grad, gain_grad, shift_grad = pl.pallas_call(
         final_kernel,
-        out_shape=(shape((PIX, C), bf16),) + (shape((C,), f32),) * 3,
+        out_shape=(shape((PIX, C), bf16),) + (shape((C,), f32),) * 2,
         in_specs=[smem()] + [vmem()] * 6,
-        out_specs=(vmem(),) * 4,
+        out_specs=(vmem(),) * 3,
         compiler_params=params(),
         name="final",
     )(at_core, joined, flip(joined), both, da, row, gain)

time: 91.5 us -> 90.2 us (0.986)
  blocking collectives: 16.9 us -> 15.1 us
    all_to_all x1, blocking collectives: 16.9 us -> 15.1 us  [body(): joined = lax.all_to_all(joined, 'z', 0, 0)]
where the time goes in v8:
time: 90.2 us; the launch traced here: 89.7 us
  starting transfers between devices  29 us (32%)
  waiting for transfers between devices  24.2 us (27%)
  Pallas kernels  18.8 us (21%)
  blocking collectives  15.1 us (17%)
  other arithmetic  1.04 us (1%)
    all_to_all x1, blocking collectives, body(): joined = lax.all_to_all(joined, 'z', 0, 0)  15.1 us
    all_to_all x1, starting transfers between devices, body(): edges = lax.all_to_all(edges, 'z', 0, 0)  8.18 us
    ppermute x1, waiting for transfers between devices, body(): mine = lax.ppermute(edge, ('z', 'y', 'core'), ways)  8.01 us
    all_to_all x1, waiting for transfers between devices, body(): slab = lax.all_to_all(packed, ('y', 'x'), 0, 0)  7.88 us
    ppermute x5, starting transfers between devices, flip(): return lax.ppermute(value, 'core', [(0, 1), (1, 0)])  7.03 us
    pallas_call x1, Pallas kernels, body(): pl.pallas_call(back_kernel, out_shape=shape((PIX, C), f32), in_specs=[sme...  5.68 us
    all_to_all x1, starting transfers between devices, body(): sums = lax.all_to_all(sums, ('y', 'x', 'core'), 0, 0)  5.54 us
    all_to_all x1, starting transfers between devices, body(): slab = lax.all_to_all(packed, ('y', 'x'), 0, 0)  5.03 us
  transfers between devices with their start and end apart: 10, of which 8 were waited for; matrix products, arithmetic and copies ran while one was open for 2% of the time, Pallas kernels for 17%

profile of v8, /device:TPU:1, one launch (start us, length us, event | category | flops | bytes accessed | tf_op | source)
XLA Modules:
  0.0 89.7 jit_solution(17069020938323131509)
XLA Ops:
  0.6 3.3 %collective-permute-start = (bf16[128,640]{1,0:T(8,128)(2,1)}, bf16[128,640]{1,0:T(8,128)(2,1)S(1)}, u32[]{:S(2)}, u32[]{:S(2)}) collective-permute-start(bf16[128,640]{1,0:T(8,128)(2,1)} %bitcast.12), channel_id=1, source_target_pairs={{0,1},{1,0},{2,3},{3,2},{4,5},{5,4},{6,7},{7,6},{8,9},{9,8},{10,11... | collective-permute-start | bytes 491528 | tf_op jit(solution)/shard_map/ppermute | solution.py:440
  4.0 0.1 collective-permute-start.1
  4.1 1.0 %pad_maximum_fusion.both_ref = bf16[256,640]{1,0:T(8,128)(2,1)S(1)} fusion(bf16[128,640]{1,0:T(8,128)(2,1)} %bitcast.11, bf16[128,640]{1,0:T(8,128)(2,1)} %bitcast.13), kind=kLoop, calls=%fused_computation | loop fusion | flops 655360 | bytes 655360 | tf_op jit(solution)/shard_map/concatenate | solution.py:453
  5.1 0.1 collective-permute-done.feat2_ref
  5.2 0.4 collective-permute-done.1.cot2_ref
  5.6 2.3 %pack.1 = bf16[16,336,128]{2,1,0:T(8,128)(2,1)} custom-call(s32[1]{0:T(128)} %bitcast.core_ref, bf16[256,640]{1,0:T(8,128)(2,1)S(1)} %pad_maximum_fusion.both_ref, bf16[128,640]{1,0:T(8,128)(2,1)S(1)} %collective-permute-done.feat2_ref, bf16[128,640]{1,0:T(8,128)(2,1)S(1)} %collective-permute-done.1.cot2_ref), custom_call_target="tpu_custom_call" | custom-call | flops 268435456 | bytes 2097152 | tf_op jit(solution)/shard_map/pack/pallas_call | solution.py:463
  7.9 5.0 %all-to-all-start = ((bf16[16,336,128]{2,1,0:T(8,128)(2,1)}), bf16[16,336,128]{2,1,0:T(8,128)(2,1)S(1)}, u32[]{:S(2)}, u32[]{:S(2)}) async-start(bf16[16,336,128]{2,1,0:T(8,128)(2,1)} %pack.1), calls=%async_computation | async-start | bytes 2752512 | tf_op jit(solution)/shard_map/all_to_all | solution.py:473
  12.9 0.8 slice_bitcast_fusion
  13.7 1.3 %collective-permute-start.2 = (bf16[32,640]{1,0:T(8,128)(2,1)S(1)}, bf16[32,640]{1,0:T(8,128)(2,1)S(1)}, u32[]{:S(2)}, u32[]{:S(2)}) collective-permute-start(bf16[32,640]{1,0:T(8,128)(2,1)S(1)} %maximum_select_fusion), channel_id=1, source_target_pairs={{0,8},{8,16},{16,24},{24,32},{32,40},{40,48},{48,56},{56,64},{64,7... | collective-permute-start | bytes 122888 | tf_op jit(solution)/shard_map/ppermute | solution.py:461
  15.0 8.0 %collective-permute-done.2.mine_ref = bf16[32,640]{1,0:T(8,128)(2,1)S(1)} collective-permute-done((bf16[32,640]{1,0:T(8,128)(2,1)S(1)}, bf16[32,640]{1,0:T(8,128)(2,1)S(1)}, u32[]{:S(2)}, u32[]{:S(2)}) %collective-permute-start.2) | collective-permute-done | bytes 40992 | tf_op jit(solution)/shard_map/ppermute | solution.py:461
  23.0 0.0 collective-permute-start.3
  23.0 1.2 %collective-permute-done.3.theirs_ref = bf16[32,640]{1,0:T(8,128)(2,1)S(1)} collective-permute-done((bf16[32,640]{1,0:T(8,128)(2,1)S(1)}, bf16[32,640]{1,0:T(8,128)(2,1)S(1)}, u32[]{:S(2)}, u32[]{:S(2)}) %collective-permute-start.3) | collective-permute-done | bytes 40992 | tf_op jit(solution)/shard_map/ppermute | solution.py:440
  24.2 2.3 %side.1 = f32[8,640]{1,0:T(8,128)S(1)} custom-call(s32[1]{0:T(128)} %bitcast.core_ref, bf16[256,640]{1,0:T(8,128)(2,1)S(1)} %pad_maximum_fusion.both_ref, bf16[32,640]{1,0:T(8,128)(2,1)S(1)} %collective-permute-done.2.mine_ref, bf16[32,640]{1,0:T(8,128)(2,1)S(1)} %collective-permute-done.3.theirs_ref, bf16[3,3,640,640]{3,2,1,0:T(8,128)(2,1)} %w_hbm.3), custom_call_target="tpu_custom_call" | custom-call | tf_op jit(solution)/shard_map/side/pallas_call | solution.py:475
  26.5 0.0 copy-start
  26.5 0.0 copy-start.1
  26.6 7.9 %all-to-all-done.slab_ref.own_ref = bf16[16,336,128]{2,1,0:T(8,128)(2,1)S(1)} async-done(((bf16[16,336,128]{2,1,0:T(8,128)(2,1)}), bf16[16,336,128]{2,1,0:T(8,128)(2,1)S(1)}, u32[]{:S(2)}, u32[]{:S(2)}) %all-to-all-start) | async-done | bytes 1376288 | tf_op jit(solution)/shard_map/all_to_all | solution.py:473
  34.4 1.7 %collective-permute-start.5 = (bf16[16,336,128]{2,1,0:T(8,128)(2,1)S(1)}, bf16[16,336,128]{2,1,0:T(8,128)(2,1)}, u32[]{:S(2)}, u32[]{:S(2)}) collective-permute-start(bf16[16,336,128]{2,1,0:T(8,128)(2,1)S(1)} %all-to-all-done.slab_ref.own_ref), channel_id=1, source_target_pairs={{0,1},{1,0},{2,3},{3,2},{4,5},{5,4},{6,7},{7,6},{8,9},{9,8},{10,11... | collective-permute-start | bytes 4128776 | tf_op jit(solution)/shard_map/ppermute | solution.py:440
  36.1 0.8 split.1
  37.0 8.2 %all-to-all-start.1 = ((bf16[8,96,128]{2,1,0:T(8,128)(2,1)}), bf16[8,96,128]{2,1,0:T(8,128)(2,1)S(1)}, u32[]{:S(2)}, u32[]{:S(2)}) async-start(bf16[8,96,128]{2,1,0:T(8,128)(2,1)} %split.1), calls=%async_computation.1 | async-start | bytes 393216 | tf_op jit(solution)/shard_map/all_to_all | solution.py:496
  45.1 0.0 copy-done
  45.2 0.0 copy-done.1
  45.2 1.9 %collective-permute-start.4 = (f32[8,640]{1,0:T(8,128)S(1)}, f32[8,640]{1,0:T(8,128)S(1)}, u32[]{:S(2)}, u32[]{:S(2)}) collective-permute-start(f32[8,640]{1,0:T(8,128)S(1)} %side.1), channel_id=1, source_target_pairs={{1,2},{3,4},{5,6},{2,1},{4,3},{6,5},{9,10},{11,12},{13,14},{10,9},... | collective-permute-start | bytes 61448 | tf_op jit(solution)/shard_map/ppermute | solution.py:486
  47.1 5.7 %back.1.back_ref = f32[128,640]{1,0:T(8,128)S(1)} custom-call(s32[1]{0:T(128)} %bitcast.core_ref, bf16[256,640]{1,0:T(8,128)(2,1)S(1)} %pad_maximum_fusion.both_ref, bf16[128,640]{1,0:T(8,128)(2,1)S(1)} %collective-permute-done.1.cot2_ref, bf16[32,640]{1,0:T(8,128)(2,1)S(1)} %collective-permute-done.2.mine_ref, ...), custom_call_target="tpu_custom_call" | custom-call | flops 943718400 | bytes 7372800 | tf_op jit(solution)/shard_map/back/pallas_call | solution.py:497
  52.8 0.0 collective-permute-done.4.side_ref
  52.8 3.1 %all-to-all-done.1.stat_ref.edge_ref = bf16[8,96,128]{2,1,0:T(8,128)(2,1)S(1)} async-done(((bf16[8,96,128]{2,1,0:T(8,128)(2,1)}), bf16[8,96,128]{2,1,0:T(8,128)(2,1)S(1)}, u32[]{:S(2)}, u32[]{:S(2)}) %all-to-all-start.1) | async-done | bytes 196640 | tf_op jit(solution)/shard_map/all_to_all | solution.py:496
  56.0 1.1 %sums.1 = (f32[8,640]{1,0:T(8,128)S(1)}, f32[128,640]{1,0:T(8,128)S(1)}, f32[8,256]{1,0:T(8,128)S(1)}, f32[32,8,128]{2,1,0:T(8,128)}, f32[640]{0:T(1024)}) custom-call(s32[1]{0:T(128)} %bitcast.core_ref, s32[1]{0:T(128)} %bitcast.1.y_ref, bf16[8,96,128]{2,1,0:T(8,128)(2,1)S(1)} %all-to-all-done.1.stat_ref.edge_ref, ...), custom_call_target="tpu_custom_call" | custom-call | tf_op jit(solution)/shard_map/sums/pallas_call | solution.py:513
  57.1 5.5 %all-to-all-start.2 = ((f32[32,8,128]{2,1,0:T(8,128)}), f32[32,8,128]{2,1,0:T(8,128)S(1)}, u32[]{:S(2)}, u32[]{:S(2)}) async-start(f32[32,8,128]{2,1,0:T(8,128)} %get-tuple-element.17), calls=%async_computation.2 | async-start | bytes 262144 | tf_op jit(solution)/shard_map/all_to_all | solution.py:527
  62.6 0.0 collective-permute-done.5.other_hbm
  62.6 4.6 %terms.1.terms_ref = bf16[8,64,256]{2,1,0:T(8,128)(2,1)S(1)} custom-call(s32[1]{0:T(128)} %bitcast.core_ref, s32[1]{0:T(128)} %bitcast.2.z_ref, bf16[16,336,128]{2,1,0:T(8,128)(2,1)S(1)} %all-to-all-done.slab_ref.own_ref, bf16[16,336,128]{2,1,0:T(8,128)(2,1)} %collective-permute-done.5.other_hbm, bf16[8,96,128]{2,1,0:T(8,128)(2,1)S(1)} %all-to-all-done.1.stat_ref.edge_ref, ...), custom_call_target="tpu_custom_call" | custom-call | flops 943718400 | bytes 4194304 | tf_op jit(solution)/shard_map/terms/pallas_call | solution.py:529
  67.2 3.0 %all-to-all-done.2.sums_ref = f32[32,8,128]{2,1,0:T(8,128)S(1)} async-done(((f32[32,8,128]{2,1,0:T(8,128)}), f32[32,8,128]{2,1,0:T(8,128)S(1)}, u32[]{:S(2)}, u32[]{:S(2)}) %all-to-all-start.2) | async-done | bytes 131104 | tf_op jit(solution)/shard_map/all_to_all | solution.py:527
  70.2 0.1 join.1
  70.4 15.1 %all_to_all.20.got_ref = bf16[8,64,256]{2,1,0:T(8,128)(2,1)S(1)} all-to-all(bf16[8,64,256]{2,1,0:T(8,128)(2,1)S(1)} %join.1), channel_id=1, replica_groups=mesh['z'=8,'y'=4,'x'=4,'core'=2] {'z'}, dimensions={0} | all-to-all | bytes 524288 | tf_op jit(solution)/shard_map/all_to_all | solution.py:557
  85.5 1.9 %collective-permute-start.6 = (bf16[8,64,256]{2,1,0:T(8,128)(2,1)S(1)}, bf16[8,64,256]{2,1,0:T(8,128)(2,1)S(1)}, u32[]{:S(2)}, u32[]{:S(2)}) collective-permute-start(bf16[8,64,256]{2,1,0:T(8,128)(2,1)S(1)} %all_to_all.20.got_ref), channel_id=1, source_target_pairs={{0,1},{1,0},{2,3},{3,2},{4,5},{5,4},{6,7},{7,6},{8,9},{9,8},{10,11... | collective-permute-start | bytes 786440 | tf_op jit(solution)/shard_map/ppermute | solution.py:440
  87.4 0.8 gather.1
  88.1 0.4 collective-permute-done.6.other_ref
  88.5 1.1 %final.1 = (bf16[128,640]{1,0:T(8,128)(2,1)}, f32[640]{0:T(1024)}, f32[640]{0:T(1024)}) custom-call(s32[1]{0:T(128)} %bitcast.core_ref, bf16[8,64,256]{2,1,0:T(8,128)(2,1)S(1)} %all_to_all.20.got_ref, bf16[8,64,256]{2,1,0:T(8,128)(2,1)S(1)} %collective-permute-done.6.other_ref, bf16[256,640]{1,0:T(8,128)(2,1)S(1)} %pad_maximum_fusion.both_ref, ...), custom_call_target="tpu_custom_call" | custom-call | tf_op jit(solution)/shard_map/final/pallas_call | solution.py:567
  (4 shorter events, 0.0 us)
Async XLA Ops:
  0.6 4.6 %collective-permute-start = (bf16[128,640]{1,0:T(8,128)(2,1)}, bf16[128,640]{1,0:T(8,128)(2,1)S(1)}, u32[]{:S(2)}, u32[]{:S(2)}) collective-permute-start(bf16[128,640]{1,0:T(8,128)(2,1)} %bitcast.12), channel_id=1, source_target_pairs={{0,1},{1,0},{2,3},{3,2},{4,5},{5,4},{6,7},{7,6},{8,9},{9,8},{10,11... | collective-permute-start | bytes 491528 | tf_op jit(solution)/shard_map/ppermute | solution.py:440
  4.0 1.6 %collective-permute-start.1 = (bf16[128,640]{1,0:T(8,128)(2,1)}, bf16[128,640]{1,0:T(8,128)(2,1)S(1)}, u32[]{:S(2)}, u32[]{:S(2)}) collective-permute-start(bf16[128,640]{1,0:T(8,128)(2,1)} %bitcast.10), channel_id=1, source_target_pairs={{0,1},{1,0},{2,3},{3,2},{4,5},{5,4},{6,7},{7,6},{8,9},{9,8},{10,11... | collective-permute-start | bytes 491528 | tf_op jit(solution)/shard_map/ppermute | solution.py:440
  7.9 26.5 %all-to-all-start = ((bf16[16,336,128]{2,1,0:T(8,128)(2,1)}), bf16[16,336,128]{2,1,0:T(8,128)(2,1)S(1)}, u32[]{:S(2)}, u32[]{:S(2)}) async-start(bf16[16,336,128]{2,1,0:T(8,128)(2,1)} %pack.1), calls=%async_computation | async-start | bytes 2752512 | tf_op jit(solution)/shard_map/all_to_all | solution.py:473
  13.7 9.3 %collective-permute-start.2 = (bf16[32,640]{1,0:T(8,128)(2,1)S(1)}, bf16[32,640]{1,0:T(8,128)(2,1)S(1)}, u32[]{:S(2)}, u32[]{:S(2)}) collective-permute-start(bf16[32,640]{1,0:T(8,128)(2,1)S(1)} %maximum_select_fusion), channel_id=1, source_target_pairs={{0,8},{8,16},{16,24},{24,32},{32,40},{40,48},{48,56},{56,64},{64,7... | collective-permute-start | bytes 122888 | tf_op jit(solution)/shard_map/ppermute | solution.py:461
  23.0 1.2 %collective-permute-start.3 = (bf16[32,640]{1,0:T(8,128)(2,1)S(1)}, bf16[32,640]{1,0:T(8,128)(2,1)S(1)}, u32[]{:S(2)}, u32[]{:S(2)}) collective-permute-start(bf16[32,640]{1,0:T(8,128)(2,1)S(1)} %collective-permute-done.2.mine_ref), channel_id=1, source_target_pairs={{0,1},{1,0},{2,3},{3,2},{4,5},{5,4},{6,7},{7,6},{8,9},{9,8},{10,11... | collective-permute-start | bytes 122888 | tf_op jit(solution)/shard_map/ppermute | solution.py:440
  26.5 18.6 %copy-start = (f32[640]{0:T(1024)S(1)}, f32[640]{0:T(1024)}, u32[]{:S(2)}) copy-start(f32[640]{0:T(1024)} %param.8) | copy-start | bytes 7684
  26.5 18.6 %copy-start.1 = (f32[640]{0:T(1024)S(1)}, f32[640]{0:T(1024)}, u32[]{:S(2)}) copy-start(f32[640]{0:T(1024)} %param.9) | copy-start | bytes 7684
  34.4 28.2 %collective-permute-start.5 = (bf16[16,336,128]{2,1,0:T(8,128)(2,1)S(1)}, bf16[16,336,128]{2,1,0:T(8,128)(2,1)}, u32[]{:S(2)}, u32[]{:S(2)}) collective-permute-start(bf16[16,336,128]{2,1,0:T(8,128)(2,1)S(1)} %all-to-all-done.slab_ref.own_ref), channel_id=1, source_target_pairs={{0,1},{1,0},{2,3},{3,2},{4,5},{5,4},{6,7},{7,6},{8,9},{9,8},{10,11... | collective-permute-start | bytes 4128776 | tf_op jit(solution)/shard_map/ppermute | solution.py:440
  37.0 19.0 %all-to-all-start.1 = ((bf16[8,96,128]{2,1,0:T(8,128)(2,1)}), bf16[8,96,128]{2,1,0:T(8,128)(2,1)S(1)}, u32[]{:S(2)}, u32[]{:S(2)}) async-start(bf16[8,96,128]{2,1,0:T(8,128)(2,1)} %split.1), calls=%async_computation.1 | async-start | bytes 393216 | tf_op jit(solution)/shard_map/all_to_all | solution.py:496
  45.2 7.6 %collective-permute-start.4 = (f32[8,640]{1,0:T(8,128)S(1)}, f32[8,640]{1,0:T(8,128)S(1)}, u32[]{:S(2)}, u32[]{:S(2)}) collective-permute-start(f32[8,640]{1,0:T(8,128)S(1)} %side.1), channel_id=1, source_target_pairs={{1,2},{3,4},{5,6},{2,1},{4,3},{6,5},{9,10},{11,12},{13,14},{10,9},... | collective-permute-start | bytes 61448 | tf_op jit(solution)/shard_map/ppermute | solution.py:486
  57.1 13.2 %all-to-all-start.2 = ((f32[32,8,128]{2,1,0:T(8,128)}), f32[32,8,128]{2,1,0:T(8,128)S(1)}, u32[]{:S(2)}, u32[]{:S(2)}) async-start(f32[32,8,128]{2,1,0:T(8,128)} %get-tuple-element.17), calls=%async_computation.2 | async-start | bytes 262144 | tf_op jit(solution)/shard_map/all_to_all | solution.py:527
  85.5 3.1 %collective-permute-start.6 = (bf16[8,64,256]{2,1,0:T(8,128)(2,1)S(1)}, bf16[8,64,256]{2,1,0:T(8,128)(2,1)S(1)}, u32[]{:S(2)}, u32[]{:S(2)}) collective-permute-start(bf16[8,64,256]{2,1,0:T(8,128)(2,1)S(1)} %all_to_all.20.got_ref), channel_id=1, source_target_pairs={{0,1},{1,0},{2,3},{3,2},{4,5},{5,4},{6,7},{7,6},{8,9},{9,8},{10,11... | collective-permute-start | bytes 786440 | tf_op jit(solution)/shard_map/ppermute | solution.py:440

commit v9 on v8

--- a/solution.py
+++ b/solution.py
@@ -228,10 +228,24 @@
             out_ref[p, 80:] = first
 
 
-def back_kernel(core_ref, both_ref, cot2_ref, mine_ref, theirs_ref, w_hbm, out_ref, shifted, w_ref, sem):
+def back_kernel(shifted, w_hbm, out_ref, w_ref, sem):
     copies = fetch([(w_hbm.at[t // 3, t % 3], w_ref.at[t]) for t in range(9)], sem)
+    total = None
+    for i in range(3):
+        for copy in copies[3 * i : 3 * i + 3]:
+            copy.wait()
+        for j in range(3):
+            pixels = shifted[2 - j, (2 - i) * TC : (2 - i) * TC + PIX]
+            part = lax.dot_general(w_ref[3 * i + j], pixels, (((1,), (1,)), ((), ())), preferred_element_type=f32)
+            total = part if total is None else total + part
+    out_ref[...] = total.T
+
+
+def side_kernel(core_ref, both_ref, cot2_ref, mine_ref, theirs_ref, w_hbm, out_ref, shifted, w_ref, sem):
+    j = 2 * core_ref[0]
+    copies = fetch([(w_hbm.at[i, j], w_ref.at[i]) for i in range(3)], sem)
+    lower = core_ref[0] == 0
     rows = (TR + 2) * TC
-    lower = core_ref[0] == 0
     mine, theirs = mine_ref[...].astype(f32), theirs_ref[...].astype(f32)
     top, bottom = jnp.where(lower, mine, theirs), jnp.where(lower, theirs, mine)
     own_top, other_top = jnp.where(lower, top[:TC], top[TC:]), jnp.where(lower, top[TC:], top[:TC])
@@ -247,28 +261,8 @@
     shifted[0] = jnp.where(col == 0, left, pltpu.roll(wide, 1, 0)).astype(bf16)
     shifted[1] = wide.astype(bf16)
     shifted[2] = jnp.where(col == TC - 1, right, pltpu.roll(wide, rows - 1, 0)).astype(bf16)
-    total = jnp.zeros((C, PIX), f32)
-    for t in range(9):
-        i, j = t // 3, t % 3
-        copies[t].wait()
-        pixels = shifted[2 - j, (2 - i) * TC : (2 - i) * TC + PIX]
-        total = total + lax.dot_general(
-            w_ref[t], pixels, (((1,), (1,)), ((), ())), preferred_element_type=f32
-        )
-    out_ref[...] = total.T
-
-
-def side_kernel(core_ref, both_ref, mine_ref, theirs_ref, w_hbm, out_ref, w_ref, sem):
-    j = 2 * core_ref[0]
-    copies = fetch([(w_hbm.at[i, j], w_ref.at[i]) for i in range(3)], sem)
-    lower = core_ref[0] == 0
-    tile = both_ref[PIX:].astype(f32).reshape(TR, TC, C)
-    tile = jnp.where(lower, tile[:, :1], tile[:, TC - 1 :])
-    mine, theirs = mine_ref[...].astype(f32), theirs_ref[...].astype(f32)
-    mine = jnp.where(lower, mine[:1], mine[2 * TC - 1 :])
-    theirs = jnp.where(lower, theirs[:1], theirs[2 * TC - 1 :])
-    top, bottom = jnp.where(lower, mine, theirs), jnp.where(lower, theirs, mine)
-    column = jnp.concatenate([top[None], tile, bottom[None]], axis=0)
+    column = wide.reshape(TR + 2, TC, C)
+    column = jnp.where(lower, column[:, :1], column[:, TC - 1 :])
     total = jnp.zeros((TR, C), f32)
     for i in range(3):
         copies[i].wait()
@@ -308,7 +302,8 @@
 
 
 def terms_kernel(core_ref, z_ref, own_ref, other_hbm, edge_ref, par_ref, out_ref,
-                 hid, strips, cot3, rest, other_ref, sem):
+                 hid0, hid1, hid2, hid3, strips, cot3, rest, totals, other_ref, sem):
+    hidden = (hid0, hid1, hid2, hid3)
     copies = fetch(((other_hbm.at[:, :F_ROWS, :], other_ref),), sem)
     core = core_ref[0]
 
@@ -325,12 +320,11 @@
             low = pltpu.roll(tail, (128 - 32 * g) % 128, 1).astype(bf16)
             for h in range(2):
                 r = 2 * g + h
-                at = pl.ds(pl.multiple_of((y * TR + r) * 128 + xx * 32 + side * TC, TC), TC)
-                hid[at, 0:128] = main[r * TC : (r + 1) * TC]
-                hid[at, 128:256] = low[h * TC : (h + 1) * TC]
+                at = pl.ds(pl.multiple_of(r * 128 + xx * 32 + side * TC, TC), TC)
+                hidden[y][at, 0:128] = main[r * TC : (r + 1) * TC]
+                hidden[y][at, 128:256] = low[h * TC : (h + 1) * TC]
 
     for peer in range(PEERS):
-        put(own_ref[peer, :F_ROWS], peer, core)
         y, xx = peer // NX, peer % NX
         tail = own_ref[peer, 288:320].astype(f32)
         for g in range(4):
@@ -340,9 +334,6 @@
                 for h in range(2):
                     at = (y * TR + 2 * g + h + 1) * 128 + xx * 32 + side * TC
                     strips[at : at + TC] = value[h * TC : (h + 1) * TC]
-    copies[0].wait()
-    for peer in range(PEERS):
-        put(other_ref[peer], peer, 1 - core)
     z = z_ref[0]
     for start, peer, there in ((0, jnp.maximum(z - 1, 0), z > 0),
                                ((ROWS + 1) * 128, jnp.minimum(z + 1, NZ - 1), z < NZ - 1)):
@@ -362,10 +353,21 @@
         cot3[NQ : 2 * NQ, at] = turned.astype(bf16)
         cot3[2 * NQ : 3 * NQ, at] = before.astype(bf16)
     cot3[3 * NQ :] = jnp.zeros((16, (ROWS + 2) * 128), bf16)
+    copies[0].wait()
+    for y in range(NY):
+        for peer in range(y * NX, (y + 1) * NX):
+            put(own_ref[peer, :F_ROWS], peer, core)
+            put(other_ref[peer], peer, 1 - core)
+        for i in range(3):
+            at = (2 - i + y * TR) * 128
+            part = jnp.dot(cot3[:, at : at + TR * 128], hidden[y][...], preferred_element_type=f32)
+            if y == 0:
+                totals[i] = part
+            else:
+                totals[i] += part
     rest[...] = jnp.zeros_like(rest)
     for i in range(3):
-        lhs = cot3[:, (2 - i) * 128 : (2 - i) * 128 + ROWS * 128]
-        turned = jnp.dot(lhs, hid[...], preferred_element_type=f32).T
+        turned = totals[i].T
         for z in range(NZ):
             out_ref[z, 16 * i : 16 * i + 16] = turned[16 * z : 16 * z + 16].astype(bf16)
             rest[z, 4 * i : 4 * i + 4] = turned[128 + 4 * z : 132 + 4 * z]
@@ -472,15 +474,15 @@
     )(at_core, both, feat2, cot2)
     slab = lax.all_to_all(packed, ("y", "x"), 0, 0)
     theirs = flip(mine)
-    side = pl.pallas_call(
+    side, shifted = pl.pallas_call(
         side_kernel,
-        out_shape=shape((TR, C), f32),
-        in_specs=[smem()] + [vmem()] * 3 + [hbm()],
-        out_specs=vmem(),
+        out_shape=(shape((TR, C), f32), shape((3, (TR + 2) * TC, C), bf16)),
+        in_specs=[smem()] + [vmem()] * 4 + [hbm()],
+        out_specs=(vmem(), vmem()),
         scratch_shapes=[pltpu.VMEM((3, C, C), bf16), pltpu.SemaphoreType.DMA((3,))],
         compiler_params=params(),
         name="side",
-    )(at_core, both, mine, theirs, conv_weight)
+    )(at_core, both, cot2, mine, theirs, conv_weight)
     slab, side = lax.optimization_barrier((slab, side))
     pairs = [(2 * k + 1, 2 * k + 2) for k in range(NX - 1)]
     side = lax.ppermute(side, ("x", "core"), pairs + [(b, a) for a, b in pairs])
@@ -497,19 +499,13 @@
     back = pl.pallas_call(
         back_kernel,
         out_shape=shape((PIX, C), f32),
-        in_specs=[smem()] + [vmem()] * 4 + [hbm()],
+        in_specs=[vmem(), hbm()],
         out_specs=vmem(),
-        scratch_shapes=[
-            pltpu.VMEM((3, (TR + 2) * TC, C), bf16),
-            pltpu.VMEM((9, C, C), bf16),
-            pltpu.SemaphoreType.DMA((9,)),
-        ],
+        scratch_shapes=[pltpu.VMEM((9, C, C), bf16), pltpu.SemaphoreType.DMA((9,))],
         compiler_params=params(),
         cost_estimate=pl.CostEstimate(flops=2 * PIX * 9 * C * C, bytes_accessed=18 * C * C, transcendentals=0),
         name="back",
-    )(at_core, both, cot2, mine, theirs, conv_weight)
-
-
+    )(shifted, conv_weight)
     row, da, table, sums, bias_grad = pl.pallas_call(
         sums_kernel,
         out_shape=(
@@ -532,10 +528,14 @@
         in_specs=[smem()] * 2 + [vmem(), hbm(), vmem(), vmem()],
         out_specs=vmem(),
         scratch_shapes=[
-            pltpu.VMEM((ROWS * 128, 256), bf16),
+            pltpu.VMEM((TR * 128, 256), bf16),
+            pltpu.VMEM((TR * 128, 256), bf16),
+            pltpu.VMEM((TR * 128, 256), bf16),
+            pltpu.VMEM((TR * 128, 256), bf16),
             pltpu.VMEM(((ROWS + 2) * 128, 128), bf16),
             pltpu.VMEM((256, (ROWS + 2) * 128), bf16),
             pltpu.VMEM((NZ, 16, 256), f32),
+            pltpu.VMEM((3, 256, 256), f32),
             pltpu.VMEM((PEERS, F_ROWS, 128), bf16),
             pltpu.SemaphoreType.DMA((1,)),
         ],

time: 90.2 us -> 89 us (0.987)
  Pallas kernels: 18.8 us -> 16.9 us
  waiting for transfers between devices: 24.2 us -> 26.1 us
  blocking collectives: 15.1 us -> 13.9 us
    all_to_all x1, blocking collectives: 15.1 us -> 13.9 us  [body(): joined = lax.all_to_all(joined, 'z', 0, 0)]
    all_to_all x1, waiting for transfers between devices: 3.15 us -> 4.37 us  [body(): edges = lax.all_to_all(edges, 'z', 0, 0)]
    pallas_call x2, Pallas kernels: 7.96 us -> 6.74 us  [the longest x1 4.46 us: body(): pl.pallas_call(back_kernel, out_shape=shape((PIX, C), f32), in_specs=[vme...]
  transfers between devices with their start and end apart: 10 -> 10, of which waited for: 8 -> 8; matrix products, arithmetic and copies ran while one was open for 2% -> 2% of each run, Pallas kernels for 17% -> 15%
where the time goes in v9:
time: 89 us; the launch traced here: 88.4 us
  starting transfers between devices  29 us (33%)
  waiting for transfers between devices  26.1 us (29%)
  Pallas kernels  16.9 us (19%)
  blocking collectives  13.9 us (16%)
  other arithmetic  1.04 us (1%)
    all_to_all x1, blocking collectives, body(): joined = lax.all_to_all(joined, 'z', 0, 0)  13.9 us
    all_to_all x1, starting transfers between devices, body(): edges = lax.all_to_all(edges, 'z', 0, 0)  8.18 us
    ppermute x1, waiting for transfers between devices, body(): mine = lax.ppermute(edge, ('z', 'y', 'core'), ways)  8.01 us
    all_to_all x1, waiting for transfers between devices, body(): slab = lax.all_to_all(packed, ('y', 'x'), 0, 0)  7.88 us
    ppermute x5, starting transfers between devices, flip(): return lax.ppermute(value, 'core', [(0, 1), (1, 0)])  7.03 us
    all_to_all x1, starting transfers between devices, body(): sums = lax.all_to_all(sums, ('y', 'x', 'core'), 0, 0)  5.54 us
    all_to_all x1, starting transfers between devices, body(): slab = lax.all_to_all(packed, ('y', 'x'), 0, 0)  5.03 us
    pallas_call x1, Pallas kernels, body(): pl.pallas_call(back_kernel, out_shape=shape((PIX, C), f32), in_specs=[vme...  4.46 us
  transfers between devices with their start and end apart: 10, of which 8 were waited for; matrix products, arithmetic and copies ran while one was open for 2% of the time, Pallas kernels for 15%

profile of v9, /device:TPU:1, one launch (start us, length us, event | category | flops | bytes accessed | tf_op | source)
XLA Modules:
  0.0 88.4 jit_solution(8793862270436257680)
XLA Ops:
  0.6 3.3 %collective-permute-start = (bf16[128,640]{1,0:T(8,128)(2,1)}, bf16[128,640]{1,0:T(8,128)(2,1)S(1)}, u32[]{:S(2)}, u32[]{:S(2)}) collective-permute-start(bf16[128,640]{1,0:T(8,128)(2,1)} %bitcast.12), channel_id=1, source_target_pairs={{0,1},{1,0},{2,3},{3,2},{4,5},{5,4},{6,7},{7,6},{8,9},{9,8},{10,11... | collective-permute-start | bytes 491528 | tf_op jit(solution)/shard_map/ppermute | solution.py:442
  4.0 0.1 collective-permute-start.1
  4.1 1.0 %pad_maximum_fusion.both_ref = bf16[256,640]{1,0:T(8,128)(2,1)S(1)} fusion(bf16[128,640]{1,0:T(8,128)(2,1)} %bitcast.11, bf16[128,640]{1,0:T(8,128)(2,1)} %bitcast.13), kind=kLoop, calls=%fused_computation | loop fusion | flops 655360 | bytes 655360 | tf_op jit(solution)/shard_map/concatenate | solution.py:455
  5.1 0.1 collective-permute-done.feat2_ref
  5.2 0.4 collective-permute-done.1.cot2_ref
  5.6 2.3 %pack.1 = bf16[16,336,128]{2,1,0:T(8,128)(2,1)} custom-call(s32[1]{0:T(128)} %bitcast.core_ref, bf16[256,640]{1,0:T(8,128)(2,1)S(1)} %pad_maximum_fusion.both_ref, bf16[128,640]{1,0:T(8,128)(2,1)S(1)} %collective-permute-done.feat2_ref, bf16[128,640]{1,0:T(8,128)(2,1)S(1)} %collective-permute-done.1.cot2_ref), custom_call_target="tpu_custom_call" | custom-call | flops 268435456 | bytes 2097152 | tf_op jit(solution)/shard_map/pack/pallas_call | solution.py:465
  7.9 5.0 %all-to-all-start = ((bf16[16,336,128]{2,1,0:T(8,128)(2,1)}), bf16[16,336,128]{2,1,0:T(8,128)(2,1)S(1)}, u32[]{:S(2)}, u32[]{:S(2)}) async-start(bf16[16,336,128]{2,1,0:T(8,128)(2,1)} %pack.1), calls=%async_computation | async-start | bytes 2752512 | tf_op jit(solution)/shard_map/all_to_all | solution.py:475
  12.9 0.8 slice_bitcast_fusion
  13.7 1.3 %collective-permute-start.2 = (bf16[32,640]{1,0:T(8,128)(2,1)S(1)}, bf16[32,640]{1,0:T(8,128)(2,1)S(1)}, u32[]{:S(2)}, u32[]{:S(2)}) collective-permute-start(bf16[32,640]{1,0:T(8,128)(2,1)S(1)} %maximum_select_fusion), channel_id=1, source_target_pairs={{0,8},{8,16},{16,24},{24,32},{32,40},{40,48},{48,56},{56,64},{64,7... | collective-permute-start | bytes 122888 | tf_op jit(solution)/shard_map/ppermute | solution.py:463
  15.0 8.0 %collective-permute-done.2.mine_ref = bf16[32,640]{1,0:T(8,128)(2,1)S(1)} collective-permute-done((bf16[32,640]{1,0:T(8,128)(2,1)S(1)}, bf16[32,640]{1,0:T(8,128)(2,1)S(1)}, u32[]{:S(2)}, u32[]{:S(2)}) %collective-permute-start.2) | collective-permute-done | bytes 40992 | tf_op jit(solution)/shard_map/ppermute | solution.py:463
  23.0 0.0 collective-permute-start.3
  23.0 1.2 %collective-permute-done.3.theirs_ref = bf16[32,640]{1,0:T(8,128)(2,1)S(1)} collective-permute-done((bf16[32,640]{1,0:T(8,128)(2,1)S(1)}, bf16[32,640]{1,0:T(8,128)(2,1)S(1)}, u32[]{:S(2)}, u32[]{:S(2)}) %collective-permute-start.3) | collective-permute-done | bytes 40992 | tf_op jit(solution)/shard_map/ppermute | solution.py:442
  24.2 2.3 %side.1 = (f32[8,640]{1,0:T(8,128)S(1)}, bf16[3,160,640]{2,1,0:T(8,128)(2,1)S(1)}) custom-call(s32[1]{0:T(128)} %bitcast.core_ref, bf16[256,640]{1,0:T(8,128)(2,1)S(1)} %pad_maximum_fusion.both_ref, bf16[128,640]{1,0:T(8,128)(2,1)S(1)} %collective-permute-done.1.cot2_ref, bf16[32,640]{1,0:T(8,128)(2,1)S(1)} %collective-permute-done.2.mine_ref, ...), custom_call_target="tpu_custom_call" | custom-call | tf_op jit(solution)/shard_map/side/pallas_call | solution.py:477
  26.5 0.0 copy-start
  26.5 0.0 copy-start.1
  26.5 7.9 %all-to-all-done.slab_ref.own_ref = bf16[16,336,128]{2,1,0:T(8,128)(2,1)S(1)} async-done(((bf16[16,336,128]{2,1,0:T(8,128)(2,1)}), bf16[16,336,128]{2,1,0:T(8,128)(2,1)S(1)}, u32[]{:S(2)}, u32[]{:S(2)}) %all-to-all-start) | async-done | bytes 1376288 | tf_op jit(solution)/shard_map/all_to_all | solution.py:475
  34.4 1.7 %collective-permute-start.5 = (bf16[16,336,128]{2,1,0:T(8,128)(2,1)S(1)}, bf16[16,336,128]{2,1,0:T(8,128)(2,1)}, u32[]{:S(2)}, u32[]{:S(2)}) collective-permute-start(bf16[16,336,128]{2,1,0:T(8,128)(2,1)S(1)} %all-to-all-done.slab_ref.own_ref), channel_id=1, source_target_pairs={{0,1},{1,0},{2,3},{3,2},{4,5},{5,4},{6,7},{7,6},{8,9},{9,8},{10,11... | collective-permute-start | bytes 4128776 | tf_op jit(solution)/shard_map/ppermute | solution.py:442
  36.1 0.9 split.1
  36.9 8.2 %all-to-all-start.1 = ((bf16[8,96,128]{2,1,0:T(8,128)(2,1)}), bf16[8,96,128]{2,1,0:T(8,128)(2,1)S(1)}, u32[]{:S(2)}, u32[]{:S(2)}) async-start(bf16[8,96,128]{2,1,0:T(8,128)(2,1)} %split.1), calls=%async_computation.1 | async-start | bytes 393216 | tf_op jit(solution)/shard_map/all_to_all | solution.py:498
  45.1 0.0 copy-done
  45.1 0.0 copy-done.1
  45.2 1.9 %collective-permute-start.4 = (f32[8,640]{1,0:T(8,128)S(1)}, f32[8,640]{1,0:T(8,128)S(1)}, u32[]{:S(2)}, u32[]{:S(2)}) collective-permute-start(f32[8,640]{1,0:T(8,128)S(1)} %get-tuple-element.20), channel_id=1, source_target_pairs={{1,2},{3,4},{5,6},{2,1},{4,3},{6,5},{9,10},{11,12},{13,14},{10,9},... | collective-permute-start | bytes 61448 | tf_op jit(solution)/shard_map/ppermute | solution.py:488
  47.1 4.5 %back.1.back_ref = f32[128,640]{1,0:T(8,128)S(1)} custom-call(bf16[3,160,640]{2,1,0:T(8,128)(2,1)S(1)} %get-tuple-element.19.shifted, bf16[3,3,640,640]{3,2,1,0:T(8,128)(2,1)} %w_hbm.3), custom_call_target="tpu_custom_call" | custom-call | flops 943718400 | bytes 7372800 | tf_op jit(solution)/shard_map/back/pallas_call | solution.py:499
  51.6 0.0 collective-permute-done.4.side_ref
  51.6 4.4 %all-to-all-done.1.stat_ref.edge_ref = bf16[8,96,128]{2,1,0:T(8,128)(2,1)S(1)} async-done(((bf16[8,96,128]{2,1,0:T(8,128)(2,1)}), bf16[8,96,128]{2,1,0:T(8,128)(2,1)S(1)}, u32[]{:S(2)}, u32[]{:S(2)}) %all-to-all-start.1) | async-done | bytes 196640 | tf_op jit(solution)/shard_map/all_to_all | solution.py:498
  55.9 1.1 %sums.1 = (f32[8,640]{1,0:T(8,128)S(1)}, f32[128,640]{1,0:T(8,128)S(1)}, f32[8,256]{1,0:T(8,128)S(1)}, f32[32,8,128]{2,1,0:T(8,128)}, f32[640]{0:T(1024)}) custom-call(s32[1]{0:T(128)} %bitcast.core_ref, s32[1]{0:T(128)} %bitcast.1.y_ref, bf16[8,96,128]{2,1,0:T(8,128)(2,1)S(1)} %all-to-all-done.1.stat_ref.edge_ref, ...), custom_call_target="tpu_custom_call" | custom-call | tf_op jit(solution)/shard_map/sums/pallas_call | solution.py:509
  57.0 5.5 %all-to-all-start.2 = ((f32[32,8,128]{2,1,0:T(8,128)}), f32[32,8,128]{2,1,0:T(8,128)S(1)}, u32[]{:S(2)}, u32[]{:S(2)}) async-start(f32[32,8,128]{2,1,0:T(8,128)} %get-tuple-element.21), calls=%async_computation.2 | async-start | bytes 262144 | tf_op jit(solution)/shard_map/all_to_all | solution.py:523
  62.6 0.0 collective-permute-done.5.other_hbm
  62.6 3.9 %terms.1.terms_ref = bf16[8,64,256]{2,1,0:T(8,128)(2,1)S(1)} custom-call(s32[1]{0:T(128)} %bitcast.core_ref, s32[1]{0:T(128)} %bitcast.2.z_ref, bf16[16,336,128]{2,1,0:T(8,128)(2,1)S(1)} %all-to-all-done.slab_ref.own_ref, bf16[16,336,128]{2,1,0:T(8,128)(2,1)} %collective-permute-done.5.other_hbm, bf16[8,96,128]{2,1,0:T(8,128)(2,1)S(1)} %all-to-all-done.1.stat_ref.edge_ref, ...), custom_call_target="tpu_custom_call" | custom-call | flops 943718400 | bytes 4194304 | tf_op jit(solution)/shard_map/terms/pallas_call | solution.py:525
  66.5 3.7 %all-to-all-done.2.sums_ref = f32[32,8,128]{2,1,0:T(8,128)S(1)} async-done(((f32[32,8,128]{2,1,0:T(8,128)}), f32[32,8,128]{2,1,0:T(8,128)S(1)}, u32[]{:S(2)}, u32[]{:S(2)}) %all-to-all-start.2) | async-done | bytes 131104 | tf_op jit(solution)/shard_map/all_to_all | solution.py:523
  70.2 0.1 join.1
  70.3 13.9 %all_to_all.20.got_ref = bf16[8,64,256]{2,1,0:T(8,128)(2,1)S(1)} all-to-all(bf16[8,64,256]{2,1,0:T(8,128)(2,1)S(1)} %join.1), channel_id=1, replica_groups=mesh['z'=8,'y'=4,'x'=4,'core'=2] {'z'}, dimensions={0} | all-to-all | bytes 524288 | tf_op jit(solution)/shard_map/all_to_all | solution.py:557
  84.2 1.9 %collective-permute-start.6 = (bf16[8,64,256]{2,1,0:T(8,128)(2,1)S(1)}, bf16[8,64,256]{2,1,0:T(8,128)(2,1)S(1)}, u32[]{:S(2)}, u32[]{:S(2)}) collective-permute-start(bf16[8,64,256]{2,1,0:T(8,128)(2,1)S(1)} %all_to_all.20.got_ref), channel_id=1, source_target_pairs={{0,1},{1,0},{2,3},{3,2},{4,5},{5,4},{6,7},{7,6},{8,9},{9,8},{10,11... | collective-permute-start | bytes 786440 | tf_op jit(solution)/shard_map/ppermute | solution.py:442
  86.1 0.8 gather.1
  86.9 0.4 collective-permute-done.6.other_ref
  87.3 1.1 %final.1 = (bf16[128,640]{1,0:T(8,128)(2,1)}, f32[640]{0:T(1024)}, f32[640]{0:T(1024)}) custom-call(s32[1]{0:T(128)} %bitcast.core_ref, bf16[8,64,256]{2,1,0:T(8,128)(2,1)S(1)} %all_to_all.20.got_ref, bf16[8,64,256]{2,1,0:T(8,128)(2,1)S(1)} %collective-permute-done.6.other_ref, bf16[256,640]{1,0:T(8,128)(2,1)S(1)} %pad_maximum_fusion.both_ref, ...), custom_call_target="tpu_custom_call" | custom-call | tf_op jit(solution)/shard_map/final/pallas_call | solution.py:567
  (4 shorter events, 0.0 us)
Async XLA Ops:
  0.6 4.6 %collective-permute-start = (bf16[128,640]{1,0:T(8,128)(2,1)}, bf16[128,640]{1,0:T(8,128)(2,1)S(1)}, u32[]{:S(2)}, u32[]{:S(2)}) collective-permute-start(bf16[128,640]{1,0:T(8,128)(2,1)} %bitcast.12), channel_id=1, source_target_pairs={{0,1},{1,0},{2,3},{3,2},{4,5},{5,4},{6,7},{7,6},{8,9},{9,8},{10,11... | collective-permute-start | bytes 491528 | tf_op jit(solution)/shard_map/ppermute | solution.py:442
  4.0 1.6 %collective-permute-start.1 = (bf16[128,640]{1,0:T(8,128)(2,1)}, bf16[128,640]{1,0:T(8,128)(2,1)S(1)}, u32[]{:S(2)}, u32[]{:S(2)}) collective-permute-start(bf16[128,640]{1,0:T(8,128)(2,1)} %bitcast.10), channel_id=1, source_target_pairs={{0,1},{1,0},{2,3},{3,2},{4,5},{5,4},{6,7},{7,6},{8,9},{9,8},{10,11... | collective-permute-start | bytes 491528 | tf_op jit(solution)/shard_map/ppermute | solution.py:442
  7.9 26.5 %all-to-all-start = ((bf16[16,336,128]{2,1,0:T(8,128)(2,1)}), bf16[16,336,128]{2,1,0:T(8,128)(2,1)S(1)}, u32[]{:S(2)}, u32[]{:S(2)}) async-start(bf16[16,336,128]{2,1,0:T(8,128)(2,1)} %pack.1), calls=%async_computation | async-start | bytes 2752512 | tf_op jit(solution)/shard_map/all_to_all | solution.py:475
  13.7 9.3 %collective-permute-start.2 = (bf16[32,640]{1,0:T(8,128)(2,1)S(1)}, bf16[32,640]{1,0:T(8,128)(2,1)S(1)}, u32[]{:S(2)}, u32[]{:S(2)}) collective-permute-start(bf16[32,640]{1,0:T(8,128)(2,1)S(1)} %maximum_select_fusion), channel_id=1, source_target_pairs={{0,8},{8,16},{16,24},{24,32},{32,40},{40,48},{48,56},{56,64},{64,7... | collective-permute-start | bytes 122888 | tf_op jit(solution)/shard_map/ppermute | solution.py:463
  23.0 1.2 %collective-permute-start.3 = (bf16[32,640]{1,0:T(8,128)(2,1)S(1)}, bf16[32,640]{1,0:T(8,128)(2,1)S(1)}, u32[]{:S(2)}, u32[]{:S(2)}) collective-permute-start(bf16[32,640]{1,0:T(8,128)(2,1)S(1)} %collective-permute-done.2.mine_ref), channel_id=1, source_target_pairs={{0,1},{1,0},{2,3},{3,2},{4,5},{5,4},{6,7},{7,6},{8,9},{9,8},{10,11... | collective-permute-start | bytes 122888 | tf_op jit(solution)/shard_map/ppermute | solution.py:442
  26.5 18.6 %copy-start = (f32[640]{0:T(1024)S(1)}, f32[640]{0:T(1024)}, u32[]{:S(2)}) copy-start(f32[640]{0:T(1024)} %param.8) | copy-start | bytes 7684
  26.5 18.6 %copy-start.1 = (f32[640]{0:T(1024)S(1)}, f32[640]{0:T(1024)}, u32[]{:S(2)}) copy-start(f32[640]{0:T(1024)} %param.9) | copy-start | bytes 7684
  34.4 28.2 %collective-permute-start.5 = (bf16[16,336,128]{2,1,0:T(8,128)(2,1)S(1)}, bf16[16,336,128]{2,1,0:T(8,128)(2,1)}, u32[]{:S(2)}, u32[]{:S(2)}) collective-permute-start(bf16[16,336,128]{2,1,0:T(8,128)(2,1)S(1)} %all-to-all-done.slab_ref.own_ref), channel_id=1, source_target_pairs={{0,1},{1,0},{2,3},{3,2},{4,5},{5,4},{6,7},{7,6},{8,9},{9,8},{10,11... | collective-permute-start | bytes 4128776 | tf_op jit(solution)/shard_map/ppermute | solution.py:442
  36.9 19.0 %all-to-all-start.1 = ((bf16[8,96,128]{2,1,0:T(8,128)(2,1)}), bf16[8,96,128]{2,1,0:T(8,128)(2,1)S(1)}, u32[]{:S(2)}, u32[]{:S(2)}) async-start(bf16[8,96,128]{2,1,0:T(8,128)(2,1)} %split.1), calls=%async_computation.1 | async-start | bytes 393216 | tf_op jit(solution)/shard_map/all_to_all | solution.py:498
  45.2 6.4 %collective-permute-start.4 = (f32[8,640]{1,0:T(8,128)S(1)}, f32[8,640]{1,0:T(8,128)S(1)}, u32[]{:S(2)}, u32[]{:S(2)}) collective-permute-start(f32[8,640]{1,0:T(8,128)S(1)} %get-tuple-element.20), channel_id=1, source_target_pairs={{1,2},{3,4},{5,6},{2,1},{4,3},{6,5},{9,10},{11,12},{13,14},{10,9},... | collective-permute-start | bytes 61448 | tf_op jit(solution)/shard_map/ppermute | solution.py:488
  57.0 13.2 %all-to-all-start.2 = ((f32[32,8,128]{2,1,0:T(8,128)}), f32[32,8,128]{2,1,0:T(8,128)S(1)}, u32[]{:S(2)}, u32[]{:S(2)}) async-start(f32[32,8,128]{2,1,0:T(8,128)} %get-tuple-element.21), calls=%async_computation.2 | async-start | bytes 262144 | tf_op jit(solution)/shard_map/all_to_all | solution.py:523
  84.2 3.1 %collective-permute-start.6 = (bf16[8,64,256]{2,1,0:T(8,128)(2,1)S(1)}, bf16[8,64,256]{2,1,0:T(8,128)(2,1)S(1)}, u32[]{:S(2)}, u32[]{:S(2)}) collective-permute-start(bf16[8,64,256]{2,1,0:T(8,128)(2,1)S(1)} %all_to_all.20.got_ref), channel_id=1, source_target_pairs={{0,1},{1,0},{2,3},{3,2},{4,5},{5,4},{6,7},{7,6},{8,9},{9,8},{10,11... | collective-permute-start | bytes 786440 | tf_op jit(solution)/shard_map/ppermute | solution.py:442

commit v10 on v9

--- a/solution.py
+++ b/solution.py
@@ -173,7 +173,7 @@
     moved = jnp.dot(feat_ref[...], pick(feature_columns()), preferred_element_type=f32)
     moved_rest = lanes32(moved[:, 512:], 32)
     for p in range(PEERS):
-        y = p // NX
+        y = p % NY
         out_ref[p, 0:128] = moved[:, y * 128 : (y + 1) * 128].astype(bf16)
         out_ref[p, 128:160] = moved_rest[y].astype(bf16)
     copies = fetch(((out_ref.at[:, :F_ROWS, :], out_hbm.at[:, :F_ROWS, :]),), sem.at[0:1])
@@ -181,7 +181,7 @@
     terms = blocks(core, first, second)
     terms_rest = lanes32(terms[:, 512:], 32)
     for p in range(PEERS):
-        xx = p % NX
+        xx = p // NY
         out_ref[p, 160:288] = terms[:, xx * 128 : (xx + 1) * 128].astype(bf16)
         out_ref[p, 288:320] = terms_rest[xx].astype(bf16)
         out_ref[p, S_AT:] = stats
@@ -207,9 +207,9 @@
     group = lax.broadcasted_iota(jnp.int32, (TC, 128), 1) // 32
     first, last = jnp.zeros((TC, 128), f32), jnp.zeros((TC, 128), f32)
     for xx in range(NX):
-        tail = slab_ref[xx, 288:304].astype(f32)
+        tail = slab_ref[xx * NY, 288:304].astype(f32)
         first = jnp.where(group == xx, pltpu.roll(tail, 32 * xx, 1) if xx else tail, first)
-        tail = slab_ref[(NY - 1) * NX + xx, 304:320].astype(f32)
+        tail = slab_ref[xx * NY + NY - 1, 304:320].astype(f32)
         last = jnp.where(group == xx, pltpu.roll(tail, (32 * xx + 32) % 128, 1) if xx < 3 else tail, last)
     first, last = first.astype(bf16), last.astype(bf16)
     for p in range(NZ):
@@ -218,13 +218,13 @@
         @pl.when(z_ref[0] < p)
         def _():
             for xx in range(NX):
-                out_ref[p, 16 + 16 * xx : 32 + 16 * xx] = slab_ref[(NY - 1) * NX + xx, 272:288]
+                out_ref[p, 16 + 16 * xx : 32 + 16 * xx] = slab_ref[xx * NY + NY - 1, 272:288]
             out_ref[p, 80:] = last
 
         @pl.when(z_ref[0] >= p)
         def _():
             for xx in range(NX):
-                out_ref[p, 16 + 16 * xx : 32 + 16 * xx] = slab_ref[xx, 160:176]
+                out_ref[p, 16 + 16 * xx : 32 + 16 * xx] = slab_ref[xx * NY, 160:176]
             out_ref[p, 80:] = first
 
 
@@ -308,7 +308,7 @@
     core = core_ref[0]
 
     def put(block, peer, side):
-        y, xx = peer // NX, peer % NX
+        xx, y = peer // NY, peer % NY
 
         def silu(x, lanes):
             a = (x.astype(f32) - par_ref[0:1, lanes]) * par_ref[1:2, lanes] + par_ref[2:3, lanes]
@@ -325,7 +325,7 @@
                 hidden[y][at, 128:256] = low[h * TC : (h + 1) * TC]
 
     for peer in range(PEERS):
-        y, xx = peer // NX, peer % NX
+        xx, y = peer // NY, peer % NY
         tail = own_ref[peer, 288:320].astype(f32)
         for g in range(4):
             main = own_ref[peer, 160 + 32 * g : 192 + 32 * g].astype(f32)
@@ -355,7 +355,7 @@
     cot3[3 * NQ :] = jnp.zeros((16, (ROWS + 2) * 128), bf16)
     copies[0].wait()
     for y in range(NY):
-        for peer in range(y * NX, (y + 1) * NX):
+        for peer in range(y, PEERS, NY):
             put(own_ref[peer, :F_ROWS], peer, core)
             put(other_ref[peer], peer, 1 - core)
         for i in range(3):
@@ -472,7 +472,7 @@
         cost_estimate=pl.CostEstimate(flops=1 << 28, bytes_accessed=2 << 20, transcendentals=0),
         name="pack",
     )(at_core, both, feat2, cot2)
-    slab = lax.all_to_all(packed, ("y", "x"), 0, 0)
+    slab = lax.all_to_all(packed, ("x", "y"), 0, 0)
     theirs = flip(mine)
     side, shifted = pl.pallas_call(
         side_kernel,
@@ -494,7 +494,8 @@
         compiler_params=params(),
         name="split",
     )(at_z, slab)
-    slab_other = flip(slab)
+    late, edges = lax.optimization_barrier((slab, edges))
+    slab_other = flip(late)
     edges = lax.all_to_all(edges, "z", 0, 0)
     back = pl.pallas_call(
         back_kernel,

time: 89 us -> 87.5 us (0.983)
  waiting for transfers between devices: 26.1 us -> 19.2 us
  starting transfers between devices: 29 us -> 34.1 us
    ppermute x5, starting transfers between devices: 7.03 us -> 13 us  [flip(): return lax.ppermute(value, 'core', [(0, 1), (1, 0)])]
    all_to_all x1, waiting for transfers between devices: 7.88 us -> 4.79 us  [body(): slab = lax.all_to_all(packed, ('x', 'y'), 0, 0)]
    ppermute x1, waiting for transfers between devices: 8.01 us -> 4.93 us  [body(): mine = lax.ppermute(edge, ('z', 'y', 'core'), ways)]
    all_to_all x1, starting transfers between devices: 5.54 us -> 4.32 us  [body(): sums = lax.all_to_all(sums, ('y', 'x', 'core'), 0, 0)]
  transfers between devices with their start and end apart: 10 -> 10, of which waited for: 8 -> 8; matrix products, arithmetic and copies ran while one was open for 2% -> 2% of each run, Pallas kernels for 15% -> 14%
where the time goes in v10:
time: 87.5 us; the launch traced here: 87 us
  starting transfers between devices  34.1 us (39%)
  waiting for transfers between devices  19.2 us (22%)
  Pallas kernels  16.9 us (19%)
  blocking collectives  14.2 us (16%)
  other arithmetic  1.04 us (1%)
    all_to_all x1, blocking collectives, body(): joined = lax.all_to_all(joined, 'z', 0, 0)  14.2 us
    ppermute x5, starting transfers between devices, flip(): return lax.ppermute(value, 'core', [(0, 1), (1, 0)])  13 us
    all_to_all x1, starting transfers between devices, body(): edges = lax.all_to_all(edges, 'z', 0, 0)  8.18 us
    all_to_all x1, starting transfers between devices, body(): slab = lax.all_to_all(packed, ('x', 'y'), 0, 0)  5.03 us
    ppermute x1, waiting for transfers between devices, body(): mine = lax.ppermute(edge, ('z', 'y', 'core'), ways)  4.93 us
    all_to_all x1, waiting for transfers between devices, body(): slab = lax.all_to_all(packed, ('x', 'y'), 0, 0)  4.79 us
    pallas_call x1, Pallas kernels, body(): pl.pallas_call(back_kernel, out_shape=shape((PIX, C), f32), in_specs=[vme...  4.46 us
    all_to_all x1, starting transfers between devices, body(): sums = lax.all_to_all(sums, ('y', 'x', 'core'), 0, 0)  4.32 us
  transfers between devices with their start and end apart: 10, of which 8 were waited for; matrix products, arithmetic and copies ran while one was open for 2% of the time, Pallas kernels for 14%

profile of v10, /device:TPU:1, one launch (start us, length us, event | category | flops | bytes accessed | tf_op | source)
XLA Modules:
  0.0 87.0 jit_solution(6268142637606487368)
XLA Ops:
  0.6 3.3 %collective-permute-start = (bf16[128,640]{1,0:T(8,128)(2,1)}, bf16[128,640]{1,0:T(8,128)(2,1)S(1)}, u32[]{:S(2)}, u32[]{:S(2)}) collective-permute-start(bf16[128,640]{1,0:T(8,128)(2,1)} %bitcast.12), channel_id=1, source_target_pairs={{0,1},{1,0},{2,3},{3,2},{4,5},{5,4},{6,7},{7,6},{8,9},{9,8},{10,11... | collective-permute-start | bytes 491528 | tf_op jit(solution)/shard_map/ppermute | solution.py:442
  4.0 0.1 collective-permute-start.1
  4.1 1.0 %pad_maximum_fusion.both_ref = bf16[256,640]{1,0:T(8,128)(2,1)S(1)} fusion(bf16[128,640]{1,0:T(8,128)(2,1)} %bitcast.11, bf16[128,640]{1,0:T(8,128)(2,1)} %bitcast.13), kind=kLoop, calls=%fused_computation | loop fusion | flops 655360 | bytes 655360 | tf_op jit(solution)/shard_map/concatenate | solution.py:455
  5.1 0.1 collective-permute-done.feat2_ref
  5.2 0.4 collective-permute-done.1.cot2_ref
  5.6 2.3 %pack.1 = bf16[16,336,128]{2,1,0:T(8,128)(2,1)} custom-call(s32[1]{0:T(128)} %bitcast.core_ref, bf16[256,640]{1,0:T(8,128)(2,1)S(1)} %pad_maximum_fusion.both_ref, bf16[128,640]{1,0:T(8,128)(2,1)S(1)} %collective-permute-done.feat2_ref, bf16[128,640]{1,0:T(8,128)(2,1)S(1)} %collective-permute-done.1.cot2_ref), custom_call_target="tpu_custom_call" | custom-call | flops 268435456 | bytes 2097152 | tf_op jit(solution)/shard_map/pack/pallas_call | solution.py:465
  7.9 5.0 %all-to-all-start = ((bf16[16,336,128]{2,1,0:T(8,128)(2,1)}), bf16[16,336,128]{2,1,0:T(8,128)(2,1)S(1)}, u32[]{:S(2)}, u32[]{:S(2)}) async-start(bf16[16,336,128]{2,1,0:T(8,128)(2,1)} %pack.1), calls=%async_computation | async-start | bytes 2752512 | tf_op jit(solution)/shard_map/all_to_all | solution.py:475
  12.9 0.8 slice_bitcast_fusion
  13.7 1.3 %collective-permute-start.2 = (bf16[32,640]{1,0:T(8,128)(2,1)S(1)}, bf16[32,640]{1,0:T(8,128)(2,1)S(1)}, u32[]{:S(2)}, u32[]{:S(2)}) collective-permute-start(bf16[32,640]{1,0:T(8,128)(2,1)S(1)} %maximum_select_fusion), channel_id=1, source_target_pairs={{0,8},{8,16},{16,24},{24,32},{32,40},{40,48},{48,56},{56,64},{64,7... | collective-permute-start | bytes 122888 | tf_op jit(solution)/shard_map/ppermute | solution.py:463
  15.0 4.9 %collective-permute-done.2.mine_ref = bf16[32,640]{1,0:T(8,128)(2,1)S(1)} collective-permute-done((bf16[32,640]{1,0:T(8,128)(2,1)S(1)}, bf16[32,640]{1,0:T(8,128)(2,1)S(1)}, u32[]{:S(2)}, u32[]{:S(2)}) %collective-permute-start.2) | collective-permute-done | bytes 40992 | tf_op jit(solution)/shard_map/ppermute | solution.py:463
  19.9 5.3 %collective-permute-start.3 = (bf16[32,640]{1,0:T(8,128)(2,1)S(1)}, bf16[32,640]{1,0:T(8,128)(2,1)S(1)}, u32[]{:S(2)}, u32[]{:S(2)}) collective-permute-start(bf16[32,640]{1,0:T(8,128)(2,1)S(1)} %collective-permute-done.2.mine_ref), channel_id=1, source_target_pairs={{0,1},{1,0},{2,3},{3,2},{4,5},{5,4},{6,7},{7,6},{8,9},{9,8},{10,11... | collective-permute-start | bytes 122888 | tf_op jit(solution)/shard_map/ppermute | solution.py:442
  25.2 0.9 %collective-permute-done.3.theirs_ref = bf16[32,640]{1,0:T(8,128)(2,1)S(1)} collective-permute-done((bf16[32,640]{1,0:T(8,128)(2,1)S(1)}, bf16[32,640]{1,0:T(8,128)(2,1)S(1)}, u32[]{:S(2)}, u32[]{:S(2)}) %collective-permute-start.3) | collective-permute-done | bytes 40992 | tf_op jit(solution)/shard_map/ppermute | solution.py:442
  26.0 2.3 %side.1 = (f32[8,640]{1,0:T(8,128)S(1)}, bf16[3,160,640]{2,1,0:T(8,128)(2,1)S(1)}) custom-call(s32[1]{0:T(128)} %bitcast.core_ref, bf16[256,640]{1,0:T(8,128)(2,1)S(1)} %pad_maximum_fusion.both_ref, bf16[128,640]{1,0:T(8,128)(2,1)S(1)} %collective-permute-done.1.cot2_ref, bf16[32,640]{1,0:T(8,128)(2,1)S(1)} %collective-permute-done.2.mine_ref, ...), custom_call_target="tpu_custom_call" | custom-call | tf_op jit(solution)/shard_map/side/pallas_call | solution.py:477
  28.3 0.0 copy-start
  28.3 0.0 copy-start.1
  28.4 4.8 %all-to-all-done.slab_ref.own_ref = bf16[16,336,128]{2,1,0:T(8,128)(2,1)S(1)} async-done(((bf16[16,336,128]{2,1,0:T(8,128)(2,1)}), bf16[16,336,128]{2,1,0:T(8,128)(2,1)S(1)}, u32[]{:S(2)}, u32[]{:S(2)}) %all-to-all-start) | async-done | bytes 1376288 | tf_op jit(solution)/shard_map/all_to_all | solution.py:475
  33.1 0.9 split.1
  34.0 2.4 %collective-permute-start.5 = (bf16[16,336,128]{2,1,0:T(8,128)(2,1)S(1)}, bf16[16,336,128]{2,1,0:T(8,128)(2,1)}, u32[]{:S(2)}, u32[]{:S(2)}) collective-permute-start(bf16[16,336,128]{2,1,0:T(8,128)(2,1)S(1)} %all-to-all-done.slab_ref.own_ref), channel_id=1, source_target_pairs={{0,1},{1,0},{2,3},{3,2},{4,5},{5,4},{6,7},{7,6},{8,9},{9,8},{10,11... | collective-permute-start | bytes 4128776 | tf_op jit(solution)/shard_map/ppermute | solution.py:442
  36.4 8.2 %all-to-all-start.1 = ((bf16[8,96,128]{2,1,0:T(8,128)(2,1)}), bf16[8,96,128]{2,1,0:T(8,128)(2,1)S(1)}, u32[]{:S(2)}, u32[]{:S(2)}) async-start(bf16[8,96,128]{2,1,0:T(8,128)(2,1)} %split.1), calls=%async_computation.1 | async-start | bytes 393216 | tf_op jit(solution)/shard_map/all_to_all | solution.py:499
  44.6 0.0 copy-done
  44.6 0.0 copy-done.1
  44.6 2.3 %collective-permute-start.4 = (f32[8,640]{1,0:T(8,128)S(1)}, f32[8,640]{1,0:T(8,128)S(1)}, u32[]{:S(2)}, u32[]{:S(2)}) collective-permute-start(f32[8,640]{1,0:T(8,128)S(1)} %get-tuple-element.23), channel_id=1, source_target_pairs={{1,2},{3,4},{5,6},{2,1},{4,3},{6,5},{9,10},{11,12},{13,14},{10,9},... | collective-permute-start | bytes 61448 | tf_op jit(solution)/shard_map/ppermute | solution.py:488
  46.9 4.5 %back.1.back_ref = f32[128,640]{1,0:T(8,128)S(1)} custom-call(bf16[3,160,640]{2,1,0:T(8,128)(2,1)S(1)} %get-tuple-element.22.shifted, bf16[3,3,640,640]{3,2,1,0:T(8,128)(2,1)} %w_hbm.3), custom_call_target="tpu_custom_call" | custom-call | flops 943718400 | bytes 7372800 | tf_op jit(solution)/shard_map/back/pallas_call | solution.py:500
  51.4 0.0 collective-permute-done.4.side_ref
  51.4 4.0 %all-to-all-done.1.stat_ref.edge_ref = bf16[8,96,128]{2,1,0:T(8,128)(2,1)S(1)} async-done(((bf16[8,96,128]{2,1,0:T(8,128)(2,1)}), bf16[8,96,128]{2,1,0:T(8,128)(2,1)S(1)}, u32[]{:S(2)}, u32[]{:S(2)}) %all-to-all-start.1) | async-done | bytes 196640 | tf_op jit(solution)/shard_map/all_to_all | solution.py:499
  55.4 1.1 %sums.1 = (f32[8,640]{1,0:T(8,128)S(1)}, f32[128,640]{1,0:T(8,128)S(1)}, f32[8,256]{1,0:T(8,128)S(1)}, f32[32,8,128]{2,1,0:T(8,128)}, f32[640]{0:T(1024)}) custom-call(s32[1]{0:T(128)} %bitcast.core_ref, s32[1]{0:T(128)} %bitcast.1.y_ref, bf16[8,96,128]{2,1,0:T(8,128)(2,1)S(1)} %all-to-all-done.1.stat_ref.edge_ref, ...), custom_call_target="tpu_custom_call" | custom-call | tf_op jit(solution)/shard_map/sums/pallas_call | solution.py:510
  56.5 4.3 %all-to-all-start.2 = ((f32[32,8,128]{2,1,0:T(8,128)}), f32[32,8,128]{2,1,0:T(8,128)S(1)}, u32[]{:S(2)}, u32[]{:S(2)}) async-start(f32[32,8,128]{2,1,0:T(8,128)} %get-tuple-element.24), calls=%async_computation.2 | async-start | bytes 262144 | tf_op jit(solution)/shard_map/all_to_all | solution.py:524
  60.8 0.0 collective-permute-done.5.other_hbm
  60.8 3.9 %terms.1.terms_ref = bf16[8,64,256]{2,1,0:T(8,128)(2,1)S(1)} custom-call(s32[1]{0:T(128)} %bitcast.core_ref, s32[1]{0:T(128)} %bitcast.6.z_ref, bf16[16,336,128]{2,1,0:T(8,128)(2,1)S(1)} %all-to-all-done.slab_ref.own_ref, bf16[16,336,128]{2,1,0:T(8,128)(2,1)} %collective-permute-done.5.other_hbm, bf16[8,96,128]{2,1,0:T(8,128)(2,1)S(1)} %all-to-all-done.1.stat_ref.edge_ref, ...), custom_call_target="tpu_custom_call" | custom-call | flops 943718400 | bytes 4194304 | tf_op jit(solution)/shard_map/terms/pallas_call | solution.py:526
  64.7 3.7 %all-to-all-done.2.sums_ref = f32[32,8,128]{2,1,0:T(8,128)S(1)} async-done(((f32[32,8,128]{2,1,0:T(8,128)}), f32[32,8,128]{2,1,0:T(8,128)S(1)}, u32[]{:S(2)}, u32[]{:S(2)}) %all-to-all-start.2) | async-done | bytes 131104 | tf_op jit(solution)/shard_map/all_to_all | solution.py:524
  68.5 0.1 join.1
  68.6 14.2 %all_to_all.20.got_ref = bf16[8,64,256]{2,1,0:T(8,128)(2,1)S(1)} all-to-all(bf16[8,64,256]{2,1,0:T(8,128)(2,1)S(1)} %join.1), channel_id=1, replica_groups=mesh['z'=8,'y'=4,'x'=4,'core'=2] {'z'}, dimensions={0} | all-to-all | bytes 524288 | tf_op jit(solution)/shard_map/all_to_all | solution.py:558
  82.8 1.9 %collective-permute-start.6 = (bf16[8,64,256]{2,1,0:T(8,128)(2,1)S(1)}, bf16[8,64,256]{2,1,0:T(8,128)(2,1)S(1)}, u32[]{:S(2)}, u32[]{:S(2)}) collective-permute-start(bf16[8,64,256]{2,1,0:T(8,128)(2,1)S(1)} %all_to_all.20.got_ref), channel_id=1, source_target_pairs={{0,1},{1,0},{2,3},{3,2},{4,5},{5,4},{6,7},{7,6},{8,9},{9,8},{10,11... | collective-permute-start | bytes 786440 | tf_op jit(solution)/shard_map/ppermute | solution.py:442
  84.7 0.8 gather.1
  85.4 0.4 collective-permute-done.6.other_ref
  85.9 1.1 %final.1 = (bf16[128,640]{1,0:T(8,128)(2,1)}, f32[640]{0:T(1024)}, f32[640]{0:T(1024)}) custom-call(s32[1]{0:T(128)} %bitcast.core_ref, bf16[8,64,256]{2,1,0:T(8,128)(2,1)S(1)} %all_to_all.20.got_ref, bf16[8,64,256]{2,1,0:T(8,128)(2,1)S(1)} %collective-permute-done.6.other_ref, bf16[256,640]{1,0:T(8,128)(2,1)S(1)} %pad_maximum_fusion.both_ref, ...), custom_call_target="tpu_custom_call" | custom-call | tf_op jit(solution)/shard_map/final/pallas_call | solution.py:568
  (4 shorter events, 0.0 us)
Async XLA Ops:
  0.6 4.6 %collective-permute-start = (bf16[128,640]{1,0:T(8,128)(2,1)}, bf16[128,640]{1,0:T(8,128)(2,1)S(1)}, u32[]{:S(2)}, u32[]{:S(2)}) collective-permute-start(bf16[128,640]{1,0:T(8,128)(2,1)} %bitcast.12), channel_id=1, source_target_pairs={{0,1},{1,0},{2,3},{3,2},{4,5},{5,4},{6,7},{7,6},{8,9},{9,8},{10,11... | collective-permute-start | bytes 491528 | tf_op jit(solution)/shard_map/ppermute | solution.py:442
  4.0 1.6 %collective-permute-start.1 = (bf16[128,640]{1,0:T(8,128)(2,1)}, bf16[128,640]{1,0:T(8,128)(2,1)S(1)}, u32[]{:S(2)}, u32[]{:S(2)}) collective-permute-start(bf16[128,640]{1,0:T(8,128)(2,1)} %bitcast.10), channel_id=1, source_target_pairs={{0,1},{1,0},{2,3},{3,2},{4,5},{5,4},{6,7},{7,6},{8,9},{9,8},{10,11... | collective-permute-start | bytes 491528 | tf_op jit(solution)/shard_map/ppermute | solution.py:442
  7.9 25.3 %all-to-all-start = ((bf16[16,336,128]{2,1,0:T(8,128)(2,1)}), bf16[16,336,128]{2,1,0:T(8,128)(2,1)S(1)}, u32[]{:S(2)}, u32[]{:S(2)}) async-start(bf16[16,336,128]{2,1,0:T(8,128)(2,1)} %pack.1), calls=%async_computation | async-start | bytes 2752512 | tf_op jit(solution)/shard_map/all_to_all | solution.py:475
  13.7 6.2 %collective-permute-start.2 = (bf16[32,640]{1,0:T(8,128)(2,1)S(1)}, bf16[32,640]{1,0:T(8,128)(2,1)S(1)}, u32[]{:S(2)}, u32[]{:S(2)}) collective-permute-start(bf16[32,640]{1,0:T(8,128)(2,1)S(1)} %maximum_select_fusion), channel_id=1, source_target_pairs={{0,8},{8,16},{16,24},{24,32},{32,40},{40,48},{48,56},{56,64},{64,7... | collective-permute-start | bytes 122888 | tf_op jit(solution)/shard_map/ppermute | solution.py:463
  19.9 6.1 %collective-permute-start.3 = (bf16[32,640]{1,0:T(8,128)(2,1)S(1)}, bf16[32,640]{1,0:T(8,128)(2,1)S(1)}, u32[]{:S(2)}, u32[]{:S(2)}) collective-permute-start(bf16[32,640]{1,0:T(8,128)(2,1)S(1)} %collective-permute-done.2.mine_ref), channel_id=1, source_target_pairs={{0,1},{1,0},{2,3},{3,2},{4,5},{5,4},{6,7},{7,6},{8,9},{9,8},{10,11... | collective-permute-start | bytes 122888 | tf_op jit(solution)/shard_map/ppermute | solution.py:442
  28.3 16.3 %copy-start = (f32[640]{0:T(1024)S(1)}, f32[640]{0:T(1024)}, u32[]{:S(2)}) copy-start(f32[640]{0:T(1024)} %param.8) | copy-start | bytes 7684
  28.3 16.3 %copy-start.1 = (f32[640]{0:T(1024)S(1)}, f32[640]{0:T(1024)}, u32[]{:S(2)}) copy-start(f32[640]{0:T(1024)} %param.9) | copy-start | bytes 7684
  34.0 26.8 %collective-permute-start.5 = (bf16[16,336,128]{2,1,0:T(8,128)(2,1)S(1)}, bf16[16,336,128]{2,1,0:T(8,128)(2,1)}, u32[]{:S(2)}, u32[]{:S(2)}) collective-permute-start(bf16[16,336,128]{2,1,0:T(8,128)(2,1)S(1)} %all-to-all-done.slab_ref.own_ref), channel_id=1, source_target_pairs={{0,1},{1,0},{2,3},{3,2},{4,5},{5,4},{6,7},{7,6},{8,9},{9,8},{10,11... | collective-permute-start | bytes 4128776 | tf_op jit(solution)/shard_map/ppermute | solution.py:442
  36.4 19.0 %all-to-all-start.1 = ((bf16[8,96,128]{2,1,0:T(8,128)(2,1)}), bf16[8,96,128]{2,1,0:T(8,128)(2,1)S(1)}, u32[]{:S(2)}, u32[]{:S(2)}) async-start(bf16[8,96,128]{2,1,0:T(8,128)(2,1)} %split.1), calls=%async_computation.1 | async-start | bytes 393216 | tf_op jit(solution)/shard_map/all_to_all | solution.py:499
  44.6 6.7 %collective-permute-start.4 = (f32[8,640]{1,0:T(8,128)S(1)}, f32[8,640]{1,0:T(8,128)S(1)}, u32[]{:S(2)}, u32[]{:S(2)}) collective-permute-start(f32[8,640]{1,0:T(8,128)S(1)} %get-tuple-element.23), channel_id=1, source_target_pairs={{1,2},{3,4},{5,6},{2,1},{4,3},{6,5},{9,10},{11,12},{13,14},{10,9},... | collective-permute-start | bytes 61448 | tf_op jit(solution)/shard_map/ppermute | solution.py:488
  56.5 12.0 %all-to-all-start.2 = ((f32[32,8,128]{2,1,0:T(8,128)}), f32[32,8,128]{2,1,0:T(8,128)S(1)}, u32[]{:S(2)}, u32[]{:S(2)}) async-start(f32[32,8,128]{2,1,0:T(8,128)} %get-tuple-element.24), calls=%async_computation.2 | async-start | bytes 262144 | tf_op jit(solution)/shard_map/all_to_all | solution.py:524
  82.8 3.1 %collective-permute-start.6 = (bf16[8,64,256]{2,1,0:T(8,128)(2,1)S(1)}, bf16[8,64,256]{2,1,0:T(8,128)(2,1)S(1)}, u32[]{:S(2)}, u32[]{:S(2)}) collective-permute-start(bf16[8,64,256]{2,1,0:T(8,128)(2,1)S(1)} %all_to_all.20.got_ref), channel_id=1, source_target_pairs={{0,1},{1,0},{2,3},{3,2},{4,5},{5,4},{6,7},{7,6},{8,9},{9,8},{10,11... | collective-permute-start | bytes 786440 | tf_op jit(solution)/shard_map/ppermute | solution.py:442

commit v11 on v10

--- a/solution.py
+++ b/solution.py
@@ -211,21 +211,13 @@
         first = jnp.where(group == xx, pltpu.roll(tail, 32 * xx, 1) if xx else tail, first)
         tail = slab_ref[xx * NY + NY - 1, 304:320].astype(f32)
         last = jnp.where(group == xx, pltpu.roll(tail, (32 * xx + 32) % 128, 1) if xx < 3 else tail, last)
-    first, last = first.astype(bf16), last.astype(bf16)
+    first = jnp.concatenate([slab_ref[xx * NY, 160:176].astype(f32) for xx in range(NX)] + [first], axis=0)
+    last = jnp.concatenate(
+        [slab_ref[xx * NY + NY - 1, 272:288].astype(f32) for xx in range(NX)] + [last], axis=0
+    )
     for p in range(NZ):
         out_ref[p, :S_ROWS] = stats
-
-        @pl.when(z_ref[0] < p)
-        def _():
-            for xx in range(NX):
-                out_ref[p, 16 + 16 * xx : 32 + 16 * xx] = slab_ref[xx * NY + NY - 1, 272:288]
-            out_ref[p, 80:] = last
-
-        @pl.when(z_ref[0] >= p)
-        def _():
-            for xx in range(NX):
-                out_ref[p, 16 + 16 * xx : 32 + 16 * xx] = slab_ref[xx * NY, 160:176]
-            out_ref[p, 80:] = first
+        out_ref[p, S_ROWS:] = jnp.where(z_ref[0] < p, last, first).astype(bf16)
 
 
 def back_kernel(shifted, w_hbm, out_ref, w_ref, sem):
@@ -398,22 +390,23 @@
             out_ref[z, at] = jnp.concatenate([left, right], axis=1).astype(bf16)
 
 
-def final_kernel(core_ref, got_ref, other_ref, both_ref, da_ref, row_ref, gain_ref,
+def total_kernel(got_ref, out_ref):
+    lane = lax.broadcasted_iota(jnp.int32, (8, 128), 1)
+    middle = jnp.zeros((8, 128), f32)
+    upper, right = got_ref[0, 48:].astype(f32), got_ref[0, :, 128:].astype(f32)
+    for z in range(1, NZ):
+        upper = upper + got_ref[z, 48:].astype(f32)
+        right = right + got_ref[z, :, 128:].astype(f32)
+    high = jnp.concatenate([upper[12:16, :128], upper[13:14, 128:]], axis=0)
+    for c in range(8):
+        part = pltpu.roll(right[8 * c : 8 * c + 8], (16 * c - 112) % 128, 1)
+        middle = jnp.where(lane // 16 == c, part, middle)
+    out_ref[...] = rows8(unfold(high + middle[:5]))
+
+
+def final_kernel(core_ref, own_ref, other_ref, both_ref, da_ref, row_ref, gain_ref,
                  grad_ref, gain_grad_ref, shift_grad_ref):
-    lane = lax.broadcasted_iota(jnp.int32, (8, 128), 1)
-
-    def total(ref):
-        out = ref[0].astype(f32)
-        for z in range(1, NZ):
-            out = out + ref[z].astype(f32)
-        high = jnp.concatenate([out[60:64, :128], out[61:62, 128:]], axis=0)
-        middle = jnp.zeros((8, 128), f32)
-        for c in range(8):
-            part = pltpu.roll(out[8 * c : 8 * c + 8, 128:], (16 * c - 112) % 128, 1)
-            middle = jnp.where(lane // 16 == c, part, middle)
-        return unfold(high + middle[:5])
-
-    own, other = total(got_ref), total(other_ref)
+    own, other = own_ref[0:1], other_ref[0:1]
     lower = core_ref[0] == 0
     sums = (jnp.where(lower, own, other), jnp.where(lower, other, own))
     shift_grad_ref[...], gain_grad_ref[...] = [value.reshape(C) for value in sums]
@@ -556,6 +549,14 @@
         name="join",
     )(sums, terms)
     joined = lax.all_to_all(joined, "z", 0, 0)
+    total = pl.pallas_call(
+        total_kernel,
+        out_shape=shape((8, C), f32),
+        in_specs=[vmem()],
+        out_specs=vmem(),
+        compiler_params=params(),
+        name="total",
+    )(joined)
     weight_grad = pl.pallas_call(
         gather_kernel,
         out_shape=shape((3, 3, 20, NQ), f32),
@@ -572,7 +573,7 @@
         out_specs=(vmem(),) * 3,
         compiler_params=params(),
         name="final",
-    )(at_core, joined, flip(joined), both, da, row, gain)
+    )(at_core, total, flip(total), both, da, row, gain)
     return grad.reshape(features.shape), weight_grad, gain_grad, shift_grad, bias_grad
 
 

time: 87.5 us -> 87.3 us (level)
  no operation moved by 1% of the time
where the time goes in v11:
time: 87.3 us; the launch traced here: 86.7 us
  starting transfers between devices  34.2 us (39%)
  waiting for transfers between devices  18.9 us (22%)
  Pallas kernels  16.8 us (19%)
  blocking collectives  14.2 us (16%)
  other arithmetic  1.04 us (1%)
    all_to_all x1, blocking collectives, body(): joined = lax.all_to_all(joined, 'z', 0, 0)  14.2 us
    ppermute x5, starting transfers between devices, flip(): return lax.ppermute(value, 'core', [(0, 1), (1, 0)])  13.1 us
    all_to_all x1, starting transfers between devices, body(): edges = lax.all_to_all(edges, 'z', 0, 0)  8.19 us
    all_to_all x1, starting transfers between devices, body(): slab = lax.all_to_all(packed, ('x', 'y'), 0, 0)  5.03 us
    ppermute x1, waiting for transfers between devices, body(): mine = lax.ppermute(edge, ('z', 'y', 'core'), ways)  4.93 us
    all_to_all x1, waiting for transfers between devices, body(): slab = lax.all_to_all(packed, ('x', 'y'), 0, 0)  4.79 us
    pallas_call x1, Pallas kernels, body(): pl.pallas_call(back_kernel, out_shape=shape((PIX, C), f32), in_specs=[vme...  4.46 us
    all_to_all x1, starting transfers between devices, body(): sums = lax.all_to_all(sums, ('y', 'x', 'core'), 0, 0)  4.32 us
  transfers between devices with their start and end apart: 10, of which 8 were waited for; matrix products, arithmetic and copies ran while one was open for 2% of the time, Pallas kernels for 14%

profile of v11, /device:TPU:1, one launch (start us, length us, event | category | flops | bytes accessed | tf_op | source)
XLA Modules:
  0.0 86.7 jit_solution(8270524607450075455)
XLA Ops:
  0.6 3.3 %collective-permute-start = (bf16[128,640]{1,0:T(8,128)(2,1)}, bf16[128,640]{1,0:T(8,128)(2,1)S(1)}, u32[]{:S(2)}, u32[]{:S(2)}) collective-permute-start(bf16[128,640]{1,0:T(8,128)(2,1)} %bitcast.12), channel_id=1, source_target_pairs={{0,1},{1,0},{2,3},{3,2},{4,5},{5,4},{6,7},{7,6},{8,9},{9,8},{10,11... | collective-permute-start | bytes 491528 | tf_op jit(solution)/shard_map/ppermute | solution.py:435
  4.0 0.1 collective-permute-start.1
  4.1 1.0 %pad_maximum_fusion.both_ref = bf16[256,640]{1,0:T(8,128)(2,1)S(1)} fusion(bf16[128,640]{1,0:T(8,128)(2,1)} %bitcast.11, bf16[128,640]{1,0:T(8,128)(2,1)} %bitcast.13), kind=kLoop, calls=%fused_computation | loop fusion | flops 655360 | bytes 655360 | tf_op jit(solution)/shard_map/concatenate | solution.py:448
  5.1 0.1 collective-permute-done.feat2_ref
  5.2 0.4 collective-permute-done.1.cot2_ref
  5.6 2.3 %pack.1 = bf16[16,336,128]{2,1,0:T(8,128)(2,1)} custom-call(s32[1]{0:T(128)} %bitcast.core_ref, bf16[256,640]{1,0:T(8,128)(2,1)S(1)} %pad_maximum_fusion.both_ref, bf16[128,640]{1,0:T(8,128)(2,1)S(1)} %collective-permute-done.feat2_ref, bf16[128,640]{1,0:T(8,128)(2,1)S(1)} %collective-permute-done.1.cot2_ref), custom_call_target="tpu_custom_call" | custom-call | flops 268435456 | bytes 2097152 | tf_op jit(solution)/shard_map/pack/pallas_call | solution.py:458
  7.9 5.0 %all-to-all-start = ((bf16[16,336,128]{2,1,0:T(8,128)(2,1)}), bf16[16,336,128]{2,1,0:T(8,128)(2,1)S(1)}, u32[]{:S(2)}, u32[]{:S(2)}) async-start(bf16[16,336,128]{2,1,0:T(8,128)(2,1)} %pack.1), calls=%async_computation | async-start | bytes 2752512 | tf_op jit(solution)/shard_map/all_to_all | solution.py:468
  12.9 0.8 slice_bitcast_fusion
  13.7 1.3 %collective-permute-start.2 = (bf16[32,640]{1,0:T(8,128)(2,1)S(1)}, bf16[32,640]{1,0:T(8,128)(2,1)S(1)}, u32[]{:S(2)}, u32[]{:S(2)}) collective-permute-start(bf16[32,640]{1,0:T(8,128)(2,1)S(1)} %maximum_select_fusion), channel_id=1, source_target_pairs={{0,8},{8,16},{16,24},{24,32},{32,40},{40,48},{48,56},{56,64},{64,7... | collective-permute-start | bytes 122888 | tf_op jit(solution)/shard_map/ppermute | solution.py:456
  15.0 4.9 %collective-permute-done.2.mine_ref = bf16[32,640]{1,0:T(8,128)(2,1)S(1)} collective-permute-done((bf16[32,640]{1,0:T(8,128)(2,1)S(1)}, bf16[32,640]{1,0:T(8,128)(2,1)S(1)}, u32[]{:S(2)}, u32[]{:S(2)}) %collective-permute-start.2) | collective-permute-done | bytes 40992 | tf_op jit(solution)/shard_map/ppermute | solution.py:456
  19.9 5.3 %collective-permute-start.3 = (bf16[32,640]{1,0:T(8,128)(2,1)S(1)}, bf16[32,640]{1,0:T(8,128)(2,1)S(1)}, u32[]{:S(2)}, u32[]{:S(2)}) collective-permute-start(bf16[32,640]{1,0:T(8,128)(2,1)S(1)} %collective-permute-done.2.mine_ref), channel_id=1, source_target_pairs={{0,1},{1,0},{2,3},{3,2},{4,5},{5,4},{6,7},{7,6},{8,9},{9,8},{10,11... | collective-permute-start | bytes 122888 | tf_op jit(solution)/shard_map/ppermute | solution.py:435
  25.2 0.9 %collective-permute-done.3.theirs_ref = bf16[32,640]{1,0:T(8,128)(2,1)S(1)} collective-permute-done((bf16[32,640]{1,0:T(8,128)(2,1)S(1)}, bf16[32,640]{1,0:T(8,128)(2,1)S(1)}, u32[]{:S(2)}, u32[]{:S(2)}) %collective-permute-start.3) | collective-permute-done | bytes 40992 | tf_op jit(solution)/shard_map/ppermute | solution.py:435
  26.0 2.3 %side.1 = (f32[8,640]{1,0:T(8,128)S(1)}, bf16[3,160,640]{2,1,0:T(8,128)(2,1)S(1)}) custom-call(s32[1]{0:T(128)} %bitcast.core_ref, bf16[256,640]{1,0:T(8,128)(2,1)S(1)} %pad_maximum_fusion.both_ref, bf16[128,640]{1,0:T(8,128)(2,1)S(1)} %collective-permute-done.1.cot2_ref, bf16[32,640]{1,0:T(8,128)(2,1)S(1)} %collective-permute-done.2.mine_ref, ...), custom_call_target="tpu_custom_call" | custom-call | tf_op jit(solution)/shard_map/side/pallas_call | solution.py:470
  28.3 0.0 copy-start
  28.3 0.0 copy-start.1
  28.4 4.8 %all-to-all-done.slab_ref.own_ref = bf16[16,336,128]{2,1,0:T(8,128)(2,1)S(1)} async-done(((bf16[16,336,128]{2,1,0:T(8,128)(2,1)}), bf16[16,336,128]{2,1,0:T(8,128)(2,1)S(1)}, u32[]{:S(2)}, u32[]{:S(2)}) %all-to-all-start) | async-done | bytes 1376288 | tf_op jit(solution)/shard_map/all_to_all | solution.py:468
  33.1 0.8 split.1
  33.9 2.4 %collective-permute-start.5 = (bf16[16,336,128]{2,1,0:T(8,128)(2,1)S(1)}, bf16[16,336,128]{2,1,0:T(8,128)(2,1)}, u32[]{:S(2)}, u32[]{:S(2)}) collective-permute-start(bf16[16,336,128]{2,1,0:T(8,128)(2,1)S(1)} %all-to-all-done.slab_ref.own_ref), channel_id=1, source_target_pairs={{0,1},{1,0},{2,3},{3,2},{4,5},{5,4},{6,7},{7,6},{8,9},{9,8},{10,11... | collective-permute-start | bytes 4128776 | tf_op jit(solution)/shard_map/ppermute | solution.py:435
  36.3 8.2 %all-to-all-start.1 = ((bf16[8,96,128]{2,1,0:T(8,128)(2,1)}), bf16[8,96,128]{2,1,0:T(8,128)(2,1)S(1)}, u32[]{:S(2)}, u32[]{:S(2)}) async-start(bf16[8,96,128]{2,1,0:T(8,128)(2,1)} %split.1), calls=%async_computation.1 | async-start | bytes 393216 | tf_op jit(solution)/shard_map/all_to_all | solution.py:492
  44.5 0.0 copy-done
  44.5 0.0 copy-done.1
  44.5 2.3 %collective-permute-start.4 = (f32[8,640]{1,0:T(8,128)S(1)}, f32[8,640]{1,0:T(8,128)S(1)}, u32[]{:S(2)}, u32[]{:S(2)}) collective-permute-start(f32[8,640]{1,0:T(8,128)S(1)} %get-tuple-element.23), channel_id=1, source_target_pairs={{1,2},{3,4},{5,6},{2,1},{4,3},{6,5},{9,10},{11,12},{13,14},{10,9},... | collective-permute-start | bytes 61448 | tf_op jit(solution)/shard_map/ppermute | solution.py:481
  46.8 4.5 %back.1.back_ref = f32[128,640]{1,0:T(8,128)S(1)} custom-call(bf16[3,160,640]{2,1,0:T(8,128)(2,1)S(1)} %get-tuple-element.22.shifted, bf16[3,3,640,640]{3,2,1,0:T(8,128)(2,1)} %w_hbm.3), custom_call_target="tpu_custom_call" | custom-call | flops 943718400 | bytes 7372800 | tf_op jit(solution)/shard_map/back/pallas_call | solution.py:493
  51.3 0.0 collective-permute-done.4.side_ref
  51.3 4.0 %all-to-all-done.1.stat_ref.edge_ref = bf16[8,96,128]{2,1,0:T(8,128)(2,1)S(1)} async-done(((bf16[8,96,128]{2,1,0:T(8,128)(2,1)}), bf16[8,96,128]{2,1,0:T(8,128)(2,1)S(1)}, u32[]{:S(2)}, u32[]{:S(2)}) %all-to-all-start.1) | async-done | bytes 196640 | tf_op jit(solution)/shard_map/all_to_all | solution.py:492
  55.3 1.1 %sums.1 = (f32[8,640]{1,0:T(8,128)S(1)}, f32[128,640]{1,0:T(8,128)S(1)}, f32[8,256]{1,0:T(8,128)S(1)}, f32[32,8,128]{2,1,0:T(8,128)}, f32[640]{0:T(1024)}) custom-call(s32[1]{0:T(128)} %bitcast.core_ref, s32[1]{0:T(128)} %bitcast.1.y_ref, bf16[8,96,128]{2,1,0:T(8,128)(2,1)S(1)} %all-to-all-done.1.stat_ref.edge_ref, ...), custom_call_target="tpu_custom_call" | custom-call | tf_op jit(solution)/shard_map/sums/pallas_call | solution.py:503
  56.4 4.3 %all-to-all-start.2 = ((f32[32,8,128]{2,1,0:T(8,128)}), f32[32,8,128]{2,1,0:T(8,128)S(1)}, u32[]{:S(2)}, u32[]{:S(2)}) async-start(f32[32,8,128]{2,1,0:T(8,128)} %get-tuple-element.24), calls=%async_computation.2 | async-start | bytes 262144 | tf_op jit(solution)/shard_map/all_to_all | solution.py:517
  60.7 0.0 collective-permute-done.5.other_hbm
  60.7 3.9 %terms.1.terms_ref = bf16[8,64,256]{2,1,0:T(8,128)(2,1)S(1)} custom-call(s32[1]{0:T(128)} %bitcast.core_ref, s32[1]{0:T(128)} %bitcast.6.z_ref, bf16[16,336,128]{2,1,0:T(8,128)(2,1)S(1)} %all-to-all-done.slab_ref.own_ref, bf16[16,336,128]{2,1,0:T(8,128)(2,1)} %collective-permute-done.5.other_hbm, bf16[8,96,128]{2,1,0:T(8,128)(2,1)S(1)} %all-to-all-done.1.stat_ref.edge_ref, ...), custom_call_target="tpu_custom_call" | custom-call | flops 943718400 | bytes 4194304 | tf_op jit(solution)/shard_map/terms/pallas_call | solution.py:519
  64.6 3.7 %all-to-all-done.2.sums_ref = f32[32,8,128]{2,1,0:T(8,128)S(1)} async-done(((f32[32,8,128]{2,1,0:T(8,128)}), f32[32,8,128]{2,1,0:T(8,128)S(1)}, u32[]{:S(2)}, u32[]{:S(2)}) %all-to-all-start.2) | async-done | bytes 131104 | tf_op jit(solution)/shard_map/all_to_all | solution.py:517
  68.4 0.1 join.1
  68.5 14.2 %all_to_all.20.got_ref = bf16[8,64,256]{2,1,0:T(8,128)(2,1)S(1)} all-to-all(bf16[8,64,256]{2,1,0:T(8,128)(2,1)S(1)} %join.1), channel_id=1, replica_groups=mesh['z'=8,'y'=4,'x'=4,'core'=2] {'z'}, dimensions={0} | all-to-all | bytes 524288 | tf_op jit(solution)/shard_map/all_to_all | solution.py:551
  82.7 0.1 total.1.own_ref
  82.8 2.0 %collective-permute-start.6 = (f32[8,640]{1,0:T(8,128)S(1)}, f32[8,640]{1,0:T(8,128)S(1)}, u32[]{:S(2)}, u32[]{:S(2)}) collective-permute-start(f32[8,640]{1,0:T(8,128)S(1)} %total.1.own_ref), channel_id=1, source_target_pairs={{0,1},{1,0},{2,3},{3,2},{4,5},{5,4},{6,7},{7,6},{8,9},{9,8},{10,11... | collective-permute-start | bytes 61448 | tf_op jit(solution)/shard_map/ppermute | solution.py:435
  84.8 0.8 gather.1
  85.5 0.1 collective-permute-done.6.other_ref
  85.6 1.1 %final.1 = (bf16[128,640]{1,0:T(8,128)(2,1)}, f32[640]{0:T(1024)}, f32[640]{0:T(1024)}) custom-call(s32[1]{0:T(128)} %bitcast.core_ref, f32[8,640]{1,0:T(8,128)S(1)} %total.1.own_ref, f32[8,640]{1,0:T(8,128)S(1)} %collective-permute-done.6.other_ref, bf16[256,640]{1,0:T(8,128)(2,1)S(1)} %pad_maximum_fusion.both_ref, ...), custom_call_target="tpu_custom_call" | custom-call | tf_op jit(solution)/shard_map/final/pallas_call | solution.py:569
  (4 shorter events, 0.0 us)
Async XLA Ops:
  0.6 4.6 %collective-permute-start = (bf16[128,640]{1,0:T(8,128)(2,1)}, bf16[128,640]{1,0:T(8,128)(2,1)S(1)}, u32[]{:S(2)}, u32[]{:S(2)}) collective-permute-start(bf16[128,640]{1,0:T(8,128)(2,1)} %bitcast.12), channel_id=1, source_target_pairs={{0,1},{1,0},{2,3},{3,2},{4,5},{5,4},{6,7},{7,6},{8,9},{9,8},{10,11... | collective-permute-start | bytes 491528 | tf_op jit(solution)/shard_map/ppermute | solution.py:435
  4.0 1.6 %collective-permute-start.1 = (bf16[128,640]{1,0:T(8,128)(2,1)}, bf16[128,640]{1,0:T(8,128)(2,1)S(1)}, u32[]{:S(2)}, u32[]{:S(2)}) collective-permute-start(bf16[128,640]{1,0:T(8,128)(2,1)} %bitcast.10), channel_id=1, source_target_pairs={{0,1},{1,0},{2,3},{3,2},{4,5},{5,4},{6,7},{7,6},{8,9},{9,8},{10,11... | collective-permute-start | bytes 491528 | tf_op jit(solution)/shard_map/ppermute | solution.py:435
  7.9 25.3 %all-to-all-start = ((bf16[16,336,128]{2,1,0:T(8,128)(2,1)}), bf16[16,336,128]{2,1,0:T(8,128)(2,1)S(1)}, u32[]{:S(2)}, u32[]{:S(2)}) async-start(bf16[16,336,128]{2,1,0:T(8,128)(2,1)} %pack.1), calls=%async_computation | async-start | bytes 2752512 | tf_op jit(solution)/shard_map/all_to_all | solution.py:468
  13.7 6.2 %collective-permute-start.2 = (bf16[32,640]{1,0:T(8,128)(2,1)S(1)}, bf16[32,640]{1,0:T(8,128)(2,1)S(1)}, u32[]{:S(2)}, u32[]{:S(2)}) collective-permute-start(bf16[32,640]{1,0:T(8,128)(2,1)S(1)} %maximum_select_fusion), channel_id=1, source_target_pairs={{0,8},{8,16},{16,24},{24,32},{32,40},{40,48},{48,56},{56,64},{64,7... | collective-permute-start | bytes 122888 | tf_op jit(solution)/shard_map/ppermute | solution.py:456
  19.9 6.1 %collective-permute-start.3 = (bf16[32,640]{1,0:T(8,128)(2,1)S(1)}, bf16[32,640]{1,0:T(8,128)(2,1)S(1)}, u32[]{:S(2)}, u32[]{:S(2)}) collective-permute-start(bf16[32,640]{1,0:T(8,128)(2,1)S(1)} %collective-permute-done.2.mine_ref), channel_id=1, source_target_pairs={{0,1},{1,0},{2,3},{3,2},{4,5},{5,4},{6,7},{7,6},{8,9},{9,8},{10,11... | collective-permute-start | bytes 122888 | tf_op jit(solution)/shard_map/ppermute | solution.py:435
  28.3 16.2 %copy-start = (f32[640]{0:T(1024)S(1)}, f32[640]{0:T(1024)}, u32[]{:S(2)}) copy-start(f32[640]{0:T(1024)} %param.8) | copy-start | bytes 7684
  28.3 16.2 %copy-start.1 = (f32[640]{0:T(1024)S(1)}, f32[640]{0:T(1024)}, u32[]{:S(2)}) copy-start(f32[640]{0:T(1024)} %param.9) | copy-start | bytes 7684
  33.9 26.8 %collective-permute-start.5 = (bf16[16,336,128]{2,1,0:T(8,128)(2,1)S(1)}, bf16[16,336,128]{2,1,0:T(8,128)(2,1)}, u32[]{:S(2)}, u32[]{:S(2)}) collective-permute-start(bf16[16,336,128]{2,1,0:T(8,128)(2,1)S(1)} %all-to-all-done.slab_ref.own_ref), channel_id=1, source_target_pairs={{0,1},{1,0},{2,3},{3,2},{4,5},{5,4},{6,7},{7,6},{8,9},{9,8},{10,11... | collective-permute-start | bytes 4128776 | tf_op jit(solution)/shard_map/ppermute | solution.py:435
  36.3 19.0 %all-to-all-start.1 = ((bf16[8,96,128]{2,1,0:T(8,128)(2,1)}), bf16[8,96,128]{2,1,0:T(8,128)(2,1)S(1)}, u32[]{:S(2)}, u32[]{:S(2)}) async-start(bf16[8,96,128]{2,1,0:T(8,128)(2,1)} %split.1), calls=%async_computation.1 | async-start | bytes 393216 | tf_op jit(solution)/shard_map/all_to_all | solution.py:492
  44.5 6.7 %collective-permute-start.4 = (f32[8,640]{1,0:T(8,128)S(1)}, f32[8,640]{1,0:T(8,128)S(1)}, u32[]{:S(2)}, u32[]{:S(2)}) collective-permute-start(f32[8,640]{1,0:T(8,128)S(1)} %get-tuple-element.23), channel_id=1, source_target_pairs={{1,2},{3,4},{5,6},{2,1},{4,3},{6,5},{9,10},{11,12},{13,14},{10,9},... | collective-permute-start | bytes 61448 | tf_op jit(solution)/shard_map/ppermute | solution.py:481
  56.4 12.0 %all-to-all-start.2 = ((f32[32,8,128]{2,1,0:T(8,128)}), f32[32,8,128]{2,1,0:T(8,128)S(1)}, u32[]{:S(2)}, u32[]{:S(2)}) async-start(f32[32,8,128]{2,1,0:T(8,128)} %get-tuple-element.24), calls=%async_computation.2 | async-start | bytes 262144 | tf_op jit(solution)/shard_map/all_to_all | solution.py:517
  82.8 2.8 %collective-permute-start.6 = (f32[8,640]{1,0:T(8,128)S(1)}, f32[8,640]{1,0:T(8,128)S(1)}, u32[]{:S(2)}, u32[]{:S(2)}) collective-permute-start(f32[8,640]{1,0:T(8,128)S(1)} %total.1.own_ref), channel_id=1, source_target_pairs={{0,1},{1,0},{2,3},{3,2},{4,5},{5,4},{6,7},{7,6},{8,9},{9,8},{10,11... | collective-permute-start | bytes 61448 | tf_op jit(solution)/shard_map/ppermute | solution.py:435

commit v12 on v11

--- a/solution.py
+++ b/solution.py
@@ -265,8 +265,8 @@
     out_ref[...] = total
 
 
-def sums_kernel(core_ref, y_ref, stat_ref, both_ref, back_ref, side_ref, gain_ref, shift_ref,
-                row_ref, da_ref, par_ref, out_ref, bias_ref):
+def sums_kernel(core_ref, stat_ref, both_ref, back_ref, side_ref, gain_ref, shift_ref,
+                row_ref, da_ref, out_ref, bias_ref):
     mean, squares, bias = merge_pieces(stat_ref[:, :S_ROWS], PEERS * CHIP)
     bias_ref[...] = unfold(bias).reshape(C)
     groups = group_matrix()
@@ -275,9 +275,7 @@
     mean, rstd = both[0:1], both[1:2]
     gain, shift = gain_ref[...], shift_ref[...]
     row = lax.broadcasted_iota(jnp.int32, (8, C), 0)
-    row_ref[...] = jnp.where(row == 0, mean, rstd)
-    table = jnp.where(row == 0, mean, jnp.where(row == 1, rstd * gain, jnp.where(row == 2, shift, 0.0)))
-    par_ref[...] = exact_dot(table, pick(term_columns(y_ref[0])), 0)
+    row_ref[...] = jnp.where(row == 0, mean, jnp.where(row == 1, rstd, jnp.where(row == 2, rstd * gain, shift)))
     xhat = (both_ref[:PIX].astype(f32) - mean) * rstd
     act = xhat * gain + shift
     sig = sigmoid(act)
@@ -293,9 +291,10 @@
             out_ref[p] = block
 
 
-def terms_kernel(core_ref, z_ref, own_ref, other_hbm, edge_ref, par_ref, out_ref,
+def terms_kernel(core_ref, y_ref, z_ref, own_ref, other_hbm, edge_ref, row_ref, out_ref,
                  hid0, hid1, hid2, hid3, strips, cot3, rest, totals, other_ref, sem):
     hidden = (hid0, hid1, hid2, hid3)
+    table = exact_dot(row_ref[...], pick(term_columns(y_ref[0])), 0)
     copies = fetch(((other_hbm.at[:, :F_ROWS, :], other_ref),), sem)
     core = core_ref[0]
 
@@ -303,7 +302,7 @@
         xx, y = peer // NY, peer % NY
 
         def silu(x, lanes):
-            a = (x.astype(f32) - par_ref[0:1, lanes]) * par_ref[1:2, lanes] + par_ref[2:3, lanes]
+            a = (x.astype(f32) - table[0:1, lanes]) * table[2:3, lanes] + table[3:4, lanes]
             return a * sigmoid(a)
 
         main = silu(block[:128], slice(0, 128)).astype(bf16)
@@ -500,26 +499,25 @@
         cost_estimate=pl.CostEstimate(flops=2 * PIX * 9 * C * C, bytes_accessed=18 * C * C, transcendentals=0),
         name="back",
     )(shifted, conv_weight)
-    row, da, table, sums, bias_grad = pl.pallas_call(
+    row, da, sums, bias_grad = pl.pallas_call(
         sums_kernel,
         out_shape=(
             shape((8, C), f32),
             shape((PIX, C), f32),
-            shape((8, 256), f32),
             shape((2 * PEERS, 8, 128), f32),
             shape((C,), f32),
         ),
-        in_specs=[smem()] * 2 + [vmem()] * 6,
-        out_specs=(vmem(),) * 5,
+        in_specs=[smem()] + [vmem()] * 6,
+        out_specs=(vmem(),) * 4,
         compiler_params=params(),
         name="sums",
-    )(at_core, at_y, edges, both, back, side, gain, shift)
+    )(at_core, edges, both, back, side, gain, shift)
     sums = lax.all_to_all(sums, ("y", "x", "core"), 0, 0)
 
     terms = pl.pallas_call(
         terms_kernel,
         out_shape=shape((NZ, W_ROWS, 256), bf16),
-        in_specs=[smem()] * 2 + [vmem(), hbm(), vmem(), vmem()],
+        in_specs=[smem()] * 3 + [vmem(), hbm(), vmem(), vmem()],
         out_specs=vmem(),
         scratch_shapes=[
             pltpu.VMEM((TR * 128, 256), bf16),
@@ -538,7 +536,7 @@
             flops=2 * PIX * 9 * C * C, bytes_accessed=4 << 20, transcendentals=ROWS * 128 * 256
         ),
         name="terms",
-    )(at_core, at_z, slab, slab_other, edges, table)
+    )(at_core, at_y, at_z, slab, slab_other, edges, row)
 
     joined = pl.pallas_call(
         join_kernel,

time: 87.3 us -> 87.2 us (level)
  transfers between devices with their start and end apart: 10 -> 10, of which waited for: 8 -> 8; matrix products, arithmetic and copies ran while one was open for 2% -> 2% of each run, Pallas kernels for 14% -> 15%
where the time goes in v12:
time: 87.2 us; the launch traced here: 86.7 us
  starting transfers between devices  34.2 us (39%)
  waiting for transfers between devices  18.3 us (21%)
  Pallas kernels  17.4 us (20%)
  blocking collectives  14.2 us (16%)
  other arithmetic  1.04 us (1%)
    all_to_all x1, blocking collectives, body(): joined = lax.all_to_all(joined, 'z', 0, 0)  14.2 us
    ppermute x5, starting transfers between devices, flip(): return lax.ppermute(value, 'core', [(0, 1), (1, 0)])  13.1 us
    all_to_all x1, starting transfers between devices, body(): edges = lax.all_to_all(edges, 'z', 0, 0)  8.19 us
    all_to_all x1, starting transfers between devices, body(): slab = lax.all_to_all(packed, ('x', 'y'), 0, 0)  5.03 us
    ppermute x1, waiting for transfers between devices, body(): mine = lax.ppermute(edge, ('z', 'y', 'core'), ways)  4.93 us
    all_to_all x1, waiting for transfers between devices, body(): slab = lax.all_to_all(packed, ('x', 'y'), 0, 0)  4.79 us
    pallas_call x1, Pallas kernels, body(): pl.pallas_call(back_kernel, out_shape=shape((PIX, C), f32), in_specs=[vme...  4.46 us
    pallas_call x1, Pallas kernels, body(): pl.pallas_call(terms_kernel, out_shape=shape((NZ, W_ROWS, 256), bf16), in...  4.45 us
  transfers between devices with their start and end apart: 10, of which 8 were waited for; matrix products, arithmetic and copies ran while one was open for 2% of the time, Pallas kernels for 15%

profile of v12, /device:TPU:1, one launch (start us, length us, event | category | flops | bytes accessed | tf_op | source)
XLA Modules:
  0.0 86.7 jit_solution(17546400174264285657)
XLA Ops:
  0.6 3.3 %collective-permute-start = (bf16[128,640]{1,0:T(8,128)(2,1)}, bf16[128,640]{1,0:T(8,128)(2,1)S(1)}, u32[]{:S(2)}, u32[]{:S(2)}) collective-permute-start(bf16[128,640]{1,0:T(8,128)(2,1)} %bitcast.12), channel_id=1, source_target_pairs={{0,1},{1,0},{2,3},{3,2},{4,5},{5,4},{6,7},{7,6},{8,9},{9,8},{10,11... | collective-permute-start | bytes 491528 | tf_op jit(solution)/shard_map/ppermute | solution.py:434
  4.0 0.1 collective-permute-start.1
  4.1 1.0 %pad_maximum_fusion.both_ref = bf16[256,640]{1,0:T(8,128)(2,1)S(1)} fusion(bf16[128,640]{1,0:T(8,128)(2,1)} %bitcast.11, bf16[128,640]{1,0:T(8,128)(2,1)} %bitcast.13), kind=kLoop, calls=%fused_computation | loop fusion | flops 655360 | bytes 655360 | tf_op jit(solution)/shard_map/concatenate | solution.py:447
  5.1 0.1 collective-permute-done.feat2_ref
  5.2 0.4 collective-permute-done.1.cot2_ref
  5.6 2.3 %pack.1 = bf16[16,336,128]{2,1,0:T(8,128)(2,1)} custom-call(s32[1]{0:T(128)} %bitcast.core_ref, bf16[256,640]{1,0:T(8,128)(2,1)S(1)} %pad_maximum_fusion.both_ref, bf16[128,640]{1,0:T(8,128)(2,1)S(1)} %collective-permute-done.feat2_ref, bf16[128,640]{1,0:T(8,128)(2,1)S(1)} %collective-permute-done.1.cot2_ref), custom_call_target="tpu_custom_call" | custom-call | flops 268435456 | bytes 2097152 | tf_op jit(solution)/shard_map/pack/pallas_call | solution.py:457
  7.9 5.0 %all-to-all-start = ((bf16[16,336,128]{2,1,0:T(8,128)(2,1)}), bf16[16,336,128]{2,1,0:T(8,128)(2,1)S(1)}, u32[]{:S(2)}, u32[]{:S(2)}) async-start(bf16[16,336,128]{2,1,0:T(8,128)(2,1)} %pack.1), calls=%async_computation | async-start | bytes 2752512 | tf_op jit(solution)/shard_map/all_to_all | solution.py:467
  12.9 0.8 slice_bitcast_fusion
  13.7 1.3 %collective-permute-start.2 = (bf16[32,640]{1,0:T(8,128)(2,1)S(1)}, bf16[32,640]{1,0:T(8,128)(2,1)S(1)}, u32[]{:S(2)}, u32[]{:S(2)}) collective-permute-start(bf16[32,640]{1,0:T(8,128)(2,1)S(1)} %maximum_select_fusion), channel_id=1, source_target_pairs={{0,8},{8,16},{16,24},{24,32},{32,40},{40,48},{48,56},{56,64},{64,7... | collective-permute-start | bytes 122888 | tf_op jit(solution)/shard_map/ppermute | solution.py:455
  15.0 4.9 %collective-permute-done.2.mine_ref = bf16[32,640]{1,0:T(8,128)(2,1)S(1)} collective-permute-done((bf16[32,640]{1,0:T(8,128)(2,1)S(1)}, bf16[32,640]{1,0:T(8,128)(2,1)S(1)}, u32[]{:S(2)}, u32[]{:S(2)}) %collective-permute-start.2) | collective-permute-done | bytes 40992 | tf_op jit(solution)/shard_map/ppermute | solution.py:455
  19.9 5.3 %collective-permute-start.3 = (bf16[32,640]{1,0:T(8,128)(2,1)S(1)}, bf16[32,640]{1,0:T(8,128)(2,1)S(1)}, u32[]{:S(2)}, u32[]{:S(2)}) collective-permute-start(bf16[32,640]{1,0:T(8,128)(2,1)S(1)} %collective-permute-done.2.mine_ref), channel_id=1, source_target_pairs={{0,1},{1,0},{2,3},{3,2},{4,5},{5,4},{6,7},{7,6},{8,9},{9,8},{10,11... | collective-permute-start | bytes 122888 | tf_op jit(solution)/shard_map/ppermute | solution.py:434
  25.2 0.9 %collective-permute-done.3.theirs_ref = bf16[32,640]{1,0:T(8,128)(2,1)S(1)} collective-permute-done((bf16[32,640]{1,0:T(8,128)(2,1)S(1)}, bf16[32,640]{1,0:T(8,128)(2,1)S(1)}, u32[]{:S(2)}, u32[]{:S(2)}) %collective-permute-start.3) | collective-permute-done | bytes 40992 | tf_op jit(solution)/shard_map/ppermute | solution.py:434
  26.0 2.3 %side.1 = (f32[8,640]{1,0:T(8,128)S(1)}, bf16[3,160,640]{2,1,0:T(8,128)(2,1)S(1)}) custom-call(s32[1]{0:T(128)} %bitcast.core_ref, bf16[256,640]{1,0:T(8,128)(2,1)S(1)} %pad_maximum_fusion.both_ref, bf16[128,640]{1,0:T(8,128)(2,1)S(1)} %collective-permute-done.1.cot2_ref, bf16[32,640]{1,0:T(8,128)(2,1)S(1)} %collective-permute-done.2.mine_ref, ...), custom_call_target="tpu_custom_call" | custom-call | tf_op jit(solution)/shard_map/side/pallas_call | solution.py:469
  28.3 0.0 copy-start
  28.3 0.0 copy-start.1
  28.4 4.8 %all-to-all-done.slab_ref.own_ref = bf16[16,336,128]{2,1,0:T(8,128)(2,1)S(1)} async-done(((bf16[16,336,128]{2,1,0:T(8,128)(2,1)}), bf16[16,336,128]{2,1,0:T(8,128)(2,1)S(1)}, u32[]{:S(2)}, u32[]{:S(2)}) %all-to-all-start) | async-done | bytes 1376288 | tf_op jit(solution)/shard_map/all_to_all | solution.py:467
  33.1 0.8 split.1
  33.9 2.4 %collective-permute-start.5 = (bf16[16,336,128]{2,1,0:T(8,128)(2,1)S(1)}, bf16[16,336,128]{2,1,0:T(8,128)(2,1)}, u32[]{:S(2)}, u32[]{:S(2)}) collective-permute-start(bf16[16,336,128]{2,1,0:T(8,128)(2,1)S(1)} %all-to-all-done.slab_ref.own_ref), channel_id=1, source_target_pairs={{0,1},{1,0},{2,3},{3,2},{4,5},{5,4},{6,7},{7,6},{8,9},{9,8},{10,11... | collective-permute-start | bytes 4128776 | tf_op jit(solution)/shard_map/ppermute | solution.py:434
  36.3 8.2 %all-to-all-start.1 = ((bf16[8,96,128]{2,1,0:T(8,128)(2,1)}), bf16[8,96,128]{2,1,0:T(8,128)(2,1)S(1)}, u32[]{:S(2)}, u32[]{:S(2)}) async-start(bf16[8,96,128]{2,1,0:T(8,128)(2,1)} %split.1), calls=%async_computation.1 | async-start | bytes 393216 | tf_op jit(solution)/shard_map/all_to_all | solution.py:491
  44.5 0.0 copy-done
  44.5 0.0 copy-done.1
  44.5 2.3 %collective-permute-start.4 = (f32[8,640]{1,0:T(8,128)S(1)}, f32[8,640]{1,0:T(8,128)S(1)}, u32[]{:S(2)}, u32[]{:S(2)}) collective-permute-start(f32[8,640]{1,0:T(8,128)S(1)} %get-tuple-element.22), channel_id=1, source_target_pairs={{1,2},{3,4},{5,6},{2,1},{4,3},{6,5},{9,10},{11,12},{13,14},{10,9},... | collective-permute-start | bytes 61448 | tf_op jit(solution)/shard_map/ppermute | solution.py:480
  46.8 4.5 %back.1.back_ref = f32[128,640]{1,0:T(8,128)S(1)} custom-call(bf16[3,160,640]{2,1,0:T(8,128)(2,1)S(1)} %get-tuple-element.21.shifted, bf16[3,3,640,640]{3,2,1,0:T(8,128)(2,1)} %w_hbm.3), custom_call_target="tpu_custom_call" | custom-call | flops 943718400 | bytes 7372800 | tf_op jit(solution)/shard_map/back/pallas_call | solution.py:492
  51.3 0.0 collective-permute-done.4.side_ref
  51.3 4.0 %all-to-all-done.1.stat_ref.edge_ref = bf16[8,96,128]{2,1,0:T(8,128)(2,1)S(1)} async-done(((bf16[8,96,128]{2,1,0:T(8,128)(2,1)}), bf16[8,96,128]{2,1,0:T(8,128)(2,1)S(1)}, u32[]{:S(2)}, u32[]{:S(2)}) %all-to-all-start.1) | async-done | bytes 196640 | tf_op jit(solution)/shard_map/all_to_all | solution.py:491
  55.3 1.1 %sums.1 = (f32[8,640]{1,0:T(8,128)S(1)}, f32[128,640]{1,0:T(8,128)S(1)}, f32[32,8,128]{2,1,0:T(8,128)}, f32[640]{0:T(1024)}) custom-call(s32[1]{0:T(128)} %bitcast.core_ref, bf16[8,96,128]{2,1,0:T(8,128)(2,1)S(1)} %all-to-all-done.1.stat_ref.edge_ref, bf16[256,640]{1,0:T(8,128)(2,1)S(1)} %pad_maximum_fusion.both_ref, f32[128,640]{1,0:T(8,128)S(1)} %back.1.back_ref, ...), custom_call_target="tpu_custom_call" | custom-call | tf_op jit(solution)/shard_map/sums/pallas_call | solution.py:502
  56.4 4.3 %all-to-all-start.2 = ((f32[32,8,128]{2,1,0:T(8,128)}), f32[32,8,128]{2,1,0:T(8,128)S(1)}, u32[]{:S(2)}, u32[]{:S(2)}) async-start(f32[32,8,128]{2,1,0:T(8,128)} %get-tuple-element.23), calls=%async_computation.2 | async-start | bytes 262144 | tf_op jit(solution)/shard_map/all_to_all | solution.py:515
  60.7 0.0 collective-permute-done.5.other_hbm
  60.7 4.4 %terms.1.terms_ref = bf16[8,64,256]{2,1,0:T(8,128)(2,1)S(1)} custom-call(s32[1]{0:T(128)} %bitcast.core_ref, s32[1]{0:T(128)} %bitcast.6.y_ref, s32[1]{0:T(128)} %bitcast.5.z_ref, bf16[16,336,128]{2,1,0:T(8,128)(2,1)S(1)} %all-to-all-done.slab_ref.own_ref, bf16[16,336,128]{2,1,0:T(8,128)(2,1)} %collective-permute-done.5.other_hbm, ...), custom_call_target="tpu_custom_call" | custom-call | flops 943718400 | bytes 4194304 | tf_op jit(solution)/shard_map/terms/pallas_call | solution.py:517
  65.2 3.2 %all-to-all-done.2.sums_ref = f32[32,8,128]{2,1,0:T(8,128)S(1)} async-done(((f32[32,8,128]{2,1,0:T(8,128)}), f32[32,8,128]{2,1,0:T(8,128)S(1)}, u32[]{:S(2)}, u32[]{:S(2)}) %all-to-all-start.2) | async-done | bytes 131104 | tf_op jit(solution)/shard_map/all_to_all | solution.py:515
  68.4 0.1 join.1
  68.5 14.2 %all_to_all.20.got_ref = bf16[8,64,256]{2,1,0:T(8,128)(2,1)S(1)} all-to-all(bf16[8,64,256]{2,1,0:T(8,128)(2,1)S(1)} %join.1), channel_id=1, replica_groups=mesh['z'=8,'y'=4,'x'=4,'core'=2] {'z'}, dimensions={0} | all-to-all | bytes 524288 | tf_op jit(solution)/shard_map/all_to_all | solution.py:549
  82.7 0.1 total.1.own_ref
  82.8 2.0 %collective-permute-start.6 = (f32[8,640]{1,0:T(8,128)S(1)}, f32[8,640]{1,0:T(8,128)S(1)}, u32[]{:S(2)}, u32[]{:S(2)}) collective-permute-start(f32[8,640]{1,0:T(8,128)S(1)} %total.1.own_ref), channel_id=1, source_target_pairs={{0,1},{1,0},{2,3},{3,2},{4,5},{5,4},{6,7},{7,6},{8,9},{9,8},{10,11... | collective-permute-start | bytes 61448 | tf_op jit(solution)/shard_map/ppermute | solution.py:434
  84.8 0.8 gather.1
  85.5 0.1 collective-permute-done.6.other_ref
  85.6 1.1 %final.1 = (bf16[128,640]{1,0:T(8,128)(2,1)}, f32[640]{0:T(1024)}, f32[640]{0:T(1024)}) custom-call(s32[1]{0:T(128)} %bitcast.core_ref, f32[8,640]{1,0:T(8,128)S(1)} %total.1.own_ref, f32[8,640]{1,0:T(8,128)S(1)} %collective-permute-done.6.other_ref, bf16[256,640]{1,0:T(8,128)(2,1)S(1)} %pad_maximum_fusion.both_ref, ...), custom_call_target="tpu_custom_call" | custom-call | tf_op jit(solution)/shard_map/final/pallas_call | solution.py:567
  (4 shorter events, 0.0 us)
Async XLA Ops:
  0.6 4.6 %collective-permute-start = (bf16[128,640]{1,0:T(8,128)(2,1)}, bf16[128,640]{1,0:T(8,128)(2,1)S(1)}, u32[]{:S(2)}, u32[]{:S(2)}) collective-permute-start(bf16[128,640]{1,0:T(8,128)(2,1)} %bitcast.12), channel_id=1, source_target_pairs={{0,1},{1,0},{2,3},{3,2},{4,5},{5,4},{6,7},{7,6},{8,9},{9,8},{10,11... | collective-permute-start | bytes 491528 | tf_op jit(solution)/shard_map/ppermute | solution.py:434
  4.0 1.6 %collective-permute-start.1 = (bf16[128,640]{1,0:T(8,128)(2,1)}, bf16[128,640]{1,0:T(8,128)(2,1)S(1)}, u32[]{:S(2)}, u32[]{:S(2)}) collective-permute-start(bf16[128,640]{1,0:T(8,128)(2,1)} %bitcast.10), channel_id=1, source_target_pairs={{0,1},{1,0},{2,3},{3,2},{4,5},{5,4},{6,7},{7,6},{8,9},{9,8},{10,11... | collective-permute-start | bytes 491528 | tf_op jit(solution)/shard_map/ppermute | solution.py:434
  7.9 25.3 %all-to-all-start = ((bf16[16,336,128]{2,1,0:T(8,128)(2,1)}), bf16[16,336,128]{2,1,0:T(8,128)(2,1)S(1)}, u32[]{:S(2)}, u32[]{:S(2)}) async-start(bf16[16,336,128]{2,1,0:T(8,128)(2,1)} %pack.1), calls=%async_computation | async-start | bytes 2752512 | tf_op jit(solution)/shard_map/all_to_all | solution.py:467
  13.7 6.2 %collective-permute-start.2 = (bf16[32,640]{1,0:T(8,128)(2,1)S(1)}, bf16[32,640]{1,0:T(8,128)(2,1)S(1)}, u32[]{:S(2)}, u32[]{:S(2)}) collective-permute-start(bf16[32,640]{1,0:T(8,128)(2,1)S(1)} %maximum_select_fusion), channel_id=1, source_target_pairs={{0,8},{8,16},{16,24},{24,32},{32,40},{40,48},{48,56},{56,64},{64,7... | collective-permute-start | bytes 122888 | tf_op jit(solution)/shard_map/ppermute | solution.py:455
  19.9 6.1 %collective-permute-start.3 = (bf16[32,640]{1,0:T(8,128)(2,1)S(1)}, bf16[32,640]{1,0:T(8,128)(2,1)S(1)}, u32[]{:S(2)}, u32[]{:S(2)}) collective-permute-start(bf16[32,640]{1,0:T(8,128)(2,1)S(1)} %collective-permute-done.2.mine_ref), channel_id=1, source_target_pairs={{0,1},{1,0},{2,3},{3,2},{4,5},{5,4},{6,7},{7,6},{8,9},{9,8},{10,11... | collective-permute-start | bytes 122888 | tf_op jit(solution)/shard_map/ppermute | solution.py:434
  28.3 16.2 %copy-start = (f32[640]{0:T(1024)S(1)}, f32[640]{0:T(1024)}, u32[]{:S(2)}) copy-start(f32[640]{0:T(1024)} %param.8) | copy-start | bytes 7684
  28.3 16.2 %copy-start.1 = (f32[640]{0:T(1024)S(1)}, f32[640]{0:T(1024)}, u32[]{:S(2)}) copy-start(f32[640]{0:T(1024)} %param.9) | copy-start | bytes 7684
  33.9 26.8 %collective-permute-start.5 = (bf16[16,336,128]{2,1,0:T(8,128)(2,1)S(1)}, bf16[16,336,128]{2,1,0:T(8,128)(2,1)}, u32[]{:S(2)}, u32[]{:S(2)}) collective-permute-start(bf16[16,336,128]{2,1,0:T(8,128)(2,1)S(1)} %all-to-all-done.slab_ref.own_ref), channel_id=1, source_target_pairs={{0,1},{1,0},{2,3},{3,2},{4,5},{5,4},{6,7},{7,6},{8,9},{9,8},{10,11... | collective-permute-start | bytes 4128776 | tf_op jit(solution)/shard_map/ppermute | solution.py:434
  36.3 19.0 %all-to-all-start.1 = ((bf16[8,96,128]{2,1,0:T(8,128)(2,1)}), bf16[8,96,128]{2,1,0:T(8,128)(2,1)S(1)}, u32[]{:S(2)}, u32[]{:S(2)}) async-start(bf16[8,96,128]{2,1,0:T(8,128)(2,1)} %split.1), calls=%async_computation.1 | async-start | bytes 393216 | tf_op jit(solution)/shard_map/all_to_all | solution.py:491
  44.5 6.7 %collective-permute-start.4 = (f32[8,640]{1,0:T(8,128)S(1)}, f32[8,640]{1,0:T(8,128)S(1)}, u32[]{:S(2)}, u32[]{:S(2)}) collective-permute-start(f32[8,640]{1,0:T(8,128)S(1)} %get-tuple-element.22), channel_id=1, source_target_pairs={{1,2},{3,4},{5,6},{2,1},{4,3},{6,5},{9,10},{11,12},{13,14},{10,9},... | collective-permute-start | bytes 61448 | tf_op jit(solution)/shard_map/ppermute | solution.py:480
  56.4 11.9 %all-to-all-start.2 = ((f32[32,8,128]{2,1,0:T(8,128)}), f32[32,8,128]{2,1,0:T(8,128)S(1)}, u32[]{:S(2)}, u32[]{:S(2)}) async-start(f32[32,8,128]{2,1,0:T(8,128)} %get-tuple-element.23), calls=%async_computation.2 | async-start | bytes 262144 | tf_op jit(solution)/shard_map/all_to_all | solution.py:515
  82.8 2.8 %collective-permute-start.6 = (f32[8,640]{1,0:T(8,128)S(1)}, f32[8,640]{1,0:T(8,128)S(1)}, u32[]{:S(2)}, u32[]{:S(2)}) collective-permute-start(f32[8,640]{1,0:T(8,128)S(1)} %total.1.own_ref), channel_id=1, source_target_pairs={{0,1},{1,0},{2,3},{3,2},{4,5},{5,4},{6,7},{7,6},{8,9},{9,8},{10,11... | collective-permute-start | bytes 61448 | tf_op jit(solution)/shard_map/ppermute | solution.py:434
